TPU v7x, 32 devices: a whole 2x2x4 slice. The times are simulated.
32 devices in a mesh: dp: 8 (over z, y), tensor: 4 (over x, core).
Axes of the slice: x: 2, y: 2, z: 4, core: 2. Of those that a mesh axis runs over, the one named last changes fastest.
Arguments:
- tokens: bfloat16 [4096, 768], P('dp'), may hold values from -6 to 6
- w_qkv: bfloat16 [3, 768, 768], P(None, None, 'tensor'), may hold values from -0.21875 to 0.21875
- bias_qv: float32 [2, 768], P(None, 'tensor'), may hold values from -3 to 3
- w_out: bfloat16 [768, 768], P('tensor'), may hold values from -0.875 to 0.875
- bias_out: float32 [768], replicated, may hold values from -3 to 3
- gain_one: float32 [768], replicated, may hold values from 0.25 to 1.75
- shift_one: float32 [768], replicated, may hold values from -3 to 3
- w_up: bfloat16 [768, 3072], P(None, 'tensor'), may hold values from -0.21875 to 0.21875
- bias_up: float32 [3072], P('tensor'), may hold values from -3 to 3
- w_down: bfloat16 [3072, 768], P('tensor'), may hold values from -0.109375 to 0.109375
- bias_down: float32 [768], replicated, may hold values from -3 to 3
- gain_two: float32 [768], replicated, may hold values from 0.25 to 1.75
- shift_two: float32 [768], replicated, may hold values from -3 to 3
- cotangent: bfloat16 [4096, 768], P('dp'), may hold values from -6 to 6
- lengths: int32 [8], P('dp'), may hold values from 128 to 512, as said below
Outputs:
- output: bfloat16 [4096, 768], P('dp')
- grad_tokens: bfloat16 [4096, 768], P('dp')
- grad_w_qkv: float32 [3, 768, 768], P(None, 'dp', 'tensor')
- grad_bias_qv: float32 [2, 768], P(None, ('tensor', 'dp'))
- grad_w_out: float32 [768, 768], P('tensor', 'dp')
- grad_bias_out: float32 [768], P('dp')
- grad_gain_one: float32 [768], P('dp')
- grad_shift_one: float32 [768], P('dp')
- grad_w_up: float32 [768, 3072], P('dp', 'tensor')
- grad_bias_up: float32 [3072], P(('tensor', 'dp'))
- grad_w_down: float32 [3072, 768], P('tensor', 'dp')
- grad_bias_down: float32 [768], P('dp')
- grad_gain_two: float32 [768], P('dp')
- grad_shift_two: float32 [768], P('dp')
Inputs may be any that keep to these rules, and one draw needn't show every extreme that they name: `lengths`: every value is at least 128; some sequence is exactly 512 long.
All inputs are finite; a program needn't handle non-finite values.
Results may differ from a plain program's by a relative error of at most 0.02.
The roundings to bfloat16 on the way count: a program that leaves them out, or rounds other values in their place, can miss the bound.
Values may be sent and summed in bfloat16 or wider, within the bound.
No kernel may reach another device: no remote copies, remote signals or barrier semaphores. Data moves between devices by JAX's collectives and lax.ppermute only.
A program may use at most 64 MiB of HBM per device.

v0:
```python
from functools import partial

import jax
import jax.numpy as jnp
from jax import lax
from jax.sharding import PartitionSpec as P

HEAD_DIM = 64


norm_epsilon = 1e-05


def normalize(resid):
    center = resid - jnp.mean(resid, -1, keepdims=True)
    inverse = lax.rsqrt(jnp.mean(center * center, -1, keepdims=True) + norm_epsilon)
    return (center * inverse, inverse)


def norm_back(grad_norm, normed, inverse):
    mean_grad = jnp.mean(grad_norm, -1, keepdims=True)
    mean_proj = jnp.mean(grad_norm * normed, -1, keepdims=True)
    return inverse * (grad_norm - mean_grad - normed * mean_proj)


def on_device(
    tokens,
    w_qkv,
    bias_qv,
    w_out,
    bias_out,
    gain_one,
    shift_one,
    w_up,
    bias_up,
    w_down,
    bias_down,
    gain_two,
    shift_two,
    cotangent,
    lengths,
):
    seq_count = lengths.shape[0]
    row_count = tokens.shape[0]
    seq_span = row_count // seq_count
    local_width = w_qkv.shape[2]
    heads_here = local_width // HEAD_DIM
    score_scale = HEAD_DIM ** (-0.5)
    share_rows = row_count // lax.axis_size("tensor")
    row_start = lax.axis_index("tensor") * share_rows

    def own_rows(full):
        return lax.dynamic_slice_in_dim(full, row_start, share_rows, 0)

    position = lax.broadcasted_iota(jnp.int32, (seq_count, seq_span), 1)
    valid_slot = position < lengths[:, None]
    row_valid = valid_slot.reshape(row_count, 1)
    key_valid = valid_slot[:, None, None, :]
    token_values = tokens.astype(jnp.float32)
    projected = jnp.einsum("rd,cde->cre", tokens, w_qkv, preferred_element_type=jnp.float32)
    head_shape = (seq_count, seq_span, heads_here, HEAD_DIM)
    query_heads = (projected[0] + bias_qv[0]).astype(jnp.bfloat16).reshape(head_shape)
    key_heads = projected[1].astype(jnp.bfloat16).reshape(head_shape)
    value_heads = (projected[2] + bias_qv[1]).astype(jnp.bfloat16).reshape(head_shape)

    def score_block():
        raw_scores = (
            jnp.einsum(
                "sqhd,skhd->shqk", query_heads, key_heads, preferred_element_type=jnp.float32
            )
            * score_scale
        )
        return jnp.where(key_valid, raw_scores, -1e30)

    scores = score_block()
    peak_score = jnp.max(scores, -1, keepdims=True)
    expo = jnp.exp(scores - peak_score)
    denominator = jnp.sum(expo, -1, keepdims=True)
    probs_low = (expo / denominator).astype(jnp.bfloat16)
    log_total = peak_score + jnp.log(denominator)
    attended = (
        jnp.einsum("shqk,skhd->sqhd", probs_low, value_heads, preferred_element_type=jnp.float32)
        .astype(jnp.bfloat16)
        .reshape(row_count, local_width)
    )
    branch_share = (
        lax.psum_scatter(
            jnp.dot(attended, w_out, preferred_element_type=jnp.float32).astype(jnp.bfloat16),
            "tensor",
            scatter_dimension=0,
            tiled=True,
        ).astype(jnp.float32)
        + bias_out
    )
    normal_one, inverse_one = normalize(own_rows(token_values) + branch_share)
    hidden = normal_one * gain_one + shift_one
    hidden_low = lax.all_gather(hidden.astype(jnp.bfloat16), "tensor", axis=0, tiled=True)
    pre_act = jnp.dot(hidden_low, w_up, preferred_element_type=jnp.float32) + bias_up
    act_low = jax.nn.gelu(pre_act, approximate=False).astype(jnp.bfloat16)
    branch_mlp = (
        lax.psum_scatter(
            jnp.dot(act_low, w_down, preferred_element_type=jnp.float32).astype(jnp.bfloat16),
            "tensor",
            scatter_dimension=0,
            tiled=True,
        ).astype(jnp.float32)
        + bias_down
    )
    valid_here = own_rows(row_valid)
    cot_here = own_rows(cotangent)
    normal_two, inverse_two = normalize(hidden + branch_mlp)
    output_low = jnp.where(valid_here, normal_two * gain_two + shift_two, 0.0).astype(jnp.bfloat16)
    grad_out = jnp.where(valid_here, cot_here.astype(jnp.float32), 0.0)
    grad_gain_two = jnp.sum(grad_out * normal_two, 0)
    grad_shift_two = jnp.sum(grad_out, 0)
    grad_resid_two = norm_back(grad_out * gain_two, normal_two, inverse_two)
    grad_mlp, output_low = (
        lax.all_gather(grad_resid_two.astype(jnp.bfloat16), "tensor", axis=0, tiled=True),
        lax.all_gather(output_low, "tensor", axis=0, tiled=True),
    )
    grad_bias_down = jnp.sum(grad_mlp.astype(jnp.float32), 0)
    grad_w_down = jnp.einsum("rf,rd->fd", act_low, grad_mlp, preferred_element_type=jnp.float32)
    grad_act = jnp.einsum("rd,fd->rf", grad_mlp, w_down, preferred_element_type=jnp.float32)
    gelu_value, gelu_pull = jax.vjp(partial(jax.nn.gelu, approximate=False), pre_act)
    grad_pre = gelu_pull(grad_act)[0].astype(jnp.bfloat16)
    grad_bias_up = jnp.sum(grad_pre.astype(jnp.float32), 0)
    grad_w_up = jnp.einsum("rd,rf->df", hidden_low, grad_pre, preferred_element_type=jnp.float32)
    grad_hidden = grad_resid_two + lax.psum_scatter(
        jnp.einsum("rf,df->rd", grad_pre, w_up, preferred_element_type=jnp.float32).astype(
            jnp.bfloat16
        ),
        "tensor",
        scatter_dimension=0,
        tiled=True,
    ).astype(jnp.float32)
    grad_gain_one = jnp.sum(grad_hidden * normal_one, 0)
    grad_shift_one = jnp.sum(grad_hidden, 0)
    grad_resid_one = norm_back(grad_hidden * gain_one, normal_one, inverse_one)
    grad_attn = lax.all_gather(grad_resid_one.astype(jnp.bfloat16), "tensor", axis=0, tiled=True)
    grad_gain_two, grad_shift_two, grad_gain_one, grad_shift_one = lax.psum(
        (grad_gain_two, grad_shift_two, grad_gain_one, grad_shift_one), "tensor"
    )
    grad_bias_out = jnp.sum(grad_attn.astype(jnp.float32), 0)
    grad_w_out = jnp.einsum("rl,rd->ld", attended, grad_attn, preferred_element_type=jnp.float32)
    grad_attended = (
        jnp.einsum("rd,ld->rl", grad_attn, w_out, preferred_element_type=jnp.float32)
        .astype(jnp.bfloat16)
        .reshape(head_shape)
    )
    probs = jnp.exp(score_block() - log_total)
    grad_probs = jnp.einsum(
        "sqhd,skhd->shqk", grad_attended, value_heads, preferred_element_type=jnp.float32
    )
    grad_values = jnp.einsum(
        "shqk,sqhd->skhd",
        probs.astype(jnp.bfloat16),
        grad_attended,
        preferred_element_type=jnp.float32,
    )
    inner_sum = jnp.sum(grad_probs * probs, -1, keepdims=True)
    grad_scores = (probs * (grad_probs - inner_sum)).astype(jnp.bfloat16)
    grad_query = (
        jnp.einsum("shqk,skhd->sqhd", grad_scores, key_heads, preferred_element_type=jnp.float32)
        * score_scale
    )
    grad_keys = (
        jnp.einsum("shqk,sqhd->skhd", grad_scores, query_heads, preferred_element_type=jnp.float32)
        * score_scale
    )
    grad_proj = (
        jnp.stack([grad_query, grad_keys, grad_values])
        .astype(jnp.bfloat16)
        .reshape(3, row_count, local_width)
    )
    grad_bias_qv = jnp.stack(
        [jnp.sum(grad_proj[0].astype(jnp.float32), 0), jnp.sum(grad_proj[2].astype(jnp.float32), 0)]
    )
    grad_w_qkv = jnp.einsum("rd,cre->cde", tokens, grad_proj, preferred_element_type=jnp.float32)
    token_term = jnp.einsum("cre,cde->rd", grad_proj, w_qkv, preferred_element_type=jnp.float32)
    token_term = lax.dynamic_update_slice_in_dim(
        token_term, own_rows(token_term) + grad_resid_one, row_start, 0
    )
    token_total = lax.psum(token_term.astype(jnp.bfloat16), "tensor")
    all_sums = (
        lax.psum_scatter(grad_w_qkv, "dp", scatter_dimension=1, tiled=True),
        lax.psum_scatter(grad_bias_qv, "dp", scatter_dimension=1, tiled=True),
        lax.psum_scatter(grad_w_out, "dp", scatter_dimension=1, tiled=True),
        lax.psum_scatter(grad_bias_out, "dp", scatter_dimension=0, tiled=True),
        lax.psum_scatter(grad_gain_one, "dp", scatter_dimension=0, tiled=True),
        lax.psum_scatter(grad_shift_one, "dp", scatter_dimension=0, tiled=True),
        lax.psum_scatter(grad_w_up, "dp", scatter_dimension=0, tiled=True),
        lax.psum_scatter(grad_bias_up, "dp", scatter_dimension=0, tiled=True),
        lax.psum_scatter(grad_w_down, "dp", scatter_dimension=1, tiled=True),
        lax.psum_scatter(grad_bias_down, "dp", scatter_dimension=0, tiled=True),
        lax.psum_scatter(grad_gain_two, "dp", scatter_dimension=0, tiled=True),
        lax.psum_scatter(grad_shift_two, "dp", scatter_dimension=0, tiled=True),
    )
    sum_w_qkv, sum_bias_qv, sum_w_out, sum_bias_out, sum_gain_one, sum_shift_one = all_sums[:6]
    sum_w_up, sum_bias_up, sum_w_down, sum_bias_down, sum_gain_two, sum_shift_two = all_sums[6:]
    return (
        output_low,
        token_total,
        sum_w_qkv,
        sum_bias_qv,
        sum_w_out,
        sum_bias_out,
        sum_gain_one,
        sum_shift_one,
        sum_w_up,
        sum_bias_up,
        sum_w_down,
        sum_bias_down,
        sum_gain_two,
        sum_shift_two,
    )


def solution(mesh):
    placed = (
        P("dp", None),
        P(None, None, "tensor"),
        P(None, "tensor"),
        P("tensor", None),
        P(),
        P(),
        P(),
        P(None, "tensor"),
        P("tensor"),
        P("tensor", None),
        P(),
        P(),
        P(),
        P("dp", None),
        P("dp"),
    )
    return jax.shard_map(
        on_device,
        mesh=mesh,
        in_specs=placed,
        out_specs=(
            P("dp", None),
            P("dp", None),
            P(None, "dp", "tensor"),
            P(None, ("tensor", "dp")),
            P("tensor", "dp"),
            P("dp"),
            P("dp"),
            P("dp"),
            P("dp", "tensor"),
            P(("tensor", "dp")),
            P("tensor", "dp"),
            P("dp"),
            P("dp"),
            P("dp"),
        ),
        check_vma=False,
    )
```

profile of v0, /device:TPU:0, one launch (start us, length us, event | category | flops | bytes accessed | tf_op | source)
XLA Modules:
  0.0 464.9 jit_solution(6419392170741433164)
XLA Ops:
  7.2 2.1 convolution_bitcast_fusion.2
  15.8 26.0 %reduce-scatter.13.cloned.1.call-done = bf16[128,768]{1,0:T(8,128)(2,1)} async-done(((bf16[512,768]{1,0:T(8,128)(2,1)}), bf16[128,768]{1,0:T(8,128)(2,1)}) %reduce-scatter.13.cloned.1.call-update) | async-done | bytes 196624 | tf_op jit(solution)/shard_map/reduce_scatter | solution.py:87
  45.1 8.2 %all_gather.12 = bf16[512,768]{1,0:T(8,128)(2,1)S(1)} all-gather(bf16[128,768]{1,0:T(8,128)(2,1)S(1)} %fusion.23), channel_id=1, replica_groups=mesh['dp'=8,'tensor'=4] {'tensor'}, dimensions={0}, use_global_device_ids=true | all-gather | bytes 983040 | tf_op jit(solution)/shard_map/all_gather | solution.py:97
  53.3 5.5 %multiply_convert_fusion.1 = (bf16[512,768]{1,0:T(8,128)(2,1)S(1)}, f32[512,768]{1,0:T(8,128)}, f32[512,768]{1,0:T(8,128)}) fusion(f32[768]{0:T(1024)S(1)} %copy-done.36, bf16[512,768]{1,0:T(8,128)(2,1)S(1)} %all_gather.12, bf16[768,768]{1,0:T(8,128)(2,1)S(1)} %copy-done), kind=kOutput, calls=%fused_computation.16 | convolution fusion | flops 629932032 | bytes 5901312 | tf_op jit(solution)/shard_map/dot_general | solution.py:98
  58.9 1.7 convolution_convert_fusion.1
  60.7 23.7 %reduce-scatter.15.cloned.1.call-done = bf16[128,768]{1,0:T(8,128)(2,1)} async-done(((bf16[512,768]{1,0:T(8,128)(2,1)}), bf16[128,768]{1,0:T(8,128)(2,1)}) %reduce-scatter.15.cloned.1.call-update) | async-done | bytes 196624 | tf_op jit(solution)/shard_map/reduce_scatter | solution.py:101
  84.4 1.4 fusion.31
  86.0 2.0 multiply_reduce_fusion.1
  88.0 1.8 fusion.30
  89.9 8.2 %all_gather.14 = bf16[512,768]{1,0:T(8,128)(2,1)S(1)} all-gather(bf16[128,768]{1,0:T(8,128)(2,1)S(1)} %get-tuple-element.68), channel_id=1, replica_groups=mesh['dp'=8,'tensor'=4] {'tensor'}, dimensions={0}, use_global_device_ids=true | all-gather | bytes 983040 | tf_op jit(solution)/shard_map/all_gather | solution.py:118
  98.0 1.8 convert_reduce_fusion.1
  100.7 1.7 convolution_convert_fusion
  102.5 23.8 %reduce-scatter.17.cloned.1.call-done = bf16[128,768]{1,0:T(8,128)(2,1)} async-done(((bf16[512,768]{1,0:T(8,128)(2,1)}), bf16[128,768]{1,0:T(8,128)(2,1)}) %reduce-scatter.17.cloned.1.call-update) | async-done | bytes 196624 | tf_op jit(solution)/shard_map/reduce_scatter | solution.py:128
  126.2 1.9 multiply_reduce_fusion.2
  128.2 2.0 fusion.29
  130.2 8.2 %all_gather.15 = bf16[512,768]{1,0:T(8,128)(2,1)S(1)} all-gather(bf16[128,768]{1,0:T(8,128)(2,1)S(1)} %get-tuple-element.66), channel_id=1, replica_groups=mesh['dp'=8,'tensor'=4] {'tensor'}, dimensions={0}, use_global_device_ids=true | all-gather | bytes 983040 | tf_op jit(solution)/shard_map/all_gather | solution.py:139
  139.5 1.3 convolution_bitcast_fusion.3
  141.1 3.1 multiply_reduce_fusion
  149.2 1.8 convolution_bitcast_fusion
  151.0 4.2 copy.43
  155.2 4.7 %reshape.286 = f32[768,576]{1,0:T(8,128)} reshape(f32[768,3,192]{2,1,0:T(4,128)} %bitcast.77) | data formatting | bytes 3538944
  160.0 2.4 convolution_bitcast_fusion.1
  163.5 3.4 fusion.36
  167.0 3.3 fusion.35
  172.8 8.9 %all_gather.13 = bf16[512,768]{1,0:T(8,128)(2,1)S(1)} all-gather(bf16[128,768]{1,0:T(8,128)(2,1)} %get-tuple-element.76), channel_id=1, replica_groups=mesh['dp'=8,'tensor'=4] {'tensor'}, dimensions={0}, use_global_device_ids=true | all-gather | bytes 983040 | tf_op jit(solution)/shard_map/all_gather | solution.py:119
  184.2 37.9 %all-reduce.8 = (f32[2,192]{1,0:T(2,128)S(1)}, f32[768]{0:T(1024)S(1)}, f32[768]{0:T(1024)S(1)}, f32[768]{0:T(1024)S(1)}, f32[768]{0:T(1024)S(1)}, /*index=5*/f3...) all-reduce(f32[2,192]{1,0:T(2,128)S(1)} %pad_maximum_fusion.3, ...), channel_id=6, replica_groups=mesh['dp'=8,'tensor'=4] {'dp'}, use_global_device_ids=true, to_apply=%region_18.19.clone | all-reduce | flops 5760 | bytes 46080
  224.2 6.1 %all-reduce.9 = (f32[96]{0:T(128)}, f32[96]{0:T(128)}, f32[96]{0:T(128)}, f32[96]{0:T(128)}) all-reduce(f32[96]{0:T(128)S(1)} %dynamic-slice.6, f32[96]{0:T(128)S(1)} %dynamic-slice.8, f32[96]{0:T(128)S(1)} %dynamic-slice.14, f32[96]{0:T(128)S(1)} %dynamic-slice.16), channel_id=1, replica_groups=mesh['dp'=8,'tensor'=4] {'tensor'}, use_global_device_ids=true, to_apply=%region_23.24 | all-reduce | flops 384 | bytes 3072 | tf_op jit(solution)/shard_map/psum | solution.py:140
  231.0 1.6 copy.48
  232.6 40.5 %reduce-scatter.23.cloned.1.call-done = f32[96,576]{1,0:T(8,128)} async-done(((f32[768,576]{1,0:T(8,128)}), f32[96,576]{1,0:T(8,128)}) %reduce-scatter.23.cloned.1.call-update) | async-done | bytes 221200
  275.0 34.6 %all-reduce.12.cloned.1.call-done = bf16[512,768]{1,0:T(8,128)(2,1)} async-done(((bf16[512,768]{1,0:T(8,128)(2,1)}), bf16[512,768]{1,0:T(8,128)(2,1)}) %all-reduce.12.cloned.1.call-update) | async-done | bytes 786448 | tf_op jit(solution)/shard_map/psum | solution.py:183
  309.6 74.0 %reduce-scatter.21.cloned.1.call-done = f32[768,96]{0,1:T(8,128)} async-done(((f32[768,768]{0,1:T(8,128)}), f32[768,96]{0,1:T(8,128)}) %reduce-scatter.21.cloned.1.call-update) | async-done | bytes 294928 | tf_op jit(solution)/shard_map/reduce_scatter | solution.py:193
  383.6 72.7 %reduce-scatter.19.cloned.1.call-done = f32[96,768]{1,0:T(8,128)} async-done(((f32[768,768]{1,0:T(8,128)}), f32[96,768]{1,0:T(8,128)}) %reduce-scatter.19.cloned.1.call-update) | async-done | bytes 294928 | tf_op jit(solution)/shard_map/reduce_scatter | solution.py:191
  (145 shorter events, 27.5 us)
Async XLA Ops:
  7.2 46.1 %copy-start = (bf16[768,768]{1,0:T(8,128)(2,1)S(1)}, bf16[768,768]{1,0:T(8,128)(2,1)}, u32[]{:S(2)}) copy-start(bf16[768,768]{1,0:T(8,128)(2,1)} %param.22) | copy-start | bytes 3538948
  7.2 34.6 %reduce-scatter.13.cloned.1.call-start = ((), (), s32[]{:S(2)}) async-start(), calls=%async_computation.7 | async-start | bytes 983040 | tf_op jit(solution)/shard_map/reduce_scatter | solution.py:87
  9.5 2.3 copy-start.12
  13.7 28.1 %copy-start.4 = (bf16[512,768]{1,0:T(8,128)(2,1)S(1)}, bf16[512,768]{1,0:T(8,128)(2,1)}, u32[]{:S(2)}) copy-start(bf16[512,768]{1,0:T(8,128)(2,1)} %param.15) | copy-start | bytes 2359300
  13.7 28.1 %copy-start.23 = (f32[768]{0:T(1024)S(1)}, f32[768]{0:T(1024)}, u32[]{:S(2)}) copy-start(f32[768]{0:T(1024)} %param.19) | copy-start | bytes 9220
  13.7 30.3 %copy-start.24 = (f32[768]{0:T(1024)S(1)}, f32[768]{0:T(1024)}, u32[]{:S(2)}) copy-start(f32[768]{0:T(1024)} %param.20) | copy-start | bytes 9220
  13.8 30.3 %copy-start.25 = (f32[768]{0:T(1024)S(1)}, f32[768]{0:T(1024)}, u32[]{:S(2)}) copy-start(f32[768]{0:T(1024)} %param.21) | copy-start | bytes 9220
  15.7 37.6 %copy-start.36 = (f32[768]{0:T(1024)S(1)}, f32[768]{0:T(1024)}, u32[]{:S(2)}) copy-start(f32[768]{0:T(1024)} %param.23) | copy-start | bytes 9220
  15.7 68.7 %reduce-scatter.15.cloned.1.call-start = ((), (), s32[]{:S(2)}) async-start(), calls=%async_computation.8 | async-start | bytes 983040 | tf_op jit(solution)/shard_map/reduce_scatter | solution.py:101
  53.3 5.5 %copy-start.34 = (bf16[768,768]{1,0:T(8,128)(2,1)S(1)}, bf16[768,768]{1,0:T(8,128)(2,1)}, u32[]{:S(2)}) copy-start(bf16[768,768]{1,0:T(8,128)(2,1)} %param.24) | copy-start | bytes 3538948
  58.9 25.5 %copy-start.3 = (bf16[128,768]{1,0:T(8,128)(2,1)S(1)}, bf16[128,768]{1,0:T(8,128)(2,1)}, u32[]{:S(2)}) copy-start(bf16[128,768]{1,0:T(8,128)(2,1)} %reduce-scatter.13.cloned.1.call-done) | copy-start | bytes 589828
  58.9 25.5 %copy-start.31 = (f32[768]{0:T(1024)S(1)}, f32[768]{0:T(1024)}, u32[]{:S(2)}) copy-start(f32[768]{0:T(1024)} %param.25) | copy-start | bytes 9220
  60.6 25.5 %copy-start.26 = (f32[768]{0:T(1024)S(1)}, f32[768]{0:T(1024)}, u32[]{:S(2)}) copy-start(f32[768]{0:T(1024)} %param.26) | copy-start | bytes 9220
  60.6 27.4 %copy-start.32 = (f32[768]{0:T(1024)S(1)}, f32[768]{0:T(1024)}, u32[]{:S(2)}) copy-start(f32[768]{0:T(1024)} %param.27) | copy-start | bytes 9220
  60.6 65.7 %reduce-scatter.17.cloned.1.call-start = ((), (), s32[]{:S(2)}) async-start(), calls=%async_computation.9 | async-start | bytes 983040 | tf_op jit(solution)/shard_map/reduce_scatter | solution.py:128
  84.4 13.6 %copy-start.39 = (f32[512,768]{1,0:T(8,128)S(1)}, f32[512,768]{1,0:T(8,128)}, u32[]{:S(2)}) copy-start(f32[512,768]{1,0:T(8,128)} %get-tuple-element.79) | copy-start | bytes 4718596
  86.0 12.0 %copy-start.35 = (bf16[768,768]{1,0:T(8,128)(2,1)S(1)}, bf16[768,768]{1,0:T(8,128)(2,1)}, u32[]{:S(2)}) copy-start(bf16[768,768]{1,0:T(8,128)(2,1)} %param.24) | copy-start | bytes 3538948
  86.0 12.0 %copy-start.38 = (f32[512,768]{1,0:T(8,128)S(1)}, f32[512,768]{1,0:T(8,128)}, u32[]{:S(2)}) copy-start(f32[512,768]{1,0:T(8,128)} %get-tuple-element.73) | copy-start | bytes 4718596
  102.4 128.6 %reduce-scatter.25.cloned.1.call-start = ((), (), s32[]{:S(2)}) async-start(), calls=%async_computation.14 | async-start | bytes 884736
  126.2 12.2 %copy-start.15 = (bf16[192,768]{1,0:T(8,128)(2,1)S(1)}, bf16[192,768]{1,0:T(8,128)(2,1)}, u32[]{:S(2)}) copy-start(bf16[192,768]{1,0:T(8,128)(2,1)} %param.18) | copy-start | bytes 884740
  128.2 11.3 %copy-start.17 = (bf16[3,64,512]{2,1,0:T(8,128)(2,1)S(1)}, bf16[3,64,512]{2,1,0:T(8,128)(2,1)}, u32[]{:S(2)}) copy-start(bf16[3,64,512]{2,1,0:T(8,128)(2,1)} %copy-done.16) | copy-start | bytes 589828
  140.9 132.3 %reduce-scatter.23.cloned.1.call-start = ((), (), s32[]{:S(2)}) async-start(), calls=%async_computation.13 | async-start | bytes 2211840
  141.1 3.1 copy-start.2
  146.2 2.3 copy-start.20
  160.0 149.6 %all-reduce.12.cloned.1.call-start = ((), (), s32[]{:S(2)}) async-start(), calls=%async_computation.10 | async-start | bytes 1572864 | tf_op jit(solution)/shard_map/psum | solution.py:183
  160.0 2.4 copy-start.13
  163.5 220.1 %reduce-scatter.21.cloned.1.call-start = ((), (), s32[]{:S(2)}) async-start(), calls=%async_computation.12 | async-start | bytes 2654208 | tf_op jit(solution)/shard_map/reduce_scatter | solution.py:193
  166.9 289.4 %reduce-scatter.19.cloned.1.call-start = ((), (), s32[]{:S(2)}) async-start(), calls=%async_computation.11 | async-start | bytes 2654208 | tf_op jit(solution)/shard_map/reduce_scatter | solution.py:191
  170.3 13.9 %copy-start.27 = (f32[768]{0:T(1024)S(1)}, f32[768]{0:T(1024)}, u32[]{:S(2)}) copy-start(f32[768]{0:T(1024)} %get-tuple-element.47) | copy-start | bytes 9220
  170.3 13.9 %copy-start.28 = (f32[768]{0:T(1024)S(1)}, f32[768]{0:T(1024)}, u32[]{:S(2)}) copy-start(f32[768]{0:T(1024)} %get-tuple-element.42) | copy-start | bytes 9220
  170.3 13.9 %copy-start.29 = (f32[768]{0:T(1024)S(1)}, f32[768]{0:T(1024)}, u32[]{:S(2)}) copy-start(f32[768]{0:T(1024)} %get-tuple-element.49) | copy-start | bytes 9220
  309.6 147.6 %copy-start.18 = (bf16[512,768]{1,0:T(8,128)(2,1)S(1)}, bf16[512,768]{1,0:T(8,128)(2,1)}, u32[]{:S(2)}) copy-start(bf16[512,768]{1,0:T(8,128)(2,1)} %all-reduce.12.cloned.1.call-done) | copy-start | bytes 2359300
  (16 other events, 19.9 us)
Sparse Core Ops, SparseCore 0:
  15.8 25.9 reduce-scatter.12
  60.7 23.6 reduce-scatter.14
  102.5 23.6 reduce-scatter.16
  141.0 62.9 reduce-scatter.24
  207.3 65.7 reduce-scatter.22
  276.0 33.5 all-reduce.11
  314.1 69.4 reduce-scatter.20
  388.0 68.1 reduce-scatter.18
where the time goes:
time: 466 us; the launch traced here: 465 us
  waiting for transfers between devices  295 us (63%)
  blocking collectives  77.6 us (17%)
  matrix products  35.1 us (8%)
  local copies, waits for them, and re-layouts  23.8 us (5%)
  between operations  16.6 us (4%)
  other arithmetic  15.9 us (3%)
    reduce_scatter x1, waiting for transfers between devices, on_device(): lax.psum_scatter(grad_w_down, 'dp', scatter_dimension=1, tiled=True)  74 us
    reduce_scatter x1, waiting for transfers between devices, on_device(): lax.psum_scatter(grad_w_up, 'dp', scatter_dimension=0, tiled=True)  72.7 us
    unnamed x10, waiting for transfers between devices  40.7 us
    unnamed x1, blocking collectives  37.9 us
    psum x1, waiting for transfers between devices, on_device(): token_total = lax.psum(token_term.astype(jnp.bfloat16), 'tensor')  34.6 us
    reduce_scatter x1, waiting for transfers between devices, on_device(): lax.psum_scatter(jnp.dot(attended, w_out, preferred_element_type=jnp.floa...  26 us
    reduce_scatter x1, waiting for transfers between devices, on_device(): lax.psum_scatter(jnp.einsum('rf,df->rd', grad_pre, w_up, preferred_elemen...  23.8 us
    reduce_scatter x1, waiting for transfers between devices, on_device(): lax.psum_scatter(jnp.dot(act_low, w_down, preferred_element_type=jnp.floa...  23.7 us
  transfers between devices with their start and end apart: 8, of which 7 were waited for; matrix products, arithmetic and copies ran while one was open for 8% of the time, Pallas kernels for 0%

commit v1 on v0

v1 whole, which is shorter than its diff:
```python
from functools import partial

import jax
import jax.numpy as jnp
from jax import lax
from jax.sharding import PartitionSpec as P

HEAD_DIM = 64

norm_epsilon = 1e-05

CORE_PAIRS = [(i, i ^ 1) for i in range(4)]
CHIP_PAIRS = [(i, i ^ 2) for i in range(4)]


def normalize(resid):
    center = resid - jnp.mean(resid, -1, keepdims=True)
    inverse = lax.rsqrt(jnp.mean(center * center, -1, keepdims=True) + norm_epsilon)
    return (center * inverse, inverse)


def norm_back(grad_norm, normed, inverse):
    mean_grad = jnp.mean(grad_norm, -1, keepdims=True)
    mean_proj = jnp.mean(grad_norm * normed, -1, keepdims=True)
    return inverse * (grad_norm - mean_grad - normed * mean_proj)


def half_rows(full, which):
    half = full.shape[0] // 2
    return lax.dynamic_slice_in_dim(full, which * half, half, 0)


def to_core(block):
    return lax.ppermute(block, "tensor", CORE_PAIRS)


def to_chip(block):
    return lax.ppermute(block, "tensor", CHIP_PAIRS)


def half_sum(row_input, weight, contract, core):
    def part(which):
        return lax.dot_general(
            half_rows(row_input, which),
            weight,
            (((1,), (contract,)), ((), ())),
            preferred_element_type=jnp.float32,
        )

    received = to_core(part(1 - core).astype(jnp.bfloat16))
    chip_sum = (part(core) + received.astype(jnp.float32)).astype(jnp.bfloat16)
    return chip_sum.astype(jnp.float32) + to_chip(chip_sum).astype(jnp.float32)


def whole_rows(own_half, core):
    other_half = to_core(own_half)
    half = own_half.shape[0]
    full = jnp.zeros((2 * half, own_half.shape[1]), own_half.dtype)
    full = lax.dynamic_update_slice_in_dim(full, own_half, core * half, 0)
    return lax.dynamic_update_slice_in_dim(full, other_half, (1 - core) * half, 0)


def sum_scatter(buffer, dp_size):
    bits = dp_size.bit_length() - 1
    if 1 << bits != dp_size:
        return lax.psum_scatter(buffer, "dp", scatter_dimension=0, tiled=False)
    mine = lax.axis_index("dp")
    held = buffer.reshape((2,) * bits + buffer.shape[1:])
    for bit in range(bits):
        axis = bits - 1 - bit
        side = (mine >> bit) & 1
        sent = lax.dynamic_index_in_dim(held, 1 - side, axis, keepdims=False)
        kept = lax.dynamic_index_in_dim(held, side, axis, keepdims=False)
        pairs = [(i, i ^ (1 << bit)) for i in range(dp_size)]
        received = lax.ppermute(sent.astype(jnp.bfloat16), "dp", pairs)
        held = kept.astype(jnp.float32) + received.astype(jnp.float32)
    return held


def small_scatter(vectors, dp_size):
    count, width = vectors.shape[0], vectors.shape[1] // dp_size
    blocks = vectors.reshape(count, dp_size, width).transpose(1, 0, 2)
    bits = dp_size.bit_length() - 1
    if 1 << bits != dp_size:
        return lax.psum_scatter(blocks, "dp", scatter_dimension=0, tiled=False)
    mine = lax.axis_index("dp")
    held = blocks.reshape((2,) * bits + blocks.shape[1:])
    for bit in range(bits):
        axis = bits - 1 - bit
        side = (mine >> bit) & 1
        sent = lax.dynamic_index_in_dim(held, 1 - side, axis, keepdims=False)
        kept = lax.dynamic_index_in_dim(held, side, axis, keepdims=False)
        pairs = [(i, i ^ (1 << bit)) for i in range(dp_size)]
        held = kept + lax.ppermute(sent, "dp", pairs)
    return held


def on_device(
    tokens,
    w_qkv,
    bias_qv,
    w_out,
    bias_out,
    gain_one,
    shift_one,
    w_up,
    bias_up,
    w_down,
    bias_down,
    gain_two,
    shift_two,
    cotangent,
    lengths,
):
    seq_count = lengths.shape[0]
    row_count, model_width = tokens.shape
    seq_span = row_count // seq_count
    local_width = w_qkv.shape[2]
    heads_here = local_width // HEAD_DIM
    score_scale = HEAD_DIM ** (-0.5)
    dp_size = lax.axis_size("dp")
    core = lax.axis_index("tensor") % 2
    block = model_width // dp_size

    position = lax.broadcasted_iota(jnp.int32, (seq_count, seq_span), 1)
    valid_slot = position < lengths[:, None]
    row_valid = valid_slot.reshape(row_count, 1)
    key_valid = valid_slot[:, None, None, :]
    projected = jnp.einsum("rd,cde->cre", tokens, w_qkv, preferred_element_type=jnp.float32)
    head_shape = (seq_count, seq_span, heads_here, HEAD_DIM)
    query_heads = (projected[0] + bias_qv[0]).astype(jnp.bfloat16).reshape(head_shape)
    key_heads = projected[1].astype(jnp.bfloat16).reshape(head_shape)
    value_heads = (projected[2] + bias_qv[1]).astype(jnp.bfloat16).reshape(head_shape)

    def score_block():
        raw_scores = (
            jnp.einsum(
                "sqhd,skhd->shqk", query_heads, key_heads, preferred_element_type=jnp.float32
            )
            * score_scale
        )
        return jnp.where(key_valid, raw_scores, -1e30)

    scores = score_block()
    peak_score = jnp.max(scores, -1, keepdims=True)
    expo = jnp.exp(scores - peak_score)
    denominator = jnp.sum(expo, -1, keepdims=True)
    probs_low = (expo / denominator).astype(jnp.bfloat16)
    log_total = peak_score + jnp.log(denominator)
    attended = (
        jnp.einsum("shqk,skhd->sqhd", probs_low, value_heads, preferred_element_type=jnp.float32)
        .astype(jnp.bfloat16)
        .reshape(row_count, local_width)
    )
    own_tokens = half_rows(tokens, core).astype(jnp.float32)
    branch_attn = half_sum(attended, w_out, 0, core) + bias_out
    normal_one, inverse_one = normalize(own_tokens + branch_attn)
    hidden = normal_one * gain_one + shift_one
    hidden_low = whole_rows(hidden.astype(jnp.bfloat16), core)
    pre_act = jnp.dot(hidden_low, w_up, preferred_element_type=jnp.float32) + bias_up
    act_low = jax.nn.gelu(pre_act, approximate=False).astype(jnp.bfloat16)
    branch_mlp = half_sum(act_low, w_down, 0, core) + bias_down
    valid_here = half_rows(row_valid, core)
    cot_here = half_rows(cotangent, core)
    normal_two, inverse_two = normalize(hidden + branch_mlp)
    output_low = jnp.where(valid_here, normal_two * gain_two + shift_two, 0.0).astype(jnp.bfloat16)
    grad_out = jnp.where(valid_here, cot_here.astype(jnp.float32), 0.0)
    grad_gain_two = jnp.sum(grad_out * normal_two, 0)
    grad_shift_two = jnp.sum(grad_out, 0)
    grad_resid_two = norm_back(grad_out * gain_two, normal_two, inverse_two)
    grad_mlp = whole_rows(grad_resid_two.astype(jnp.bfloat16), core)
    output_low = whole_rows(output_low, core)
    grad_bias_down = jnp.sum(grad_mlp.astype(jnp.float32), 0)
    grad_act = jnp.einsum("rd,fd->rf", grad_mlp, w_down, preferred_element_type=jnp.float32)
    gelu_value, gelu_pull = jax.vjp(partial(jax.nn.gelu, approximate=False), pre_act)
    grad_pre = gelu_pull(grad_act)[0].astype(jnp.bfloat16)
    grad_bias_up = jnp.sum(grad_pre.astype(jnp.float32), 0)
    grad_hidden = grad_resid_two + half_sum(grad_pre, w_up, 1, core)
    grad_w_down = jnp.einsum("rd,rf->df", grad_mlp, act_low, preferred_element_type=jnp.float32)
    grad_w_up = jnp.einsum("rd,rf->df", hidden_low, grad_pre, preferred_element_type=jnp.float32)
    sum_w_down = sum_scatter(grad_w_down.reshape(dp_size, block, -1), dp_size)
    sum_w_up = sum_scatter(grad_w_up.reshape(dp_size, block, -1), dp_size)

    grad_gain_one = jnp.sum(grad_hidden * normal_one, 0)
    grad_shift_one = jnp.sum(grad_hidden, 0)
    grad_resid_one = norm_back(grad_hidden * gain_one, normal_one, inverse_one)
    grad_attn = whole_rows(grad_resid_one.astype(jnp.bfloat16), core)
    half_vectors = jnp.stack([grad_gain_two, grad_shift_two, grad_gain_one, grad_shift_one])
    half_vectors = half_vectors + to_core(half_vectors)
    grad_bias_out = jnp.sum(grad_attn.astype(jnp.float32), 0)
    grad_w_out = jnp.einsum("rl,rd->dl", attended, grad_attn, preferred_element_type=jnp.float32)
    grad_attended = (
        jnp.einsum("rd,ld->rl", grad_attn, w_out, preferred_element_type=jnp.float32)
        .astype(jnp.bfloat16)
        .reshape(head_shape)
    )
    probs = jnp.exp(score_block() - log_total)
    grad_probs = jnp.einsum(
        "sqhd,skhd->shqk", grad_attended, value_heads, preferred_element_type=jnp.float32
    )
    grad_values = jnp.einsum(
        "shqk,sqhd->skhd",
        probs.astype(jnp.bfloat16),
        grad_attended,
        preferred_element_type=jnp.float32,
    )
    inner_sum = jnp.sum(grad_probs * probs, -1, keepdims=True)
    grad_scores = (probs * (grad_probs - inner_sum)).astype(jnp.bfloat16)
    grad_query = (
        jnp.einsum("shqk,skhd->sqhd", grad_scores, key_heads, preferred_element_type=jnp.float32)
        * score_scale
    )
    grad_keys = (
        jnp.einsum("shqk,sqhd->skhd", grad_scores, query_heads, preferred_element_type=jnp.float32)
        * score_scale
    )
    grad_proj = jnp.concatenate(
        [
            part.astype(jnp.bfloat16).reshape(row_count, local_width)
            for part in (grad_query, grad_keys, grad_values)
        ],
        1,
    )
    bias_sums = jnp.sum(grad_proj.astype(jnp.float32), 0).reshape(3, local_width)
    grad_bias_qv = jnp.stack([bias_sums[0], bias_sums[2]])
    grad_w_qkv = jnp.einsum("rd,re->de", tokens, grad_proj, preferred_element_type=jnp.float32)
    grad_w_attn = jnp.concatenate([grad_w_qkv, grad_w_out], 1)
    sum_w_attn = sum_scatter(grad_w_attn.reshape(dp_size, block, -1), dp_size)
    sum_w_qkv = sum_w_attn[:, : 3 * local_width].reshape(block, 3, local_width).transpose(1, 0, 2)
    sum_w_out = sum_w_attn[:, 3 * local_width :]
    w_flat = w_qkv.transpose(1, 0, 2).reshape(model_width, 3 * local_width)
    own_grad = (grad_resid_one + half_sum(grad_proj, w_flat, 1, core)).astype(jnp.bfloat16)
    token_total = whole_rows(own_grad, core)

    vectors = jnp.concatenate(
        [half_vectors, jnp.stack([grad_bias_down, grad_bias_out, grad_bias_up])], 0
    )
    sums = small_scatter(vectors, dp_size)
    sum_bias_qv = small_scatter(grad_bias_qv, dp_size)
    return (
        output_low,
        token_total,
        sum_w_qkv,
        sum_bias_qv,
        sum_w_out.T,
        sums[5],
        sums[2],
        sums[3],
        sum_w_up,
        sums[6],
        sum_w_down.T,
        sums[4],
        sums[0],
        sums[1],
    )


def solution(mesh):
    placed = (
        P("dp", None),
        P(None, None, "tensor"),
        P(None, "tensor"),
        P("tensor", None),
        P(),
        P(),
        P(),
        P(None, "tensor"),
        P("tensor"),
        P("tensor", None),
        P(),
        P(),
        P(),
        P("dp", None),
        P("dp"),
    )
    return jax.shard_map(
        on_device,
        mesh=mesh,
        in_specs=placed,
        out_specs=(
            P("dp", None),
            P("dp", None),
            P(None, "dp", "tensor"),
            P(None, ("tensor", "dp")),
            P("tensor", "dp"),
            P("dp"),
            P("dp"),
            P("dp"),
            P("dp", "tensor"),
            P(("tensor", "dp")),
            P("tensor", "dp"),
            P("dp"),
            P("dp"),
            P("dp"),
        ),
        check_vma=False,
    )
```

time: 466 us -> 163 us (0.35)
  waiting for transfers between devices: 295 us -> 57.6 us
  blocking collectives: 77.6 us -> 0 us
  starting transfers between devices: 0.51 us -> 33.6 us
  between operations: 16.6 us -> 2.49 us
  matrix products: 35.1 us -> 24.6 us
    reduce_scatter x5 -> x0, waiting for transfers between devices: 220 us -> none  [the longest x1 74 us: on_device(): lax.psum_scatter(grad_w_down, 'dp', scatter_dimension=1, tiled=True)]
    ppermute x0 -> x29, waiting for transfers between devices: none -> 57.6 us  [the longest x9 28.5 us: sum_scatter(): received = lax.ppermute(sent.astype(jnp.bfloat16), 'dp', pairs)]
    unnamed x10 -> x0, waiting for transfers between devices: 40.7 us -> none
    unnamed x1 -> x0, blocking collectives: 37.9 us -> none
    psum x1 -> x0, waiting for transfers between devices: 34.6 us -> none  [on_device(): token_total = lax.psum(token_term.astype(jnp.bfloat16), 'tensor')]
    ppermute x0 -> x29, starting transfers between devices: none -> 33.6 us  [the longest x9 17 us: sum_scatter(): received = lax.ppermute(sent.astype(jnp.bfloat16), 'dp', pairs)]
    all_gather x4 -> x0, blocking collectives: 33.5 us -> none  [the longest x1 8.94 us: on_device(): lax.all_gather(output_low, 'tensor', axis=0, tiled=True)]
    unnamed x96 -> x141, local copies, waits for them, and re-layouts: 22.1 us -> 10 us
  transfers between devices with their start and end apart: 8 -> 29, of which waited for: 7 -> 16; matrix products, arithmetic and copies ran while one was open for 8% -> 24% of each run, Pallas kernels for 0% -> 0%
where the time goes in v1:
time: 163 us; the launch traced here: 162 us
  waiting for transfers between devices  57.6 us (35%)
  starting transfers between devices  33.6 us (21%)
  local copies, waits for them, and re-layouts  25.9 us (16%)
  matrix products  24.6 us (15%)
  other arithmetic  18.1 us (11%)
  between operations  2.49 us (2%)
    ppermute x9, waiting for transfers between devices, sum_scatter(): received = lax.ppermute(sent.astype(jnp.bfloat16), 'dp', pairs)  28.5 us
    ppermute x4, waiting for transfers between devices, to_chip(): return lax.ppermute(block, 'tensor', CHIP_PAIRS)  19.7 us
    ppermute x9, starting transfers between devices, sum_scatter(): received = lax.ppermute(sent.astype(jnp.bfloat16), 'dp', pairs)  17 us
    unnamed x141, local copies, waits for them, and re-layouts  10 us
    ppermute x4, starting transfers between devices, to_chip(): return lax.ppermute(block, 'tensor', CHIP_PAIRS)  8.1 us
    dot_general x8, matrix products, part(): lax.dot_general(half_rows(row_input, which), weight, (((1,), (contract,))...  6.98 us
    add x8, other arithmetic, sum_scatter(): held = kept.astype(jnp.float32) + received.astype(jnp.float32)  6.73 us
    ppermute x6, starting transfers between devices, small_scatter(): held = kept + lax.ppermute(sent, 'dp', pairs)  6.66 us
  transfers between devices with their start and end apart: 29, of which 16 were waited for; matrix products, arithmetic and copies ran while one was open for 24% of the time, Pallas kernels for 0%

profile of v1, /device:TPU:0, one launch (start us, length us, event | category | flops | bytes accessed | tf_op | source)
XLA Modules:
  0.0 162.3 jit_solution(12643302289742595558)
XLA Ops:
  0.7 2.1 %convolution_bitcast_fusion.1 = f32[3,512,192]{1,2,0:T(8,128)S(1)} fusion(bf16[3,768,192]{1,2,0:T(8,128)(2,1)} %param.16, bf16[512,768]{1,0:T(8,128)(2,1)} %param.15), kind=kOutput, calls=%fused_computation.34 | convolution fusion | flops 452984832 | bytes 2850816 | tf_op jit(solution)/shard_map/rd,cde->cre/dot_general | solution.py:129
  10.4 2.9 %collective-permute-start.1 = (bf16[256,768]{1,0:T(8,128)(2,1)S(1)}, bf16[256,768]{1,0:T(8,128)(2,1)S(1)}, u32[]{:S(2)}, u32[]{:S(2)}) collective-permute-start(bf16[256,768]{1,0:T(8,128)(2,1)S(1)} %add_convert_fusion.5), channel_id=1, source_target_pairs={{0,2},{1,3},{2,0},{3,1},{4,6},{5,7},{6,4},{7,5},{8,10},{9,11},{10,... | collective-permute-start | bytes 1179656 | tf_op jit(solution)/shard_map/ppermute | solution.py:38
  13.3 9.4 %collective-permute-done.1 = bf16[256,768]{1,0:T(8,128)(2,1)S(1)} collective-permute-done((bf16[256,768]{1,0:T(8,128)(2,1)S(1)}, bf16[256,768]{1,0:T(8,128)(2,1)S(1)}, u32[]{:S(2)}, u32[]{:S(2)}) %collective-permute-start.1) | collective-permute-done | bytes 393248 | tf_op jit(solution)/shard_map/ppermute | solution.py:38
  23.6 1.7 %collective-permute-done.2 = bf16[256,768]{1,0:T(8,128)(2,1)S(1)} collective-permute-done((bf16[256,768]{1,0:T(8,128)(2,1)S(1)}, bf16[256,768]{1,0:T(8,128)(2,1)S(1)}, u32[]{:S(2)}, u32[]{:S(2)}) %collective-permute-start.2) | collective-permute-done | bytes 393248 | tf_op jit(solution)/shard_map/ppermute | solution.py:34
  25.4 5.6 %multiply_convert_fusion.1 = (bf16[512,768]{1,0:T(8,128)(2,1)S(1)}, f32[512,768]{1,0:T(8,128)}, f32[512,768]{1,0:T(8,128)}) fusion(f32[768]{0:T(1024)S(1)} %copy-done.66, bf16[512,768]{1,0:T(8,128)(2,1)S(1)} %constant_dynamic-update-slice_fusion.8, bf16[768,768]{1,0:T(8,128)(2,1)S(1)} %copy-done), kind=kOutput, calls=%fused_computation.17 | convolution fusion | flops 629932032 | bytes 5901312 | tf_op jit(solution)/shard_map/dot_general | solution.py:160
  31.8 1.6 collective-permute-done.3
  33.9 1.8 %collective-permute-start.4 = (bf16[256,768]{1,0:T(8,128)(2,1)S(1)}, bf16[256,768]{1,0:T(8,128)(2,1)S(1)}, u32[]{:S(2)}, u32[]{:S(2)}) collective-permute-start(bf16[256,768]{1,0:T(8,128)(2,1)S(1)} %add_convert_fusion.4), channel_id=1, source_target_pairs={{0,2},{1,3},{2,0},{3,1},{4,6},{5,7},{6,4},{7,5},{8,10},{9,11},{10,... | collective-permute-start | bytes 1179656 | tf_op jit(solution)/shard_map/ppermute | solution.py:38
  35.7 9.4 %collective-permute-done.4 = bf16[256,768]{1,0:T(8,128)(2,1)S(1)} collective-permute-done((bf16[256,768]{1,0:T(8,128)(2,1)S(1)}, bf16[256,768]{1,0:T(8,128)(2,1)S(1)}, u32[]{:S(2)}, u32[]{:S(2)}) %collective-permute-start.4) | collective-permute-done | bytes 393248 | tf_op jit(solution)/shard_map/ppermute | solution.py:38
  52.5 1.8 %convert_reduce_fusion = (f32[768]{0:T(1024)}, bf16[512,768]{1,0:T(8,128)(2,1)S(1)}) fusion(f32[512,768]{1,0:T(8,128)S(1)} %copy-done.67, f32[512,768]{1,0:T(8,128)S(1)} %copy-done.68, bf16[512,768]{1,0:T(8,128)(2,1)S(1)} %constant_dynamic-update-slice_fusion.4, bf16[768,768]{1,0:T(8,128)(2,1)S(1)} %copy-done.13), kind=kOutput, calls=%fused_computation.12 | convolution fusion | flops 610270464 | bytes 5901312 | tf_op jit(solution)/shard_map/rd,fd->rf/dot_general | solution.py:174
  57.5 1.8 %collective-permute-start.26 = (bf16[2,2,96,768]{3,2,0,1:T(8,128)(2,1)}, bf16[2,2,96,768]{3,2,0,1:T(8,128)(2,1)}, u32[]{:S(2)}, u32[]{:S(2)}) collective-permute-start(bf16[2,2,96,768]{3,2,0,1:T(8,128)(2,1)} %fusion.25), channel_id=1, source_target_pairs={{0,4},{4,0},{8,12},{12,8},{16,20},{20,16},{24,28},{28,24},{1,5},{5... | collective-permute-start | bytes 1769480 | tf_op jit(solution)/shard_map/ppermute | solution.py:75
  63.3 1.9 %constant_dynamic-update-slice_fusion.6 = bf16[512,768]{1,0:T(8,128)(2,1)} fusion(bf16[512,768]{1,0:T(8,128)(2,1)} %copy-done.36, bf16[256,768]{1,0:T(8,128)(2,1)} %collective-permute-done.5, s32[]{:T(128)S(6)} %select_n.99), kind=kLoop, calls=%fused_computation.149 | loop fusion | bytes 786436 | tf_op jit(solution)/shard_map/dynamic_update_slice | solution.py:60
  65.2 1.6 add_convert_fusion.3
  66.9 1.8 %collective-permute-start.8 = (bf16[256,768]{1,0:T(8,128)(2,1)S(1)}, bf16[256,768]{1,0:T(8,128)(2,1)S(1)}, u32[]{:S(2)}, u32[]{:S(2)}) collective-permute-start(bf16[256,768]{1,0:T(8,128)(2,1)S(1)} %add_convert_fusion.3), channel_id=1, source_target_pairs={{0,2},{1,3},{2,0},{3,1},{4,6},{5,7},{6,4},{7,5},{8,10},{9,11},{10,... | collective-permute-start | bytes 1179656 | tf_op jit(solution)/shard_map/ppermute | solution.py:38
  68.7 5.3 %collective-permute-done.26 = bf16[2,2,96,768]{3,2,0,1:T(8,128)(2,1)} collective-permute-done((bf16[2,2,96,768]{3,2,0,1:T(8,128)(2,1)}, bf16[2,2,96,768]{3,2,0,1:T(8,128)(2,1)}, u32[]{:S(2)}, u32[]{:S(2)}) %collective-permute-start.26) | collective-permute-done | bytes 589856 | tf_op jit(solution)/shard_map/ppermute | solution.py:75
  75.4 1.9 %collective-permute-start.27 = (bf16[2,96,768]{2,1,0:T(8,128)(2,1)S(1)}, bf16[2,96,768]{2,1,0:T(8,128)(2,1)}, u32[]{:S(2)}, u32[]{:S(2)}) collective-permute-start(bf16[2,96,768]{2,1,0:T(8,128)(2,1)S(1)} %fusion.38), channel_id=1, source_target_pairs={{0,8},{4,12},{8,0},{12,4},{16,24},{20,28},{24,16},{28,20},{1,9},{5... | collective-permute-start | bytes 884744 | tf_op jit(solution)/shard_map/ppermute | solution.py:75
  77.3 8.7 %collective-permute-done.23 = bf16[2,2,96,768]{3,2,0,1:T(8,128)(2,1)} collective-permute-done((bf16[2,2,96,768]{3,2,0,1:T(8,128)(2,1)}, bf16[2,2,96,768]{3,2,0,1:T(8,128)(2,1)}, u32[]{:S(2)}, u32[]{:S(2)}) %collective-permute-start.23) | collective-permute-done | bytes 589856 | tf_op jit(solution)/shard_map/ppermute | solution.py:75
  86.0 2.2 %bitcast_add_fusion.1 = f32[2,2,96,768]{3,2,0,1:T(8,128)} fusion(bf16[2,2,96,768]{3,2,0,1:T(8,128)(2,1)} %collective-permute-done.23, f32[2,2,2,96,768]{4,3,2,1,0:T(8,128)S(1)} %bitcast.167, s32[]{:T(128)S(6)} %select_n.102), kind=kLoop, calls=%fused_computation.44 | loop fusion | flops 589824 | bytes 2949124 | tf_op jit(solution)/shard_map/add | solution.py:76
  88.2 1.8 %fusion.37 = bf16[2,96,768]{2,1,0:T(8,128)(2,1)} fusion(f32[2,2,96,768]{3,2,0,1:T(8,128)} %bitcast_add_fusion.1, s32[]{:T(128)S(6)} %select_n.105), kind=kLoop, calls=%fused_computation.100 | loop fusion | bytes 589828 | tf_op jit(solution)/shard_map/convert_element_type | solution.py:75
  90.0 1.8 %collective-permute-start.24 = (bf16[2,96,768]{2,1,0:T(8,128)(2,1)}, bf16[2,96,768]{2,1,0:T(8,128)(2,1)}, u32[]{:S(2)}, u32[]{:S(2)}) collective-permute-start(bf16[2,96,768]{2,1,0:T(8,128)(2,1)} %fusion.37), channel_id=1, source_target_pairs={{0,8},{4,12},{8,0},{12,4},{16,24},{20,28},{24,16},{28,20},{1,9},{5... | collective-permute-start | bytes 884744 | tf_op jit(solution)/shard_map/ppermute | solution.py:75
  95.9 2.7 %collective-permute-start.28 = (bf16[96,768]{1,0:T(8,128)(2,1)S(1)}, bf16[96,768]{1,0:T(8,128)(2,1)S(1)}, u32[]{:S(2)}, u32[]{:S(2)}) collective-permute-start(bf16[96,768]{1,0:T(8,128)(2,1)S(1)} %fusion.47), channel_id=1, source_target_pairs={{0,16},{4,20},{8,24},{12,28},{16,0},{20,4},{24,8},{28,12},{1,17},{... | collective-permute-start | bytes 442376 | tf_op jit(solution)/shard_map/ppermute | solution.py:75
  100.0 4.2 %collective-permute-start.25 = (bf16[96,768]{1,0:T(8,128)(2,1)S(1)}, bf16[96,768]{1,0:T(8,128)(2,1)S(1)}, u32[]{:S(2)}, u32[]{:S(2)}) collective-permute-start(bf16[96,768]{1,0:T(8,128)(2,1)S(1)} %fusion.46), channel_id=1, source_target_pairs={{0,16},{4,20},{8,24},{12,28},{16,0},{20,4},{24,8},{28,12},{1,17},{... | collective-permute-start | bytes 442376 | tf_op jit(solution)/shard_map/ppermute | solution.py:75
  104.2 5.3 %collective-permute-done.28 = bf16[96,768]{1,0:T(8,128)(2,1)S(1)} collective-permute-done((bf16[96,768]{1,0:T(8,128)(2,1)S(1)}, bf16[96,768]{1,0:T(8,128)(2,1)S(1)}, u32[]{:S(2)}, u32[]{:S(2)}) %collective-permute-start.28) | collective-permute-done | bytes 147488 | tf_op jit(solution)/shard_map/ppermute | solution.py:75
  110.2 2.0 %collective-permute-done.25 = bf16[96,768]{1,0:T(8,128)(2,1)S(1)} collective-permute-done((bf16[96,768]{1,0:T(8,128)(2,1)S(1)}, bf16[96,768]{1,0:T(8,128)(2,1)S(1)}, u32[]{:S(2)}, u32[]{:S(2)}) %collective-permute-start.25) | collective-permute-done | bytes 147488 | tf_op jit(solution)/shard_map/ppermute | solution.py:75
  125.3 2.0 %copy.69 = f32[768,768]{1,0:T(8,128)} copy(f32[768,768]{0,1:T(8,128)S(1)} %pad_maximum_fusion) | data formatting | bytes 4718592 | tf_op jit(solution)/shard_map/concatenate | solution.py:227
  128.8 1.6 collective-permute-start.13
  131.1 1.8 %convolution_convert_fusion = bf16[256,768]{1,0:T(8,128)(2,1)S(1)} fusion(bf16[768,576]{0,1:T(8,128)(2,1)} %bitcast.181, bf16[512,576]{0,1:T(8,128)(2,1)} %copy-done.24, s32[]{:T(128)S(6)} %select_n.99), kind=kOutput, calls=%fused_computation.35 | convolution fusion | flops 226689024 | bytes 1572868 | tf_op jit(solution)/shard_map/dot_general | solution.py:43
  132.9 1.7 %collective-permute-done.17 = f32[2,2,24]{2,1,0:T(2,128)S(1)} collective-permute-done((f32[2,2,24]{2,1,0:T(2,128)S(1)}, f32[2,2,24]{2,1,0:T(2,128)S(1)}, u32[]{:S(2)}, u32[]{:S(2)}) %collective-permute-start.17) | collective-permute-done | bytes 416 | tf_op jit(solution)/shard_map/ppermute | solution.py:94
  135.8 2.8 %collective-permute-start.18 = (f32[2,24]{1,0:T(2,128)S(1)}, f32[2,24]{1,0:T(2,128)S(1)}, u32[]{:S(2)}, u32[]{:S(2)}) collective-permute-start(f32[2,24]{1,0:T(2,128)S(1)} %fusion.67), channel_id=1, source_target_pairs={{0,16},{4,20},{8,24},{12,28},{16,0},{20,4},{24,8},{28,12},{1,17},{... | collective-permute-start | bytes 584 | tf_op jit(solution)/shard_map/ppermute | solution.py:94
  141.2 2.5 %collective-permute-done.22 = f32[7,96]{1,0:T(8,128)S(1)} collective-permute-done((f32[7,96]{1,0:T(8,128)S(1)}, f32[7,96]{1,0:T(8,128)S(1)}, u32[]{:S(2)}, u32[]{:S(2)}) %collective-permute-start.22) | collective-permute-done | bytes 2720 | tf_op jit(solution)/shard_map/ppermute | solution.py:94
  147.7 3.0 %collective-permute-done.14 = bf16[2,96,768]{2,1,0:T(8,128)(2,1)S(1)} collective-permute-done((bf16[2,96,768]{2,1,0:T(8,128)(2,1)S(1)}, bf16[2,96,768]{2,1,0:T(8,128)(2,1)S(1)}, u32[]{:S(2)}, u32[]{:S(2)}) %collective-permute-start.14) | collective-permute-done | bytes 294944 | tf_op jit(solution)/shard_map/ppermute | solution.py:75
  150.8 2.4 %collective-permute-start.15 = (bf16[96,768]{1,0:T(8,128)(2,1)S(1)}, bf16[96,768]{1,0:T(8,128)(2,1)S(1)}, u32[]{:S(2)}, u32[]{:S(2)}) collective-permute-start(bf16[96,768]{1,0:T(8,128)(2,1)S(1)} %fusion.45), channel_id=1, source_target_pairs={{0,16},{4,20},{8,24},{12,28},{16,0},{20,4},{24,8},{28,12},{1,17},{... | collective-permute-start | bytes 442376 | tf_op jit(solution)/shard_map/ppermute | solution.py:75
  154.4 4.1 %collective-permute-done.15 = bf16[96,768]{1,0:T(8,128)(2,1)S(1)} collective-permute-done((bf16[96,768]{1,0:T(8,128)(2,1)S(1)}, bf16[96,768]{1,0:T(8,128)(2,1)S(1)}, u32[]{:S(2)}, u32[]{:S(2)}) %collective-permute-start.15) | collective-permute-done | bytes 147488 | tf_op jit(solution)/shard_map/ppermute | solution.py:75
  (284 shorter events, 58.6 us)
Async XLA Ops:
  0.6 24.8 %copy-start = (bf16[768,768]{1,0:T(8,128)(2,1)S(1)}, bf16[768,768]{1,0:T(8,128)(2,1)}, u32[]{:S(2)}) copy-start(bf16[768,768]{1,0:T(8,128)(2,1)} %param.22) | copy-start | bytes 3538948
  8.2 1.9 %collective-permute-start = (bf16[256,768]{1,0:T(8,128)(2,1)S(1)}, bf16[256,768]{1,0:T(8,128)(2,1)S(1)}, u32[]{:S(2)}, u32[]{:S(2)}) collective-permute-start(bf16[256,768]{1,0:T(8,128)(2,1)S(1)} %convolution_convert_fusion.3), channel_id=1, source_target_pairs={{0,1},{1,0},{2,3},{3,2},{4,5},{5,4},{6,7},{7,6},{8,9},{9,8},{10,11... | collective-permute-start | bytes 1179656 | tf_op jit(solution)/shard_map/ppermute | solution.py:34
  10.4 12.3 %collective-permute-start.1 = (bf16[256,768]{1,0:T(8,128)(2,1)S(1)}, bf16[256,768]{1,0:T(8,128)(2,1)S(1)}, u32[]{:S(2)}, u32[]{:S(2)}) collective-permute-start(bf16[256,768]{1,0:T(8,128)(2,1)S(1)} %add_convert_fusion.5), channel_id=1, source_target_pairs={{0,2},{1,3},{2,0},{3,1},{4,6},{5,7},{6,4},{7,5},{8,10},{9,11},{10,... | collective-permute-start | bytes 1179656 | tf_op jit(solution)/shard_map/ppermute | solution.py:38
  23.0 22.1 %copy-start.41 = (f32[256]{0:T(256)}, f32[256]{0:T(256)S(1)}, u32[]{:S(2)}) copy-start(f32[256]{0:T(256)S(1)} %broadcast_multiply_fusion.5) | copy-start | bytes 3076
  23.6 1.8 %collective-permute-start.2 = (bf16[256,768]{1,0:T(8,128)(2,1)S(1)}, bf16[256,768]{1,0:T(8,128)(2,1)S(1)}, u32[]{:S(2)}, u32[]{:S(2)}) collective-permute-start(bf16[256,768]{1,0:T(8,128)(2,1)S(1)} %get-tuple-element.85), channel_id=1, source_target_pairs={{0,1},{1,0},{2,3},{3,2},{4,5},{5,4},{6,7},{7,6},{8,9},{9,8},{10,11... | collective-permute-start | bytes 1179656 | tf_op jit(solution)/shard_map/ppermute | solution.py:34
  31.6 1.8 %collective-permute-start.3 = (bf16[256,768]{1,0:T(8,128)(2,1)S(1)}, bf16[256,768]{1,0:T(8,128)(2,1)S(1)}, u32[]{:S(2)}, u32[]{:S(2)}) collective-permute-start(bf16[256,768]{1,0:T(8,128)(2,1)S(1)} %convolution_convert_fusion.2), channel_id=1, source_target_pairs={{0,1},{1,0},{2,3},{3,2},{4,5},{5,4},{6,7},{7,6},{8,9},{9,8},{10,11... | collective-permute-start | bytes 1179656 | tf_op jit(solution)/shard_map/ppermute | solution.py:34
  33.9 11.2 %collective-permute-start.4 = (bf16[256,768]{1,0:T(8,128)(2,1)S(1)}, bf16[256,768]{1,0:T(8,128)(2,1)S(1)}, u32[]{:S(2)}, u32[]{:S(2)}) collective-permute-start(bf16[256,768]{1,0:T(8,128)(2,1)S(1)} %add_convert_fusion.4), channel_id=1, source_target_pairs={{0,2},{1,3},{2,0},{3,1},{4,6},{5,7},{6,4},{7,5},{8,10},{9,11},{10,... | collective-permute-start | bytes 1179656 | tf_op jit(solution)/shard_map/ppermute | solution.py:38
  47.5 1.8 %collective-permute-start.6 = (bf16[256,768]{1,0:T(8,128)(2,1)S(1)}, bf16[256,768]{1,0:T(8,128)(2,1)S(1)}, u32[]{:S(2)}, u32[]{:S(2)}) collective-permute-start(bf16[256,768]{1,0:T(8,128)(2,1)S(1)} %get-tuple-element.77), channel_id=1, source_target_pairs={{0,1},{1,0},{2,3},{3,2},{4,5},{5,4},{6,7},{7,6},{8,9},{9,8},{10,11... | collective-permute-start | bytes 1179656 | tf_op jit(solution)/shard_map/ppermute | solution.py:34
  48.9 14.4 %collective-permute-start.5 = (bf16[256,768]{1,0:T(8,128)(2,1)}, bf16[256,768]{1,0:T(8,128)(2,1)}, u32[]{:S(2)}, u32[]{:S(2)}) collective-permute-start(bf16[256,768]{1,0:T(8,128)(2,1)} %get-tuple-element.79), channel_id=1, source_target_pairs={{0,1},{1,0},{2,3},{3,2},{4,5},{5,4},{6,7},{7,6},{8,9},{9,8},{10,11... | collective-permute-start | bytes 1179656 | tf_op jit(solution)/shard_map/ppermute | solution.py:34
  57.5 16.5 %collective-permute-start.26 = (bf16[2,2,96,768]{3,2,0,1:T(8,128)(2,1)}, bf16[2,2,96,768]{3,2,0,1:T(8,128)(2,1)}, u32[]{:S(2)}, u32[]{:S(2)}) collective-permute-start(bf16[2,2,96,768]{3,2,0,1:T(8,128)(2,1)} %fusion.25), channel_id=1, source_target_pairs={{0,4},{4,0},{8,12},{12,8},{16,20},{20,16},{24,28},{28,24},{1,5},{5... | collective-permute-start | bytes 1769480 | tf_op jit(solution)/shard_map/ppermute | solution.py:75
  59.3 5.9 %collective-permute-start.7 = (bf16[256,768]{1,0:T(8,128)(2,1)}, bf16[256,768]{1,0:T(8,128)(2,1)}, u32[]{:S(2)}, u32[]{:S(2)}) collective-permute-start(bf16[256,768]{1,0:T(8,128)(2,1)} %convolution_convert_fusion.1), channel_id=1, source_target_pairs={{0,1},{1,0},{2,3},{3,2},{4,5},{5,4},{6,7},{7,6},{8,9},{9,8},{10,11... | collective-permute-start | bytes 1179656 | tf_op jit(solution)/shard_map/ppermute | solution.py:34
  60.2 25.8 %collective-permute-start.23 = (bf16[2,2,96,768]{3,2,0,1:T(8,128)(2,1)}, bf16[2,2,96,768]{3,2,0,1:T(8,128)(2,1)}, u32[]{:S(2)}, u32[]{:S(2)}) collective-permute-start(bf16[2,2,96,768]{3,2,0,1:T(8,128)(2,1)} %fusion.24), channel_id=1, source_target_pairs={{0,4},{4,0},{8,12},{12,8},{16,20},{20,16},{24,28},{28,24},{1,5},{5... | collective-permute-start | bytes 1769480 | tf_op jit(solution)/shard_map/ppermute | solution.py:75
  66.8 19.1 %copy-start.4 = (f32[768,768]{1,0:T(8,128)S(1)}, f32[768,768]{1,0:T(8,128)}, u32[]{:S(2)}) copy-start(f32[768,768]{1,0:T(8,128)} %copy-done.3) | copy-start | bytes 7077892
  66.9 25.0 %collective-permute-start.8 = (bf16[256,768]{1,0:T(8,128)(2,1)S(1)}, bf16[256,768]{1,0:T(8,128)(2,1)S(1)}, u32[]{:S(2)}, u32[]{:S(2)}) collective-permute-start(bf16[256,768]{1,0:T(8,128)(2,1)S(1)} %add_convert_fusion.3), channel_id=1, source_target_pairs={{0,2},{1,3},{2,0},{3,1},{4,6},{5,7},{6,4},{7,5},{8,10},{9,11},{10,... | collective-permute-start | bytes 1179656 | tf_op jit(solution)/shard_map/ppermute | solution.py:38
  75.4 19.3 %collective-permute-start.27 = (bf16[2,96,768]{2,1,0:T(8,128)(2,1)S(1)}, bf16[2,96,768]{2,1,0:T(8,128)(2,1)}, u32[]{:S(2)}, u32[]{:S(2)}) collective-permute-start(bf16[2,96,768]{2,1,0:T(8,128)(2,1)S(1)} %fusion.38), channel_id=1, source_target_pairs={{0,8},{4,12},{8,0},{12,4},{16,24},{20,28},{24,16},{28,20},{1,9},{5... | collective-permute-start | bytes 884744 | tf_op jit(solution)/shard_map/ppermute | solution.py:75
  90.0 8.7 %collective-permute-start.24 = (bf16[2,96,768]{2,1,0:T(8,128)(2,1)}, bf16[2,96,768]{2,1,0:T(8,128)(2,1)}, u32[]{:S(2)}, u32[]{:S(2)}) collective-permute-start(bf16[2,96,768]{2,1,0:T(8,128)(2,1)} %fusion.37), channel_id=1, source_target_pairs={{0,8},{4,12},{8,0},{12,4},{16,24},{20,28},{24,16},{28,20},{1,9},{5... | collective-permute-start | bytes 884744 | tf_op jit(solution)/shard_map/ppermute | solution.py:75
  92.8 1.8 %collective-permute-start.19 = (f32[4,768]{1,0:T(4,128)S(1)}, f32[4,768]{1,0:T(4,128)S(1)}, u32[]{:S(2)}, u32[]{:S(2)}) collective-permute-start(f32[4,768]{1,0:T(4,128)S(1)} %pad_maximum_fusion.3), channel_id=1, source_target_pairs={{0,1},{1,0},{2,3},{3,2},{4,5},{5,4},{6,7},{7,6},{8,9},{9,8},{10,11... | collective-permute-start | bytes 36872 | tf_op jit(solution)/shard_map/ppermute | solution.py:34
  94.1 18.8 %collective-permute-start.9 = (bf16[256,768]{1,0:T(8,128)(2,1)S(1)}, bf16[256,768]{1,0:T(8,128)(2,1)S(1)}, u32[]{:S(2)}, u32[]{:S(2)}) collective-permute-start(bf16[256,768]{1,0:T(8,128)(2,1)S(1)} %get-tuple-element.73), channel_id=1, source_target_pairs={{0,1},{1,0},{2,3},{3,2},{4,5},{5,4},{6,7},{7,6},{8,9},{9,8},{10,11... | collective-permute-start | bytes 1179656 | tf_op jit(solution)/shard_map/ppermute | solution.py:34
  95.9 13.5 %collective-permute-start.28 = (bf16[96,768]{1,0:T(8,128)(2,1)S(1)}, bf16[96,768]{1,0:T(8,128)(2,1)S(1)}, u32[]{:S(2)}, u32[]{:S(2)}) collective-permute-start(bf16[96,768]{1,0:T(8,128)(2,1)S(1)} %fusion.47), channel_id=1, source_target_pairs={{0,16},{4,20},{8,24},{12,28},{16,0},{20,4},{24,8},{28,12},{1,17},{... | collective-permute-start | bytes 442376 | tf_op jit(solution)/shard_map/ppermute | solution.py:75
  100.0 12.2 %collective-permute-start.25 = (bf16[96,768]{1,0:T(8,128)(2,1)S(1)}, bf16[96,768]{1,0:T(8,128)(2,1)S(1)}, u32[]{:S(2)}, u32[]{:S(2)}) collective-permute-start(bf16[96,768]{1,0:T(8,128)(2,1)S(1)} %fusion.46), channel_id=1, source_target_pairs={{0,16},{4,20},{8,24},{12,28},{16,0},{20,4},{24,8},{28,12},{1,17},{... | collective-permute-start | bytes 442376 | tf_op jit(solution)/shard_map/ppermute | solution.py:75
  120.5 14.2 %collective-permute-start.20 = (f32[2,2,7,96]{3,1,2,0:T(2,128)}, f32[2,2,7,96]{3,1,2,0:T(2,128)}, u32[]{:S(2)}, u32[]{:S(2)}) collective-permute-start(f32[2,2,7,96]{3,1,2,0:T(2,128)} %bitcast.160), channel_id=1, source_target_pairs={{0,4},{4,0},{8,12},{12,8},{16,20},{20,16},{24,28},{28,24},{1,5},{5... | collective-permute-start | bytes 32264 | tf_op jit(solution)/shard_map/ppermute | solution.py:94
  123.6 6.8 %collective-permute-start.16 = (f32[2,2,2,24]{3,2,1,0:T(2,128)}, f32[2,2,2,24]{3,2,1,0:T(2,128)}, u32[]{:S(2)}, u32[]{:S(2)}) collective-permute-start(f32[2,2,2,24]{3,2,1,0:T(2,128)} %bitcast.163), channel_id=1, source_target_pairs={{0,4},{4,0},{8,12},{12,8},{16,20},{20,16},{24,28},{28,24},{1,5},{5... | collective-permute-start | bytes 2312 | tf_op jit(solution)/shard_map/ppermute | solution.py:94
  128.8 15.0 %collective-permute-start.13 = (bf16[2,2,96,768]{3,2,1,0:T(8,128)(2,1)S(1)}, bf16[2,2,96,768]{3,2,1,0:T(8,128)(2,1)S(1)}, u32[]{:S(2)}, u32[]{:S(2)}) collective-permute-start(bf16[2,2,96,768]{3,2,1,0:T(8,128)(2,1)S(1)} %fusion.23), channel_id=1, source_target_pairs={{0,4},{4,0},{8,12},{12,8},{16,20},{20,16},{24,28},{28,24},{1,5},{5... | collective-permute-start | bytes 1769480 | tf_op jit(solution)/shard_map/ppermute | solution.py:75
  131.1 3.6 %collective-permute-start.17 = (f32[2,2,24]{2,1,0:T(2,128)S(1)}, f32[2,2,24]{2,1,0:T(2,128)S(1)}, u32[]{:S(2)}, u32[]{:S(2)}) collective-permute-start(f32[2,2,24]{2,1,0:T(2,128)S(1)} %fusion.64), channel_id=1, source_target_pairs={{0,8},{4,12},{8,0},{12,4},{16,24},{20,28},{24,16},{28,20},{1,9},{5... | collective-permute-start | bytes 1160 | tf_op jit(solution)/shard_map/ppermute | solution.py:94
  132.9 11.5 %collective-permute-start.10 = (bf16[256,768]{1,0:T(8,128)(2,1)S(1)}, bf16[256,768]{1,0:T(8,128)(2,1)S(1)}, u32[]{:S(2)}, u32[]{:S(2)}) collective-permute-start(bf16[256,768]{1,0:T(8,128)(2,1)S(1)} %convolution_convert_fusion), channel_id=1, source_target_pairs={{0,1},{1,0},{2,3},{3,2},{4,5},{5,4},{6,7},{7,6},{8,9},{9,8},{10,11... | collective-permute-start | bytes 1179656 | tf_op jit(solution)/shard_map/ppermute | solution.py:34
  135.4 3.7 %collective-permute-start.21 = (f32[2,7,96]{2,0,1:T(2,128)S(1)}, f32[2,7,96]{2,0,1:T(2,128)S(1)}, u32[]{:S(2)}, u32[]{:S(2)}) collective-permute-start(f32[2,7,96]{2,0,1:T(2,128)S(1)} %bitcast.191), channel_id=1, source_target_pairs={{0,8},{4,12},{8,0},{12,4},{16,24},{20,28},{24,16},{28,20},{1,9},{5... | collective-permute-start | bytes 16136 | tf_op jit(solution)/shard_map/ppermute | solution.py:94
  135.8 4.8 %collective-permute-start.18 = (f32[2,24]{1,0:T(2,128)S(1)}, f32[2,24]{1,0:T(2,128)S(1)}, u32[]{:S(2)}, u32[]{:S(2)}) collective-permute-start(f32[2,24]{1,0:T(2,128)S(1)} %fusion.67), channel_id=1, source_target_pairs={{0,16},{4,20},{8,24},{12,28},{16,0},{20,4},{24,8},{28,12},{1,17},{... | collective-permute-start | bytes 584 | tf_op jit(solution)/shard_map/ppermute | solution.py:94
  139.2 4.6 %collective-permute-start.22 = (f32[7,96]{1,0:T(8,128)S(1)}, f32[7,96]{1,0:T(8,128)S(1)}, u32[]{:S(2)}, u32[]{:S(2)}) collective-permute-start(f32[7,96]{1,0:T(8,128)S(1)} %bitcast.192), channel_id=1, source_target_pairs={{0,16},{4,20},{8,24},{12,28},{16,0},{20,4},{24,8},{28,12},{1,17},{... | collective-permute-start | bytes 8072 | tf_op jit(solution)/shard_map/ppermute | solution.py:94
  143.9 6.8 %collective-permute-start.14 = (bf16[2,96,768]{2,1,0:T(8,128)(2,1)S(1)}, bf16[2,96,768]{2,1,0:T(8,128)(2,1)S(1)}, u32[]{:S(2)}, u32[]{:S(2)}) collective-permute-start(bf16[2,96,768]{2,1,0:T(8,128)(2,1)S(1)} %fusion.36), channel_id=1, source_target_pairs={{0,8},{4,12},{8,0},{12,4},{16,24},{20,28},{24,16},{28,20},{1,9},{5... | collective-permute-start | bytes 884744 | tf_op jit(solution)/shard_map/ppermute | solution.py:75
  145.6 8.5 %collective-permute-start.11 = (bf16[256,768]{1,0:T(8,128)(2,1)S(1)}, bf16[256,768]{1,0:T(8,128)(2,1)S(1)}, u32[]{:S(2)}, u32[]{:S(2)}) collective-permute-start(bf16[256,768]{1,0:T(8,128)(2,1)S(1)} %add_convert_fusion.2), channel_id=1, source_target_pairs={{0,2},{1,3},{2,0},{3,1},{4,6},{5,7},{6,4},{7,5},{8,10},{9,11},{10,... | collective-permute-start | bytes 1179656 | tf_op jit(solution)/shard_map/ppermute | solution.py:38
  150.8 7.7 %collective-permute-start.15 = (bf16[96,768]{1,0:T(8,128)(2,1)S(1)}, bf16[96,768]{1,0:T(8,128)(2,1)S(1)}, u32[]{:S(2)}, u32[]{:S(2)}) collective-permute-start(bf16[96,768]{1,0:T(8,128)(2,1)S(1)} %fusion.45), channel_id=1, source_target_pairs={{0,16},{4,20},{8,24},{12,28},{16,0},{20,4},{24,8},{28,12},{1,17},{... | collective-permute-start | bytes 442376 | tf_op jit(solution)/shard_map/ppermute | solution.py:75
  154.3 6.1 %collective-permute-start.12 = (bf16[256,768]{1,0:T(8,128)(2,1)S(1)}, bf16[256,768]{1,0:T(8,128)(2,1)}, u32[]{:S(2)}, u32[]{:S(2)}) collective-permute-start(bf16[256,768]{1,0:T(8,128)(2,1)S(1)} %get-tuple-element.71), channel_id=1, source_target_pairs={{0,1},{1,0},{2,3},{3,2},{4,5},{5,4},{6,7},{7,6},{8,9},{9,8},{10,11... | collective-permute-start | bytes 1179656 | tf_op jit(solution)/shard_map/ppermute | solution.py:34
  (66 other events, 417.4 us)

commit v2 on v0

v2 whole, which is shorter than its diff:
```python
import jax
import jax.numpy as jnp
import numpy as np
from jax import lax
from jax.experimental import pallas as pl
from jax.experimental.pallas import tpu as pltpu
from jax.sharding import PartitionSpec as P

HEAD_DIM = 64
NORM_EPSILON = 1e-05
CORES = 2
F32 = jnp.float32
LOW = jnp.bfloat16
MIB = 1 << 20

VECTOR_ROWS = 8
PAIR_ROWS = 2 * VECTOR_ROWS


def nn(left, right):
    return lax.dot_general(left, right, (((1,), (0,)), ((), ())), preferred_element_type=F32)


def nt(left, right):
    return lax.dot_general(left, right, (((1,), (1,)), ((), ())), preferred_element_type=F32)


def tn(left, right):
    return lax.dot_general(left, right, (((0,), (0,)), ((), ())), preferred_element_type=F32)


def normalize(resid):
    center = resid - jnp.mean(resid, -1, keepdims=True)
    inverse = lax.rsqrt(jnp.mean(center * center, -1, keepdims=True) + NORM_EPSILON)
    return center * inverse, inverse


def norm_back(grad_norm, normed, inverse):
    mean_grad = jnp.mean(grad_norm, -1, keepdims=True)
    mean_proj = jnp.mean(grad_norm * normed, -1, keepdims=True)
    return inverse * (grad_norm - mean_grad - normed * mean_proj)


def call(kernel, outs, scalars, *arrays, scratch=(), flops=0, mib=40):
    shapes = tuple(jax.ShapeDtypeStruct(shape, dtype) for shape, dtype in outs)
    moved = sum(a.size * a.dtype.itemsize for a in arrays)
    moved += sum(int(np.prod(s)) * jnp.dtype(d).itemsize for s, d in outs)
    whole = pl.BlockSpec(memory_space=pltpu.VMEM)
    return pl.pallas_call(
        kernel,
        out_shape=shapes,
        in_specs=[pl.BlockSpec(memory_space=pltpu.SMEM)] + [whole] * len(arrays),
        out_specs=tuple(whole for _ in outs),
        scratch_shapes=list(scratch),
        compiler_params=pltpu.CompilerParams(vmem_limit_bytes=mib * MIB),
        cost_estimate=pl.CostEstimate(flops=int(flops), bytes_accessed=int(moved), transcendentals=0),
    )(scalars, *arrays)


def attn_forward(info, tokens, w_qkv, bias_qv, w_out, q_o, k_o, v_o, att_o, send_o, keep_o):
    core, length = info[0], info[1]
    rows, width = q_o.shape
    half = rows // 2
    x = tokens[...]
    query = (nn(x, w_qkv[0]) + bias_qv[0:1, :]).astype(LOW)
    keys = nn(x, w_qkv[1]).astype(LOW)
    values = (nn(x, w_qkv[2]) + bias_qv[1:2, :]).astype(LOW)
    q_o[...] = query
    k_o[...] = keys
    v_o[...] = values
    head_of = lax.broadcasted_iota(jnp.int32, (rows, width), 1) // HEAD_DIM
    key_valid = lax.broadcasted_iota(jnp.int32, (rows, rows), 1) < length
    scaled = query.astype(F32) * HEAD_DIM ** -0.5
    value_full = values.astype(F32)
    total = jnp.zeros((rows, width), F32)
    for head in range(width // HEAD_DIM):
        here = head_of == head
        scores = nt(jnp.where(here, scaled, 0.0).astype(LOW), keys)
        scores = jnp.where(key_valid, scores, -1e30)
        expo = jnp.exp(scores - jnp.max(scores, -1, keepdims=True))
        probs = (expo * (1.0 / jnp.sum(expo, -1, keepdims=True))).astype(LOW)
        total = total + nn(probs, jnp.where(here, value_full, 0.0).astype(LOW))
    att_o[...] = total.astype(LOW)
    other_start = pl.multiple_of((1 - core) * half, half)
    own_start = pl.multiple_of(core * half, half)
    send_o[...] = nn(att_o[pl.ds(other_start, half), :], w_out[...]).astype(LOW)
    keep_o[...] = nn(att_o[pl.ds(own_start, half), :], w_out[...])


def mlp_forward(
    info, tokens, own, received, bias_out, gain_one, shift_one,
    up_own, up_other, bias_own, bias_other, down_own, down_other,
    pass_o, act_o, slope_own_o, slope_other_o, normed_o, inverse_o, part_o,
):
    half, width = own.shape
    units = up_own.shape[1]
    start = pl.multiple_of(info[0] * half, half)
    resid = tokens[pl.ds(start, half), :].astype(F32) + bias_out[...]
    resid = resid + (own[...].astype(F32) + received[...].astype(F32))
    normed, inverse = normalize(resid)
    normed_o[...] = normed
    inverse_o[...] = inverse
    hidden_low = (normed * gain_one[...] + shift_one[...]).astype(LOW)
    pass_o[:, :width] = hidden_low

    def units_of(up, bias, slope_o):
        pre = nn(hidden_low, up[...]) + bias[...]
        cdf = 0.5 * (1.0 + lax.erf(pre * 0.7071067811865476))
        slope_o[...] = cdf + pre * (jnp.exp(-0.5 * pre * pre) * 0.3989422804014327)
        return (pre * cdf).astype(LOW)

    act_other = units_of(up_other, bias_other, slope_other_o)
    pass_o[:, width : width + units] = act_other
    act_own = units_of(up_own, bias_own, slope_own_o)
    act_o[...] = act_own
    part_o[...] = (nn(act_own, down_own[...]) + nn(act_other, down_other[...])).astype(LOW)


def mlp_backward(
    info, cotangent, own, received, normed_one, gain_one, shift_one, bias_down, gain_two, shift_two,
    slope_own, slope_other, up_own, up_other, down_own, down_other,
    out_o, resid_o, pass_o, pre_o, part_o, sums_o,
):
    half, width = own.shape
    units = up_own.shape[1]
    core, length = info[0], info[1]
    start = pl.multiple_of(core * half, half)
    hidden = normed_one[...] * gain_one[...] + shift_one[...]
    branch = own[...].astype(F32) + received[...].astype(F32) + bias_down[...]
    normed, inverse = normalize(hidden + branch)
    valid = lax.broadcasted_iota(jnp.int32, (half, width), 0) + core * half < length
    out_o[...] = jnp.where(valid, normed * gain_two[...] + shift_two[...], 0.0).astype(LOW)
    grad_out = jnp.where(valid, cotangent[pl.ds(start, half), :].astype(F32), 0.0)
    sums_o[0:1, :] = jnp.sum(grad_out * normed, 0, keepdims=True)
    sums_o[1:2, :] = jnp.sum(grad_out, 0, keepdims=True)
    grad_resid = norm_back(grad_out * gain_two[...], normed, inverse)
    resid_o[...] = grad_resid
    grad_mlp = grad_resid.astype(LOW)
    pass_o[:, :width] = grad_mlp
    pre_other = (nt(grad_mlp, down_other[...]) * slope_other[...]).astype(LOW)
    pass_o[:, width : width + units] = pre_other
    pre_own = (nt(grad_mlp, down_own[...]) * slope_own[...]).astype(LOW)
    pre_o[...] = pre_own
    part_o[...] = (nt(pre_own, up_own[...]) + nt(pre_other, up_other[...])).astype(LOW)


def spread(blocks, grad):
    block = blocks.shape[1]
    for index in range(blocks.shape[0]):
        blocks[index] = grad[index * block : (index + 1) * block, :]


def mlp_weights(
    ids, fwd_own, fwd_other, act_own, bwd_own, bwd_other, pre_own,
    send_o, keep_o, sums_o, up_blocks, down_blocks,
):
    width = up_blocks.shape[2]
    model = fwd_own.shape[1] - width
    grad_mlp_own, grad_mlp_other = bwd_own[:, :model], bwd_other[:, :model]
    pre_other = bwd_other[:, model:]
    spread(down_blocks, tn(grad_mlp_own, act_own[...]) + tn(grad_mlp_other, fwd_other[:, model:]))
    spread(up_blocks, tn(fwd_own[:, :model], pre_own[...]) + tn(fwd_other[:, :model], pre_other))
    count = keep_o.shape[0]
    for index in range(count):
        source = ids[index + count]
        send_o[index, 0] = down_blocks[source].astype(LOW)
        send_o[index, 1] = up_blocks[source].astype(LOW)
    for index in range(count):
        source = ids[index]
        keep_o[index, 0] = down_blocks[source]
        keep_o[index, 1] = up_blocks[source]

    def column_sum(first, second):
        return jnp.sum(first.astype(F32), 0, keepdims=True) + jnp.sum(
            second.astype(F32), 0, keepdims=True
        )

    sums_o[0:1, :] = column_sum(grad_mlp_own, grad_mlp_other)
    sums_o[1:2, :] = column_sum(pre_own[...], pre_other)


def norm_one_back(info, resid_two, own, received, normed, inverse, gain_one, resid_o, low_o, sums_o):
    grad_hidden = resid_two[...] + (own[...].astype(F32) + received[...].astype(F32))
    sums_o[0:1, :] = jnp.sum(grad_hidden * normed[...], 0, keepdims=True)
    sums_o[1:2, :] = jnp.sum(grad_hidden, 0, keepdims=True)
    grad_resid = norm_back(grad_hidden * gain_one[...], normed[...], inverse[...])
    resid_o[...] = grad_resid
    low = grad_resid.astype(LOW)
    low_o[...] = low
    sums_o[2:3, :] = jnp.sum(low.astype(F32), 0, keepdims=True)


def split_pair(vectors):
    high = vectors.astype(LOW)
    return jnp.concatenate([high.astype(F32), vectors - high.astype(F32)], 0).astype(LOW)


def attn_backward(
    info, grad_own, grad_other, w_out, q_i, k_i, v_i, att_i, tokens, vectors,
    gq_o, gk_o, gv_o, send_o, keep_o, grad_attn, blocks, sums,
):
    core, length = info[0], info[1]
    rows, width = q_i.shape
    half = rows // 2
    grad_attn[pl.ds(pl.multiple_of(core * half, half), half), :] = grad_own[...]
    grad_attn[pl.ds(pl.multiple_of((1 - core) * half, half), half), :] = grad_other[...]
    grad_rows = grad_attn[...]
    grad_att = nt(grad_rows, w_out[...]).astype(LOW)
    scale = HEAD_DIM ** -0.5
    head_of = lax.broadcasted_iota(jnp.int32, (rows, width), 1) // HEAD_DIM
    key_valid = lax.broadcasted_iota(jnp.int32, (rows, rows), 0) < length
    query, keys, values = q_i[...], k_i[...], v_i[...]
    scaled = query.astype(F32) * scale
    scaled_keys = keys.astype(F32) * scale
    grad_att_full = grad_att.astype(F32)
    grad_q = jnp.zeros((rows, width), F32)
    grad_k = jnp.zeros((rows, width), F32)
    grad_v = jnp.zeros((rows, width), F32)
    for head in range(width // HEAD_DIM):
        here = head_of == head
        scaled_here = jnp.where(here, scaled, 0.0).astype(LOW)
        scores = jnp.where(key_valid, nt(keys, scaled_here), -1e30)
        expo = jnp.exp(scores - jnp.max(scores, 0, keepdims=True))
        probs = expo * (1.0 / jnp.sum(expo, 0, keepdims=True))
        grad_here = jnp.where(here, grad_att_full, 0.0).astype(LOW)
        grad_probs = nt(values, grad_here)
        grad_v = grad_v + nn(probs.astype(LOW), grad_here)
        inner = jnp.sum(probs * grad_probs, 0, keepdims=True)
        grad_scores = (probs * (grad_probs - inner)).astype(LOW)
        grad_k = grad_k + nn(grad_scores, scaled_here)
        grad_q = grad_q + tn(grad_scores, jnp.where(here, scaled_keys, 0.0).astype(LOW))
    low_q, low_k, low_v = grad_q.astype(LOW), grad_k.astype(LOW), grad_v.astype(LOW)
    gq_o[...] = low_q
    gk_o[...] = low_k
    gv_o[...] = low_v
    x = tokens[...]
    weight = jnp.concatenate(
        [tn(x, low_q), tn(x, low_k), tn(x, low_v), tn(grad_rows, att_i[...])], 1
    )
    spread(blocks, weight)
    sums[...] = vectors[...]
    last = VECTOR_ROWS - 1
    sums[last : last + 1, :width] = jnp.sum(low_q.astype(F32), 0, keepdims=True)
    sums[last : last + 1, 2 * width : 3 * width] = jnp.sum(low_v.astype(F32), 0, keepdims=True)
    vector_sums = sums[...]
    block = blocks.shape[1]
    pair = split_pair(vector_sums)
    count = keep_o.shape[0]
    for index in range(count):
        send_o[index, :block] = blocks[info[2 + index + count]].astype(LOW)
        send_o[index, block:] = pair
    for index in range(count):
        keep_o[index, :block] = blocks[info[2 + index]]
        keep_o[index, block : block + VECTOR_ROWS] = vector_sums
        keep_o[index, block + VECTOR_ROWS :] = jnp.zeros_like(vector_sums)


def token_back(info, gq, gk, gv, w_qkv, send_o, keep_o):
    half = send_o.shape[0]

    def rows_from(start):
        picked = pl.ds(pl.multiple_of(start, half), half)
        return (
            nt(gq[picked, :], w_qkv[0]) + nt(gk[picked, :], w_qkv[1]) + nt(gv[picked, :], w_qkv[2])
        )

    send_o[...] = rows_from((1 - info[0]) * half).astype(LOW)
    keep_o[...] = rows_from(info[0] * half)


def merge_weights(info, keep, received, send_o, keep_o):
    count = keep_o.shape[0]
    for index in range(count):
        send_o[index] = (keep[count + index] + received[count + index].astype(F32)).astype(LOW)
    for index in range(count):
        keep_o[index] = keep[index] + received[index].astype(F32)


def merge_last_weights(info, keep, received, down_o, up_o):
    down_o[...] = (keep[0, 0] + received[0, 0].astype(F32)).T
    up_o[...] = keep[0, 1] + received[0, 1].astype(F32)


def merged_vectors(keep, received, index, block):
    high = received[index, block : block + VECTOR_ROWS].astype(F32)
    low = received[index, block + VECTOR_ROWS :].astype(F32)
    return keep[index, block : block + VECTOR_ROWS] + high + low


def merge_attn(info, keep, received, send_o, keep_o):
    count = keep_o.shape[0]
    block = keep_o.shape[1] - PAIR_ROWS
    for index in range(count):
        at = count + index
        send_o[index, :block] = (keep[at, :block] + received[at, :block].astype(F32)).astype(LOW)
        send_o[index, block:] = split_pair(merged_vectors(keep, received, at, block))
    for index in range(count):
        keep_o[index, :block] = keep[index, :block] + received[index, :block].astype(F32)
        vectors = merged_vectors(keep, received, index, block)
        keep_o[index, block : block + VECTOR_ROWS] = vectors
        keep_o[index, block + VECTOR_ROWS :] = jnp.zeros_like(vectors)


def merge_last_attn(info, keep, received, qkv_o, out_o, vectors_o):
    block, width = qkv_o.shape[1], qkv_o.shape[2]
    total = keep[0, :block] + received[0, :block].astype(F32)
    for part in range(3):
        qkv_o[part] = total[:, part * width : (part + 1) * width]
    out_o[...] = total[:, 3 * width :].T
    vectors_o[...] = merged_vectors(keep, received, 0, block)


CORE_PAIRS = [(i, i ^ 1) for i in range(4)]
CHIP_PAIRS = [(i, i ^ 2) for i in range(4)]


def to_core(block):
    return lax.ppermute(block, "tensor", CORE_PAIRS)


def to_chip(block):
    return lax.ppermute(block, "tensor", CHIP_PAIRS)


def dp_orders(dp_size):
    bits = list(range(dp_size.bit_length() - 1))
    swapped = bits[:2][::-1] + bits[2:]
    return (bits, swapped)


def to_dp(block, step, dp_size, tensor_size):
    orders = dp_orders(dp_size)
    pairs = []
    for d in range(dp_size):
        for t in range(tensor_size):
            partner = d ^ (1 << orders[t % CORES][step])
            pairs.append((d * tensor_size + t, partner * tensor_size + t))
    return lax.ppermute(block, ("dp", "tensor"), pairs)


def block_order(dp_size, core):
    tables = []
    for order in dp_orders(dp_size):
        table = []
        for index in range(dp_size):
            pattern = 0
            for step, bit in enumerate(order):
                if (index >> (len(order) - 1 - step)) & 1:
                    pattern |= 1 << bit
            table.append(pattern)
        tables.append(table)
    relative = jnp.asarray(tables, jnp.int32)[core]
    return relative ^ lax.axis_index("dp").astype(jnp.int32)


def in_order(own, other, core):
    return jnp.where(
        core == 0, jnp.concatenate([own, other], 0), jnp.concatenate([other, own], 0)
    )


def on_device(
    tokens,
    w_qkv,
    bias_qv,
    w_out,
    bias_out,
    gain_one,
    shift_one,
    w_up,
    bias_up,
    w_down,
    bias_down,
    gain_two,
    shift_two,
    cotangent,
    lengths,
):
    rows, model = tokens.shape
    half = rows // 2
    width = w_qkv.shape[2]
    units = w_up.shape[1]
    dp_size = lax.axis_size("dp")
    tensor_size = lax.axis_size("tensor")
    steps = dp_size.bit_length() - 1
    block = model // dp_size
    core = (lax.axis_index("tensor") % CORES).astype(jnp.int32)
    info = jnp.stack([core, lengths[0].astype(jnp.int32)])
    order = block_order(dp_size, core)
    row = lambda vector: vector.reshape(1, -1)

    up_other, down_other = to_core(w_up), to_core(w_down)
    bias_up_other = to_core(row(bias_up))

    heads_shape = (rows, width)
    query, keys, values, attended, attn_send, attn_keep = call(
        attn_forward,
        [(heads_shape, LOW)] * 4 + [((half, model), LOW), ((half, model), F32)],
        info, tokens, w_qkv, bias_qv, w_out,
        flops=2 * rows * (4 * model + 2 * rows) * width,
    )
    attn_own = (attn_keep + to_core(attn_send).astype(F32)).astype(LOW)
    attn_received = to_chip(attn_own)

    fwd_own, act_own, slope_own, slope_other, normed_one, inverse_one, mlp_own = call(
        mlp_forward,
        [
            ((half, model + units), LOW), ((half, units), LOW), ((half, units), F32),
            ((half, units), F32), ((half, model), F32), ((half, 1), F32), ((half, model), LOW),
        ],
        info, tokens, attn_own, attn_received, row(bias_out), row(gain_one), row(shift_one),
        w_up, up_other, row(bias_up), bias_up_other, w_down, down_other,
        flops=8 * half * model * units,
    )
    mlp_received = to_chip(mlp_own)
    fwd_other = to_core(fwd_own)

    out_half, resid_two, bwd_own, pre_own, back_own, sums_two = call(
        mlp_backward,
        [
            ((half, model), LOW), ((half, model), F32), ((half, model + units), LOW),
            ((half, units), LOW), ((half, model), LOW), ((2, model), F32),
        ],
        info, cotangent, mlp_own, mlp_received, normed_one, row(gain_one), row(shift_one),
        row(bias_down), row(gain_two), row(shift_two), slope_own, slope_other,
        w_up, up_other, w_down, down_other,
        flops=8 * half * model * units,
    )
    back_received = to_chip(back_own)
    bwd_other = to_core(bwd_own)
    output_low = in_order(out_half, to_core(out_half), core)

    count = dp_size // 2
    mlp_send, mlp_keep, sums_mlp = call(
        mlp_weights,
        [
            ((count, 2, block, units), LOW), ((count, 2, block, units), F32), ((2, units), F32),
        ],
        order, fwd_own, fwd_other, act_own, bwd_own, bwd_other, pre_own,
        scratch=[pltpu.VMEM((dp_size, block, units), F32)] * 2,
        flops=4 * rows * model * units,
    )
    mlp_got = to_dp(mlp_send, 0, dp_size, tensor_size)

    resid_one, grad_attn, sums_one = call(
        norm_one_back,
        [((half, model), F32), ((half, model), LOW), ((3, model), F32)],
        info, resid_two, back_own, back_received, normed_one, inverse_one, row(gain_one),
    )
    grad_attn_other = to_core(grad_attn)
    half_sums = jnp.concatenate([sums_two, sums_one], 0)
    half_sums = half_sums + to_core(half_sums)
    vectors = jnp.concatenate(
        [half_sums, sums_mlp, jnp.zeros((VECTOR_ROWS - 7, model), F32)], 0
    )

    grad_q, grad_k, grad_v, attn_w_send, attn_w_keep = call(
        attn_backward,
        [(heads_shape, LOW)] * 3
        + [
            ((count, block + PAIR_ROWS, model), LOW),
            ((count, block + PAIR_ROWS, model), F32),
        ],
        jnp.concatenate([info, order]),
        grad_attn, grad_attn_other, w_out, query, keys, values, attended, tokens, vectors,
        scratch=[
            pltpu.VMEM((rows, model), LOW),
            pltpu.VMEM((dp_size, block, model), F32),
            pltpu.VMEM((VECTOR_ROWS, model), F32),
        ],
        flops=2 * rows * (5 * model + 5 * rows) * width,
    )
    attn_got = to_dp(attn_w_send, 0, dp_size, tensor_size)
    token_send, token_keep = call(
        token_back,
        [((half, model), LOW), ((half, model), F32)],
        info, grad_q, grad_k, grad_v, w_qkv,
        flops=6 * rows * model * width,
    )
    token_own = (token_keep + to_core(token_send).astype(F32)).astype(LOW)
    token_received = to_chip(token_own)

    for step in range(1, steps):
        kept = dp_size >> (step + 1)
        mlp_send, mlp_keep = call(
            merge_weights,
            [((kept, 2, block, units), LOW), ((kept, 2, block, units), F32)],
            info, mlp_keep, mlp_got,
        )
        mlp_got = to_dp(mlp_send, step, dp_size, tensor_size)
    sum_w_down, sum_w_up = call(
        merge_last_weights, [((units, block), F32), ((block, units), F32)], info, mlp_keep, mlp_got
    )
    for step in range(1, steps):
        kept = dp_size >> (step + 1)
        attn_w_send, attn_w_keep = call(
            merge_attn,
            [((kept, block + PAIR_ROWS, model), LOW), ((kept, block + PAIR_ROWS, model), F32)],
            info, attn_w_keep, attn_got,
        )
        attn_got = to_dp(attn_w_send, step, dp_size, tensor_size)

    token_half = (
        resid_one + (token_own.astype(F32) + token_received.astype(F32))
    ).astype(LOW)
    token_total = in_order(token_half, to_core(token_half), core)

    sum_w_qkv, sum_w_out, sum_vectors = call(
        merge_last_attn,
        [((3, block, width), F32), ((width, block), F32), ((VECTOR_ROWS, model), F32)],
        info, attn_w_keep, attn_got,
    )
    me = lax.axis_index("dp")
    mine = lax.dynamic_slice_in_dim(sum_vectors[:7], me * block, block, 1)
    small = width // dp_size
    pair = sum_vectors[7, : 4 * width].reshape(2, 2 * width)[:, :width]
    sum_bias_qv = lax.dynamic_slice_in_dim(pair, me * small, small, 1)
    return (
        output_low,
        token_total,
        sum_w_qkv,
        sum_bias_qv,
        sum_w_out,
        mine[4],
        mine[2],
        mine[3],
        sum_w_up,
        mine[6],
        sum_w_down,
        mine[5],
        mine[0],
        mine[1],
    )


def solution(mesh):
    placed = (
        P("dp", None),
        P(None, None, "tensor"),
        P(None, "tensor"),
        P("tensor", None),
        P(),
        P(),
        P(),
        P(None, "tensor"),
        P("tensor"),
        P("tensor", None),
        P(),
        P(),
        P(),
        P("dp", None),
        P("dp"),
    )
    return jax.shard_map(
        on_device,
        mesh=mesh,
        in_specs=placed,
        out_specs=(
            P("dp", None),
            P("dp", None),
            P(None, "dp", "tensor"),
            P(None, ("tensor", "dp")),
            P("tensor", "dp"),
            P("dp"),
            P("dp"),
            P("dp"),
            P("dp", "tensor"),
            P(("tensor", "dp")),
            P("tensor", "dp"),
            P("dp"),
            P("dp"),
            P("dp"),
        ),
        check_vma=False,
    )
```

time: 466 us -> 129 us (0.28)
  waiting for transfers between devices: 295 us -> 60.9 us
  blocking collectives: 77.6 us -> 0 us
  matrix products: 35.1 us -> 0 us
  Pallas kernels: 0 us -> 27.3 us
  starting transfers between devices: 0.51 us -> 19.5 us
  between operations: 16.6 us -> 1.78 us
  local copies, waits for them, and re-layouts: 23.8 us -> 12.2 us
  other arithmetic: 15.9 us -> 6.67 us
    reduce_scatter x5 -> x0, waiting for transfers between devices: 220 us -> none  [the longest x1 74 us: on_device(): lax.psum_scatter(grad_w_down, 'dp', scatter_dimension=1, tiled=True)]
    ppermute x0 -> x21, waiting for transfers between devices: none -> 60.9 us  [the longest x6 33.6 us: to_dp(): return lax.ppermute(block, ('dp', 'tensor'), pairs)]
    unnamed x10 -> x0, waiting for transfers between devices: 40.7 us -> none
    unnamed x1 -> x0, blocking collectives: 37.9 us -> none
    psum x1 -> x0, waiting for transfers between devices: 34.6 us -> none  [on_device(): token_total = lax.psum(token_term.astype(jnp.bfloat16), 'tensor')]
    dot_general x17 -> x0, matrix products: 33.7 us -> none  [the longest x1 5.54 us: on_device(): jnp.dot(hidden_low, w_up, preferred_element_type=jnp.float32) + bias_up]
    all_gather x4 -> x0, blocking collectives: 33.5 us -> none  [the longest x1 8.94 us: on_device(): lax.all_gather(output_low, 'tensor', axis=0, tiled=True)]
    pallas_call x0 -> x13, Pallas kernels: none -> 27.3 us  [call(): pl.pallas_call(kernel, out_shape=shapes, in_specs=[pl.BlockSpec(memory_sp...]
  transfers between devices with their start and end apart: 8 -> 21, of which waited for: 7 -> 10; matrix products, arithmetic and copies ran while one was open for 8% -> 7% of each run, Pallas kernels for 0% -> 10%
where the time goes in v2:
time: 129 us; the launch traced here: 128 us
  waiting for transfers between devices  60.9 us (47%)
  Pallas kernels  27.3 us (21%)
  starting transfers between devices  19.5 us (15%)
  local copies, waits for them, and re-layouts  12.2 us (9%)
  other arithmetic  6.67 us (5%)
  between operations  1.78 us (1%)
    ppermute x6, waiting for transfers between devices, to_dp(): return lax.ppermute(block, ('dp', 'tensor'), pairs)  33.6 us
    pallas_call x13, Pallas kernels, call(): pl.pallas_call(kernel, out_shape=shapes, in_specs=[pl.BlockSpec(memory_sp...  27.3 us
    ppermute x4, waiting for transfers between devices, to_chip(): return lax.ppermute(block, 'tensor', CHIP_PAIRS)  24.4 us
    unnamed x72, local copies, waits for them, and re-layouts  10.8 us
    ppermute x6, starting transfers between devices, to_dp(): return lax.ppermute(block, ('dp', 'tensor'), pairs)  9.88 us
    ppermute x4, starting transfers between devices, to_chip(): return lax.ppermute(block, 'tensor', CHIP_PAIRS)  7.23 us
    select_n x2, other arithmetic, in_order(): jnp.where(core == 0, jnp.concatenate([own, other], 0), jnp.concatenate([o...  4.65 us
    ppermute x11, waiting for transfers between devices, to_core(): return lax.ppermute(block, 'tensor', CORE_PAIRS)  2.91 us
  transfers between devices with their start and end apart: 21, of which 10 were waited for; matrix products, arithmetic and copies ran while one was open for 7% of the time, Pallas kernels for 10%

profile of v2, /device:TPU:0, one launch (start us, length us, event | category | flops | bytes accessed | tf_op | source)
XLA Modules:
  0.0 128.4 jit_solution(12735926684152938465)
XLA Ops:
  2.0 1.5 %copy.30.w_qkv = bf16[3,768,192]{2,1,0:T(8,128)(2,1)S(1)} copy(bf16[3,768,192]{1,2,0:T(8,128)(2,1)} %param.17) | data formatting | bytes 1769472 | tf_op args[1]
  3.5 1.1 copy-done.7
  5.7 3.4 %shard_map.263 = (bf16[512,192]{1,0:T(8,128)(2,1)S(1)}, bf16[512,192]{1,0:T(8,128)(2,1)S(1)}, bf16[512,192]{1,0:T(8,128)(2,1)S(1)}, bf16[512,192]{1,0:T(8,128)(2...) custom-call(s32[2]{0:T(128)S(1)} %pad_add_fusion.info, bf16[512,768]{1,0:T(8,128)(2,1)S(1)} %copy-done.7, ...), custom_call_target="tpu_custom_call" | custom-call | flops 805306368 | bytes 3933696 | tf_op jit(solution)/shard_map/pallas_call | solution.py:49
  9.6 1.3 %collective-permute-done = bf16[256,768]{1,0:T(8,128)(2,1)S(1)} collective-permute-done((bf16[256,768]{1,0:T(8,128)(2,1)S(1)}, bf16[256,768]{1,0:T(8,128)(2,1)S(1)}, u32[]{:S(2)}, u32[]{:S(2)}) %collective-permute-start) | collective-permute-done | bytes 393248 | tf_op jit(solution)/shard_map/ppermute | solution.py:318
  11.0 2.9 %collective-permute-start.1 = (bf16[256,768]{1,0:T(8,128)(2,1)S(1)}, bf16[256,768]{1,0:T(8,128)(2,1)S(1)}, u32[]{:S(2)}, u32[]{:S(2)}) collective-permute-start(bf16[256,768]{1,0:T(8,128)(2,1)S(1)} %add_convert_fusion.2.own), channel_id=1, source_target_pairs={{0,2},{1,3},{2,0},{3,1},{4,6},{5,7},{6,4},{7,5},{8,10},{9,11},{10,... | collective-permute-start | bytes 1179656 | tf_op jit(solution)/shard_map/ppermute | solution.py:322
  15.1 8.2 %collective-permute-done.1.received = bf16[256,768]{1,0:T(8,128)(2,1)S(1)} collective-permute-done((bf16[256,768]{1,0:T(8,128)(2,1)S(1)}, bf16[256,768]{1,0:T(8,128)(2,1)S(1)}, u32[]{:S(2)}, u32[]{:S(2)}) %collective-permute-start.1) | collective-permute-done | bytes 393248 | tf_op jit(solution)/shard_map/ppermute | solution.py:322
  23.4 2.5 %shard_map.264 = (bf16[256,1536]{1,0:T(8,128)(2,1)}, bf16[256,768]{1,0:T(8,128)(2,1)S(1)}, f32[256,768]{1,0:T(8,128)S(1)}, f32[256,768]{1,0:T(8,128)S(1)}, f32[2...) custom-call(s32[2]{0:T(128)S(1)} %pad_add_fusion.info, bf16[512,768]{1,0:T(8,128)(2,1)S(1)} %copy-done.7, ...), custom_call_target="tpu_custom_call" | custom-call | flops 1207959552 | bytes 10240000 | tf_op jit(solution)/shard_map/pallas_call | solution.py:49
  26.6 1.7 %collective-permute-start.5 = (bf16[256,768]{1,0:T(8,128)(2,1)S(1)}, bf16[256,768]{1,0:T(8,128)(2,1)S(1)}, u32[]{:S(2)}, u32[]{:S(2)}) collective-permute-start(bf16[256,768]{1,0:T(8,128)(2,1)S(1)} %get-tuple-element.61.own), channel_id=1, source_target_pairs={{0,2},{1,3},{2,0},{3,1},{4,6},{5,7},{6,4},{7,5},{8,10},{9,11},{10,... | collective-permute-start | bytes 1179656 | tf_op jit(solution)/shard_map/ppermute | solution.py:322
  28.3 8.9 %collective-permute-done.5.received = bf16[256,768]{1,0:T(8,128)(2,1)S(1)} collective-permute-done((bf16[256,768]{1,0:T(8,128)(2,1)S(1)}, bf16[256,768]{1,0:T(8,128)(2,1)S(1)}, u32[]{:S(2)}, u32[]{:S(2)}) %collective-permute-start.5) | collective-permute-done | bytes 393248 | tf_op jit(solution)/shard_map/ppermute | solution.py:322
  37.2 3.6 %shard_map.265 = (bf16[256,768]{1,0:T(8,128)(2,1)S(1)}, f32[256,768]{1,0:T(8,128)S(1)}, bf16[256,1536]{1,0:T(8,128)(2,1)}, bf16[256,768]{1,0:T(8,128)(2,1)S(1)},...) custom-call(s32[2]{0:T(128)S(1)} %pad_add_fusion.info, bf16[512,768]{1,0:T(8,128)(2,1)S(1)} %copy-done.4, ...), custom_call_target="tpu_custom_call" | custom-call | flops 1207959552 | bytes 11424768 | tf_op jit(solution)/shard_map/pallas_call | solution.py:49
  43.2 1.4 %collective-permute-start.7 = (bf16[256,768]{1,0:T(8,128)(2,1)}, bf16[256,768]{1,0:T(8,128)(2,1)S(1)}, u32[]{:S(2)}, u32[]{:S(2)}) collective-permute-start(bf16[256,768]{1,0:T(8,128)(2,1)} %get-tuple-element.67.own), channel_id=1, source_target_pairs={{0,2},{1,3},{2,0},{3,1},{4,6},{5,7},{6,4},{7,5},{8,10},{9,11},{10,... | collective-permute-start | bytes 1179656 | tf_op jit(solution)/shard_map/ppermute | solution.py:322
  45.8 7.3 %collective-permute-done.7.received = bf16[256,768]{1,0:T(8,128)(2,1)S(1)} collective-permute-done((bf16[256,768]{1,0:T(8,128)(2,1)}, bf16[256,768]{1,0:T(8,128)(2,1)S(1)}, u32[]{:S(2)}, u32[]{:S(2)}) %collective-permute-start.7) | collective-permute-done | bytes 393248 | tf_op jit(solution)/shard_map/ppermute | solution.py:322
  53.2 1.1 copy-done.3
  54.3 1.1 copy-done.6
  56.3 1.7 %shard_map.266 = (f32[256,768]{1,0:T(8,128)S(1)}, bf16[256,768]{1,0:T(8,128)(2,1)S(1)}, f32[3,768]{1,0:T(4,128)S(1)}) custom-call(s32[2]{0:T(128)S(1)} %pad_add_fusion.info, f32[256,768]{1,0:T(8,128)S(1)} %copy-done.6, bf16[256,768]{1,0:T(8,128)(2,1)} %get-tuple-element.67.own, bf16[256,768]{1,0:T(8,128)(2,1)S(1)} %collective-permute-done.7.received, ...), custom_call_target="tpu_custom_call" | custom-call | bytes 3552256 | tf_op jit(solution)/shard_map/pallas_call | solution.py:49
  59.5 3.2 %shard_map.267 = (bf16[4,2,96,768]{3,2,1,0:T(8,128)(2,1)S(1)}, f32[4,2,96,768]{3,2,1,0:T(8,128)S(1)}, f32[2,768]{1,0:T(2,128)S(1)}) custom-call(s32[8]{0:T(128)S(1)} %fusion.1.ids, bf16[256,1536]{1,0:T(8,128)(2,1)} %get-tuple-element.77.fwd_own, bf16[256,1536]{1,0:T(8,128)(2,1)S(1)} %collective-permute-done.10.fwd_other, bf16[256,768]{1,0:T(8,128)(2,1)S(1)} %copy-done.14, ...), custom_call_target="tpu_custom_call" | custom-call | flops 1207959552 | bytes 7477248 | tf_op jit(solution)/shard_map/pallas_call | solution.py:49
  62.9 5.1 %shard_map.268 = (bf16[512,192]{1,0:T(8,128)(2,1)S(1)}, bf16[512,192]{1,0:T(8,128)(2,1)S(1)}, bf16[512,192]{1,0:T(8,128)(2,1)S(1)}, bf16[4,112,768]{2,1,0:T(8,128)(2,1)S(1)}, f32[4,112,768]{2,1,0:T(8,128)S(1)}) custom-call(s32[10]{0:T(128)S(1)} %pad_add_fusion.1.info, bf16[256,768]{1,0:T(8,128)(2,1)S(1)} %get-tuple-element.70.grad_own, ...), custom_call_target="tpu_custom_call" | custom-call | flops 1258291200 | bytes 5332992 | tf_op jit(solution)/shard_map/pallas_call | solution.py:49
  68.0 1.4 %shard_map.269 = (bf16[256,768]{1,0:T(8,128)(2,1)S(1)}, f32[256,768]{1,0:T(8,128)S(1)}) custom-call(s32[2]{0:T(128)S(1)} %pad_add_fusion.info, bf16[512,192]{1,0:T(8,128)(2,1)S(1)} %get-tuple-element.82.gq, bf16[512,192]{1,0:T(8,128)(2,1)S(1)} %get-tuple-element.83.gk, bf16[512,192]{1,0:T(8,128)(2,1)S(1)} %get-tuple-element.84.gv, ...), custom_call_target="tpu_custom_call" | custom-call | flops 452984832 | bytes 2654208 | tf_op jit(solution)/shard_map/pallas_call | solution.py:49
  69.6 1.1 collective-permute-start.18
  71.7 1.1 collective-permute-start.13
  72.9 20.3 %collective-permute-done.15.received = bf16[4,112,768]{2,1,0:T(8,128)(2,1)S(1)} collective-permute-done((bf16[4,112,768]{2,1,0:T(8,128)(2,1)S(1)}, bf16[4,112,768]{2,1,0:T(8,128)(2,1)S(1)}, u32[]{:S(2)}, u32[]{:S(2)}) %collective-permute-start.15) | collective-permute-done | bytes 688160 | tf_op jit(solution)/shard_map/ppermute | solution.py:338
  93.9 1.2 collective-permute-start.16
  96.0 1.6 %shard_map.273 = (bf16[2,2,96,768]{3,2,1,0:T(8,128)(2,1)}, f32[2,2,96,768]{3,2,1,0:T(8,128)S(1)}) custom-call(s32[2]{0:T(128)S(1)} %pad_add_fusion.info, f32[4,2,96,768]{3,2,1,0:T(8,128)S(1)} %get-tuple-element.96.keep, bf16[4,2,96,768]{3,2,1,0:T(8,128)(2,1)S(1)} %collective-permute-done.18.received), custom_call_target="tpu_custom_call" | custom-call | bytes 5308416 | tf_op jit(solution)/shard_map/pallas_call | solution.py:49
  98.5 2.7 %collective-permute-done.16.received = bf16[2,112,768]{2,1,0:T(8,128)(2,1)S(1)} collective-permute-done((bf16[2,112,768]{2,1,0:T(8,128)(2,1)S(1)}, bf16[2,112,768]{2,1,0:T(8,128)(2,1)S(1)}, u32[]{:S(2)}, u32[]{:S(2)}) %collective-permute-start.16) | collective-permute-done | bytes 344096 | tf_op jit(solution)/shard_map/ppermute | solution.py:338
  101.8 2.3 %collective-permute-start.17 = (bf16[1,112,768]{2,1,0:T(8,128)(2,1)S(1)}, bf16[1,112,768]{2,1,0:T(8,128)(2,1)S(1)}, u32[]{:S(2)}, u32[]{:S(2)}) collective-permute-start(bf16[1,112,768]{2,1,0:T(8,128)(2,1)S(1)} %get-tuple-element.92), channel_id=1, source_target_pairs={{0,16},{1,17},{2,18},{3,19},{4,20},{5,21},{6,22},{7,23},{8,24},{9,... | collective-permute-start | bytes 516104 | tf_op jit(solution)/shard_map/ppermute | solution.py:338
  104.0 2.2 %maximum_select_fusion = bf16[512,768]{1,0:T(8,128)(2,1)} fusion(bf16[256,768]{1,0:T(8,128)(2,1)} %collective-permute-done.6, bf16[256,768]{1,0:T(8,128)(2,1)S(1)} %copy-done.10, pred[]{:T(512)S(6)} %eq.6), kind=kLoop, calls=%fused_computation | loop fusion | flops 3538944 | bytes 1572865 | tf_op jit(solution)/shard_map/jit(_where)/select_n | solution.py:357
  106.3 2.4 %maximum_select_fusion.1 = bf16[512,768]{1,0:T(8,128)(2,1)} fusion(bf16[256,768]{1,0:T(8,128)(2,1)} %collective-permute-done.14, bf16[256,768]{1,0:T(8,128)(2,1)} %add_convert_fusion, pred[]{:T(512)S(6)} %eq.6), kind=kLoop, calls=%fused_computation.1 | loop fusion | flops 3538944 | bytes 1572865 | tf_op jit(solution)/shard_map/jit(_where)/select_n | solution.py:357
  108.7 1.2 collective-permute-done.17.received
  109.9 1.4 %shard_map.272 = (f32[3,96,192]{2,1,0:T(8,128)}, f32[192,96]{1,0:T(8,128)}, f32[8,768]{1,0:T(8,128)S(1)}) custom-call(s32[2]{0:T(128)S(1)} %pad_add_fusion.info, f32[1,112,768]{2,1,0:T(8,128)S(1)} %get-tuple-element.91.keep, bf16[1,112,768]{2,1,0:T(8,128)(2,1)S(1)} %collective-permute-done.17.received), custom_call_target="tpu_custom_call" | custom-call | bytes 835584 | tf_op jit(solution)/shard_map/pallas_call | solution.py:49
  112.1 3.5 %collective-permute-start.20 = (bf16[1,2,96,768]{3,2,1,0:T(8,128)(2,1)S(1)}, bf16[1,2,96,768]{3,2,1,0:T(8,128)(2,1)S(1)}, u32[]{:S(2)}, u32[]{:S(2)}) collective-permute-start(bf16[1,2,96,768]{3,2,1,0:T(8,128)(2,1)S(1)} %get-tuple-element.101), channel_id=1, source_target_pairs={{0,16},{1,17},{2,18},{3,19},{4,20},{5,21},{6,22},{7,23},{8,24},{9,... | collective-permute-start | bytes 884744 | tf_op jit(solution)/shard_map/ppermute | solution.py:338
  116.8 9.3 %collective-permute-done.20.received = bf16[1,2,96,768]{3,2,1,0:T(8,128)(2,1)S(1)} collective-permute-done((bf16[1,2,96,768]{3,2,1,0:T(8,128)(2,1)S(1)}, bf16[1,2,96,768]{3,2,1,0:T(8,128)(2,1)S(1)}, u32[]{:S(2)}, u32[]{:S(2)}) %collective-permute-start.20) | collective-permute-done | bytes 294944 | tf_op jit(solution)/shard_map/ppermute | solution.py:338
  126.1 1.4 %shard_map.275 = (f32[768,96]{1,0:T(8,128)S(1)}, f32[96,768]{1,0:T(8,128)}) custom-call(s32[2]{0:T(128)S(1)} %pad_add_fusion.info, f32[1,2,96,768]{3,2,1,0:T(8,128)S(1)} %get-tuple-element.100.keep, bf16[1,2,96,768]{3,2,1,0:T(8,128)(2,1)S(1)} %collective-permute-done.20.received), custom_call_target="tpu_custom_call" | custom-call | bytes 1474560 | tf_op jit(solution)/shard_map/pallas_call | solution.py:49
  (120 shorter events, 17.0 us)
Async XLA Ops:
  0.7 22.7 %collective-permute-start.2 = (bf16[768,768]{1,0:T(8,128)(2,1)}, bf16[768,768]{1,0:T(8,128)(2,1)S(1)}, u32[]{:S(2)}, u32[]{:S(2)}) collective-permute-start(bf16[768,768]{1,0:T(8,128)(2,1)} %up_own.3), channel_id=1, source_target_pairs={{0,1},{1,0},{2,3},{3,2},{4,5},{5,4},{6,7},{7,6},{8,9},{9,8},{10,11... | collective-permute-start | bytes 3538952 | tf_op jit(solution)/shard_map/ppermute | solution.py:318
  1.2 22.2 %collective-permute-start.4 = (bf16[768,768]{1,0:T(8,128)(2,1)}, bf16[768,768]{1,0:T(8,128)(2,1)S(1)}, u32[]{:S(2)}, u32[]{:S(2)}) collective-permute-start(bf16[768,768]{1,0:T(8,128)(2,1)} %down_own.3), channel_id=1, source_target_pairs={{0,1},{1,0},{2,3},{3,2},{4,5},{5,4},{6,7},{7,6},{8,9},{9,8},{10,11... | collective-permute-start | bytes 3538952 | tf_op jit(solution)/shard_map/ppermute | solution.py:318
  5.6 8.4 %copy-start.30 = (f32[768]{0:T(1024)S(1)}, f32[768]{0:T(1024)}, u32[]{:S(2)}) copy-start(f32[768]{0:T(1024)} %param.21) | copy-start | bytes 9220
  5.6 8.4 %copy-start.31 = (f32[768]{0:T(1024)S(1)}, f32[768]{0:T(1024)}, u32[]{:S(2)}) copy-start(f32[768]{0:T(1024)} %param.22) | copy-start | bytes 9220
  5.6 17.8 %copy-start = (bf16[768,768]{1,0:T(8,128)(2,1)S(1)}, bf16[768,768]{1,0:T(8,128)(2,1)}, u32[]{:S(2)}) copy-start(bf16[768,768]{1,0:T(8,128)(2,1)} %up_own.3) | copy-start | bytes 3538948
  5.6 17.7 %copy-start.1 = (bf16[768,768]{1,0:T(8,128)(2,1)S(1)}, bf16[768,768]{1,0:T(8,128)(2,1)}, u32[]{:S(2)}) copy-start(bf16[768,768]{1,0:T(8,128)(2,1)} %down_own.3) | copy-start | bytes 3538948
  9.1 16.8 %copy-start.26 = (bf16[512,192]{1,0:T(8,128)(2,1)}, bf16[512,192]{1,0:T(8,128)(2,1)S(1)}, u32[]{:S(2)}) copy-start(bf16[512,192]{1,0:T(8,128)(2,1)S(1)} %get-tuple-element.74.att_i) | copy-start | bytes 589828
  9.1 1.8 %collective-permute-start = (bf16[256,768]{1,0:T(8,128)(2,1)S(1)}, bf16[256,768]{1,0:T(8,128)(2,1)S(1)}, u32[]{:S(2)}, u32[]{:S(2)}) collective-permute-start(bf16[256,768]{1,0:T(8,128)(2,1)S(1)} %get-tuple-element.60), channel_id=1, source_target_pairs={{0,1},{1,0},{2,3},{3,2},{4,5},{5,4},{6,7},{7,6},{8,9},{9,8},{10,11... | collective-permute-start | bytes 1179656 | tf_op jit(solution)/shard_map/ppermute | solution.py:318
  11.0 12.3 %collective-permute-start.1 = (bf16[256,768]{1,0:T(8,128)(2,1)S(1)}, bf16[256,768]{1,0:T(8,128)(2,1)S(1)}, u32[]{:S(2)}, u32[]{:S(2)}) collective-permute-start(bf16[256,768]{1,0:T(8,128)(2,1)S(1)} %add_convert_fusion.2.own), channel_id=1, source_target_pairs={{0,2},{1,3},{2,0},{3,1},{4,6},{5,7},{6,4},{7,5},{8,10},{9,11},{10,... | collective-permute-start | bytes 1179656 | tf_op jit(solution)/shard_map/ppermute | solution.py:322
  14.0 1.2 collective-permute-start.3
  14.1 14.2 %copy-start.32 = (f32[768]{0:T(1024)S(1)}, f32[768]{0:T(1024)}, u32[]{:S(2)}) copy-start(f32[768]{0:T(1024)} %param.26) | copy-start | bytes 9220
  14.1 14.2 %copy-start.33 = (f32[768]{0:T(1024)S(1)}, f32[768]{0:T(1024)}, u32[]{:S(2)}) copy-start(f32[768]{0:T(1024)} %param.27) | copy-start | bytes 9220
  14.1 14.2 %copy-start.34 = (f32[768]{0:T(1024)S(1)}, f32[768]{0:T(1024)}, u32[]{:S(2)}) copy-start(f32[768]{0:T(1024)} %param.28) | copy-start | bytes 9220
  14.1 23.1 %copy-start.4 = (bf16[512,768]{1,0:T(8,128)(2,1)S(1)}, bf16[512,768]{1,0:T(8,128)(2,1)}, u32[]{:S(2)}) copy-start(bf16[512,768]{1,0:T(8,128)(2,1)} %cotangent.1) | copy-start | bytes 2359300
  26.6 14.3 %copy-start.2 = (f32[256,768]{1,0:T(8,128)}, f32[256,768]{1,0:T(8,128)S(1)}, u32[]{:S(2)}) copy-start(f32[256,768]{1,0:T(8,128)S(1)} %get-tuple-element.62.normed_one.normed) | copy-start | bytes 2359300
  26.6 14.3 %copy-start.13 = (bf16[256,768]{1,0:T(8,128)(2,1)}, bf16[256,768]{1,0:T(8,128)(2,1)S(1)}, u32[]{:S(2)}) copy-start(bf16[256,768]{1,0:T(8,128)(2,1)S(1)} %get-tuple-element.78.act_own) | copy-start | bytes 1179652
  26.6 10.6 %collective-permute-start.5 = (bf16[256,768]{1,0:T(8,128)(2,1)S(1)}, bf16[256,768]{1,0:T(8,128)(2,1)S(1)}, u32[]{:S(2)}, u32[]{:S(2)}) collective-permute-start(bf16[256,768]{1,0:T(8,128)(2,1)S(1)} %get-tuple-element.61.own), channel_id=1, source_target_pairs={{0,2},{1,3},{2,0},{3,1},{4,6},{5,7},{6,4},{7,5},{8,10},{9,11},{10,... | collective-permute-start | bytes 1179656 | tf_op jit(solution)/shard_map/ppermute | solution.py:322
  43.2 10.0 %collective-permute-start.7 = (bf16[256,768]{1,0:T(8,128)(2,1)}, bf16[256,768]{1,0:T(8,128)(2,1)S(1)}, u32[]{:S(2)}, u32[]{:S(2)}) collective-permute-start(bf16[256,768]{1,0:T(8,128)(2,1)} %get-tuple-element.67.own), channel_id=1, source_target_pairs={{0,2},{1,3},{2,0},{3,1},{4,6},{5,7},{6,4},{7,5},{8,10},{9,11},{10,... | collective-permute-start | bytes 1179656 | tf_op jit(solution)/shard_map/ppermute | solution.py:322
  44.6 14.8 %collective-permute-start.10 = (bf16[256,1536]{1,0:T(8,128)(2,1)}, bf16[256,1536]{1,0:T(8,128)(2,1)S(1)}, u32[]{:S(2)}, u32[]{:S(2)}) collective-permute-start(bf16[256,1536]{1,0:T(8,128)(2,1)} %get-tuple-element.77.fwd_own), channel_id=1, source_target_pairs={{0,1},{1,0},{2,3},{3,2},{4,5},{5,4},{6,7},{7,6},{8,9},{9,8},{10,11... | collective-permute-start | bytes 2359304 | tf_op jit(solution)/shard_map/ppermute | solution.py:318
  44.6 14.8 %collective-permute-start.11 = (bf16[256,1536]{1,0:T(8,128)(2,1)}, bf16[256,1536]{1,0:T(8,128)(2,1)S(1)}, u32[]{:S(2)}, u32[]{:S(2)}) collective-permute-start(bf16[256,1536]{1,0:T(8,128)(2,1)} %get-tuple-element.79.bwd_own), channel_id=1, source_target_pairs={{0,1},{1,0},{2,3},{3,2},{4,5},{5,4},{6,7},{7,6},{8,9},{9,8},{10,11... | collective-permute-start | bytes 2359304 | tf_op jit(solution)/shard_map/ppermute | solution.py:318
  58.1 1.3 collective-permute-start.9
  58.3 4.5 %collective-permute-start.8 = (bf16[256,768]{1,0:T(8,128)(2,1)S(1)}, bf16[256,768]{1,0:T(8,128)(2,1)S(1)}, u32[]{:S(2)}, u32[]{:S(2)}) collective-permute-start(bf16[256,768]{1,0:T(8,128)(2,1)S(1)} %get-tuple-element.70.grad_own), channel_id=1, source_target_pairs={{0,1},{1,0},{2,3},{3,2},{4,5},{5,4},{6,7},{7,6},{8,9},{9,8},{10,11... | collective-permute-start | bytes 1179656 | tf_op jit(solution)/shard_map/ppermute | solution.py:318
  69.4 2.3 %collective-permute-start.12 = (bf16[256,768]{1,0:T(8,128)(2,1)S(1)}, bf16[256,768]{1,0:T(8,128)(2,1)S(1)}, u32[]{:S(2)}, u32[]{:S(2)}) collective-permute-start(bf16[256,768]{1,0:T(8,128)(2,1)S(1)} %get-tuple-element.86), channel_id=1, source_target_pairs={{0,1},{1,0},{2,3},{3,2},{4,5},{5,4},{6,7},{7,6},{8,9},{9,8},{10,11... | collective-permute-start | bytes 1179656 | tf_op jit(solution)/shard_map/ppermute | solution.py:318
  69.6 26.4 %collective-permute-start.18 = (bf16[4,2,96,768]{3,2,1,0:T(8,128)(2,1)S(1)}, bf16[4,2,96,768]{3,2,1,0:T(8,128)(2,1)S(1)}, u32[]{:S(2)}, u32[]{:S(2)}) collective-permute-start(bf16[4,2,96,768]{3,2,1,0:T(8,128)(2,1)S(1)} %get-tuple-element.97), channel_id=1, source_target_pairs={{0,4},{1,9},{2,6},{3,11},{4,0},{5,13},{6,2},{7,15},{8,12},{9,1},{1... | collective-permute-start | bytes 3538952 | tf_op jit(solution)/shard_map/ppermute | solution.py:338
  70.7 22.5 %collective-permute-start.15 = (bf16[4,112,768]{2,1,0:T(8,128)(2,1)S(1)}, bf16[4,112,768]{2,1,0:T(8,128)(2,1)S(1)}, u32[]{:S(2)}, u32[]{:S(2)}) collective-permute-start(bf16[4,112,768]{2,1,0:T(8,128)(2,1)S(1)} %get-tuple-element.88), channel_id=1, source_target_pairs={{0,4},{1,9},{2,6},{3,11},{4,0},{5,13},{6,2},{7,15},{8,12},{9,1},{1... | collective-permute-start | bytes 2064392 | tf_op jit(solution)/shard_map/ppermute | solution.py:338
  71.7 23.4 %collective-permute-start.13 = (bf16[256,768]{1,0:T(8,128)(2,1)S(1)}, bf16[256,768]{1,0:T(8,128)(2,1)S(1)}, u32[]{:S(2)}, u32[]{:S(2)}) collective-permute-start(bf16[256,768]{1,0:T(8,128)(2,1)S(1)} %add_convert_fusion.1), channel_id=1, source_target_pairs={{0,2},{1,3},{2,0},{3,1},{4,6},{5,7},{6,4},{7,5},{8,10},{9,11},{10,... | collective-permute-start | bytes 1179656 | tf_op jit(solution)/shard_map/ppermute | solution.py:322
  72.9 31.2 %collective-permute-start.6 = (bf16[256,768]{1,0:T(8,128)(2,1)S(1)}, bf16[256,768]{1,0:T(8,128)(2,1)}, u32[]{:S(2)}, u32[]{:S(2)}) collective-permute-start(bf16[256,768]{1,0:T(8,128)(2,1)S(1)} %copy-done.10), channel_id=1, source_target_pairs={{0,1},{1,0},{2,3},{3,2},{4,5},{5,4},{6,7},{7,6},{8,9},{9,8},{10,11... | collective-permute-start | bytes 1179656 | tf_op jit(solution)/shard_map/ppermute | solution.py:318
  93.9 7.3 %collective-permute-start.16 = (bf16[2,112,768]{2,1,0:T(8,128)(2,1)S(1)}, bf16[2,112,768]{2,1,0:T(8,128)(2,1)S(1)}, u32[]{:S(2)}, u32[]{:S(2)}) collective-permute-start(bf16[2,112,768]{2,1,0:T(8,128)(2,1)S(1)} %get-tuple-element.90), channel_id=1, source_target_pairs={{0,8},{1,5},{2,10},{3,7},{4,12},{5,1},{6,14},{7,3},{8,0},{9,13},{1... | collective-permute-start | bytes 1032200 | tf_op jit(solution)/shard_map/ppermute | solution.py:338
  96.0 10.3 %collective-permute-start.14 = (bf16[256,768]{1,0:T(8,128)(2,1)}, bf16[256,768]{1,0:T(8,128)(2,1)}, u32[]{:S(2)}, u32[]{:S(2)}) collective-permute-start(bf16[256,768]{1,0:T(8,128)(2,1)} %add_convert_fusion), channel_id=1, source_target_pairs={{0,1},{1,0},{2,3},{3,2},{4,5},{5,4},{6,7},{7,6},{8,9},{9,8},{10,11... | collective-permute-start | bytes 1179656 | tf_op jit(solution)/shard_map/ppermute | solution.py:318
  97.6 13.8 %collective-permute-start.19 = (bf16[2,2,96,768]{3,2,1,0:T(8,128)(2,1)}, bf16[2,2,96,768]{3,2,1,0:T(8,128)(2,1)S(1)}, u32[]{:S(2)}, u32[]{:S(2)}) collective-permute-start(bf16[2,2,96,768]{3,2,1,0:T(8,128)(2,1)} %get-tuple-element.99), channel_id=1, source_target_pairs={{0,8},{1,5},{2,10},{3,7},{4,12},{5,1},{6,14},{7,3},{8,0},{9,13},{1... | collective-permute-start | bytes 1769480 | tf_op jit(solution)/shard_map/ppermute | solution.py:338
  101.8 8.1 %collective-permute-start.17 = (bf16[1,112,768]{2,1,0:T(8,128)(2,1)S(1)}, bf16[1,112,768]{2,1,0:T(8,128)(2,1)S(1)}, u32[]{:S(2)}, u32[]{:S(2)}) collective-permute-start(bf16[1,112,768]{2,1,0:T(8,128)(2,1)S(1)} %get-tuple-element.92), channel_id=1, source_target_pairs={{0,16},{1,17},{2,18},{3,19},{4,20},{5,21},{6,22},{7,23},{8,24},{9,... | collective-permute-start | bytes 516104 | tf_op jit(solution)/shard_map/ppermute | solution.py:338
  112.1 14.0 %collective-permute-start.20 = (bf16[1,2,96,768]{3,2,1,0:T(8,128)(2,1)S(1)}, bf16[1,2,96,768]{3,2,1,0:T(8,128)(2,1)S(1)}, u32[]{:S(2)}, u32[]{:S(2)}) collective-permute-start(bf16[1,2,96,768]{3,2,1,0:T(8,128)(2,1)S(1)} %get-tuple-element.101), channel_id=1, source_target_pairs={{0,16},{1,17},{2,18},{3,19},{4,20},{5,21},{6,22},{7,23},{8,24},{9,... | collective-permute-start | bytes 884744 | tf_op jit(solution)/shard_map/ppermute | solution.py:338
  (24 other events, 74.1 us)

commit v3 on v2

v3 whole, which is shorter than its diff:
```python
from functools import partial

import jax
import jax.numpy as jnp
import numpy as np
from jax import lax
from jax.experimental import pallas as pl
from jax.experimental.pallas import tpu as pltpu
from jax.sharding import PartitionSpec as P

HEAD_DIM = 64
NORM_EPSILON = 1e-05
CORES = 2
CHUNKS = 1
F32 = jnp.float32
LOW = jnp.bfloat16
MIB = 1 << 20
COST_FLOPS = 0
COST_BYTES = 0

VECTOR_ROWS = 8
PAIR_ROWS = 2 * VECTOR_ROWS


def nn(left, right):
    return lax.dot_general(left, right, (((1,), (0,)), ((), ())), preferred_element_type=F32)


def nt(left, right):
    return lax.dot_general(left, right, (((1,), (1,)), ((), ())), preferred_element_type=F32)


def tn(left, right):
    return lax.dot_general(left, right, (((0,), (0,)), ((), ())), preferred_element_type=F32)


def normalize(resid):
    center = resid - jnp.mean(resid, -1, keepdims=True)
    inverse = lax.rsqrt(jnp.mean(center * center, -1, keepdims=True) + NORM_EPSILON)
    return center * inverse, inverse


def norm_back(grad_norm, normed, inverse):
    mean_grad = jnp.mean(grad_norm, -1, keepdims=True)
    mean_proj = jnp.mean(grad_norm * normed, -1, keepdims=True)
    return inverse * (grad_norm - mean_grad - normed * mean_proj)


class State:
    def __init__(self):
        self.arrays = {}

    def drop(self, *names):
        for name in names:
            del self.arrays[name]

    def call(self, kernel, outs, *inputs, mib=16, scratch=(), loose=False):
        names = list(self.arrays)
        direct = [item for item in inputs if not isinstance(item, str)]
        read = {item for item in inputs if isinstance(item, str)}
        vmem = pl.BlockSpec(memory_space=pltpu.VMEM)
        anywhere = pl.BlockSpec(memory_space=pl.ANY)
        scalar = pl.BlockSpec(memory_space=pltpu.SMEM)
        held_shapes = [
            jax.ShapeDtypeStruct(self.arrays[name].shape, self.arrays[name].dtype) for name in names
        ]
        out_shapes = [jax.ShapeDtypeStruct(out[0], out[1]) for out in outs]

        def body(*refs):
            refs = list(refs)
            arrays, refs = refs[: len(direct)], refs[len(direct) :]
            held, refs = dict(zip(names, refs)), refs[len(names) :]
            results, refs = refs[: len(outs)], refs[len(outs) :]
            rest = refs[len(names) :]
            ins = [held[item] if isinstance(item, str) else arrays.pop(0) for item in inputs]
            kernel(*ins, *results, *rest)

        results = pl.pallas_call(
            body,
            name=getattr(kernel, "__name__", None) or kernel.func.__name__,
            out_shape=tuple(out_shapes + held_shapes),
            in_specs=[
                anywhere if loose else scalar if array.dtype == jnp.int32 else vmem
                for array in direct
            ]
            + [vmem if name in read else anywhere for name in names],
            out_specs=tuple([vmem] * len(outs) + [anywhere] * len(names)),
            input_output_aliases={
                len(direct) + index: len(outs) + index for index in range(len(names))
            },
            scratch_shapes=list(scratch),
            compiler_params=pltpu.CompilerParams(vmem_limit_bytes=mib * MIB),
            cost_estimate=pl.CostEstimate(flops=COST_FLOPS, bytes_accessed=COST_BYTES, transcendentals=0),
        )(*direct, *self.arrays.values())
        for name, array in zip(names, results[len(outs) :]):
            self.arrays[name] = array
        returned = []
        for out, array in zip(outs, results):
            if len(out) == 3:
                self.arrays[out[2]] = array
            else:
                returned.append(array)
        return returned


def my_core():
    return lax.rem(lax.axis_index("tensor"), CORES)


BIAS_OUT, GAIN_ONE, SHIFT_ONE, BIAS_UP, BIAS_DOWN, GAIN_TWO, SHIFT_TWO = range(7)


def row(packed, index):
    return packed[index : index + 1, :]


def attn_forward(lengths, tokens, w_qkv, bias_qv, w_out, saved_o, send_o, keep_o):
    core, length = my_core(), lengths[0]
    rows, width = saved_o.shape[1:]
    half = rows // 2
    x = tokens[...]
    query = (nt(x, w_qkv[0]) + bias_qv[0:1, :]).astype(LOW)
    keys = nt(x, w_qkv[1]).astype(LOW)
    values = (nt(x, w_qkv[2]) + bias_qv[1:2, :]).astype(LOW)
    saved_o[0] = query
    saved_o[1] = keys
    saved_o[2] = values
    head_of = lax.broadcasted_iota(jnp.int32, (rows, width), 1) // HEAD_DIM
    key_valid = lax.broadcasted_iota(jnp.int32, (rows, rows), 1) < length
    scaled = query.astype(F32) * HEAD_DIM ** -0.5
    value_full = values.astype(F32)
    total = jnp.zeros((rows, width), F32)
    for head in range(width // HEAD_DIM):
        here = head_of == head
        scores = nt(jnp.where(here, scaled, 0.0).astype(LOW), keys)
        scores = jnp.where(key_valid, scores, -1e30)
        expo = jnp.exp(scores - jnp.max(scores, -1, keepdims=True))
        probs = (expo * (1.0 / jnp.sum(expo, -1, keepdims=True))).astype(LOW)
        total = total + nn(probs, jnp.where(here, value_full, 0.0).astype(LOW))
    saved_o[3] = total.astype(LOW)
    other_start = pl.multiple_of((1 - core) * half, half)
    own_start = pl.multiple_of(core * half, half)
    send_o[...] = nn(saved_o[3, pl.ds(other_start, half), :], w_out[...]).astype(LOW)
    keep_o[...] = nn(saved_o[3, pl.ds(own_start, half), :], w_out[...])


def add_chunks(kept, received, *outs):
    rows = outs[0].shape[0]
    count = len(outs) // 2
    for index in range(count):
        picked = slice(index * rows, (index + 1) * rows)
        total = (kept[picked, :] + received[picked, :].astype(F32)).astype(LOW)
        outs[index][...] = total
        outs[count + index][...] = total


def hold(*refs):
    sems = refs[-1]
    count = (len(refs) - 1) // 2
    copies = [
        pltpu.make_async_copy(refs[index], refs[count + index], sems.at[index])
        for index in range(count)
    ]
    for copy in copies:
        copy.start()
    for copy in copies:
        copy.wait()


def add_rows(kept, received, out):
    out[...] = (kept[...] + received[...].astype(F32)).astype(LOW)


def final_rows(*refs):
    resids, (own, received, out) = refs[:-3], refs[-3:]
    rows = resids[0].shape[0]
    for index, resid in enumerate(resids):
        picked = slice(index * rows, (index + 1) * rows)
        out[picked, :] = (
            resid[...] + (own[picked, :].astype(F32) + received[picked, :].astype(F32))
        ).astype(LOW)


def place_rows(*refs):
    out = refs[-1]
    pieces = refs[:-1]
    count = len(pieces) // 2
    rows = pieces[0].shape[0]
    half = count * rows
    core = my_core()
    for index in range(count):
        own_start = pl.multiple_of(core * half + index * rows, rows)
        other_start = pl.multiple_of((1 - core) * half + index * rows, rows)
        out[pl.ds(own_start, rows), :] = pieces[index][...]
        out[pl.ds(other_start, rows), :] = pieces[count + index][...]


def mlp_forward(
    index, received, tokens, own, packed, packed_other, up_own, up_other, down_own, down_other,
    part_o, pass_o, kept_o, hidden_o, act_o, slopes_o, normed_o, inverse_o,
):
    rows, width = part_o.shape
    units = up_own.shape[1]
    start = pl.multiple_of((my_core() * CHUNKS + index) * rows, rows)
    resid = tokens[pl.ds(start, rows), :].astype(F32) + row(packed, BIAS_OUT)
    resid = resid + (own[...].astype(F32) + received[...].astype(F32))
    normed, inverse = normalize(resid)
    normed_o[...] = normed
    inverse_o[...] = inverse
    hidden_low = (normed * row(packed, GAIN_ONE) + row(packed, SHIFT_ONE)).astype(LOW)
    pass_o[:, :width] = hidden_low
    hidden_o[...] = hidden_low

    def units_of(up, vectors, side):
        pre = nn(hidden_low, up[...]) + row(vectors, BIAS_UP)
        cdf = 0.5 * (1.0 + lax.erf(pre * 0.7071067811865476))
        slopes_o[side] = cdf + pre * (jnp.exp(-0.5 * pre * pre) * 0.3989422804014327)
        return (pre * cdf).astype(LOW)

    act_own = units_of(up_own, packed, 0)
    act_o[...] = act_own
    act_other = units_of(up_other, packed_other, 1)
    pass_o[:, width : width + units] = act_other
    part = (nn(act_own, down_own[...]) + nn(act_other, down_other[...])).astype(LOW)
    part_o[...] = part
    kept_o[...] = part


def mlp_backward(
    index, lengths, received, normed_one, own, packed, cotangent, down_own, down_other, slopes,
    up_own, up_other,
    part_o, pass_o, kept_o, grad_o, pre_o, resid_o, out_o, sums_o,
):
    rows, width = part_o.shape
    units = up_own.shape[1]
    length = lengths[0]
    start = pl.multiple_of((my_core() * CHUNKS + index) * rows, rows)
    hidden = normed_one[...] * row(packed, GAIN_ONE) + row(packed, SHIFT_ONE)
    branch = own[...].astype(F32) + received[...].astype(F32) + row(packed, BIAS_DOWN)
    normed, inverse = normalize(hidden + branch)
    valid = lax.broadcasted_iota(jnp.int32, (rows, width), 0) + start < length
    out = jnp.where(valid, normed * row(packed, GAIN_TWO) + row(packed, SHIFT_TWO), 0.0)
    out_o[...] = out.astype(LOW)
    grad_out = jnp.where(valid, cotangent[pl.ds(start, rows), :].astype(F32), 0.0)
    sums_o[0:1, :] = jnp.sum(grad_out * normed, 0, keepdims=True)
    sums_o[1:2, :] = jnp.sum(grad_out, 0, keepdims=True)
    grad_resid = norm_back(grad_out * row(packed, GAIN_TWO), normed, inverse)
    resid_o[...] = grad_resid
    grad_mlp = grad_resid.astype(LOW)
    pass_o[:, :width] = grad_mlp
    grad_o[...] = grad_mlp
    pre_own = (nt(grad_mlp, down_own[...]) * slopes[0]).astype(LOW)
    pre_o[...] = pre_own
    pre_other = (nt(grad_mlp, down_other[...]) * slopes[1]).astype(LOW)
    pass_o[:, width : width + units] = pre_other
    part = (nt(pre_own, up_own[...]) + nt(pre_other, up_other[...])).astype(LOW)
    part_o[...] = part
    kept_o[...] = part


def spread(blocks, grad):
    block = blocks.shape[1]
    for index in range(blocks.shape[0]):
        blocks[index] = grad[index * block : (index + 1) * block, :]


def block_of(dp_size, slot):
    patterns = []
    for order in dp_orders(dp_size):
        pattern = 0
        for step, bit in enumerate(order):
            if (slot >> (len(order) - 1 - step)) & 1:
                pattern |= 1 << bit
        patterns.append(pattern)
    return jnp.where(my_core() == 0, patterns[0], patterns[1]) ^ lax.axis_index("dp")


def weight_grad(take, *refs):
    pieces, (send_o, keep_o, sum_o, left, right, blocks) = refs[:-6], refs[-6:]
    model = left.shape[1]
    rows = pieces[0].shape[0]
    half = len(pieces) // 2
    for target, sources, columns in (
        (left, pieces[:half], take[:half]), (right, pieces[half:], take[half:])
    ):
        for index, (source, column) in enumerate(zip(sources, columns)):
            picked = slice(column * model, (column + 1) * model)
            target[index * rows : (index + 1) * rows, :] = source[:, picked]
    spread(blocks, tn(left[...], right[...]))
    summed = left if sum_o.shape[0] == 1 else right
    sum_o[0:1, :] = jnp.sum(summed[...].astype(F32), 0, keepdims=True)
    count = keep_o.shape[0]
    for index in range(count):
        send_o[index] = blocks[block_of(2 * count, index + count)].astype(LOW)
    for index in range(count):
        keep_o[index] = blocks[block_of(2 * count, index)]


def norm_one_back(
    received, own, resid_two, normed, inverse, packed, sums_two, sums_before,
    low_o, sums_o, resid_o,
):
    grad_hidden = resid_two[...] + (own[...].astype(F32) + received[...].astype(F32))
    xhat = normed[...]
    grad_resid = norm_back(grad_hidden * row(packed, GAIN_ONE), xhat, inverse[...])
    resid_o[...] = grad_resid
    low = grad_resid.astype(LOW)
    low_o[...] = low
    sums_o[...] = sums_before[...]
    sums_o[0:2, :] += sums_two[...]
    sums_o[2:3, :] += jnp.sum(grad_hidden * xhat, 0, keepdims=True)
    sums_o[3:4, :] += jnp.sum(grad_hidden, 0, keepdims=True)
    sums_o[4:5, :] += jnp.sum(low.astype(F32), 0, keepdims=True)


def split_pair(vectors):
    high = vectors.astype(LOW)
    return jnp.concatenate([high.astype(F32), vectors - high.astype(F32)], 0).astype(LOW)


def attn_backward(
    lengths, *refs,
):
    pieces, refs = refs[: 2 * CHUNKS], refs[2 * CHUNKS :]
    sums_own, sums_other, w_out, saved, tokens, sum_down, sum_up = refs[:7]
    send_o, keep_o, gq_o, gk_o, gv_o, grad_attn, blocks, sums = refs[7:]
    length = lengths[0]
    rows, width = saved.shape[1:]
    place_rows(*pieces, grad_attn)
    grad_rows = grad_attn[...]
    grad_att = nt(grad_rows, w_out[...]).astype(LOW)
    scale = HEAD_DIM ** -0.5
    head_of = lax.broadcasted_iota(jnp.int32, (rows, width), 1) // HEAD_DIM
    key_valid = lax.broadcasted_iota(jnp.int32, (rows, rows), 0) < length
    query, keys, values = saved[0], saved[1], saved[2]
    scaled = query.astype(F32) * scale
    scaled_keys = keys.astype(F32) * scale
    grad_att_full = grad_att.astype(F32)
    grad_q = jnp.zeros((rows, width), F32)
    grad_k = jnp.zeros((rows, width), F32)
    grad_v = jnp.zeros((rows, width), F32)
    for head in range(width // HEAD_DIM):
        here = head_of == head
        scaled_here = jnp.where(here, scaled, 0.0).astype(LOW)
        scores = jnp.where(key_valid, nt(keys, scaled_here), -1e30)
        expo = jnp.exp(scores - jnp.max(scores, 0, keepdims=True))
        probs = expo * (1.0 / jnp.sum(expo, 0, keepdims=True))
        grad_here = jnp.where(here, grad_att_full, 0.0).astype(LOW)
        grad_probs = nt(values, grad_here)
        grad_v = grad_v + nn(probs.astype(LOW), grad_here)
        inner = jnp.sum(probs * grad_probs, 0, keepdims=True)
        grad_scores = (probs * (grad_probs - inner)).astype(LOW)
        grad_k = grad_k + nn(grad_scores, scaled_here)
        grad_q = grad_q + tn(grad_scores, jnp.where(here, scaled_keys, 0.0).astype(LOW))
    low_q, low_k, low_v = grad_q.astype(LOW), grad_k.astype(LOW), grad_v.astype(LOW)
    gq_o[...] = low_q
    gk_o[...] = low_k
    gv_o[...] = low_v
    x = tokens[...]
    weight = jnp.concatenate(
        [tn(x, low_q), tn(x, low_k), tn(x, low_v), tn(grad_rows, saved[3])], 1
    )
    spread(blocks, weight)
    sums[...] = sums_own[...] + sums_other[...]
    sums[5:6, :] = sum_down[0:1, :]
    sums[6:7, :] = sum_up[0:1, :]
    last = VECTOR_ROWS - 1
    sums[last : last + 1, :width] = jnp.sum(low_q.astype(F32), 0, keepdims=True)
    sums[last : last + 1, 2 * width : 3 * width] = jnp.sum(low_v.astype(F32), 0, keepdims=True)
    vector_sums = sums[...]
    block = blocks.shape[1]
    pair = split_pair(vector_sums)
    count = keep_o.shape[0]
    for index in range(count):
        send_o[index, :block] = blocks[block_of(2 * count, index + count)].astype(LOW)
        send_o[index, block:] = pair
    for index in range(count):
        keep_o[index, :block] = blocks[block_of(2 * count, index)]
        keep_o[index, block : block + VECTOR_ROWS] = vector_sums
        keep_o[index, block + VECTOR_ROWS :] = jnp.zeros_like(vector_sums)


def token_back(gq, gk, gv, w_qkv, send_o, keep_o):
    half = send_o.shape[0]
    core = my_core()

    def rows_from(start):
        picked = pl.ds(pl.multiple_of(start, half), half)
        return (
            nn(gq[picked, :], w_qkv[0]) + nn(gk[picked, :], w_qkv[1]) + nn(gv[picked, :], w_qkv[2])
        )

    send_o[...] = rows_from((1 - core) * half).astype(LOW)
    keep_o[...] = rows_from(core * half)


def merge_weights(keep, received, send_o, keep_o):
    count = keep_o.shape[0]
    for index in range(count):
        send_o[index] = (keep[count + index] + received[count + index].astype(F32)).astype(LOW)
    for index in range(count):
        keep_o[index] = keep[index] + received[index].astype(F32)


def merge_last_weights(keep, received, out):
    out[...] = keep[0] + received[0].astype(F32)


def merged_vectors(keep, received, index, block):
    high = received[index, block : block + VECTOR_ROWS].astype(F32)
    low = received[index, block + VECTOR_ROWS :].astype(F32)
    return keep[index, block : block + VECTOR_ROWS] + high + low


def merge_attn(keep, received, send_o, keep_o):
    count = keep_o.shape[0]
    block = keep_o.shape[1] - PAIR_ROWS
    for index in range(count):
        at = count + index
        send_o[index, :block] = (keep[at, :block] + received[at, :block].astype(F32)).astype(LOW)
        send_o[index, block:] = split_pair(merged_vectors(keep, received, at, block))
    for index in range(count):
        keep_o[index, :block] = keep[index, :block] + received[index, :block].astype(F32)
        vectors = merged_vectors(keep, received, index, block)
        keep_o[index, block : block + VECTOR_ROWS] = vectors
        keep_o[index, block + VECTOR_ROWS :] = jnp.zeros_like(vectors)


def merge_last_attn(keep, received, qkv_o, out_o, vectors_o, pair_o):
    block, width = qkv_o.shape[1], qkv_o.shape[2]
    total = keep[0, :block] + received[0, :block].astype(F32)
    for part in range(3):
        qkv_o[part] = total[:, part * width : (part + 1) * width]
    out_o[...] = total[:, 3 * width :].T
    vectors = merged_vectors(keep, received, 0, block)
    model = vectors.shape[1]
    me = lax.axis_index("dp")
    vectors_o[...] = pltpu.roll(vectors, lax.rem(model - me * block, model), 1)[:, :block]
    small = pair_o.shape[1]
    turned = pltpu.roll(vectors, lax.rem(model - me * small, model), 1)
    last = VECTOR_ROWS - 1
    pair_o[0:1, :] = turned[last : last + 1, :small]
    pair_o[1:2, :] = turned[last : last + 1, 2 * width : 2 * width + small]


CORE_PAIRS = [(i, i ^ 1) for i in range(4)]
CHIP_PAIRS = [(i, i ^ 2) for i in range(4)]


def to_core(block):
    return lax.ppermute(block, "tensor", CORE_PAIRS)


def to_chip(block):
    return lax.ppermute(block, "tensor", CHIP_PAIRS)


def dp_orders(dp_size):
    bits = list(range(dp_size.bit_length() - 1))
    swapped = bits[:2][::-1] + bits[2:]
    return (bits, swapped)


def to_dp(block, step, dp_size, tensor_size):
    orders = dp_orders(dp_size)
    pairs = []
    for d in range(dp_size):
        for t in range(tensor_size):
            partner = d ^ (1 << orders[t % CORES][step])
            pairs.append((d * tensor_size + t, partner * tensor_size + t))
    return lax.ppermute(block, ("dp", "tensor"), pairs)


def on_device(
    tokens,
    w_qkv,
    bias_qv,
    w_out,
    bias_out,
    gain_one,
    shift_one,
    w_up,
    bias_up,
    w_down,
    bias_down,
    gain_two,
    shift_two,
    cotangent,
    lengths,
):
    rows, model = tokens.shape
    half = rows // 2
    chunk = half // CHUNKS
    width = w_qkv.shape[2]
    units = w_up.shape[1]
    dp_size = lax.axis_size("dp")
    tensor_size = lax.axis_size("tensor")
    steps = dp_size.bit_length() - 1
    block = model // dp_size
    count = dp_size // 2
    chunks = range(CHUNKS)
    packed = jnp.stack(
        [bias_out, gain_one, shift_one, bias_up, bias_down, gain_two, shift_two, shift_two]
    )
    w_turned = w_qkv.transpose(0, 2, 1)
    up_other, down_other = to_core(w_up), to_core(w_down)
    packed_other = to_core(packed)

    state = State()
    attn_send, attn_keep = state.call(
        attn_forward,
        [((4, rows, width), LOW, "saved"), ((half, model), LOW), ((half, model), F32)],
        lengths, tokens, w_turned, bias_qv, w_out,
        mib=20,
    )
    attn_parts = state.call(
        add_chunks,
        [((chunk, model), LOW)] * CHUNKS + [((chunk, model), LOW, f"attn{c}") for c in chunks],
        attn_keep, to_core(attn_send),
    )
    received = [to_chip(part) for part in attn_parts]
    held = {
        "tokens": tokens, "w_out": w_out, "w_qkv": w_turned, "cotangent": cotangent,
        "up_own": w_up, "up_other": up_other, "down_own": w_down, "down_other": down_other,
        "packed": packed, "packed_other": packed_other,
    }
    state.call(
        hold,
        [(array.shape, array.dtype, name) for name, array in held.items()],
        *held.values(),
        scratch=[pltpu.SemaphoreType.DMA((len(held),))], loose=True,
    )

    passed, fwd_other = [], []
    for c in chunks:
        part, fwd = state.call(
            partial(mlp_forward, c),
            [
                ((chunk, model), LOW), ((chunk, model + units), LOW),
                ((chunk, model), LOW, f"mlp{c}"), ((chunk, model), LOW, f"hid{c}"),
                ((chunk, units), LOW, f"act{c}"), ((2, chunk, units), F32, f"slopes{c}"),
                ((chunk, model), F32, f"normed{c}"), ((chunk, 1), F32, f"inverse{c}"),
            ],
            received[c], "tokens", f"attn{c}", "packed", "packed_other",
            "up_own", "up_other", "down_own", "down_other",
        )
        state.drop(f"attn{c}")
        passed.append(to_chip(part))
        fwd_other.append(to_core(fwd))
    received = passed

    passed, bwd_other, out_half = [], [], []
    for c in chunks:
        part, bwd, out_c = state.call(
            partial(mlp_backward, c),
            [
                ((chunk, model), LOW), ((chunk, model + units), LOW),
                ((chunk, model), LOW, f"back{c}"), ((chunk, model), LOW, f"grad{c}"),
                ((chunk, units), LOW, f"pre{c}"), ((chunk, model), F32, f"resid{c}"),
                ((chunk, model), LOW), ((2, model), F32, f"sums{c}"),
            ],
            lengths, received[c], f"normed{c}", f"mlp{c}", "packed", "cotangent",
            "down_own", "down_other", f"slopes{c}", "up_own", "up_other",
        )
        state.drop(f"mlp{c}", f"slopes{c}")
        passed.append(to_chip(part))
        bwd_other.append(to_core(bwd))
        out_half.append(out_c)
    state.drop("cotangent", "up_own", "up_other", "down_own", "down_other")
    received = passed
    out_other = [to_core(part) for part in out_half]

    scratch = [pltpu.VMEM((rows, model), LOW)] * 2 + [pltpu.VMEM((dp_size, block, units), F32)]
    grad_shape = (count, block, units)
    pairs = [0, 0] * CHUNKS

    def both(own, other):
        return [piece for c in chunks for piece in (f"{own}{c}", other[c])]

    (down_send,) = state.call(
        partial(weight_grad, pairs + [0, 1] * CHUNKS),
        [(grad_shape, LOW), (grad_shape, F32, "down_keep"), ((1, model), F32, "sum_down")],
        *both("grad", bwd_other),
        *[piece for c in chunks for piece in (f"act{c}", fwd_other[c])],
        scratch=scratch, mib=20,
    )
    down_got = to_dp(down_send, 0, dp_size, tensor_size)
    (up_send,) = state.call(
        partial(weight_grad, pairs + [0, 1] * CHUNKS),
        [(grad_shape, LOW), (grad_shape, F32, "up_keep"), ((2, units), F32, "sum_up")],
        *both("hid", fwd_other),
        *[piece for c in chunks for piece in (f"pre{c}", bwd_other[c])],
        scratch=scratch, mib=20,
    )
    up_got = to_dp(up_send, 0, dp_size, tensor_size)
    for c in chunks:
        state.drop(f"hid{c}", f"act{c}", f"grad{c}", f"pre{c}")
    for c in chunks:
        state.arrays[f"out_half{c}"] = out_half[c]
        state.arrays[f"out_other{c}"] = out_other[c]

    sums = jnp.zeros((VECTOR_ROWS, model), F32)
    grad_attn, grad_attn_other = [], []
    for c in chunks:
        low, sums = state.call(
            norm_one_back,
            [((chunk, model), LOW), ((VECTOR_ROWS, model), F32), ((chunk, model), F32, f"last{c}")],
            received[c], f"back{c}", f"resid{c}", f"normed{c}", f"inverse{c}", "packed", f"sums{c}",
            sums,
        )
        state.drop(f"back{c}", f"resid{c}", f"normed{c}", f"inverse{c}", f"sums{c}")
        grad_attn.append(low)
        grad_attn_other.append(to_core(low))
    sums_other = to_core(sums)

    def merge(name, got, step):
        kept = dp_size >> (step + 1)
        shape = state.arrays[name].shape[1:]
        kernel = merge_attn if name == "attn_keep" else merge_weights
        (send,) = state.call(
            kernel, [((kept,) + shape, LOW), ((kept,) + shape, F32, "next")], name, got
        )
        state.drop(name)
        state.arrays[name] = state.arrays.pop("next")
        return to_dp(send, step, dp_size, tensor_size)

    if steps > 1:
        down_got = merge("down_keep", down_got, 1)

    attn_w_send, grad_q, grad_k, grad_v = state.call(
        attn_backward,
        [
            ((count, block + PAIR_ROWS, model), LOW),
            ((count, block + PAIR_ROWS, model), F32, "attn_keep"),
        ]
        + [((rows, width), LOW)] * 3,
        lengths, *grad_attn, *grad_attn_other, sums, sums_other,
        "w_out", "saved", "tokens", "sum_down", "sum_up",
        scratch=[
            pltpu.VMEM((rows, model), LOW),
            pltpu.VMEM((dp_size, block, model), F32),
            pltpu.VMEM((VECTOR_ROWS, model), F32),
        ],
        mib=24,
    )
    state.drop("saved", "sum_down", "sum_up", "w_out", "tokens", "packed", "packed_other")
    attn_got = to_dp(attn_w_send, 0, dp_size, tensor_size)
    if steps > 1:
        up_got = merge("up_keep", up_got, 1)
    token_send, token_keep = state.call(
        token_back,
        [((half, model), LOW), ((half, model), F32)],
        grad_q, grad_k, grad_v, "w_qkv",
    )
    state.drop("w_qkv")
    (token_own,) = state.call(add_rows, [((half, model), LOW)], token_keep, to_core(token_send))
    token_received = to_chip(token_own)
    for step in range(2, steps):
        down_got = merge("down_keep", down_got, step)
    if steps > 1:
        attn_got = merge("attn_keep", attn_got, 1)
    for step in range(2, steps):
        up_got = merge("up_keep", up_got, step)
    (token_half,) = state.call(
        final_rows, [((half, model), LOW)], *[f"last{c}" for c in chunks],
        token_own, token_received,
    )
    state.drop(*[f"last{c}" for c in chunks])
    for step in range(2, steps):
        attn_got = merge("attn_keep", attn_got, step)
    (output_low,) = state.call(
        place_rows, [((rows, model), LOW)],
        *[f"out_half{c}" for c in chunks], *[f"out_other{c}" for c in chunks],
    )
    state.drop(*[f"out_half{c}" for c in chunks], *[f"out_other{c}" for c in chunks])
    (token_total,) = state.call(
        place_rows, [((rows, model), LOW)], token_half, to_core(token_half),
    )
    (sum_w_down,) = state.call(merge_last_weights, [((block, units), F32)], "down_keep", down_got)
    state.drop("down_keep")
    (sum_w_up,) = state.call(merge_last_weights, [((block, units), F32)], "up_keep", up_got)
    state.drop("up_keep")
    sum_w_qkv, sum_w_out, mine, sum_bias_qv = state.call(
        merge_last_attn,
        [
            ((3, block, width), F32), ((width, block), F32), ((VECTOR_ROWS, block), F32),
            ((2, width // dp_size), F32),
        ],
        "attn_keep", attn_got,
    )
    return (
        output_low,
        token_total,
        sum_w_qkv,
        sum_bias_qv,
        sum_w_out,
        mine[4],
        mine[2],
        mine[3],
        sum_w_up,
        mine[6],
        sum_w_down.T,
        mine[5],
        mine[0],
        mine[1],
    )


def solution(mesh):
    placed = (
        P("dp", None),
        P(None, None, "tensor"),
        P(None, "tensor"),
        P("tensor", None),
        P(),
        P(),
        P(),
        P(None, "tensor"),
        P("tensor"),
        P("tensor", None),
        P(),
        P(),
        P(),
        P("dp", None),
        P("dp"),
    )
    return jax.shard_map(
        on_device,
        mesh=mesh,
        in_specs=placed,
        out_specs=(
            P("dp", None),
            P("dp", None),
            P(None, "dp", "tensor"),
            P(None, ("tensor", "dp")),
            P("tensor", "dp"),
            P("dp"),
            P("dp"),
            P("dp"),
            P("dp", "tensor"),
            P(("tensor", "dp")),
            P("tensor", "dp"),
            P("dp"),
            P("dp"),
            P("dp"),
        ),
        check_vma=False,
    )
```

time: 129 us -> 106 us (0.82)
  waiting for transfers between devices: 60.9 us -> 47.8 us
  other arithmetic: 6.67 us -> 0 us
  starting transfers between devices: 19.5 us -> 23.6 us
  local copies, waits for them, and re-layouts: 12.2 us -> 8.29 us
  Pallas kernels: 27.3 us -> 24.6 us
    ppermute x4, waiting for transfers between devices: 24.4 us -> 16.2 us  [to_chip(): return lax.ppermute(block, 'tensor', CHIP_PAIRS)]
    ppermute x6 -> x9, waiting for transfers between devices: 33.6 us -> 27.6 us  [to_dp(): return lax.ppermute(block, ('dp', 'tensor'), pairs)]
    select_n x2 -> x0, other arithmetic: 4.65 us -> none  [in_order(): jnp.where(core == 0, jnp.concatenate([own, other], 0), jnp.concatenate([o...]
    ppermute x6 -> x9, starting transfers between devices: 9.88 us -> 13.8 us  [to_dp(): return lax.ppermute(block, ('dp', 'tensor'), pairs)]
    unnamed x72 -> x34, local copies, waits for them, and re-layouts: 10.8 us -> 7.67 us
    pallas_call x13 -> x23, Pallas kernels: 27.3 us -> 24.6 us  [call(): pl.pallas_call(body, name=getattr(kernel, '__name__', None) or kernel.fun...]
  transfers between devices with their start and end apart: 21 -> 24, of which waited for: 10 -> 14; matrix products, arithmetic and copies ran while one was open for 7% -> 0% of each run, Pallas kernels for 10% -> 19%
where the time goes in v3:
time: 106 us
  waiting for transfers between devices  47.8 us (45%)
  Pallas kernels  24.6 us (23%)
  starting transfers between devices  23.6 us (22%)
  local copies, waits for them, and re-layouts  8.29 us (8%)
  between operations  1.66 us (2%)
    ppermute x9, waiting for transfers between devices, to_dp(): return lax.ppermute(block, ('dp', 'tensor'), pairs)  27.6 us
    pallas_call x23, Pallas kernels, call(): pl.pallas_call(body, name=getattr(kernel, '__name__', None) or kernel.fun...  24.6 us
    ppermute x4, waiting for transfers between devices, to_chip(): return lax.ppermute(block, 'tensor', CHIP_PAIRS)  16.2 us
    ppermute x9, starting transfers between devices, to_dp(): return lax.ppermute(block, ('dp', 'tensor'), pairs)  13.8 us
    ppermute x4, starting transfers between devices, to_chip(): return lax.ppermute(block, 'tensor', CHIP_PAIRS)  7.72 us
    unnamed x34, local copies, waits for them, and re-layouts  7.67 us
    ppermute x11, waiting for transfers between devices, to_core(): return lax.ppermute(block, 'tensor', CORE_PAIRS)  3.95 us
  transfers between devices with their start and end apart: 24, of which 14 were waited for; matrix products, arithmetic and copies ran while one was open for 0% of the time, Pallas kernels for 19%

profile of v3, /device:TPU:0, one launch (start us, length us, event | category | flops | bytes accessed | tf_op | source)
XLA Modules:
  0.0 105.9 jit_solution(10666200668625575013)
XLA Ops:
  1.9 1.2 %copy-done = bf16[3,768,192]{1,2,0:T(8,128)(2,1)S(1)} copy-done((bf16[3,768,192]{1,2,0:T(8,128)(2,1)S(1)}, bf16[3,768,192]{1,2,0:T(8,128)(2,1)}, u32[]{:S(2)}) %copy-start) | copy-done | bytes 884760
  3.1 1.1 %copy-done.2 = bf16[512,768]{1,0:T(8,128)(2,1)S(1)} copy-done((bf16[512,768]{1,0:T(8,128)(2,1)S(1)}, bf16[512,768]{1,0:T(8,128)(2,1)}, u32[]{:S(2)}) %copy-start.2) | copy-done | bytes 786456
  4.2 1.0 copy-done.6
  5.8 2.8 %attn_forward.1 = (bf16[4,512,192]{2,1,0:T(8,128)(2,1)S(1)}, bf16[256,768]{1,0:T(8,128)(2,1)S(1)}, f32[256,768]{1,0:T(8,128)S(1)}) custom-call(s32[1]{0:T(128)S(6)} %copy.369.refs_0_, bf16[512,768]{1,0:T(8,128)(2,1)S(1)} %copy-done.2, bf16[3,192,768]{2,1,0:T(8,128)(2,1)S(1)} %bitcast.16, f32[2,192]{1,0:T(2,128)S(1)} %copy-done.9, bf16[192,768]{1,0:T(8,128)(2,1)S(1)} %copy-done.6), custom_call_target="tpu_custom_call" | custom-call | tf_op jit(solution)/shard_map/attn_forward/pallas_call | solution.py:78
  9.3 1.3 %collective-permute-done.refs_1_ = bf16[256,768]{1,0:T(8,128)(2,1)S(1)} collective-permute-done((bf16[256,768]{1,0:T(8,128)(2,1)S(1)}, bf16[256,768]{1,0:T(8,128)(2,1)S(1)}, u32[]{:S(2)}, u32[]{:S(2)}) %collective-permute-start) | collective-permute-done | bytes 393248 | tf_op jit(solution)/shard_map/ppermute | solution.py:451
  11.4 2.9 %collective-permute-start.1 = (bf16[256,768]{1,0:T(8,128)(2,1)}, bf16[256,768]{1,0:T(8,128)(2,1)}, u32[]{:S(2)}, u32[]{:S(2)}) collective-permute-start(bf16[256,768]{1,0:T(8,128)(2,1)} %get-tuple-element.219), channel_id=1, source_target_pairs={{0,2},{1,3},{2,0},{3,1},{4,6},{5,7},{6,4},{7,5},{8,10},{9,11},{10,... | collective-permute-start | bytes 1179656 | tf_op jit(solution)/shard_map/ppermute | solution.py:455
  14.6 1.2 %collective-permute-done.4.refs_9_ = f32[8,768]{1,0:T(8,128)S(1)} collective-permute-done((f32[8,768]{1,0:T(8,128)S(1)}, f32[8,768]{1,0:T(8,128)S(1)}, u32[]{:S(2)}, u32[]{:S(2)}) %collective-permute-start.4) | collective-permute-done | bytes 24608 | tf_op jit(solution)/shard_map/ppermute | solution.py:451
  15.8 1.3 %copy-done.4 = bf16[768,768]{1,0:T(8,128)(2,1)S(1)} copy-done((bf16[768,768]{1,0:T(8,128)(2,1)S(1)}, bf16[768,768]{1,0:T(8,128)(2,1)}, u32[]{:S(2)}) %copy-start.4) | copy-done | bytes 1179672
  17.1 1.3 %copy-done.5 = bf16[768,768]{1,0:T(8,128)(2,1)S(1)} copy-done((bf16[768,768]{1,0:T(8,128)(2,1)S(1)}, bf16[768,768]{1,0:T(8,128)(2,1)}, u32[]{:S(2)}) %copy-start.5) | copy-done | bytes 1179672
  18.3 1.1 %copy-done.8 = bf16[512,768]{1,0:T(8,128)(2,1)S(1)} copy-done((bf16[512,768]{1,0:T(8,128)(2,1)S(1)}, bf16[512,768]{1,0:T(8,128)(2,1)}, u32[]{:S(2)}) %copy-start.8) | copy-done | bytes 786456
  19.5 2.4 %hold.1 = (bf16[512,768]{1,0:T(8,128)(2,1)S(1)}, bf16[192,768]{1,0:T(8,128)(2,1)S(1)}, bf16[3,192,768]{2,1,0:T(8,128)(2,1)S(1)}, bf16[512,768]{1,0:T(8,128)(2,1)...) custom-call(bf16[512,768]{1,0:T(8,128)(2,1)S(1)} %copy-done.3, ...), custom_call_target="tpu_custom_call", output_to_operand_aliasing={{10}: (10, {}), {11}: (11, {})} | custom-call | tf_op jit(solution)/shard_map/hold/pallas_call | solution.py:78
  21.9 2.1 %collective-permute-done.1.refs_0_ = bf16[256,768]{1,0:T(8,128)(2,1)} collective-permute-done((bf16[256,768]{1,0:T(8,128)(2,1)}, bf16[256,768]{1,0:T(8,128)(2,1)}, u32[]{:S(2)}, u32[]{:S(2)}) %collective-permute-start.1) | collective-permute-done | bytes 393248 | tf_op jit(solution)/shard_map/ppermute | solution.py:455
  24.0 3.2 %mlp_forward.1 = (bf16[256,768]{1,0:T(8,128)(2,1)S(1)}, bf16[256,1536]{1,0:T(8,128)(2,1)S(1)}, bf16[256,768]{1,0:T(8,128)(2,1)S(1)}, bf16[256,768]{1,0:T(8,128)(...) custom-call(bf16[256,768]{1,0:T(8,128)(2,1)} %collective-permute-don, ...), custom_call_target="tpu_custom_call", output_to_operand_aliasing={{8}: (1, {}), {9}: (2, {}), {10}: (3, {}), {11}: (4, {}), {... | custom-call | tf_op jit(solution)/shard_map/mlp_forward/pallas_call | solution.py:78
  27.2 1.8 %collective-permute-start.5 = (bf16[256,768]{1,0:T(8,128)(2,1)S(1)}, bf16[256,768]{1,0:T(8,128)(2,1)S(1)}, u32[]{:S(2)}, u32[]{:S(2)}) collective-permute-start(bf16[256,768]{1,0:T(8,128)(2,1)S(1)} %get-tuple-element.234), channel_id=1, source_target_pairs={{0,2},{1,3},{2,0},{3,1},{4,6},{5,7},{6,4},{7,5},{8,10},{9,11},{10,... | collective-permute-start | bytes 1179656 | tf_op jit(solution)/shard_map/ppermute | solution.py:455
  29.0 8.9 %collective-permute-done.5.refs_1_ = bf16[256,768]{1,0:T(8,128)(2,1)S(1)} collective-permute-done((bf16[256,768]{1,0:T(8,128)(2,1)S(1)}, bf16[256,768]{1,0:T(8,128)(2,1)S(1)}, u32[]{:S(2)}, u32[]{:S(2)}) %collective-permute-start.5) | collective-permute-done | bytes 393248 | tf_op jit(solution)/shard_map/ppermute | solution.py:455
  37.9 2.6 %mlp_backward.1 = (bf16[256,768]{1,0:T(8,128)(2,1)S(1)}, bf16[256,1536]{1,0:T(8,128)(2,1)S(1)}, bf16[256,768]{1,0:T(8,128)(2,1)S(1)}, bf16[256,768]{1,0:T(8,128)...) custom-call(s32[1]{0:T(128)S(6)} %copy.369.refs_0_, ...), custom_call_target="tpu_custom_call", output_to_operand_aliasing={{8}: (2, {}), {9}: (3, {}), {10}: (4, {}), {11}: (5, {}), {... | custom-call | tf_op jit(solution)/shard_map/mlp_backward/pallas_call | solution.py:78
  40.6 1.5 %collective-permute-start.6 = (bf16[256,768]{1,0:T(8,128)(2,1)S(1)}, bf16[256,768]{1,0:T(8,128)(2,1)S(1)}, u32[]{:S(2)}, u32[]{:S(2)}) collective-permute-start(bf16[256,768]{1,0:T(8,128)(2,1)S(1)} %get-tuple-element.252), channel_id=1, source_target_pairs={{0,2},{1,3},{2,0},{3,1},{4,6},{5,7},{6,4},{7,5},{8,10},{9,11},{10,... | collective-permute-start | bytes 1179656 | tf_op jit(solution)/shard_map/ppermute | solution.py:455
  42.9 1.0 weight_grad.2
  43.8 1.5 %collective-permute-start.12 = (bf16[4,96,768]{2,1,0:T(8,128)(2,1)S(1)}, bf16[4,96,768]{2,1,0:T(8,128)(2,1)S(1)}, u32[]{:S(2)}, u32[]{:S(2)}) collective-permute-start(bf16[4,96,768]{2,1,0:T(8,128)(2,1)S(1)} %get-tuple-element.305), channel_id=1, source_target_pairs={{0,4},{1,9},{2,6},{3,11},{4,0},{5,13},{6,2},{7,15},{8,12},{9,1},{1... | collective-permute-start | bytes 1769480 | tf_op jit(solution)/shard_map/ppermute | solution.py:471
  46.9 5.2 %collective-permute-done.6.refs_0_ = bf16[256,768]{1,0:T(8,128)(2,1)S(1)} collective-permute-done((bf16[256,768]{1,0:T(8,128)(2,1)S(1)}, bf16[256,768]{1,0:T(8,128)(2,1)S(1)}, u32[]{:S(2)}, u32[]{:S(2)}) %collective-permute-start.6) | collective-permute-done | bytes 393248 | tf_op jit(solution)/shard_map/ppermute | solution.py:455
  54.6 4.3 %attn_backward.1 = (bf16[4,112,768]{2,1,0:T(8,128)(2,1)S(1)}, f32[4,112,768]{2,1,0:T(8,128)S(1)}, bf16[512,192]{1,0:T(8,128)(2,1)S(1)}, bf16[512,192]{1,0:T(8,12...) custom-call(s32[1]{0:T(128)S(6)} %copy.369.refs_0_, ...), custom_call_target="tpu_custom_call", output_to_operand_aliasing={{5}: (5, {}), {6}: (6, {}), {7}: (7, {}), {8}: (8, {}), {9}... | custom-call | tf_op jit(solution)/shard_map/attn_backward/pallas_call | solution.py:78
  59.0 1.5 %collective-permute-start.13 = (bf16[4,112,768]{2,1,0:T(8,128)(2,1)S(1)}, bf16[4,112,768]{2,1,0:T(8,128)(2,1)S(1)}, u32[]{:S(2)}, u32[]{:S(2)}) collective-permute-start(bf16[4,112,768]{2,1,0:T(8,128)(2,1)S(1)} %get-tuple-element.332), channel_id=1, source_target_pairs={{0,4},{1,9},{2,6},{3,11},{4,0},{5,13},{6,2},{7,15},{8,12},{9,1},{1... | collective-permute-start | bytes 2064392 | tf_op jit(solution)/shard_map/ppermute | solution.py:471
  61.5 1.6 %collective-permute-start.14 = (bf16[2,96,768]{2,1,0:T(8,128)(2,1)S(1)}, bf16[2,96,768]{2,1,0:T(8,128)(2,1)S(1)}, u32[]{:S(2)}, u32[]{:S(2)}) collective-permute-start(bf16[2,96,768]{2,1,0:T(8,128)(2,1)S(1)} %get-tuple-element.333), channel_id=1, source_target_pairs={{0,8},{1,5},{2,10},{3,7},{4,12},{5,1},{6,14},{7,3},{8,0},{9,13},{1... | collective-permute-start | bytes 884744 | tf_op jit(solution)/shard_map/ppermute | solution.py:471
  63.3 1.6 %collective-permute-start.18 = (bf16[256,768]{1,0:T(8,128)(2,1)S(1)}, bf16[256,768]{1,0:T(8,128)(2,1)S(1)}, u32[]{:S(2)}, u32[]{:S(2)}) collective-permute-start(bf16[256,768]{1,0:T(8,128)(2,1)S(1)} %get-tuple-element.373.refs_0_), channel_id=1, source_target_pairs={{0,2},{1,3},{2,0},{3,1},{4,6},{5,7},{6,4},{7,5},{8,10},{9,11},{10,... | collective-permute-start | bytes 1179656 | tf_op jit(solution)/shard_map/ppermute | solution.py:455
  64.8 1.6 %collective-permute-start.19 = (bf16[2,96,768]{2,1,0:T(8,128)(2,1)S(1)}, bf16[2,96,768]{2,1,0:T(8,128)(2,1)S(1)}, u32[]{:S(2)}, u32[]{:S(2)}) collective-permute-start(bf16[2,96,768]{2,1,0:T(8,128)(2,1)S(1)} %get-tuple-element.374), channel_id=1, source_target_pairs={{0,8},{1,5},{2,10},{3,7},{4,12},{5,1},{6,14},{7,3},{8,0},{9,13},{1... | collective-permute-start | bytes 884744 | tf_op jit(solution)/shard_map/ppermute | solution.py:471
  66.4 5.1 %collective-permute-done.14.refs_0_ = bf16[2,96,768]{2,1,0:T(8,128)(2,1)S(1)} collective-permute-done((bf16[2,96,768]{2,1,0:T(8,128)(2,1)S(1)}, bf16[2,96,768]{2,1,0:T(8,128)(2,1)S(1)}, u32[]{:S(2)}, u32[]{:S(2)}) %collective-permute-start.14) | collective-permute-done | bytes 294944 | tf_op jit(solution)/shard_map/ppermute | solution.py:471
  71.6 3.8 %collective-permute-done.13.refs_0_ = bf16[4,112,768]{2,1,0:T(8,128)(2,1)S(1)} collective-permute-done((bf16[4,112,768]{2,1,0:T(8,128)(2,1)S(1)}, bf16[4,112,768]{2,1,0:T(8,128)(2,1)S(1)}, u32[]{:S(2)}, u32[]{:S(2)}) %collective-permute-start.13) | collective-permute-done | bytes 688160 | tf_op jit(solution)/shard_map/ppermute | solution.py:471
  75.5 1.5 %collective-permute-start.17 = (bf16[2,112,768]{2,1,0:T(8,128)(2,1)S(1)}, bf16[2,112,768]{2,1,0:T(8,128)(2,1)S(1)}, u32[]{:S(2)}, u32[]{:S(2)}) collective-permute-start(bf16[2,112,768]{2,1,0:T(8,128)(2,1)S(1)} %get-tuple-element.372), channel_id=1, source_target_pairs={{0,8},{1,5},{2,10},{3,7},{4,12},{5,1},{6,14},{7,3},{8,0},{9,13},{1... | collective-permute-start | bytes 1032200 | tf_op jit(solution)/shard_map/ppermute | solution.py:471
  77.3 5.5 %collective-permute-done.17.refs_0_ = bf16[2,112,768]{2,1,0:T(8,128)(2,1)S(1)} collective-permute-done((bf16[2,112,768]{2,1,0:T(8,128)(2,1)S(1)}, bf16[2,112,768]{2,1,0:T(8,128)(2,1)S(1)}, u32[]{:S(2)}, u32[]{:S(2)}) %collective-permute-start.17) | collective-permute-done | bytes 344096 | tf_op jit(solution)/shard_map/ppermute | solution.py:471
  82.8 2.5 %collective-permute-start.21 = (bf16[1,112,768]{2,1,0:T(8,128)(2,1)S(1)}, bf16[1,112,768]{2,1,0:T(8,128)(2,1)S(1)}, u32[]{:S(2)}, u32[]{:S(2)}) collective-permute-start(bf16[1,112,768]{2,1,0:T(8,128)(2,1)S(1)} %get-tuple-element.403), channel_id=1, source_target_pairs={{0,16},{1,17},{2,18},{3,19},{4,20},{5,21},{6,22},{7,23},{8,24},{9,... | collective-permute-start | bytes 516104 | tf_op jit(solution)/shard_map/ppermute | solution.py:471
  85.8 2.4 %collective-permute-start.22 = (bf16[1,96,768]{2,1,0:T(8,128)(2,1)S(1)}, bf16[1,96,768]{2,1,0:T(8,128)(2,1)S(1)}, u32[]{:S(2)}, u32[]{:S(2)}) collective-permute-start(bf16[1,96,768]{2,1,0:T(8,128)(2,1)S(1)} %get-tuple-element.404), channel_id=1, source_target_pairs={{0,16},{1,17},{2,18},{3,19},{4,20},{5,21},{6,22},{7,23},{8,24},{9,... | collective-permute-start | bytes 442376 | tf_op jit(solution)/shard_map/ppermute | solution.py:471
  90.2 11.9 %collective-permute-done.23.refs_0_ = bf16[1,96,768]{2,1,0:T(8,128)(2,1)S(1)} collective-permute-done((bf16[1,96,768]{2,1,0:T(8,128)(2,1)S(1)}, bf16[1,96,768]{2,1,0:T(8,128)(2,1)S(1)}, u32[]{:S(2)}, u32[]{:S(2)}) %collective-permute-start.23) | collective-permute-done | bytes 147488 | tf_op jit(solution)/shard_map/ppermute | solution.py:471
  (83 shorter events, 15.6 us)
Async XLA Ops:
  0.6 15.1 %collective-permute-start.2 = (bf16[768,768]{1,0:T(8,128)(2,1)}, bf16[768,768]{1,0:T(8,128)(2,1)}, u32[]{:S(2)}, u32[]{:S(2)}) collective-permute-start(bf16[768,768]{1,0:T(8,128)(2,1)} %refs_4_.3), channel_id=1, source_target_pairs={{0,1},{1,0},{2,3},{3,2},{4,5},{5,4},{6,7},{7,6},{8,9},{9,8},{10,11... | collective-permute-start | bytes 3538952 | tf_op jit(solution)/shard_map/ppermute | solution.py:451
  1.2 14.6 %collective-permute-start.3 = (bf16[768,768]{1,0:T(8,128)(2,1)}, bf16[768,768]{1,0:T(8,128)(2,1)}, u32[]{:S(2)}, u32[]{:S(2)}) collective-permute-start(bf16[768,768]{1,0:T(8,128)(2,1)} %refs_6_.1), channel_id=1, source_target_pairs={{0,1},{1,0},{2,3},{3,2},{4,5},{5,4},{6,7},{7,6},{8,9},{9,8},{10,11... | collective-permute-start | bytes 3538952 | tf_op jit(solution)/shard_map/ppermute | solution.py:451
  8.7 5.7 %copy-start.10 = (f32[768]{0:T(1024)S(1)}, f32[768]{0:T(1024)}, u32[]{:S(2)}) copy-start(f32[768]{0:T(1024)} %param.19) | copy-start | bytes 9220
  8.7 5.7 %copy-start.13 = (f32[768]{0:T(1024)S(1)}, f32[768]{0:T(1024)}, u32[]{:S(2)}) copy-start(f32[768]{0:T(1024)} %param.23) | copy-start | bytes 9220
  8.7 5.7 %copy-start.14 = (f32[768]{0:T(1024)S(1)}, f32[768]{0:T(1024)}, u32[]{:S(2)}) copy-start(f32[768]{0:T(1024)} %param.25) | copy-start | bytes 9220
  8.7 5.7 %copy-start.15 = (f32[768]{0:T(1024)S(1)}, f32[768]{0:T(1024)}, u32[]{:S(2)}) copy-start(f32[768]{0:T(1024)} %param.26) | copy-start | bytes 9220
  8.7 5.7 %copy-start.16 = (f32[768]{0:T(1024)S(1)}, f32[768]{0:T(1024)}, u32[]{:S(2)}) copy-start(f32[768]{0:T(1024)} %param.27) | copy-start | bytes 9220
  8.8 7.0 %copy-start.1 = (bf16[3,768,192]{1,2,0:T(8,128)(2,1)S(1)}, bf16[3,768,192]{1,2,0:T(8,128)(2,1)}, u32[]{:S(2)}) copy-start(bf16[3,768,192]{1,2,0:T(8,128)(2,1)} %param.16) | copy-start | bytes 2654212
  8.8 7.0 %copy-start.3 = (bf16[512,768]{1,0:T(8,128)(2,1)S(1)}, bf16[512,768]{1,0:T(8,128)(2,1)}, u32[]{:S(2)}) copy-start(bf16[512,768]{1,0:T(8,128)(2,1)} %refs_0_.4) | copy-start | bytes 2359300
  8.8 7.0 %copy-start.7 = (bf16[192,768]{1,0:T(8,128)(2,1)S(1)}, bf16[192,768]{1,0:T(8,128)(2,1)}, u32[]{:S(2)}) copy-start(bf16[192,768]{1,0:T(8,128)(2,1)} %refs_1_.3) | copy-start | bytes 884740
  8.8 1.8 %collective-permute-start = (bf16[256,768]{1,0:T(8,128)(2,1)S(1)}, bf16[256,768]{1,0:T(8,128)(2,1)S(1)}, u32[]{:S(2)}, u32[]{:S(2)}) collective-permute-start(bf16[256,768]{1,0:T(8,128)(2,1)S(1)} %get-tuple-element.217), channel_id=1, source_target_pairs={{0,1},{1,0},{2,3},{3,2},{4,5},{5,4},{6,7},{7,6},{8,9},{9,8},{10,11... | collective-permute-start | bytes 1179656 | tf_op jit(solution)/shard_map/ppermute | solution.py:451
  11.4 12.6 %collective-permute-start.1 = (bf16[256,768]{1,0:T(8,128)(2,1)}, bf16[256,768]{1,0:T(8,128)(2,1)}, u32[]{:S(2)}, u32[]{:S(2)}) collective-permute-start(bf16[256,768]{1,0:T(8,128)(2,1)} %get-tuple-element.219), channel_id=1, source_target_pairs={{0,2},{1,3},{2,0},{3,1},{4,6},{5,7},{6,4},{7,5},{8,10},{9,11},{10,... | collective-permute-start | bytes 1179656 | tf_op jit(solution)/shard_map/ppermute | solution.py:455
  14.5 1.3 %collective-permute-start.4 = (f32[8,768]{1,0:T(8,128)S(1)}, f32[8,768]{1,0:T(8,128)S(1)}, u32[]{:S(2)}, u32[]{:S(2)}) collective-permute-start(f32[8,768]{1,0:T(8,128)S(1)} %stack.32.refs_8_), channel_id=1, source_target_pairs={{0,1},{1,0},{2,3},{3,2},{4,5},{5,4},{6,7},{7,6},{8,9},{9,8},{10,11... | collective-permute-start | bytes 73736 | tf_op jit(solution)/shard_map/ppermute | solution.py:451
  27.2 10.7 %collective-permute-start.5 = (bf16[256,768]{1,0:T(8,128)(2,1)S(1)}, bf16[256,768]{1,0:T(8,128)(2,1)S(1)}, u32[]{:S(2)}, u32[]{:S(2)}) collective-permute-start(bf16[256,768]{1,0:T(8,128)(2,1)S(1)} %get-tuple-element.234), channel_id=1, source_target_pairs={{0,2},{1,3},{2,0},{3,1},{4,6},{5,7},{6,4},{7,5},{8,10},{9,11},{10,... | collective-permute-start | bytes 1179656 | tf_op jit(solution)/shard_map/ppermute | solution.py:455
  29.0 13.2 %collective-permute-start.7 = (bf16[256,1536]{1,0:T(8,128)(2,1)S(1)}, bf16[256,1536]{1,0:T(8,128)(2,1)S(1)}, u32[]{:S(2)}, u32[]{:S(2)}) collective-permute-start(bf16[256,1536]{1,0:T(8,128)(2,1)S(1)} %get-tuple-element.253), channel_id=1, source_target_pairs={{0,1},{1,0},{2,3},{3,2},{4,5},{5,4},{6,7},{7,6},{8,9},{9,8},{10,11... | collective-permute-start | bytes 2359304 | tf_op jit(solution)/shard_map/ppermute | solution.py:451
  40.5 2.4 %collective-permute-start.8 = (bf16[256,1536]{1,0:T(8,128)(2,1)S(1)}, bf16[256,1536]{1,0:T(8,128)(2,1)S(1)}, u32[]{:S(2)}, u32[]{:S(2)}) collective-permute-start(bf16[256,1536]{1,0:T(8,128)(2,1)S(1)} %get-tuple-element.254), channel_id=1, source_target_pairs={{0,1},{1,0},{2,3},{3,2},{4,5},{5,4},{6,7},{7,6},{8,9},{9,8},{10,11... | collective-permute-start | bytes 2359304 | tf_op jit(solution)/shard_map/ppermute | solution.py:451
  40.6 11.5 %collective-permute-start.6 = (bf16[256,768]{1,0:T(8,128)(2,1)S(1)}, bf16[256,768]{1,0:T(8,128)(2,1)S(1)}, u32[]{:S(2)}, u32[]{:S(2)}) collective-permute-start(bf16[256,768]{1,0:T(8,128)(2,1)S(1)} %get-tuple-element.252), channel_id=1, source_target_pairs={{0,2},{1,3},{2,0},{3,1},{4,6},{5,7},{6,4},{7,5},{8,10},{9,11},{10,... | collective-permute-start | bytes 1179656 | tf_op jit(solution)/shard_map/ppermute | solution.py:455
  42.1 10.1 %collective-permute-start.9 = (bf16[256,768]{1,0:T(8,128)(2,1)S(1)}, bf16[256,768]{1,0:T(8,128)(2,1)S(1)}, u32[]{:S(2)}, u32[]{:S(2)}) collective-permute-start(bf16[256,768]{1,0:T(8,128)(2,1)S(1)} %get-tuple-element.302.refs_17_), channel_id=1, source_target_pairs={{0,1},{1,0},{2,3},{3,2},{4,5},{5,4},{6,7},{7,6},{8,9},{9,8},{10,11... | collective-permute-start | bytes 1179656 | tf_op jit(solution)/shard_map/ppermute | solution.py:451
  43.8 9.9 %collective-permute-start.12 = (bf16[4,96,768]{2,1,0:T(8,128)(2,1)S(1)}, bf16[4,96,768]{2,1,0:T(8,128)(2,1)S(1)}, u32[]{:S(2)}, u32[]{:S(2)}) collective-permute-start(bf16[4,96,768]{2,1,0:T(8,128)(2,1)S(1)} %get-tuple-element.305), channel_id=1, source_target_pairs={{0,4},{1,9},{2,6},{3,11},{4,0},{5,13},{6,2},{7,15},{8,12},{9,1},{1... | collective-permute-start | bytes 1769480 | tf_op jit(solution)/shard_map/ppermute | solution.py:471
  46.3 14.2 %collective-permute-start.15 = (bf16[4,96,768]{2,1,0:T(8,128)(2,1)S(1)}, bf16[4,96,768]{2,1,0:T(8,128)(2,1)S(1)}, u32[]{:S(2)}, u32[]{:S(2)}) collective-permute-start(bf16[4,96,768]{2,1,0:T(8,128)(2,1)S(1)} %get-tuple-element.337), channel_id=1, source_target_pairs={{0,4},{1,9},{2,6},{3,11},{4,0},{5,13},{6,2},{7,15},{8,12},{9,1},{1... | collective-permute-start | bytes 1769480 | tf_op jit(solution)/shard_map/ppermute | solution.py:471
  52.8 1.8 %collective-permute-start.10 = (bf16[256,768]{1,0:T(8,128)(2,1)S(1)}, bf16[256,768]{1,0:T(8,128)(2,1)S(1)}, u32[]{:S(2)}, u32[]{:S(2)}) collective-permute-start(bf16[256,768]{1,0:T(8,128)(2,1)S(1)} %get-tuple-element.303.refs_1_), channel_id=1, source_target_pairs={{0,1},{1,0},{2,3},{3,2},{4,5},{5,4},{6,7},{7,6},{8,9},{9,8},{10,11... | collective-permute-start | bytes 1179656 | tf_op jit(solution)/shard_map/ppermute | solution.py:451
  52.9 1.7 %collective-permute-start.11 = (f32[8,768]{1,0:T(8,128)S(1)}, f32[8,768]{1,0:T(8,128)S(1)}, u32[]{:S(2)}, u32[]{:S(2)}) collective-permute-start(f32[8,768]{1,0:T(8,128)S(1)} %get-tuple-element.304.refs_3_), channel_id=1, source_target_pairs={{0,1},{1,0},{2,3},{3,2},{4,5},{5,4},{6,7},{7,6},{8,9},{9,8},{10,11... | collective-permute-start | bytes 73736 | tf_op jit(solution)/shard_map/ppermute | solution.py:451
  59.0 16.4 %collective-permute-start.13 = (bf16[4,112,768]{2,1,0:T(8,128)(2,1)S(1)}, bf16[4,112,768]{2,1,0:T(8,128)(2,1)S(1)}, u32[]{:S(2)}, u32[]{:S(2)}) collective-permute-start(bf16[4,112,768]{2,1,0:T(8,128)(2,1)S(1)} %get-tuple-element.332), channel_id=1, source_target_pairs={{0,4},{1,9},{2,6},{3,11},{4,0},{5,13},{6,2},{7,15},{8,12},{9,1},{1... | collective-permute-start | bytes 2064392 | tf_op jit(solution)/shard_map/ppermute | solution.py:471
  61.4 1.8 %collective-permute-start.16 = (bf16[256,768]{1,0:T(8,128)(2,1)S(1)}, bf16[256,768]{1,0:T(8,128)(2,1)S(1)}, u32[]{:S(2)}, u32[]{:S(2)}) collective-permute-start(bf16[256,768]{1,0:T(8,128)(2,1)S(1)} %get-tuple-element.353), channel_id=1, source_target_pairs={{0,1},{1,0},{2,3},{3,2},{4,5},{5,4},{6,7},{7,6},{8,9},{9,8},{10,11... | collective-permute-start | bytes 1179656 | tf_op jit(solution)/shard_map/ppermute | solution.py:451
  61.5 10.0 %collective-permute-start.14 = (bf16[2,96,768]{2,1,0:T(8,128)(2,1)S(1)}, bf16[2,96,768]{2,1,0:T(8,128)(2,1)S(1)}, u32[]{:S(2)}, u32[]{:S(2)}) collective-permute-start(bf16[2,96,768]{2,1,0:T(8,128)(2,1)S(1)} %get-tuple-element.333), channel_id=1, source_target_pairs={{0,8},{1,5},{2,10},{3,7},{4,12},{5,1},{6,14},{7,3},{8,0},{9,13},{1... | collective-permute-start | bytes 884744 | tf_op jit(solution)/shard_map/ppermute | solution.py:471
  63.3 13.8 %collective-permute-start.18 = (bf16[256,768]{1,0:T(8,128)(2,1)S(1)}, bf16[256,768]{1,0:T(8,128)(2,1)S(1)}, u32[]{:S(2)}, u32[]{:S(2)}) collective-permute-start(bf16[256,768]{1,0:T(8,128)(2,1)S(1)} %get-tuple-element.373.refs_0_), channel_id=1, source_target_pairs={{0,2},{1,3},{2,0},{3,1},{4,6},{5,7},{6,4},{7,5},{8,10},{9,11},{10,... | collective-permute-start | bytes 1179656 | tf_op jit(solution)/shard_map/ppermute | solution.py:455
  64.8 12.1 %collective-permute-start.19 = (bf16[2,96,768]{2,1,0:T(8,128)(2,1)S(1)}, bf16[2,96,768]{2,1,0:T(8,128)(2,1)S(1)}, u32[]{:S(2)}, u32[]{:S(2)}) collective-permute-start(bf16[2,96,768]{2,1,0:T(8,128)(2,1)S(1)} %get-tuple-element.374), channel_id=1, source_target_pairs={{0,8},{1,5},{2,10},{3,7},{4,12},{5,1},{6,14},{7,3},{8,0},{9,13},{1... | collective-permute-start | bytes 884744 | tf_op jit(solution)/shard_map/ppermute | solution.py:471
  75.5 7.3 %collective-permute-start.17 = (bf16[2,112,768]{2,1,0:T(8,128)(2,1)S(1)}, bf16[2,112,768]{2,1,0:T(8,128)(2,1)S(1)}, u32[]{:S(2)}, u32[]{:S(2)}) collective-permute-start(bf16[2,112,768]{2,1,0:T(8,128)(2,1)S(1)} %get-tuple-element.372), channel_id=1, source_target_pairs={{0,8},{1,5},{2,10},{3,7},{4,12},{5,1},{6,14},{7,3},{8,0},{9,13},{1... | collective-permute-start | bytes 1032200 | tf_op jit(solution)/shard_map/ppermute | solution.py:471
  77.2 12.0 %collective-permute-start.20 = (bf16[256,768]{1,0:T(8,128)(2,1)S(1)}, bf16[256,768]{1,0:T(8,128)(2,1)S(1)}, u32[]{:S(2)}, u32[]{:S(2)}) collective-permute-start(bf16[256,768]{1,0:T(8,128)(2,1)S(1)} %get-tuple-element.398.refs_0_), channel_id=1, source_target_pairs={{0,1},{1,0},{2,3},{3,2},{4,5},{5,4},{6,7},{7,6},{8,9},{9,8},{10,11... | collective-permute-start | bytes 1179656 | tf_op jit(solution)/shard_map/ppermute | solution.py:451
  82.8 21.7 %collective-permute-start.21 = (bf16[1,112,768]{2,1,0:T(8,128)(2,1)S(1)}, bf16[1,112,768]{2,1,0:T(8,128)(2,1)S(1)}, u32[]{:S(2)}, u32[]{:S(2)}) collective-permute-start(bf16[1,112,768]{2,1,0:T(8,128)(2,1)S(1)} %get-tuple-element.403), channel_id=1, source_target_pairs={{0,16},{1,17},{2,18},{3,19},{4,20},{5,21},{6,22},{7,23},{8,24},{9,... | collective-permute-start | bytes 516104 | tf_op jit(solution)/shard_map/ppermute | solution.py:471
  85.3 16.7 %collective-permute-start.23 = (bf16[1,96,768]{2,1,0:T(8,128)(2,1)S(1)}, bf16[1,96,768]{2,1,0:T(8,128)(2,1)S(1)}, u32[]{:S(2)}, u32[]{:S(2)}) collective-permute-start(bf16[1,96,768]{2,1,0:T(8,128)(2,1)S(1)} %get-tuple-element.405), channel_id=1, source_target_pairs={{0,16},{1,17},{2,18},{3,19},{4,20},{5,21},{6,22},{7,23},{8,24},{9,... | collective-permute-start | bytes 442376 | tf_op jit(solution)/shard_map/ppermute | solution.py:471
  85.8 17.9 %collective-permute-start.22 = (bf16[1,96,768]{2,1,0:T(8,128)(2,1)S(1)}, bf16[1,96,768]{2,1,0:T(8,128)(2,1)S(1)}, u32[]{:S(2)}, u32[]{:S(2)}) collective-permute-start(bf16[1,96,768]{2,1,0:T(8,128)(2,1)S(1)} %get-tuple-element.404), channel_id=1, source_target_pairs={{0,16},{1,17},{2,18},{3,19},{4,20},{5,21},{6,22},{7,23},{8,24},{9,... | collective-permute-start | bytes 442376 | tf_op jit(solution)/shard_map/ppermute | solution.py:471
  (9 other events, 18.9 us)

commit v4 on v3

--- a/solution.py
+++ b/solution.py
@@ -11,7 +11,10 @@
 HEAD_DIM = 64
 NORM_EPSILON = 1e-05
 CORES = 2
-CHUNKS = 1
+CHUNKS = 2
+DOWN_PARTS = 2
+UP_PARTS = 1
+PIECES = 2
 F32 = jnp.float32
 LOW = jnp.bfloat16
 MIB = 1 << 20
@@ -46,6 +49,45 @@
     return inverse * (grad_norm - mean_grad - normed * mean_proj)
 
 
+(
+    H_ACT,
+    H_ACT_PASS,
+    H_ATTN,
+    H_ATTN_KEEP,
+    H_BACK,
+    H_COTANGENT,
+    H_DOWN_KEEP,
+    H_DOWN_OTHER,
+    H_DOWN_OWN,
+    H_FWD_OTHER,
+    H_GRAD,
+    H_HID,
+    H_INVERSE,
+    H_LAST,
+    H_MLP,
+    H_NEXT,
+    H_NORMED,
+    H_OUT_HALF,
+    H_OUT_OTHER,
+    H_PACKED,
+    H_PACKED_OTHER,
+    H_PRE,
+    H_PRE_PASS,
+    H_RESID,
+    H_SAVED,
+    H_SLOPES,
+    H_SUM_DOWN,
+    H_SUM_UP,
+    H_SUMS,
+    H_TOKENS,
+    H_UP_KEEP,
+    H_UP_OTHER,
+    H_UP_OWN,
+    H_W_OUT,
+    H_W_QKV,
+) = range(35)
+
+
 class State:
     def __init__(self):
         self.arrays = {}
@@ -56,8 +98,8 @@
 
     def call(self, kernel, outs, *inputs, mib=16, scratch=(), loose=False):
         names = list(self.arrays)
-        direct = [item for item in inputs if not isinstance(item, str)]
-        read = {item for item in inputs if isinstance(item, str)}
+        direct = [item for item in inputs if not isinstance(item, tuple)]
+        read = {item for item in inputs if isinstance(item, tuple)}
         vmem = pl.BlockSpec(memory_space=pltpu.VMEM)
         anywhere = pl.BlockSpec(memory_space=pl.ANY)
         scalar = pl.BlockSpec(memory_space=pltpu.SMEM)
@@ -72,12 +114,12 @@
             held, refs = dict(zip(names, refs)), refs[len(names) :]
             results, refs = refs[: len(outs)], refs[len(outs) :]
             rest = refs[len(names) :]
-            ins = [held[item] if isinstance(item, str) else arrays.pop(0) for item in inputs]
+            ins = [held[item] if isinstance(item, tuple) else arrays.pop(0) for item in inputs]
             kernel(*ins, *results, *rest)
 
         results = pl.pallas_call(
             body,
-            name=getattr(kernel, "__name__", None) or kernel.func.__name__,
+            name=getattr(kernel, "func", kernel).__name__,
             out_shape=tuple(out_shapes + held_shapes),
             in_specs=[
                 anywhere if loose else scalar if array.dtype == jnp.int32 else vmem
@@ -167,8 +209,12 @@
         copy.wait()
 
 
-def add_rows(kept, received, out):
-    out[...] = (kept[...] + received[...].astype(F32)).astype(LOW)
+def add_rows(kept, *refs):
+    received, out = refs[:-1], refs[-1]
+    rows = received[0].shape[0]
+    for index, part in enumerate(received):
+        picked = slice(index * rows, (index + 1) * rows)
+        out[picked, :] = (kept[picked, :] + part[...].astype(F32)).astype(LOW)
 
 
 def final_rows(*refs):
@@ -196,11 +242,10 @@
 
 
 def mlp_forward(
-    index, received, tokens, own, packed, packed_other, up_own, up_other, down_own, down_other,
-    part_o, pass_o, kept_o, hidden_o, act_o, slopes_o, normed_o, inverse_o,
+    index, received, tokens, own, packed, packed_other, up_own, up_other, down_own, down_other, *refs
 ):
+    part_o, hidden_pass_o, act_pass_o, kept_o, hidden_o, act_o, slopes_o, normed_o, inverse_o = refs
     rows, width = part_o.shape
-    units = up_own.shape[1]
     start = pl.multiple_of((my_core() * CHUNKS + index) * rows, rows)
     resid = tokens[pl.ds(start, rows), :].astype(F32) + row(packed, BIAS_OUT)
     resid = resid + (own[...].astype(F32) + received[...].astype(F32))
@@ -208,8 +253,8 @@
     normed_o[...] = normed
     inverse_o[...] = inverse
     hidden_low = (normed * row(packed, GAIN_ONE) + row(packed, SHIFT_ONE)).astype(LOW)
-    pass_o[:, :width] = hidden_low
     hidden_o[...] = hidden_low
+    hidden_pass_o[...] = hidden_low
 
     def units_of(up, vectors, side):
         pre = nn(hidden_low, up[...]) + row(vectors, BIAS_UP)
@@ -220,7 +265,7 @@
     act_own = units_of(up_own, packed, 0)
     act_o[...] = act_own
     act_other = units_of(up_other, packed_other, 1)
-    pass_o[:, width : width + units] = act_other
+    act_pass_o[...] = act_other
     part = (nn(act_own, down_own[...]) + nn(act_other, down_other[...])).astype(LOW)
     part_o[...] = part
     kept_o[...] = part
@@ -228,34 +273,39 @@
 
 def mlp_backward(
     index, lengths, received, normed_one, own, packed, cotangent, down_own, down_other, slopes,
-    up_own, up_other,
-    part_o, pass_o, kept_o, grad_o, pre_o, resid_o, out_o, sums_o,
+    up_own, up_other, *refs
 ):
-    rows, width = part_o.shape
-    units = up_own.shape[1]
+    before, refs = refs[: 4 * index], refs[4 * index :]
+    kept_o, grad_o, pre_o, pre_pass_o, out_o, resid_o, sums_o = refs[:7]
+    rows, width = kept_o.shape
     length = lengths[0]
     start = pl.multiple_of((my_core() * CHUNKS + index) * rows, rows)
     hidden = normed_one[...] * row(packed, GAIN_ONE) + row(packed, SHIFT_ONE)
     branch = own[...].astype(F32) + received[...].astype(F32) + row(packed, BIAS_DOWN)
     normed, inverse = normalize(hidden + branch)
     valid = lax.broadcasted_iota(jnp.int32, (rows, width), 0) + start < length
-    out = jnp.where(valid, normed * row(packed, GAIN_TWO) + row(packed, SHIFT_TWO), 0.0)
-    out_o[...] = out.astype(LOW)
+    out = jnp.where(valid, normed * row(packed, GAIN_TWO) + row(packed, SHIFT_TWO), 0.0).astype(LOW)
+    out_o[...] = out
     grad_out = jnp.where(valid, cotangent[pl.ds(start, rows), :].astype(F32), 0.0)
     sums_o[0:1, :] = jnp.sum(grad_out * normed, 0, keepdims=True)
     sums_o[1:2, :] = jnp.sum(grad_out, 0, keepdims=True)
     grad_resid = norm_back(grad_out * row(packed, GAIN_TWO), normed, inverse)
     resid_o[...] = grad_resid
     grad_mlp = grad_resid.astype(LOW)
-    pass_o[:, :width] = grad_mlp
     grad_o[...] = grad_mlp
     pre_own = (nt(grad_mlp, down_own[...]) * slopes[0]).astype(LOW)
     pre_o[...] = pre_own
     pre_other = (nt(grad_mlp, down_other[...]) * slopes[1]).astype(LOW)
-    pass_o[:, width : width + units] = pre_other
+    pre_pass_o[...] = pre_other
     part = (nt(pre_own, up_own[...]) + nt(pre_other, up_other[...])).astype(LOW)
-    part_o[...] = part
     kept_o[...] = part
+    if len(refs) > 7:
+        sends = refs[7:]
+        for send, last in zip(sends, (part, grad_mlp, pre_other, out)):
+            send[index * rows :, :] = last
+        for piece in range(index):
+            for send, early in zip(sends, before[4 * piece : 4 * piece + 4]):
+                send[piece * rows : (piece + 1) * rows, :] = early[...]
 
 
 def spread(blocks, grad):
@@ -275,42 +325,45 @@
     return jnp.where(my_core() == 0, patterns[0], patterns[1]) ^ lax.axis_index("dp")
 
 
-def weight_grad(take, *refs):
-    pieces, (send_o, keep_o, sum_o, left, right, blocks) = refs[:-6], refs[-6:]
-    model = left.shape[1]
-    rows = pieces[0].shape[0]
-    half = len(pieces) // 2
-    for target, sources, columns in (
-        (left, pieces[:half], take[:half]), (right, pieces[half:], take[half:])
-    ):
-        for index, (source, column) in enumerate(zip(sources, columns)):
-            picked = slice(column * model, (column + 1) * model)
-            target[index * rows : (index + 1) * rows, :] = source[:, picked]
+def weight_grad(left_count, right_count, *refs):
+    left_pieces, refs = refs[:left_count], refs[left_count:]
+    right_pieces, refs = refs[:right_count], refs[right_count:]
+    *sends, keep_o, sum_o, left, right, blocks = refs
+    for target, sources in ((left, left_pieces), (right, right_pieces)):
+        at = 0
+        for source in sources:
+            rows = source.shape[0]
+            target[at : at + rows, :] = source[...]
+            at += rows
     spread(blocks, tn(left[...], right[...]))
     summed = left if sum_o.shape[0] == 1 else right
     sum_o[0:1, :] = jnp.sum(summed[...].astype(F32), 0, keepdims=True)
     count = keep_o.shape[0]
-    for index in range(count):
-        send_o[index] = blocks[block_of(2 * count, index + count)].astype(LOW)
+    each = sends[0].shape[0]
+    for index in range(count):
+        sent = blocks[block_of(2 * count, index + count)].astype(LOW)
+        sends[index // each][index % each] = sent
     for index in range(count):
         keep_o[index] = blocks[block_of(2 * count, index)]
 
 
-def norm_one_back(
-    received, own, resid_two, normed, inverse, packed, sums_two, sums_before,
-    low_o, sums_o, resid_o,
-):
-    grad_hidden = resid_two[...] + (own[...].astype(F32) + received[...].astype(F32))
-    xhat = normed[...]
-    grad_resid = norm_back(grad_hidden * row(packed, GAIN_ONE), xhat, inverse[...])
-    resid_o[...] = grad_resid
-    low = grad_resid.astype(LOW)
-    low_o[...] = low
-    sums_o[...] = sums_before[...]
-    sums_o[0:2, :] += sums_two[...]
-    sums_o[2:3, :] += jnp.sum(grad_hidden * xhat, 0, keepdims=True)
-    sums_o[3:4, :] += jnp.sum(grad_hidden, 0, keepdims=True)
-    sums_o[4:5, :] += jnp.sum(low.astype(F32), 0, keepdims=True)
+def norm_one_back(received, packed, *refs):
+    pieces, (low_o, sums_o, resid_o) = refs[:-3], refs[-3:]
+    rows = pieces[0].shape[0]
+    sums_o[...] = jnp.zeros(sums_o.shape, F32)
+    for index in range(CHUNKS):
+        own, resid_two, normed, inverse, sums_two = pieces[5 * index : 5 * index + 5]
+        picked = slice(index * rows, (index + 1) * rows)
+        grad_hidden = resid_two[...] + (own[...].astype(F32) + received[picked, :].astype(F32))
+        xhat = normed[...]
+        grad_resid = norm_back(grad_hidden * row(packed, GAIN_ONE), xhat, inverse[...])
+        resid_o[picked, :] = grad_resid
+        low = grad_resid.astype(LOW)
+        low_o[picked, :] = low
+        sums_o[0:2, :] += sums_two[...]
+        sums_o[2:3, :] += jnp.sum(grad_hidden * xhat, 0, keepdims=True)
+        sums_o[3:4, :] += jnp.sum(grad_hidden, 0, keepdims=True)
+        sums_o[4:5, :] += jnp.sum(low.astype(F32), 0, keepdims=True)
 
 
 def split_pair(vectors):
@@ -321,7 +374,7 @@
 def attn_backward(
     lengths, *refs,
 ):
-    pieces, refs = refs[: 2 * CHUNKS], refs[2 * CHUNKS :]
+    pieces, refs = refs[:2], refs[2:]
     sums_own, sums_other, w_out, saved, tokens, sum_down, sum_up = refs[:7]
     send_o, keep_o, gq_o, gk_o, gv_o, grad_attn, blocks, sums = refs[7:]
     length = lengths[0]
@@ -380,8 +433,9 @@
         keep_o[index, block + VECTOR_ROWS :] = jnp.zeros_like(vector_sums)
 
 
-def token_back(gq, gk, gv, w_qkv, send_o, keep_o):
-    half = send_o.shape[0]
+def token_back(gq, gk, gv, w_qkv, *outs):
+    sends, keep_o = outs[:-1], outs[-1]
+    half, rows = keep_o.shape[0], sends[0].shape[0]
     core = my_core()
 
     def rows_from(start):
@@ -390,49 +444,77 @@
             nn(gq[picked, :], w_qkv[0]) + nn(gk[picked, :], w_qkv[1]) + nn(gv[picked, :], w_qkv[2])
         )
 
-    send_o[...] = rows_from((1 - core) * half).astype(LOW)
+    other = rows_from((1 - core) * half).astype(LOW)
+    for index, send_o in enumerate(sends):
+        send_o[...] = other[index * rows : (index + 1) * rows, :]
     keep_o[...] = rows_from(core * half)
 
 
-def merge_weights(keep, received, send_o, keep_o):
+def merge_weights(keep, *refs):
+    parts, (send_o, keep_o) = refs[:-2], refs[-2:]
     count = keep_o.shape[0]
-    for index in range(count):
-        send_o[index] = (keep[count + index] + received[count + index].astype(F32)).astype(LOW)
-    for index in range(count):
-        keep_o[index] = keep[index] + received[index].astype(F32)
+    each = parts[0].shape[0]
+
+    def total(index):
+        return keep[index] + parts[index // each][index % each].astype(F32)
+
+    for index in range(count):
+        send_o[index] = total(count + index).astype(LOW)
+    for index in range(count):
+        keep_o[index] = total(index)
 
 
 def merge_last_weights(keep, received, out):
     out[...] = keep[0] + received[0].astype(F32)
 
 
-def merged_vectors(keep, received, index, block):
-    high = received[index, block : block + VECTOR_ROWS].astype(F32)
-    low = received[index, block + VECTOR_ROWS :].astype(F32)
+def merged_vectors(keep, received, index, at, block):
+    high = received[at, block : block + VECTOR_ROWS].astype(F32)
+    low = received[at, block + VECTOR_ROWS :].astype(F32)
     return keep[index, block : block + VECTOR_ROWS] + high + low
 
 
-def merge_attn(keep, received, send_o, keep_o):
+def merge_attn(part_count, keep, *refs):
+    parts, (*sends, keep_o) = refs[:part_count], refs[part_count:]
     count = keep_o.shape[0]
     block = keep_o.shape[1] - PAIR_ROWS
-    for index in range(count):
-        at = count + index
-        send_o[index, :block] = (keep[at, :block] + received[at, :block].astype(F32)).astype(LOW)
-        send_o[index, block:] = split_pair(merged_vectors(keep, received, at, block))
-    for index in range(count):
-        keep_o[index, :block] = keep[index, :block] + received[index, :block].astype(F32)
-        vectors = merged_vectors(keep, received, index, block)
+    each = parts[0].shape[0]
+
+    def weights_at(index):
+        part = parts[index // each]
+        return keep[index, :block] + part[index % each, :block].astype(F32)
+
+    def vectors_at(index):
+        return merged_vectors(keep, parts[index // each], index, index % each, block)
+
+    for index in range(count):
+        sent = weights_at(count + index).astype(LOW)
+        if len(sends) == 1:
+            sends[0][index, :block] = sent
+            sends[0][index, block:] = split_pair(vectors_at(count + index))
+        else:
+            first = sends[0].shape[1]
+            sends[0][index] = sent[:first]
+            sends[1][index, : block - first] = sent[first:]
+            sends[1][index, block - first :] = split_pair(vectors_at(count + index))
+    for index in range(count):
+        keep_o[index, :block] = weights_at(index)
+        vectors = vectors_at(index)
         keep_o[index, block : block + VECTOR_ROWS] = vectors
         keep_o[index, block + VECTOR_ROWS :] = jnp.zeros_like(vectors)
 
 
-def merge_last_attn(keep, received, qkv_o, out_o, vectors_o, pair_o):
+def merge_last_attn(keep, first, second, qkv_o, out_o, vectors_o, pair_o):
     block, width = qkv_o.shape[1], qkv_o.shape[2]
-    total = keep[0, :block] + received[0, :block].astype(F32)
+    rows = first.shape[1]
+    received = jnp.concatenate([first[0].astype(F32), second[0, : block - rows].astype(F32)], 0)
+    total = keep[0, :block] + received
     for part in range(3):
         qkv_o[part] = total[:, part * width : (part + 1) * width]
     out_o[...] = total[:, 3 * width :].T
-    vectors = merged_vectors(keep, received, 0, block)
+    high = second[0, block - rows : block - rows + VECTOR_ROWS].astype(F32)
+    low = second[0, block - rows + VECTOR_ROWS :].astype(F32)
+    vectors = keep[0, block : block + VECTOR_ROWS] + high + low
     model = vectors.shape[1]
     me = lax.axis_index("dp")
     vectors_o[...] = pltpu.roll(vectors, lax.rem(model - me * block, model), 1)[:, :block]
@@ -441,6 +523,14 @@
     last = VECTOR_ROWS - 1
     pair_o[0:1, :] = turned[last : last + 1, :small]
     pair_o[1:2, :] = turned[last : last + 1, 2 * width : 2 * width + small]
+
+
+def run_parts(plan, *refs):
+    refs = list(refs)
+    ins, outs = refs[: sum(part[1] for part in plan)], refs[sum(part[1] for part in plan) :]
+    for kernel, taken, given in plan:
+        kernel(*ins[:taken], *outs[:given])
+        ins, outs = ins[taken:], outs[given:]
 
 
 CORE_PAIRS = [(i, i ^ 1) for i in range(4)]
@@ -509,20 +599,20 @@
     state = State()
     attn_send, attn_keep = state.call(
         attn_forward,
-        [((4, rows, width), LOW, "saved"), ((half, model), LOW), ((half, model), F32)],
+        [((4, rows, width), LOW, (H_SAVED,)), ((half, model), LOW), ((half, model), F32)],
         lengths, tokens, w_turned, bias_qv, w_out,
         mib=20,
     )
     attn_parts = state.call(
         add_chunks,
-        [((chunk, model), LOW)] * CHUNKS + [((chunk, model), LOW, f"attn{c}") for c in chunks],
+        [((chunk, model), LOW)] * CHUNKS + [((chunk, model), LOW, (H_ATTN, c)) for c in chunks],
         attn_keep, to_core(attn_send),
     )
     received = [to_chip(part) for part in attn_parts]
     held = {
-        "tokens": tokens, "w_out": w_out, "w_qkv": w_turned, "cotangent": cotangent,
-        "up_own": w_up, "up_other": up_other, "down_own": w_down, "down_other": down_other,
-        "packed": packed, "packed_other": packed_other,
+        (H_TOKENS,): tokens, (H_W_OUT,): w_out, (H_W_QKV,): w_turned, (H_COTANGENT,): cotangent,
+        (H_UP_OWN,): w_up, (H_UP_OTHER,): up_other, (H_DOWN_OWN,): w_down, (H_DOWN_OTHER,): down_other,
+        (H_PACKED,): packed, (H_PACKED_OTHER,): packed_other,
     }
     state.call(
         hold,
@@ -531,111 +621,154 @@
         scratch=[pltpu.SemaphoreType.DMA((len(held),))], loose=True,
     )
 
-    passed, fwd_other = [], []
+    last = CHUNKS - 1
+    passed, hidden_other, act_other = [], [], []
     for c in chunks:
-        part, fwd = state.call(
+        part, hidden_pass, act_pass = state.call(
             partial(mlp_forward, c),
-            [
-                ((chunk, model), LOW), ((chunk, model + units), LOW),
-                ((chunk, model), LOW, f"mlp{c}"), ((chunk, model), LOW, f"hid{c}"),
-                ((chunk, units), LOW, f"act{c}"), ((2, chunk, units), F32, f"slopes{c}"),
-                ((chunk, model), F32, f"normed{c}"), ((chunk, 1), F32, f"inverse{c}"),
+            [((chunk, model), LOW)] * 2
+            + [
+                ((chunk, units), LOW), ((chunk, model), LOW, (H_MLP, c)),
+                ((chunk, model), LOW, (H_HID, c)), ((chunk, units), LOW, (H_ACT, c)),
+                ((2, chunk, units), F32, (H_SLOPES, c)),
+                ((chunk, model), F32, (H_NORMED, c)), ((chunk, 1), F32, (H_INVERSE, c)),
             ],
-            received[c], "tokens", f"attn{c}", "packed", "packed_other",
-            "up_own", "up_other", "down_own", "down_other",
+            received[c], (H_TOKENS,), (H_ATTN, c), (H_PACKED,), (H_PACKED_OTHER,),
+            (H_UP_OWN,), (H_UP_OTHER,), (H_DOWN_OWN,), (H_DOWN_OTHER,),
         )
-        state.drop(f"attn{c}")
+        state.drop((H_ATTN, c))
         passed.append(to_chip(part))
-        fwd_other.append(to_core(fwd))
+        hidden_other.append(to_core(hidden_pass))
+        act_other.append(to_core(act_pass))
     received = passed
 
-    passed, bwd_other, out_half = [], [], []
     for c in chunks:
-        part, bwd, out_c = state.call(
+        sends = state.call(
             partial(mlp_backward, c),
             [
-                ((chunk, model), LOW), ((chunk, model + units), LOW),
-                ((chunk, model), LOW, f"back{c}"), ((chunk, model), LOW, f"grad{c}"),
-                ((chunk, units), LOW, f"pre{c}"), ((chunk, model), F32, f"resid{c}"),
-                ((chunk, model), LOW), ((2, model), F32, f"sums{c}"),
+                ((chunk, model), LOW, (H_BACK, c)), ((chunk, model), LOW, (H_GRAD, c)),
+                ((chunk, units), LOW, (H_PRE, c)), ((chunk, units), LOW, (H_PRE_PASS, c)),
+                ((chunk, model), LOW, (H_OUT_HALF, c)), ((chunk, model), F32, (H_RESID, c)),
+                ((2, model), F32, (H_SUMS, c)),
+            ]
+            + [((half, model), LOW)] * (4 * (c == last)),
+            lengths, received[c], (H_NORMED, c), (H_MLP, c), (H_PACKED,), (H_COTANGENT,),
+            (H_DOWN_OWN,), (H_DOWN_OTHER,), (H_SLOPES, c), (H_UP_OWN,), (H_UP_OTHER,),
+            *[
+                (name, early)
+                for early in range(c)
+                for name in (H_BACK, H_GRAD, H_PRE_PASS, H_OUT_HALF)
             ],
-            lengths, received[c], f"normed{c}", f"mlp{c}", "packed", "cotangent",
-            "down_own", "down_other", f"slopes{c}", "up_own", "up_other",
         )
-        state.drop(f"mlp{c}", f"slopes{c}")
-        passed.append(to_chip(part))
-        bwd_other.append(to_core(bwd))
-        out_half.append(out_c)
-    state.drop("cotangent", "up_own", "up_other", "down_own", "down_other")
-    received = passed
-    out_other = [to_core(part) for part in out_half]
+        state.drop((H_MLP, c), (H_SLOPES, c))
+    for c in chunks:
+        state.drop((H_PRE_PASS, c), (H_OUT_HALF, c))
+    state.drop((H_COTANGENT,), (H_UP_OWN,), (H_UP_OTHER,), (H_DOWN_OWN,), (H_DOWN_OTHER,))
+    back_part, grad_pass, pre_pass, out_half = sends
+    received = to_chip(back_part)
+    grad_other, pre_other = to_core(grad_pass), to_core(pre_pass)
+    out_other = to_core(out_half)
 
     scratch = [pltpu.VMEM((rows, model), LOW)] * 2 + [pltpu.VMEM((dp_size, block, units), F32)]
     grad_shape = (count, block, units)
-    pairs = [0, 0] * CHUNKS
-
-    def both(own, other):
-        return [piece for c in chunks for piece in (f"{own}{c}", other[c])]
-
-    (down_send,) = state.call(
-        partial(weight_grad, pairs + [0, 1] * CHUNKS),
-        [(grad_shape, LOW), (grad_shape, F32, "down_keep"), ((1, model), F32, "sum_down")],
-        *both("grad", bwd_other),
-        *[piece for c in chunks for piece in (f"act{c}", fwd_other[c])],
-        scratch=scratch, mib=20,
-    )
-    down_got = to_dp(down_send, 0, dp_size, tensor_size)
-    (up_send,) = state.call(
-        partial(weight_grad, pairs + [0, 1] * CHUNKS),
-        [(grad_shape, LOW), (grad_shape, F32, "up_keep"), ((2, units), F32, "sum_up")],
-        *both("hid", fwd_other),
-        *[piece for c in chunks for piece in (f"pre{c}", bwd_other[c])],
-        scratch=scratch, mib=20,
-    )
-    up_got = to_dp(up_send, 0, dp_size, tensor_size)
+
+    def weight_parts(parts, keep, sum_shape, sum_name, left, right):
+        sent = state.call(
+            partial(weight_grad, len(left), len(right)),
+            [((count // parts, block, units), LOW)] * parts
+            + [(grad_shape, F32, (keep,)), (sum_shape, F32, (sum_name,))],
+            *left, *right,
+            scratch=scratch, mib=20,
+        )
+        return [to_dp(part, 0, dp_size, tensor_size) for part in sent]
+
+    def held_chunks(name):
+        return [(name, c) for c in chunks]
+
+    down_got = weight_parts(
+        DOWN_PARTS, H_DOWN_KEEP, (1, model), H_SUM_DOWN,
+        held_chunks(H_GRAD) + [grad_other], held_chunks(H_ACT) + act_other,
+    )
+    up_got = weight_parts(
+        UP_PARTS, H_UP_KEEP, (2, units), H_SUM_UP,
+        held_chunks(H_HID) + hidden_other, held_chunks(H_PRE) + [pre_other],
+    )
     for c in chunks:
-        state.drop(f"hid{c}", f"act{c}", f"grad{c}", f"pre{c}")
+        state.drop((H_HID, c), (H_ACT, c), (H_GRAD, c), (H_PRE, c))
+    state.arrays[(H_OUT_HALF,)] = out_half
+    state.arrays[(H_OUT_OTHER,)] = out_other
+
+    grad_attn, sums = state.call(
+        norm_one_back,
+        [((half, model), LOW), ((VECTOR_ROWS, model), F32), ((half, model), F32, (H_LAST,))],
+        received, (H_PACKED,),
+        *[
+            (name, c) for c in chunks for name in (H_BACK, H_RESID, H_NORMED, H_INVERSE, H_SUMS)
+        ],
+    )
     for c in chunks:
-        state.arrays[f"out_half{c}"] = out_half[c]
-        state.arrays[f"out_other{c}"] = out_other[c]
-
-    sums = jnp.zeros((VECTOR_ROWS, model), F32)
-    grad_attn, grad_attn_other = [], []
-    for c in chunks:
-        low, sums = state.call(
-            norm_one_back,
-            [((chunk, model), LOW), ((VECTOR_ROWS, model), F32), ((chunk, model), F32, f"last{c}")],
-            received[c], f"back{c}", f"resid{c}", f"normed{c}", f"inverse{c}", "packed", f"sums{c}",
-            sums,
-        )
-        state.drop(f"back{c}", f"resid{c}", f"normed{c}", f"inverse{c}", f"sums{c}")
-        grad_attn.append(low)
-        grad_attn_other.append(to_core(low))
+        state.drop((H_BACK, c), (H_RESID, c), (H_NORMED, c), (H_INVERSE, c), (H_SUMS, c))
+    grad_attn_other = to_core(grad_attn)
     sums_other = to_core(sums)
 
-    def merge(name, got, step):
-        kept = dp_size >> (step + 1)
-        shape = state.arrays[name].shape[1:]
-        kernel = merge_attn if name == "attn_keep" else merge_weights
-        (send,) = state.call(
-            kernel, [((kept,) + shape, LOW), ((kept,) + shape, F32, "next")], name, got
-        )
-        state.drop(name)
-        state.arrays[name] = state.arrays.pop("next")
-        return to_dp(send, step, dp_size, tensor_size)
-
-    if steps > 1:
-        down_got = merge("down_keep", down_got, 1)
+    running = {(H_DOWN_KEEP,): (down_got, 1), (H_UP_KEEP,): (up_got, 1)}
+    finished = {}
+
+    def advance(*names):
+        plan, outs, inputs, ends = [], [], [], []
+        for name in names:
+            got, step = running[name]
+            attn = name == (H_ATTN_KEEP,)
+            shape = state.arrays[name].shape[1:]
+            inputs += [name, *got]
+            if step < steps:
+                kept = (dp_size >> (step + 1),) + shape
+                sends = [(kept, LOW)]
+                if attn and step == steps - 1:
+                    sends = [
+                        (kept[:1] + (rows_of,) + kept[2:], LOW)
+                        for rows_of in (block // 2, block - block // 2 + PAIR_ROWS)
+                    ]
+                kernel = partial(merge_attn, len(got)) if attn else merge_weights
+                given = len(sends) + 1
+                outs += sends + [(kept, F32, (H_NEXT, name))]
+            elif attn:
+                kernel, given = merge_last_attn, 4
+                outs += [
+                    ((3, block, width), F32), ((width, block), F32),
+                    ((VECTOR_ROWS, block), F32), ((2, width // dp_size), F32),
+                ]
+            else:
+                kernel, given = merge_last_weights, 1
+                outs += [(shape, F32)]
+            plan.append((kernel, 1 + len(got), given))
+        results = state.call(partial(run_parts, tuple(plan)), outs, *inputs)
+        for name in names:
+            got, step = running.pop(name)
+            state.drop(name)
+            if step < steps:
+                state.arrays[name] = state.arrays.pop((H_NEXT, name))
+                parts = 2 if name == (H_ATTN_KEEP,) and step == steps - 1 else 1
+                sent, results = results[:parts], results[parts:]
+                running[name] = (
+                    [to_dp(part, step, dp_size, tensor_size) for part in sent], step + 1
+                )
+            elif name == (H_ATTN_KEEP,):
+                finished[name], results = results[:4], results[4:]
+            else:
+                finished[name] = results.pop(0)
+
+    advance((H_DOWN_KEEP,))
 
     attn_w_send, grad_q, grad_k, grad_v = state.call(
         attn_backward,
         [
             ((count, block + PAIR_ROWS, model), LOW),
-            ((count, block + PAIR_ROWS, model), F32, "attn_keep"),
+            ((count, block + PAIR_ROWS, model), F32, (H_ATTN_KEEP,)),
         ]
         + [((rows, width), LOW)] * 3,
-        lengths, *grad_attn, *grad_attn_other, sums, sums_other,
-        "w_out", "saved", "tokens", "sum_down", "sum_up",
+        lengths, grad_attn, grad_attn_other, sums, sums_other,
+        (H_W_OUT,), (H_SAVED,), (H_TOKENS,), (H_SUM_DOWN,), (H_SUM_UP,),
         scratch=[
             pltpu.VMEM((rows, model), LOW),
             pltpu.VMEM((dp_size, block, model), F32),
@@ -643,51 +776,41 @@
         ],
         mib=24,
     )
-    state.drop("saved", "sum_down", "sum_up", "w_out", "tokens", "packed", "packed_other")
-    attn_got = to_dp(attn_w_send, 0, dp_size, tensor_size)
-    if steps > 1:
-        up_got = merge("up_keep", up_got, 1)
-    token_send, token_keep = state.call(
+    state.drop((H_SAVED,), (H_SUM_DOWN,), (H_SUM_UP,), (H_W_OUT,), (H_TOKENS,))
+    state.drop((H_PACKED,), (H_PACKED_OTHER,))
+    running_attn = ([to_dp(attn_w_send, 0, dp_size, tensor_size)], 1)
+    advance((H_UP_KEEP,), (H_DOWN_KEEP,))
+    *token_parts, token_keep = state.call(
         token_back,
-        [((half, model), LOW), ((half, model), F32)],
-        grad_q, grad_k, grad_v, "w_qkv",
-    )
-    state.drop("w_qkv")
-    (token_own,) = state.call(add_rows, [((half, model), LOW)], token_keep, to_core(token_send))
+        [((half // PIECES, model), LOW)] * PIECES + [((half, model), F32)],
+        grad_q, grad_k, grad_v, (H_W_QKV,),
+    )
+    state.drop((H_W_QKV,))
+    token_other = [to_core(part) for part in token_parts]
+    (token_own,) = state.call(add_rows, [((half, model), LOW)], token_keep, *token_other)
     token_received = to_chip(token_own)
-    for step in range(2, steps):
-        down_got = merge("down_keep", down_got, step)
-    if steps > 1:
-        attn_got = merge("attn_keep", attn_got, 1)
-    for step in range(2, steps):
-        up_got = merge("up_keep", up_got, step)
-    (token_half,) = state.call(
-        final_rows, [((half, model), LOW)], *[f"last{c}" for c in chunks],
-        token_own, token_received,
-    )
-    state.drop(*[f"last{c}" for c in chunks])
-    for step in range(2, steps):
-        attn_got = merge("attn_keep", attn_got, step)
+    running[(H_ATTN_KEEP,)] = running_attn
+    others = [(H_DOWN_KEEP,), (H_UP_KEEP,)]
+    while running[(H_ATTN_KEEP,)][1] < steps:
+        if running[(H_ATTN_KEEP,)][1] == steps - 1:
+            (token_half,) = state.call(
+                final_rows, [((half, model), LOW)], (H_LAST,), token_own, token_received
+            )
+            state.drop((H_LAST,))
+        advance((H_ATTN_KEEP,))
+        left = [name for name in others if name in running]
+        if left != [(H_UP_KEEP,)]:
+            advance(*left)
     (output_low,) = state.call(
-        place_rows, [((rows, model), LOW)],
-        *[f"out_half{c}" for c in chunks], *[f"out_other{c}" for c in chunks],
-    )
-    state.drop(*[f"out_half{c}" for c in chunks], *[f"out_other{c}" for c in chunks])
+        place_rows, [((rows, model), LOW)], (H_OUT_HALF,), (H_OUT_OTHER,)
+    )
+    state.drop((H_OUT_HALF,), (H_OUT_OTHER,))
     (token_total,) = state.call(
         place_rows, [((rows, model), LOW)], token_half, to_core(token_half),
     )
-    (sum_w_down,) = state.call(merge_last_weights, [((block, units), F32)], "down_keep", down_got)
-    state.drop("down_keep")
-    (sum_w_up,) = state.call(merge_last_weights, [((block, units), F32)], "up_keep", up_got)
-    state.drop("up_keep")
-    sum_w_qkv, sum_w_out, mine, sum_bias_qv = state.call(
-        merge_last_attn,
-        [
-            ((3, block, width), F32), ((width, block), F32), ((VECTOR_ROWS, block), F32),
-            ((2, width // dp_size), F32),
-        ],
-        "attn_keep", attn_got,
-    )
+    advance(*[name for name in others if name in running], (H_ATTN_KEEP,))
+    sum_w_down, sum_w_up = finished[(H_DOWN_KEEP,)], finished[(H_UP_KEEP,)]
+    sum_w_qkv, sum_w_out, mine, sum_bias_qv = finished[(H_ATTN_KEEP,)]
     return (
         output_low,
         token_total,

time: 106 us -> 97.8 us (0.923)
  waiting for transfers between devices: 47.8 us -> 32.4 us
  starting transfers between devices: 23.6 us -> 27.4 us
  Pallas kernels: 24.6 us -> 27.7 us
    ppermute x4 -> x6, waiting for transfers between devices: 16.2 us -> 7.59 us  [to_chip(): return lax.ppermute(block, 'tensor', CHIP_PAIRS)]
    ppermute x9 -> x11, waiting for transfers between devices: 27.6 us -> 19.4 us  [to_dp(): return lax.ppermute(block, ('dp', 'tensor'), pairs)]
    pallas_call x23 -> x22, Pallas kernels: 24.6 us -> 27.7 us  [call(): pl.pallas_call(body, name=getattr(kernel, 'func', kernel).__name__, out_s...]
    ppermute x9 -> x11, starting transfers between devices: 13.8 us -> 16 us  [to_dp(): return lax.ppermute(block, ('dp', 'tensor'), pairs)]
    ppermute x11 -> x16, waiting for transfers between devices: 3.95 us -> 5.4 us  [to_core(): return lax.ppermute(block, 'tensor', CORE_PAIRS)]
    ppermute x11 -> x16, starting transfers between devices: 2.1 us -> 3.46 us  [to_core(): return lax.ppermute(block, 'tensor', CORE_PAIRS)]
    ppermute x4 -> x6, starting transfers between devices: 7.72 us -> 7.87 us  [to_chip(): return lax.ppermute(block, 'tensor', CHIP_PAIRS)]
  transfers between devices with their start and end apart: 24 -> 33, of which waited for: 14 -> 17; matrix products, arithmetic and copies ran while one was open for 0% -> 0% of each run, Pallas kernels for 19% -> 25%
where the time goes in v4:
time: 97.8 us; the launch traced here: 97.4 us
  waiting for transfers between devices  32.4 us (33%)
  Pallas kernels  27.7 us (28%)
  starting transfers between devices  27.4 us (28%)
  local copies, waits for them, and re-layouts  8.29 us (8%)
  between operations  1.68 us (2%)
    pallas_call x22, Pallas kernels, call(): pl.pallas_call(body, name=getattr(kernel, 'func', kernel).__name__, out_s...  27.7 us
    ppermute x11, waiting for transfers between devices, to_dp(): return lax.ppermute(block, ('dp', 'tensor'), pairs)  19.4 us
    ppermute x11, starting transfers between devices, to_dp(): return lax.ppermute(block, ('dp', 'tensor'), pairs)  16 us
    ppermute x6, starting transfers between devices, to_chip(): return lax.ppermute(block, 'tensor', CHIP_PAIRS)  7.87 us
    unnamed x34, local copies, waits for them, and re-layouts  7.67 us
    ppermute x6, waiting for transfers between devices, to_chip(): return lax.ppermute(block, 'tensor', CHIP_PAIRS)  7.59 us
    ppermute x16, waiting for transfers between devices, to_core(): return lax.ppermute(block, 'tensor', CORE_PAIRS)  5.4 us
    ppermute x16, starting transfers between devices, to_core(): return lax.ppermute(block, 'tensor', CORE_PAIRS)  3.46 us
  transfers between devices with their start and end apart: 33, of which 17 were waited for; matrix products, arithmetic and copies ran while one was open for 0% of the time, Pallas kernels for 25%

profile of v4, /device:TPU:0, one launch (start us, length us, event | category | flops | bytes accessed | tf_op | source)
XLA Modules:
  0.0 97.4 jit_solution(367894249669209916)
XLA Ops:
  5.8 2.8 %attn_forward.1 = (bf16[4,512,192]{2,1,0:T(8,128)(2,1)S(1)}, bf16[256,768]{1,0:T(8,128)(2,1)S(1)}, f32[256,768]{1,0:T(8,128)S(1)}) custom-call(s32[1]{0:T(128)S(6)} %copy.495.refs_0_, bf16[512,768]{1,0:T(8,128)(2,1)S(1)} %copy-done.2, bf16[3,192,768]{2,1,0:T(8,128)(2,1)S(1)} %bitcast.16, f32[2,192]{1,0:T(2,128)S(1)} %copy-done.9, bf16[192,768]{1,0:T(8,128)(2,1)S(1)} %copy-done.6), custom_call_target="tpu_custom_call" | custom-call | tf_op jit(solution)/shard_map/attn_forward/pallas_call | solution.py:120
  9.3 1.3 %collective-permute-done.refs_1_ = bf16[256,768]{1,0:T(8,128)(2,1)S(1)} collective-permute-done((bf16[256,768]{1,0:T(8,128)(2,1)S(1)}, bf16[256,768]{1,0:T(8,128)(2,1)S(1)}, u32[]{:S(2)}, u32[]{:S(2)}) %collective-permute-start) | collective-permute-done | bytes 393248 | tf_op jit(solution)/shard_map/ppermute | solution.py:541
  11.4 2.9 %collective-permute-start.2 = (bf16[128,768]{1,0:T(8,128)(2,1)}, bf16[128,768]{1,0:T(8,128)(2,1)}, u32[]{:S(2)}, u32[]{:S(2)}) collective-permute-start(bf16[128,768]{1,0:T(8,128)(2,1)} %get-tuple-element.292), channel_id=1, source_target_pairs={{0,2},{1,3},{2,0},{3,1},{4,6},{5,7},{6,4},{7,5},{8,10},{9,11},{10,... | collective-permute-start | bytes 589832 | tf_op jit(solution)/shard_map/ppermute | solution.py:545
  14.6 1.2 %collective-permute-done.5.refs_9_ = f32[8,768]{1,0:T(8,128)S(1)} collective-permute-done((f32[8,768]{1,0:T(8,128)S(1)}, f32[8,768]{1,0:T(8,128)S(1)}, u32[]{:S(2)}, u32[]{:S(2)}) %collective-permute-start.5) | collective-permute-done | bytes 24608 | tf_op jit(solution)/shard_map/ppermute | solution.py:541
  15.8 1.3 %copy-done.4 = bf16[768,768]{1,0:T(8,128)(2,1)S(1)} copy-done((bf16[768,768]{1,0:T(8,128)(2,1)S(1)}, bf16[768,768]{1,0:T(8,128)(2,1)}, u32[]{:S(2)}) %copy-start.4) | copy-done | bytes 1179672
  17.1 1.3 %copy-done.5 = bf16[768,768]{1,0:T(8,128)(2,1)S(1)} copy-done((bf16[768,768]{1,0:T(8,128)(2,1)S(1)}, bf16[768,768]{1,0:T(8,128)(2,1)}, u32[]{:S(2)}) %copy-start.5) | copy-done | bytes 1179672
  19.5 2.4 %hold.1 = (bf16[512,768]{1,0:T(8,128)(2,1)S(1)}, bf16[192,768]{1,0:T(8,128)(2,1)S(1)}, bf16[3,192,768]{2,1,0:T(8,128)(2,1)S(1)}, bf16[512,768]{1,0:T(8,128)(2,1)...) custom-call(bf16[512,768]{1,0:T(8,128)(2,1)S(1)} %copy-done.3, ...), custom_call_target="tpu_custom_call", output_to_operand_aliasing={{10}: (10, {}), {11}: (11, {}), {12}: (12, {})} | custom-call | tf_op jit(solution)/shard_map/hold/pallas_call | solution.py:120
  21.9 2.3 %mlp_forward.2 = (bf16[128,768]{1,0:T(8,128)(2,1)S(1)}, bf16[128,768]{1,0:T(8,128)(2,1)S(1)}, bf16[128,768]{1,0:T(8,128)(2,1)S(1)}, bf16[128,768]{1,0:T(8,128)(2...) custom-call(bf16[128,768]{1,0:T(8,128)(2,1)} %collective-permute-don, ...), custom_call_target="tpu_custom_call", output_to_operand_aliasing={{9}: (1, {}), {10}: (2, {}), {11}: (3, {}), {12}: (4, {}), ... | custom-call | tf_op jit(solution)/shard_map/mlp_forward/pallas_call | solution.py:120
  24.2 2.1 %collective-permute-start.7 = (bf16[128,768]{1,0:T(8,128)(2,1)S(1)}, bf16[128,768]{1,0:T(8,128)(2,1)S(1)}, u32[]{:S(2)}, u32[]{:S(2)}) collective-permute-start(bf16[128,768]{1,0:T(8,128)(2,1)S(1)} %get-tuple-element.328), channel_id=1, source_target_pairs={{0,2},{1,3},{2,0},{3,1},{4,6},{5,7},{6,4},{7,5},{8,10},{9,11},{10,... | collective-permute-start | bytes 589832 | tf_op jit(solution)/shard_map/ppermute | solution.py:545
  26.3 2.2 %mlp_forward.3 = (bf16[128,768]{1,0:T(8,128)(2,1)S(1)}, bf16[128,768]{1,0:T(8,128)(2,1)S(1)}, bf16[128,768]{1,0:T(8,128)(2,1)S(1)}, bf16[128,768]{1,0:T(8,128)(2...) custom-call(bf16[128,768]{1,0:T(8,128)(2,1)} %collective-permute-don, ...), custom_call_target="tpu_custom_call", output_to_operand_aliasing={{9}: (1, {}), {10}: (2, {}), {11}: (3, {}), {12}: (4, {}), ... | custom-call | tf_op jit(solution)/shard_map/mlp_forward/pallas_call | solution.py:120
  28.6 3.3 %collective-permute-done.7.refs_1_ = bf16[128,768]{1,0:T(8,128)(2,1)S(1)} collective-permute-done((bf16[128,768]{1,0:T(8,128)(2,1)S(1)}, bf16[128,768]{1,0:T(8,128)(2,1)S(1)}, u32[]{:S(2)}, u32[]{:S(2)}) %collective-permute-start.7) | collective-permute-done | bytes 196640 | tf_op jit(solution)/shard_map/ppermute | solution.py:545
  31.9 2.2 %mlp_backward.2 = (bf16[128,768]{1,0:T(8,128)(2,1)S(1)}, bf16[128,768]{1,0:T(8,128)(2,1)S(1)}, bf16[128,768]{1,0:T(8,128)(2,1)S(1)}, bf16[128,768]{1,0:T(8,128)(...) custom-call(s32[1]{0:T(128)S(6)} %copy.495.refs_0_, ...), custom_call_target="tpu_custom_call", output_to_operand_aliasing={{7}: (2, {}), {8}: (3, {}), {9}: (4, {}), {10}: (5, {}), {1... | custom-call | tf_op jit(solution)/shard_map/mlp_backward/pallas_call | solution.py:120
  34.0 1.7 %collective-permute-done.6.refs_1_ = bf16[128,768]{1,0:T(8,128)(2,1)S(1)} collective-permute-done((bf16[128,768]{1,0:T(8,128)(2,1)S(1)}, bf16[128,768]{1,0:T(8,128)(2,1)S(1)}, u32[]{:S(2)}, u32[]{:S(2)}) %collective-permute-start.6) | collective-permute-done | bytes 196640 | tf_op jit(solution)/shard_map/ppermute | solution.py:545
  35.7 2.7 %mlp_backward.3 = (bf16[128,768]{1,0:T(8,128)(2,1)S(1)}, bf16[128,768]{1,0:T(8,128)(2,1)S(1)}, bf16[128,768]{1,0:T(8,128)(2,1)S(1)}, bf16[128,768]{1,0:T(8,128)(...) custom-call(s32[1]{0:T(128)S(6)} %copy.495.refs_0_, ...), custom_call_target="tpu_custom_call", output_to_operand_aliasing={{11}: (2, {}), {12}: (3, {}), {13}: (4, {}), {14}: (5, {}),... | custom-call | tf_op jit(solution)/shard_map/mlp_backward/pallas_call | solution.py:120
  39.5 1.7 %collective-permute-start.8 = (bf16[256,768]{1,0:T(8,128)(2,1)S(1)}, bf16[256,768]{1,0:T(8,128)(2,1)S(1)}, u32[]{:S(2)}, u32[]{:S(2)}) collective-permute-start(bf16[256,768]{1,0:T(8,128)(2,1)S(1)} %get-tuple-element.380), channel_id=1, source_target_pairs={{0,2},{1,3},{2,0},{3,1},{4,6},{5,7},{6,4},{7,5},{8,10},{9,11},{10,... | collective-permute-start | bytes 1179656 | tf_op jit(solution)/shard_map/ppermute | solution.py:545
  43.2 1.6 %collective-permute-start.18 = (bf16[2,96,768]{2,1,0:T(8,128)(2,1)S(1)}, bf16[2,96,768]{2,1,0:T(8,128)(2,1)S(1)}, u32[]{:S(2)}, u32[]{:S(2)}) collective-permute-start(bf16[2,96,768]{2,1,0:T(8,128)(2,1)S(1)} %get-tuple-element.460), channel_id=1, source_target_pairs={{0,4},{1,9},{2,6},{3,11},{4,0},{5,13},{6,2},{7,15},{8,12},{9,1},{1... | collective-permute-start | bytes 884744 | tf_op jit(solution)/shard_map/ppermute | solution.py:561
  46.2 1.6 %collective-permute-start.21 = (bf16[4,96,768]{2,1,0:T(8,128)(2,1)S(1)}, bf16[4,96,768]{2,1,0:T(8,128)(2,1)S(1)}, u32[]{:S(2)}, u32[]{:S(2)}) collective-permute-start(bf16[4,96,768]{2,1,0:T(8,128)(2,1)S(1)} %get-tuple-element.492), channel_id=1, source_target_pairs={{0,4},{1,9},{2,6},{3,11},{4,0},{5,13},{6,2},{7,15},{8,12},{9,1},{1... | collective-permute-start | bytes 1769480 | tf_op jit(solution)/shard_map/ppermute | solution.py:561
  47.8 2.7 %collective-permute-done.8.refs_0_ = bf16[256,768]{1,0:T(8,128)(2,1)S(1)} collective-permute-done((bf16[256,768]{1,0:T(8,128)(2,1)S(1)}, bf16[256,768]{1,0:T(8,128)(2,1)S(1)}, u32[]{:S(2)}, u32[]{:S(2)}) %collective-permute-start.8) | collective-permute-done | bytes 393248 | tf_op jit(solution)/shard_map/ppermute | solution.py:545
  51.2 1.9 %collective-permute-done.19.refs_1_ = bf16[2,96,768]{2,1,0:T(8,128)(2,1)S(1)} collective-permute-done((bf16[2,96,768]{2,1,0:T(8,128)(2,1)S(1)}, bf16[2,96,768]{2,1,0:T(8,128)(2,1)S(1)}, u32[]{:S(2)}, u32[]{:S(2)}) %collective-permute-start.19) | collective-permute-done | bytes 294944 | tf_op jit(solution)/shard_map/ppermute | solution.py:561
  53.2 1.7 %collective-permute-start.22 = (bf16[2,96,768]{2,1,0:T(8,128)(2,1)S(1)}, bf16[2,96,768]{2,1,0:T(8,128)(2,1)S(1)}, u32[]{:S(2)}, u32[]{:S(2)}) collective-permute-start(bf16[2,96,768]{2,1,0:T(8,128)(2,1)S(1)} %get-tuple-element.493), channel_id=1, source_target_pairs={{0,8},{1,5},{2,10},{3,7},{4,12},{5,1},{6,14},{7,3},{8,0},{9,13},{1... | collective-permute-start | bytes 884744 | tf_op jit(solution)/shard_map/ppermute | solution.py:561
  54.9 1.2 %collective-permute-done.17.refs_4_ = f32[8,768]{1,0:T(8,128)S(1)} collective-permute-done((f32[8,768]{1,0:T(8,128)S(1)}, f32[8,768]{1,0:T(8,128)S(1)}, u32[]{:S(2)}, u32[]{:S(2)}) %collective-permute-start.17) | collective-permute-done | bytes 24608 | tf_op jit(solution)/shard_map/ppermute | solution.py:541
  56.1 4.6 %attn_backward.1 = (bf16[4,112,768]{2,1,0:T(8,128)(2,1)S(1)}, f32[4,112,768]{2,1,0:T(8,128)S(1)}, bf16[512,192]{1,0:T(8,128)(2,1)S(1)}, bf16[512,192]{1,0:T(8,12...) custom-call(s32[1]{0:T(128)S(6)} %copy.495.refs_0_, ...), custom_call_target="tpu_custom_call", output_to_operand_aliasing={{5}: (5, {}), {6}: (6, {}), {7}: (7, {}), {8}: (8, {}), {9}... | custom-call | tf_op jit(solution)/shard_map/attn_backward/pallas_call | solution.py:120
  60.7 1.6 %collective-permute-start.20 = (bf16[4,112,768]{2,1,0:T(8,128)(2,1)S(1)}, bf16[4,112,768]{2,1,0:T(8,128)(2,1)S(1)}, u32[]{:S(2)}, u32[]{:S(2)}) collective-permute-start(bf16[4,112,768]{2,1,0:T(8,128)(2,1)S(1)} %get-tuple-element.488), channel_id=1, source_target_pairs={{0,4},{1,9},{2,6},{3,11},{4,0},{5,13},{6,2},{7,15},{8,12},{9,1},{1... | collective-permute-start | bytes 2064392 | tf_op jit(solution)/shard_map/ppermute | solution.py:561
  66.5 1.6 %collective-permute-start.28 = (bf16[2,96,768]{2,1,0:T(8,128)(2,1)S(1)}, bf16[2,96,768]{2,1,0:T(8,128)(2,1)S(1)}, u32[]{:S(2)}, u32[]{:S(2)}) collective-permute-start(bf16[2,96,768]{2,1,0:T(8,128)(2,1)S(1)} %get-tuple-element.526), channel_id=1, source_target_pairs={{0,8},{1,5},{2,10},{3,7},{4,12},{5,1},{6,14},{7,3},{8,0},{9,13},{1... | collective-permute-start | bytes 884744 | tf_op jit(solution)/shard_map/ppermute | solution.py:561
  68.1 2.6 %collective-permute-start.27 = (bf16[1,96,768]{2,1,0:T(8,128)(2,1)S(1)}, bf16[1,96,768]{2,1,0:T(8,128)(2,1)S(1)}, u32[]{:S(2)}, u32[]{:S(2)}) collective-permute-start(bf16[1,96,768]{2,1,0:T(8,128)(2,1)S(1)} %get-tuple-element.525), channel_id=1, source_target_pairs={{0,16},{1,17},{2,18},{3,19},{4,20},{5,21},{6,22},{7,23},{8,24},{9,... | collective-permute-start | bytes 442376 | tf_op jit(solution)/shard_map/ppermute | solution.py:561
  70.7 3.5 %collective-permute-done.20.refs_0_ = bf16[4,112,768]{2,1,0:T(8,128)(2,1)S(1)} collective-permute-done((bf16[4,112,768]{2,1,0:T(8,128)(2,1)S(1)}, bf16[4,112,768]{2,1,0:T(8,128)(2,1)S(1)}, u32[]{:S(2)}, u32[]{:S(2)}) %collective-permute-start.20) | collective-permute-done | bytes 688160 | tf_op jit(solution)/shard_map/ppermute | solution.py:561
  75.5 1.6 %collective-permute-done.28.refs_1_ = bf16[2,96,768]{2,1,0:T(8,128)(2,1)S(1)} collective-permute-done((bf16[2,96,768]{2,1,0:T(8,128)(2,1)S(1)}, bf16[2,96,768]{2,1,0:T(8,128)(2,1)S(1)}, u32[]{:S(2)}, u32[]{:S(2)}) %collective-permute-start.28) | collective-permute-done | bytes 294944 | tf_op jit(solution)/shard_map/ppermute | solution.py:561
  78.2 1.9 %collective-permute-start.30 = (bf16[1,96,768]{2,1,0:T(8,128)(2,1)S(1)}, bf16[1,96,768]{2,1,0:T(8,128)(2,1)S(1)}, u32[]{:S(2)}, u32[]{:S(2)}) collective-permute-start(bf16[1,96,768]{2,1,0:T(8,128)(2,1)S(1)} %get-tuple-element.551), channel_id=1, source_target_pairs={{0,16},{1,17},{2,18},{3,19},{4,20},{5,21},{6,22},{7,23},{8,24},{9,... | collective-permute-start | bytes 442376 | tf_op jit(solution)/shard_map/ppermute | solution.py:561
  80.1 1.6 %collective-permute-done.25.refs_0_ = bf16[2,112,768]{2,1,0:T(8,128)(2,1)S(1)} collective-permute-done((bf16[2,112,768]{2,1,0:T(8,128)(2,1)S(1)}, bf16[2,112,768]{2,1,0:T(8,128)(2,1)S(1)}, u32[]{:S(2)}, u32[]{:S(2)}) %collective-permute-start.25) | collective-permute-done | bytes 344096 | tf_op jit(solution)/shard_map/ppermute | solution.py:561
  81.7 2.6 %collective-permute-start.32 = (bf16[1,64,768]{2,1,0:T(8,128)(2,1)S(1)}, bf16[1,64,768]{2,1,0:T(8,128)(2,1)S(1)}, u32[]{:S(2)}, u32[]{:S(2)}) collective-permute-start(bf16[1,64,768]{2,1,0:T(8,128)(2,1)S(1)} %get-tuple-element.553), channel_id=1, source_target_pairs={{0,16},{1,17},{2,18},{3,19},{4,20},{5,21},{6,22},{7,23},{8,24},{9,... | collective-permute-start | bytes 294920 | tf_op jit(solution)/shard_map/ppermute | solution.py:561
  86.6 6.0 %collective-permute-done.30.refs_0_ = bf16[1,96,768]{2,1,0:T(8,128)(2,1)S(1)} collective-permute-done((bf16[1,96,768]{2,1,0:T(8,128)(2,1)S(1)}, bf16[1,96,768]{2,1,0:T(8,128)(2,1)S(1)}, u32[]{:S(2)}, u32[]{:S(2)}) %collective-permute-start.30) | collective-permute-done | bytes 147488 | tf_op jit(solution)/shard_map/ppermute | solution.py:561
  92.6 3.2 %collective-permute-done.31.refs_1_ = bf16[1,48,768]{2,1,0:T(8,128)(2,1)S(1)} collective-permute-done((bf16[1,48,768]{2,1,0:T(8,128)(2,1)S(1)}, bf16[1,48,768]{2,1,0:T(8,128)(2,1)S(1)}, u32[]{:S(2)}, u32[]{:S(2)}) %collective-permute-start.31) | collective-permute-done | bytes 73760 | tf_op jit(solution)/shard_map/ppermute | solution.py:561
  (99 shorter events, 22.9 us)
Async XLA Ops:
  0.6 15.1 %collective-permute-start.3 = (bf16[768,768]{1,0:T(8,128)(2,1)}, bf16[768,768]{1,0:T(8,128)(2,1)}, u32[]{:S(2)}, u32[]{:S(2)}) collective-permute-start(bf16[768,768]{1,0:T(8,128)(2,1)} %refs_4_.3), channel_id=1, source_target_pairs={{0,1},{1,0},{2,3},{3,2},{4,5},{5,4},{6,7},{7,6},{8,9},{9,8},{10,11... | collective-permute-start | bytes 3538952 | tf_op jit(solution)/shard_map/ppermute | solution.py:541
  1.2 14.6 %collective-permute-start.4 = (bf16[768,768]{1,0:T(8,128)(2,1)}, bf16[768,768]{1,0:T(8,128)(2,1)}, u32[]{:S(2)}, u32[]{:S(2)}) collective-permute-start(bf16[768,768]{1,0:T(8,128)(2,1)} %refs_6_.1), channel_id=1, source_target_pairs={{0,1},{1,0},{2,3},{3,2},{4,5},{5,4},{6,7},{7,6},{8,9},{9,8},{10,11... | collective-permute-start | bytes 3538952 | tf_op jit(solution)/shard_map/ppermute | solution.py:541
  8.8 1.8 %collective-permute-start = (bf16[256,768]{1,0:T(8,128)(2,1)S(1)}, bf16[256,768]{1,0:T(8,128)(2,1)S(1)}, u32[]{:S(2)}, u32[]{:S(2)}) collective-permute-start(bf16[256,768]{1,0:T(8,128)(2,1)S(1)} %get-tuple-element.289), channel_id=1, source_target_pairs={{0,1},{1,0},{2,3},{3,2},{4,5},{5,4},{6,7},{7,6},{8,9},{9,8},{10,11... | collective-permute-start | bytes 1179656 | tf_op jit(solution)/shard_map/ppermute | solution.py:541
  11.4 10.5 %collective-permute-start.2 = (bf16[128,768]{1,0:T(8,128)(2,1)}, bf16[128,768]{1,0:T(8,128)(2,1)}, u32[]{:S(2)}, u32[]{:S(2)}) collective-permute-start(bf16[128,768]{1,0:T(8,128)(2,1)} %get-tuple-element.292), channel_id=1, source_target_pairs={{0,2},{1,3},{2,0},{3,1},{4,6},{5,7},{6,4},{7,5},{8,10},{9,11},{10,... | collective-permute-start | bytes 589832 | tf_op jit(solution)/shard_map/ppermute | solution.py:545
  14.3 12.0 %collective-permute-start.1 = (bf16[128,768]{1,0:T(8,128)(2,1)}, bf16[128,768]{1,0:T(8,128)(2,1)}, u32[]{:S(2)}, u32[]{:S(2)}) collective-permute-start(bf16[128,768]{1,0:T(8,128)(2,1)} %get-tuple-element.291), channel_id=1, source_target_pairs={{0,2},{1,3},{2,0},{3,1},{4,6},{5,7},{6,4},{7,5},{8,10},{9,11},{10,... | collective-permute-start | bytes 589832 | tf_op jit(solution)/shard_map/ppermute | solution.py:545
  14.5 1.3 %collective-permute-start.5 = (f32[8,768]{1,0:T(8,128)S(1)}, f32[8,768]{1,0:T(8,128)S(1)}, u32[]{:S(2)}, u32[]{:S(2)}) collective-permute-start(f32[8,768]{1,0:T(8,128)S(1)} %stack.32.refs_8_), channel_id=1, source_target_pairs={{0,1},{1,0},{2,3},{3,2},{4,5},{5,4},{6,7},{7,6},{8,9},{9,8},{10,11... | collective-permute-start | bytes 73736 | tf_op jit(solution)/shard_map/ppermute | solution.py:541
  24.2 7.7 %collective-permute-start.7 = (bf16[128,768]{1,0:T(8,128)(2,1)S(1)}, bf16[128,768]{1,0:T(8,128)(2,1)S(1)}, u32[]{:S(2)}, u32[]{:S(2)}) collective-permute-start(bf16[128,768]{1,0:T(8,128)(2,1)S(1)} %get-tuple-element.328), channel_id=1, source_target_pairs={{0,2},{1,3},{2,0},{3,1},{4,6},{5,7},{6,4},{7,5},{8,10},{9,11},{10,... | collective-permute-start | bytes 589832 | tf_op jit(solution)/shard_map/ppermute | solution.py:545
  28.5 7.2 %collective-permute-start.6 = (bf16[128,768]{1,0:T(8,128)(2,1)S(1)}, bf16[128,768]{1,0:T(8,128)(2,1)S(1)}, u32[]{:S(2)}, u32[]{:S(2)}) collective-permute-start(bf16[128,768]{1,0:T(8,128)(2,1)S(1)} %get-tuple-element.327), channel_id=1, source_target_pairs={{0,2},{1,3},{2,0},{3,1},{4,6},{5,7},{6,4},{7,5},{8,10},{9,11},{10,... | collective-permute-start | bytes 589832 | tf_op jit(solution)/shard_map/ppermute | solution.py:545
  38.5 3.3 %collective-permute-start.12 = (bf16[256,768]{1,0:T(8,128)(2,1)S(1)}, bf16[256,768]{1,0:T(8,128)(2,1)S(1)}, u32[]{:S(2)}, u32[]{:S(2)}) collective-permute-start(bf16[256,768]{1,0:T(8,128)(2,1)S(1)} %get-tuple-element.384), channel_id=1, source_target_pairs={{0,1},{1,0},{2,3},{3,2},{4,5},{5,4},{6,7},{7,6},{8,9},{9,8},{10,11... | collective-permute-start | bytes 1179656 | tf_op jit(solution)/shard_map/ppermute | solution.py:541
  38.5 2.8 %collective-permute-start.13 = (bf16[128,768]{1,0:T(8,128)(2,1)S(1)}, bf16[128,768]{1,0:T(8,128)(2,1)S(1)}, u32[]{:S(2)}, u32[]{:S(2)}) collective-permute-start(bf16[128,768]{1,0:T(8,128)(2,1)S(1)} %get-tuple-element.385), channel_id=1, source_target_pairs={{0,1},{1,0},{2,3},{3,2},{4,5},{5,4},{6,7},{7,6},{8,9},{9,8},{10,11... | collective-permute-start | bytes 589832 | tf_op jit(solution)/shard_map/ppermute | solution.py:541
  39.0 2.3 %collective-permute-start.14 = (bf16[128,768]{1,0:T(8,128)(2,1)S(1)}, bf16[128,768]{1,0:T(8,128)(2,1)S(1)}, u32[]{:S(2)}, u32[]{:S(2)}) collective-permute-start(bf16[128,768]{1,0:T(8,128)(2,1)S(1)} %get-tuple-element.386), channel_id=1, source_target_pairs={{0,1},{1,0},{2,3},{3,2},{4,5},{5,4},{6,7},{7,6},{8,9},{9,8},{10,11... | collective-permute-start | bytes 589832 | tf_op jit(solution)/shard_map/ppermute | solution.py:541
  39.0 6.3 %collective-permute-start.11 = (bf16[256,768]{1,0:T(8,128)(2,1)S(1)}, bf16[256,768]{1,0:T(8,128)(2,1)S(1)}, u32[]{:S(2)}, u32[]{:S(2)}) collective-permute-start(bf16[256,768]{1,0:T(8,128)(2,1)S(1)} %get-tuple-element.383), channel_id=1, source_target_pairs={{0,1},{1,0},{2,3},{3,2},{4,5},{5,4},{6,7},{7,6},{8,9},{9,8},{10,11... | collective-permute-start | bytes 1179656 | tf_op jit(solution)/shard_map/ppermute | solution.py:541
  39.5 11.0 %collective-permute-start.8 = (bf16[256,768]{1,0:T(8,128)(2,1)S(1)}, bf16[256,768]{1,0:T(8,128)(2,1)S(1)}, u32[]{:S(2)}, u32[]{:S(2)}) collective-permute-start(bf16[256,768]{1,0:T(8,128)(2,1)S(1)} %get-tuple-element.380), channel_id=1, source_target_pairs={{0,2},{1,3},{2,0},{3,1},{4,6},{5,7},{6,4},{7,5},{8,10},{9,11},{10,... | collective-permute-start | bytes 1179656 | tf_op jit(solution)/shard_map/ppermute | solution.py:545
  41.2 9.3 %collective-permute-start.15 = (bf16[256,768]{1,0:T(8,128)(2,1)S(1)}, bf16[256,768]{1,0:T(8,128)(2,1)S(1)}, u32[]{:S(2)}, u32[]{:S(2)}) collective-permute-start(bf16[256,768]{1,0:T(8,128)(2,1)S(1)} %get-tuple-element.457.refs_21_), channel_id=1, source_target_pairs={{0,1},{1,0},{2,3},{3,2},{4,5},{5,4},{6,7},{7,6},{8,9},{9,8},{10,11... | collective-permute-start | bytes 1179656 | tf_op jit(solution)/shard_map/ppermute | solution.py:541
  41.2 2.0 %collective-permute-start.9 = (bf16[128,768]{1,0:T(8,128)(2,1)S(1)}, bf16[128,768]{1,0:T(8,128)(2,1)S(1)}, u32[]{:S(2)}, u32[]{:S(2)}) collective-permute-start(bf16[128,768]{1,0:T(8,128)(2,1)S(1)} %get-tuple-element.381), channel_id=1, source_target_pairs={{0,1},{1,0},{2,3},{3,2},{4,5},{5,4},{6,7},{7,6},{8,9},{9,8},{10,11... | collective-permute-start | bytes 589832 | tf_op jit(solution)/shard_map/ppermute | solution.py:541
  41.7 3.0 %collective-permute-start.10 = (bf16[128,768]{1,0:T(8,128)(2,1)S(1)}, bf16[128,768]{1,0:T(8,128)(2,1)S(1)}, u32[]{:S(2)}, u32[]{:S(2)}) collective-permute-start(bf16[128,768]{1,0:T(8,128)(2,1)S(1)} %get-tuple-element.382), channel_id=1, source_target_pairs={{0,1},{1,0},{2,3},{3,2},{4,5},{5,4},{6,7},{7,6},{8,9},{9,8},{10,11... | collective-permute-start | bytes 589832 | tf_op jit(solution)/shard_map/ppermute | solution.py:541
  43.2 8.0 %collective-permute-start.18 = (bf16[2,96,768]{2,1,0:T(8,128)(2,1)S(1)}, bf16[2,96,768]{2,1,0:T(8,128)(2,1)S(1)}, u32[]{:S(2)}, u32[]{:S(2)}) collective-permute-start(bf16[2,96,768]{2,1,0:T(8,128)(2,1)S(1)} %get-tuple-element.460), channel_id=1, source_target_pairs={{0,4},{1,9},{2,6},{3,11},{4,0},{5,13},{6,2},{7,15},{8,12},{9,1},{1... | collective-permute-start | bytes 884744 | tf_op jit(solution)/shard_map/ppermute | solution.py:561
  44.8 8.3 %collective-permute-start.19 = (bf16[2,96,768]{2,1,0:T(8,128)(2,1)S(1)}, bf16[2,96,768]{2,1,0:T(8,128)(2,1)S(1)}, u32[]{:S(2)}, u32[]{:S(2)}) collective-permute-start(bf16[2,96,768]{2,1,0:T(8,128)(2,1)S(1)} %get-tuple-element.461), channel_id=1, source_target_pairs={{0,4},{1,9},{2,6},{3,11},{4,0},{5,13},{6,2},{7,15},{8,12},{9,1},{1... | collective-permute-start | bytes 884744 | tf_op jit(solution)/shard_map/ppermute | solution.py:561
  46.2 16.4 %collective-permute-start.21 = (bf16[4,96,768]{2,1,0:T(8,128)(2,1)S(1)}, bf16[4,96,768]{2,1,0:T(8,128)(2,1)S(1)}, u32[]{:S(2)}, u32[]{:S(2)}) collective-permute-start(bf16[4,96,768]{2,1,0:T(8,128)(2,1)S(1)} %get-tuple-element.492), channel_id=1, source_target_pairs={{0,4},{1,9},{2,6},{3,11},{4,0},{5,13},{6,2},{7,15},{8,12},{9,1},{1... | collective-permute-start | bytes 1769480 | tf_op jit(solution)/shard_map/ppermute | solution.py:561
  51.1 5.0 %collective-permute-start.16 = (bf16[256,768]{1,0:T(8,128)(2,1)S(1)}, bf16[256,768]{1,0:T(8,128)(2,1)S(1)}, u32[]{:S(2)}, u32[]{:S(2)}) collective-permute-start(bf16[256,768]{1,0:T(8,128)(2,1)S(1)} %get-tuple-element.458.refs_1_), channel_id=1, source_target_pairs={{0,1},{1,0},{2,3},{3,2},{4,5},{5,4},{6,7},{7,6},{8,9},{9,8},{10,11... | collective-permute-start | bytes 1179656 | tf_op jit(solution)/shard_map/ppermute | solution.py:541
  53.2 9.0 %collective-permute-start.22 = (bf16[2,96,768]{2,1,0:T(8,128)(2,1)S(1)}, bf16[2,96,768]{2,1,0:T(8,128)(2,1)S(1)}, u32[]{:S(2)}, u32[]{:S(2)}) collective-permute-start(bf16[2,96,768]{2,1,0:T(8,128)(2,1)S(1)} %get-tuple-element.493), channel_id=1, source_target_pairs={{0,8},{1,5},{2,10},{3,7},{4,12},{5,1},{6,14},{7,3},{8,0},{9,13},{1... | collective-permute-start | bytes 884744 | tf_op jit(solution)/shard_map/ppermute | solution.py:561
  60.7 13.6 %collective-permute-start.20 = (bf16[4,112,768]{2,1,0:T(8,128)(2,1)S(1)}, bf16[4,112,768]{2,1,0:T(8,128)(2,1)S(1)}, u32[]{:S(2)}, u32[]{:S(2)}) collective-permute-start(bf16[4,112,768]{2,1,0:T(8,128)(2,1)S(1)} %get-tuple-element.488), channel_id=1, source_target_pairs={{0,4},{1,9},{2,6},{3,11},{4,0},{5,13},{6,2},{7,15},{8,12},{9,1},{1... | collective-permute-start | bytes 2064392 | tf_op jit(solution)/shard_map/ppermute | solution.py:561
  63.5 1.5 %collective-permute-start.23 = (bf16[128,768]{1,0:T(8,128)(2,1)S(1)}, bf16[128,768]{1,0:T(8,128)(2,1)S(1)}, u32[]{:S(2)}, u32[]{:S(2)}) collective-permute-start(bf16[128,768]{1,0:T(8,128)(2,1)S(1)} %get-tuple-element.509), channel_id=1, source_target_pairs={{0,1},{1,0},{2,3},{3,2},{4,5},{5,4},{6,7},{7,6},{8,9},{9,8},{10,11... | collective-permute-start | bytes 589832 | tf_op jit(solution)/shard_map/ppermute | solution.py:541
  63.6 1.7 %collective-permute-start.24 = (bf16[128,768]{1,0:T(8,128)(2,1)S(1)}, bf16[128,768]{1,0:T(8,128)(2,1)S(1)}, u32[]{:S(2)}, u32[]{:S(2)}) collective-permute-start(bf16[128,768]{1,0:T(8,128)(2,1)S(1)} %get-tuple-element.510), channel_id=1, source_target_pairs={{0,1},{1,0},{2,3},{3,2},{4,5},{5,4},{6,7},{7,6},{8,9},{9,8},{10,11... | collective-permute-start | bytes 589832 | tf_op jit(solution)/shard_map/ppermute | solution.py:541
  65.4 12.5 %collective-permute-start.26 = (bf16[256,768]{1,0:T(8,128)(2,1)S(1)}, bf16[256,768]{1,0:T(8,128)(2,1)S(1)}, u32[]{:S(2)}, u32[]{:S(2)}) collective-permute-start(bf16[256,768]{1,0:T(8,128)(2,1)S(1)} %get-tuple-element.524.refs_0_), channel_id=1, source_target_pairs={{0,2},{1,3},{2,0},{3,1},{4,6},{5,7},{6,4},{7,5},{8,10},{9,11},{10,... | collective-permute-start | bytes 1179656 | tf_op jit(solution)/shard_map/ppermute | solution.py:545
  66.5 10.7 %collective-permute-start.28 = (bf16[2,96,768]{2,1,0:T(8,128)(2,1)S(1)}, bf16[2,96,768]{2,1,0:T(8,128)(2,1)S(1)}, u32[]{:S(2)}, u32[]{:S(2)}) collective-permute-start(bf16[2,96,768]{2,1,0:T(8,128)(2,1)S(1)} %get-tuple-element.526), channel_id=1, source_target_pairs={{0,8},{1,5},{2,10},{3,7},{4,12},{5,1},{6,14},{7,3},{8,0},{9,13},{1... | collective-permute-start | bytes 884744 | tf_op jit(solution)/shard_map/ppermute | solution.py:561
  68.1 7.4 %collective-permute-start.27 = (bf16[1,96,768]{2,1,0:T(8,128)(2,1)S(1)}, bf16[1,96,768]{2,1,0:T(8,128)(2,1)S(1)}, u32[]{:S(2)}, u32[]{:S(2)}) collective-permute-start(bf16[1,96,768]{2,1,0:T(8,128)(2,1)S(1)} %get-tuple-element.525), channel_id=1, source_target_pairs={{0,16},{1,17},{2,18},{3,19},{4,20},{5,21},{6,22},{7,23},{8,24},{9,... | collective-permute-start | bytes 442376 | tf_op jit(solution)/shard_map/ppermute | solution.py:561
  74.3 7.3 %collective-permute-start.25 = (bf16[2,112,768]{2,1,0:T(8,128)(2,1)S(1)}, bf16[2,112,768]{2,1,0:T(8,128)(2,1)S(1)}, u32[]{:S(2)}, u32[]{:S(2)}) collective-permute-start(bf16[2,112,768]{2,1,0:T(8,128)(2,1)S(1)} %get-tuple-element.523), channel_id=1, source_target_pairs={{0,8},{1,5},{2,10},{3,7},{4,12},{5,1},{6,14},{7,3},{8,0},{9,13},{1... | collective-permute-start | bytes 1032200 | tf_op jit(solution)/shard_map/ppermute | solution.py:561
  78.1 7.6 %collective-permute-start.29 = (bf16[256,768]{1,0:T(8,128)(2,1)S(1)}, bf16[256,768]{1,0:T(8,128)(2,1)S(1)}, u32[]{:S(2)}, u32[]{:S(2)}) collective-permute-start(bf16[256,768]{1,0:T(8,128)(2,1)S(1)} %get-tuple-element.547.refs_0_), channel_id=1, source_target_pairs={{0,1},{1,0},{2,3},{3,2},{4,5},{5,4},{6,7},{7,6},{8,9},{9,8},{10,11... | collective-permute-start | bytes 1179656 | tf_op jit(solution)/shard_map/ppermute | solution.py:541
  78.2 14.5 %collective-permute-start.30 = (bf16[1,96,768]{2,1,0:T(8,128)(2,1)S(1)}, bf16[1,96,768]{2,1,0:T(8,128)(2,1)S(1)}, u32[]{:S(2)}, u32[]{:S(2)}) collective-permute-start(bf16[1,96,768]{2,1,0:T(8,128)(2,1)S(1)} %get-tuple-element.551), channel_id=1, source_target_pairs={{0,16},{1,17},{2,18},{3,19},{4,20},{5,21},{6,22},{7,23},{8,24},{9,... | collective-permute-start | bytes 442376 | tf_op jit(solution)/shard_map/ppermute | solution.py:561
  81.7 14.2 %collective-permute-start.32 = (bf16[1,64,768]{2,1,0:T(8,128)(2,1)S(1)}, bf16[1,64,768]{2,1,0:T(8,128)(2,1)S(1)}, u32[]{:S(2)}, u32[]{:S(2)}) collective-permute-start(bf16[1,64,768]{2,1,0:T(8,128)(2,1)S(1)} %get-tuple-element.553), channel_id=1, source_target_pairs={{0,16},{1,17},{2,18},{3,19},{4,20},{5,21},{6,22},{7,23},{8,24},{9,... | collective-permute-start | bytes 294920 | tf_op jit(solution)/shard_map/ppermute | solution.py:561
  84.3 11.5 %collective-permute-start.31 = (bf16[1,48,768]{2,1,0:T(8,128)(2,1)S(1)}, bf16[1,48,768]{2,1,0:T(8,128)(2,1)S(1)}, u32[]{:S(2)}, u32[]{:S(2)}) collective-permute-start(bf16[1,48,768]{2,1,0:T(8,128)(2,1)S(1)} %get-tuple-element.552), channel_id=1, source_target_pairs={{0,16},{1,17},{2,18},{3,19},{4,20},{5,21},{6,22},{7,23},{8,24},{9,... | collective-permute-start | bytes 221192 | tf_op jit(solution)/shard_map/ppermute | solution.py:561
  (18 other events, 69.6 us)

commit v5 on v4

--- a/solution.py
+++ b/solution.py
@@ -14,7 +14,7 @@
 CHUNKS = 2
 DOWN_PARTS = 2
 UP_PARTS = 1
-PIECES = 2
+PIECES = 4
 F32 = jnp.float32
 LOW = jnp.bfloat16
 MIB = 1 << 20
@@ -23,6 +23,7 @@
 
 VECTOR_ROWS = 8
 PAIR_ROWS = 2 * VECTOR_ROWS
+EXTRA_ROWS = VECTOR_ROWS
 
 
 def nn(left, right):
@@ -96,7 +97,7 @@
         for name in names:
             del self.arrays[name]
 
-    def call(self, kernel, outs, *inputs, mib=16, scratch=(), loose=False):
+    def call(self, kernel, outs, *inputs, mib=16, scratch=(), loose=()):
         names = list(self.arrays)
         direct = [item for item in inputs if not isinstance(item, tuple)]
         read = {item for item in inputs if isinstance(item, tuple)}
@@ -122,8 +123,8 @@
             name=getattr(kernel, "func", kernel).__name__,
             out_shape=tuple(out_shapes + held_shapes),
             in_specs=[
-                anywhere if loose else scalar if array.dtype == jnp.int32 else vmem
-                for array in direct
+                anywhere if index in loose else scalar if array.dtype == jnp.int32 else vmem
+                for index, array in enumerate(direct)
             ]
             + [vmem if name in read else anywhere for name in names],
             out_specs=tuple([vmem] * len(outs) + [anywhere] * len(names)),
@@ -350,6 +351,7 @@
 def norm_one_back(received, packed, *refs):
     pieces, (low_o, sums_o, resid_o) = refs[:-3], refs[-3:]
     rows = pieces[0].shape[0]
+    half = CHUNKS * rows
     sums_o[...] = jnp.zeros(sums_o.shape, F32)
     for index in range(CHUNKS):
         own, resid_two, normed, inverse, sums_two = pieces[5 * index : 5 * index + 5]
@@ -364,6 +366,7 @@
         sums_o[2:3, :] += jnp.sum(grad_hidden * xhat, 0, keepdims=True)
         sums_o[3:4, :] += jnp.sum(grad_hidden, 0, keepdims=True)
         sums_o[4:5, :] += jnp.sum(low.astype(F32), 0, keepdims=True)
+    low_o[half:, :] = split_pair(sums_o[...])
 
 
 def split_pair(vectors):
@@ -375,11 +378,12 @@
     lengths, *refs,
 ):
     pieces, refs = refs[:2], refs[2:]
-    sums_own, sums_other, w_out, saved, tokens, sum_down, sum_up = refs[:7]
-    send_o, keep_o, gq_o, gk_o, gv_o, grad_attn, blocks, sums = refs[7:]
+    sums_own, w_out, saved, tokens, sum_down, sum_up = refs[:6]
+    send_o, keep_o, gq_o, gk_o, gv_o, grad_attn, blocks, sums = refs[6:]
     length = lengths[0]
     rows, width = saved.shape[1:]
-    place_rows(*pieces, grad_attn)
+    half = rows // 2
+    place_rows(*[piece.at[pl.ds(0, half)] for piece in pieces], grad_attn)
     grad_rows = grad_attn[...]
     grad_att = nt(grad_rows, w_out[...]).astype(LOW)
     scale = HEAD_DIM ** -0.5
@@ -414,7 +418,8 @@
         [tn(x, low_q), tn(x, low_k), tn(x, low_v), tn(grad_rows, saved[3])], 1
     )
     spread(blocks, weight)
-    sums[...] = sums_own[...] + sums_other[...]
+    others = pieces[1][half:, :].astype(F32)
+    sums[...] = sums_own[...] + others[:VECTOR_ROWS] + others[VECTOR_ROWS:]
     sums[5:6, :] = sum_down[0:1, :]
     sums[6:7, :] = sum_up[0:1, :]
     last = VECTOR_ROWS - 1
@@ -422,15 +427,14 @@
     sums[last : last + 1, 2 * width : 3 * width] = jnp.sum(low_v.astype(F32), 0, keepdims=True)
     vector_sums = sums[...]
     block = blocks.shape[1]
-    pair = split_pair(vector_sums)
+    pair = vector_sums.astype(LOW)
     count = keep_o.shape[0]
     for index in range(count):
         send_o[index, :block] = blocks[block_of(2 * count, index + count)].astype(LOW)
         send_o[index, block:] = pair
     for index in range(count):
         keep_o[index, :block] = blocks[block_of(2 * count, index)]
-        keep_o[index, block : block + VECTOR_ROWS] = vector_sums
-        keep_o[index, block + VECTOR_ROWS :] = jnp.zeros_like(vector_sums)
+        keep_o[index, block:] = vector_sums
 
 
 def token_back(gq, gk, gv, w_qkv, *outs):
@@ -469,15 +473,13 @@
 
 
 def merged_vectors(keep, received, index, at, block):
-    high = received[at, block : block + VECTOR_ROWS].astype(F32)
-    low = received[at, block + VECTOR_ROWS :].astype(F32)
-    return keep[index, block : block + VECTOR_ROWS] + high + low
+    return keep[index, block:] + received[at, block:].astype(F32)
 
 
 def merge_attn(part_count, keep, *refs):
     parts, (*sends, keep_o) = refs[:part_count], refs[part_count:]
     count = keep_o.shape[0]
-    block = keep_o.shape[1] - PAIR_ROWS
+    block = keep_o.shape[1] - EXTRA_ROWS
     each = parts[0].shape[0]
 
     def weights_at(index):
@@ -491,20 +493,18 @@
         sent = weights_at(count + index).astype(LOW)
         if len(sends) == 1:
             sends[0][index, :block] = sent
-            sends[0][index, block:] = split_pair(vectors_at(count + index))
+            sends[0][index, block:] = vectors_at(count + index).astype(LOW)
         else:
             first = sends[0].shape[1]
             sends[0][index] = sent[:first]
             sends[1][index, : block - first] = sent[first:]
-            sends[1][index, block - first :] = split_pair(vectors_at(count + index))
+            sends[1][index, block - first :] = vectors_at(count + index).astype(LOW)
     for index in range(count):
         keep_o[index, :block] = weights_at(index)
-        vectors = vectors_at(index)
-        keep_o[index, block : block + VECTOR_ROWS] = vectors
-        keep_o[index, block + VECTOR_ROWS :] = jnp.zeros_like(vectors)
-
-
-def merge_last_attn(keep, first, second, qkv_o, out_o, vectors_o, pair_o):
+        keep_o[index, block:] = vectors_at(index)
+
+
+def merge_last_attn(keep, first, second, qkv_o, out_o, pair_o, *vectors_o):
     block, width = qkv_o.shape[1], qkv_o.shape[2]
     rows = first.shape[1]
     received = jnp.concatenate([first[0].astype(F32), second[0, : block - rows].astype(F32)], 0)
@@ -512,12 +512,12 @@
     for part in range(3):
         qkv_o[part] = total[:, part * width : (part + 1) * width]
     out_o[...] = total[:, 3 * width :].T
-    high = second[0, block - rows : block - rows + VECTOR_ROWS].astype(F32)
-    low = second[0, block - rows + VECTOR_ROWS :].astype(F32)
-    vectors = keep[0, block : block + VECTOR_ROWS] + high + low
+    vectors = keep[0, block:] + second[0, block - rows :].astype(F32)
     model = vectors.shape[1]
     me = lax.axis_index("dp")
-    vectors_o[...] = pltpu.roll(vectors, lax.rem(model - me * block, model), 1)[:, :block]
+    mine = pltpu.roll(vectors, lax.rem(model - me * block, model), 1)
+    for index, vector_o in enumerate(vectors_o):
+        vector_o[...] = mine[index, :block]
     small = pair_o.shape[1]
     turned = pltpu.roll(vectors, lax.rem(model - me * small, model), 1)
     last = VECTOR_ROWS - 1
@@ -618,7 +618,7 @@
         hold,
         [(array.shape, array.dtype, name) for name, array in held.items()],
         *held.values(),
-        scratch=[pltpu.SemaphoreType.DMA((len(held),))], loose=True,
+        scratch=[pltpu.SemaphoreType.DMA((len(held),))], loose=range(len(held)),
     )
 
     last = CHUNKS - 1
@@ -700,7 +700,10 @@
 
     grad_attn, sums = state.call(
         norm_one_back,
-        [((half, model), LOW), ((VECTOR_ROWS, model), F32), ((half, model), F32, (H_LAST,))],
+        [
+            ((half + PAIR_ROWS, model), LOW), ((VECTOR_ROWS, model), F32),
+            ((half, model), F32, (H_LAST,)),
+        ],
         received, (H_PACKED,),
         *[
             (name, c) for c in chunks for name in (H_BACK, H_RESID, H_NORMED, H_INVERSE, H_SUMS)
@@ -709,7 +712,6 @@
     for c in chunks:
         state.drop((H_BACK, c), (H_RESID, c), (H_NORMED, c), (H_INVERSE, c), (H_SUMS, c))
     grad_attn_other = to_core(grad_attn)
-    sums_other = to_core(sums)
 
     running = {(H_DOWN_KEEP,): (down_got, 1), (H_UP_KEEP,): (up_got, 1)}
     finished = {}
@@ -727,17 +729,17 @@
                 if attn and step == steps - 1:
                     sends = [
                         (kept[:1] + (rows_of,) + kept[2:], LOW)
-                        for rows_of in (block // 2, block - block // 2 + PAIR_ROWS)
+                        for rows_of in (block // 2, block - block // 2 + EXTRA_ROWS)
                     ]
                 kernel = partial(merge_attn, len(got)) if attn else merge_weights
                 given = len(sends) + 1
                 outs += sends + [(kept, F32, (H_NEXT, name))]
             elif attn:
-                kernel, given = merge_last_attn, 4
+                kernel, given = merge_last_attn, 3 + VECTOR_ROWS - 1
                 outs += [
-                    ((3, block, width), F32), ((width, block), F32),
-                    ((VECTOR_ROWS, block), F32), ((2, width // dp_size), F32),
+                    ((3, block, width), F32), ((width, block), F32), ((2, width // dp_size), F32),
                 ]
+                outs += [((block,), F32)] * (VECTOR_ROWS - 1)
             else:
                 kernel, given = merge_last_weights, 1
                 outs += [(shape, F32)]
@@ -754,7 +756,8 @@
                     [to_dp(part, step, dp_size, tensor_size) for part in sent], step + 1
                 )
             elif name == (H_ATTN_KEEP,):
-                finished[name], results = results[:4], results[4:]
+                given = 3 + VECTOR_ROWS - 1
+                finished[name], results = results[:given], results[given:]
             else:
                 finished[name] = results.pop(0)
 
@@ -763,11 +766,11 @@
     attn_w_send, grad_q, grad_k, grad_v = state.call(
         attn_backward,
         [
-            ((count, block + PAIR_ROWS, model), LOW),
-            ((count, block + PAIR_ROWS, model), F32, (H_ATTN_KEEP,)),
+            ((count, block + EXTRA_ROWS, model), LOW),
+            ((count, block + EXTRA_ROWS, model), F32, (H_ATTN_KEEP,)),
         ]
         + [((rows, width), LOW)] * 3,
-        lengths, grad_attn, grad_attn_other, sums, sums_other,
+        lengths, grad_attn, grad_attn_other, sums,
         (H_W_OUT,), (H_SAVED,), (H_TOKENS,), (H_SUM_DOWN,), (H_SUM_UP,),
         scratch=[
             pltpu.VMEM((rows, model), LOW),
@@ -779,7 +782,6 @@
     state.drop((H_SAVED,), (H_SUM_DOWN,), (H_SUM_UP,), (H_W_OUT,), (H_TOKENS,))
     state.drop((H_PACKED,), (H_PACKED_OTHER,))
     running_attn = ([to_dp(attn_w_send, 0, dp_size, tensor_size)], 1)
-    advance((H_UP_KEEP,), (H_DOWN_KEEP,))
     *token_parts, token_keep = state.call(
         token_back,
         [((half // PIECES, model), LOW)] * PIECES + [((half, model), F32)],
@@ -787,6 +789,7 @@
     )
     state.drop((H_W_QKV,))
     token_other = [to_core(part) for part in token_parts]
+    advance((H_UP_KEEP,), (H_DOWN_KEEP,))
     (token_own,) = state.call(add_rows, [((half, model), LOW)], token_keep, *token_other)
     token_received = to_chip(token_own)
     running[(H_ATTN_KEEP,)] = running_attn
@@ -810,7 +813,7 @@
     )
     advance(*[name for name in others if name in running], (H_ATTN_KEEP,))
     sum_w_down, sum_w_up = finished[(H_DOWN_KEEP,)], finished[(H_UP_KEEP,)]
-    sum_w_qkv, sum_w_out, mine, sum_bias_qv = finished[(H_ATTN_KEEP,)]
+    sum_w_qkv, sum_w_out, sum_bias_qv, *mine = finished[(H_ATTN_KEEP,)]
     return (
         output_low,
         token_total,

time: 97.8 us -> 94.5 us (0.966)
  waiting for transfers between devices: 32.4 us -> 27.7 us
  starting transfers between devices: 27.4 us -> 29.3 us
    ppermute x11, waiting for transfers between devices: 19.4 us -> 16.4 us  [to_dp(): return lax.ppermute(block, ('dp', 'tensor'), pairs)]
    ppermute x16 -> x17, waiting for transfers between devices: 5.4 us -> 3.78 us  [to_core(): return lax.ppermute(block, 'tensor', CORE_PAIRS)]
    ppermute x11, starting transfers between devices: 16 us -> 17.5 us  [to_dp(): return lax.ppermute(block, ('dp', 'tensor'), pairs)]
    ppermute x16 -> x17, starting transfers between devices: 3.46 us -> 3.89 us  [to_core(): return lax.ppermute(block, 'tensor', CORE_PAIRS)]
  transfers between devices with their start and end apart: 33 -> 34, of which waited for: 17 -> 18; matrix products, arithmetic and copies ran while one was open for 0% -> 0% of each run, Pallas kernels for 25% -> 25%
where the time goes in v5:
time: 94.5 us; the launch traced here: 94.1 us
  starting transfers between devices  29.3 us (31%)
  waiting for transfers between devices  27.7 us (29%)
  Pallas kernels  27.6 us (29%)
  local copies, waits for them, and re-layouts  7.75 us (8%)
  between operations  1.67 us (2%)
    pallas_call x22, Pallas kernels, call(): pl.pallas_call(body, name=getattr(kernel, 'func', kernel).__name__, out_s...  27.6 us
    ppermute x11, starting transfers between devices, to_dp(): return lax.ppermute(block, ('dp', 'tensor'), pairs)  17.5 us
    ppermute x11, waiting for transfers between devices, to_dp(): return lax.ppermute(block, ('dp', 'tensor'), pairs)  16.4 us
    ppermute x6, starting transfers between devices, to_chip(): return lax.ppermute(block, 'tensor', CHIP_PAIRS)  7.88 us
    unnamed x34, local copies, waits for them, and re-layouts  7.67 us
    ppermute x6, waiting for transfers between devices, to_chip(): return lax.ppermute(block, 'tensor', CHIP_PAIRS)  7.59 us
    ppermute x17, starting transfers between devices, to_core(): return lax.ppermute(block, 'tensor', CORE_PAIRS)  3.89 us
    ppermute x17, waiting for transfers between devices, to_core(): return lax.ppermute(block, 'tensor', CORE_PAIRS)  3.78 us
  transfers between devices with their start and end apart: 34, of which 18 were waited for; matrix products, arithmetic and copies ran while one was open for 0% of the time, Pallas kernels for 25%

profile of v5, /device:TPU:0, one launch (start us, length us, event | category | flops | bytes accessed | tf_op | source)
XLA Modules:
  0.0 94.1 jit_solution(14801011380831255361)
XLA Ops:
  1.9 1.2 %copy-done = bf16[3,768,192]{1,2,0:T(8,128)(2,1)S(1)} copy-done((bf16[3,768,192]{1,2,0:T(8,128)(2,1)S(1)}, bf16[3,768,192]{1,2,0:T(8,128)(2,1)}, u32[]{:S(2)}) %copy-start) | copy-done | bytes 884760
  5.8 2.8 %attn_forward.1 = (bf16[4,512,192]{2,1,0:T(8,128)(2,1)S(1)}, bf16[256,768]{1,0:T(8,128)(2,1)S(1)}, f32[256,768]{1,0:T(8,128)S(1)}) custom-call(s32[1]{0:T(128)S(6)} %copy.493.refs_0_, bf16[512,768]{1,0:T(8,128)(2,1)S(1)} %copy-done.2, bf16[3,192,768]{2,1,0:T(8,128)(2,1)S(1)} %bitcast.2, f32[2,192]{1,0:T(2,128)S(1)} %copy-done.9, bf16[192,768]{1,0:T(8,128)(2,1)S(1)} %copy-done.6), custom_call_target="tpu_custom_call" | custom-call | tf_op jit(solution)/shard_map/attn_forward/pallas_call | solution.py:121
  9.3 1.3 %collective-permute-done.refs_1_ = bf16[256,768]{1,0:T(8,128)(2,1)S(1)} collective-permute-done((bf16[256,768]{1,0:T(8,128)(2,1)S(1)}, bf16[256,768]{1,0:T(8,128)(2,1)S(1)}, u32[]{:S(2)}, u32[]{:S(2)}) %collective-permute-start) | collective-permute-done | bytes 393248 | tf_op jit(solution)/shard_map/ppermute | solution.py:541
  11.4 2.9 %collective-permute-start.2 = (bf16[128,768]{1,0:T(8,128)(2,1)}, bf16[128,768]{1,0:T(8,128)(2,1)}, u32[]{:S(2)}, u32[]{:S(2)}) collective-permute-start(bf16[128,768]{1,0:T(8,128)(2,1)} %get-tuple-element.299), channel_id=1, source_target_pairs={{0,2},{1,3},{2,0},{3,1},{4,6},{5,7},{6,4},{7,5},{8,10},{9,11},{10,... | collective-permute-start | bytes 589832 | tf_op jit(solution)/shard_map/ppermute | solution.py:545
  14.6 1.2 %collective-permute-done.5.refs_9_ = f32[8,768]{1,0:T(8,128)S(1)} collective-permute-done((f32[8,768]{1,0:T(8,128)S(1)}, f32[8,768]{1,0:T(8,128)S(1)}, u32[]{:S(2)}, u32[]{:S(2)}) %collective-permute-start.5) | collective-permute-done | bytes 24608 | tf_op jit(solution)/shard_map/ppermute | solution.py:541
  15.8 1.3 %copy-done.4 = bf16[768,768]{1,0:T(8,128)(2,1)S(1)} copy-done((bf16[768,768]{1,0:T(8,128)(2,1)S(1)}, bf16[768,768]{1,0:T(8,128)(2,1)}, u32[]{:S(2)}) %copy-start.4) | copy-done | bytes 1179672
  17.1 1.3 %copy-done.5 = bf16[768,768]{1,0:T(8,128)(2,1)S(1)} copy-done((bf16[768,768]{1,0:T(8,128)(2,1)S(1)}, bf16[768,768]{1,0:T(8,128)(2,1)}, u32[]{:S(2)}) %copy-start.5) | copy-done | bytes 1179672
  18.4 1.1 %copy-done.8 = bf16[512,768]{1,0:T(8,128)(2,1)S(1)} copy-done((bf16[512,768]{1,0:T(8,128)(2,1)S(1)}, bf16[512,768]{1,0:T(8,128)(2,1)}, u32[]{:S(2)}) %copy-start.8) | copy-done | bytes 786456
  19.5 2.4 %hold.1 = (bf16[512,768]{1,0:T(8,128)(2,1)S(1)}, bf16[192,768]{1,0:T(8,128)(2,1)S(1)}, bf16[3,192,768]{2,1,0:T(8,128)(2,1)S(1)}, bf16[512,768]{1,0:T(8,128)(2,1)...) custom-call(bf16[512,768]{1,0:T(8,128)(2,1)S(1)} %copy-done.3, ...), custom_call_target="tpu_custom_call", output_to_operand_aliasing={{10}: (10, {}), {11}: (11, {}), {12}: (12, {})} | custom-call | tf_op jit(solution)/shard_map/hold/pallas_call | solution.py:121
  21.9 2.2 %mlp_forward.2 = (bf16[128,768]{1,0:T(8,128)(2,1)S(1)}, bf16[128,768]{1,0:T(8,128)(2,1)S(1)}, bf16[128,768]{1,0:T(8,128)(2,1)S(1)}, bf16[128,768]{1,0:T(8,128)(2...) custom-call(bf16[128,768]{1,0:T(8,128)(2,1)} %collective-permute-don, ...), custom_call_target="tpu_custom_call", output_to_operand_aliasing={{9}: (1, {}), {10}: (2, {}), {11}: (3, {}), {12}: (4, {}), ... | custom-call | tf_op jit(solution)/shard_map/mlp_forward/pallas_call | solution.py:121
  24.2 2.1 %collective-permute-start.7 = (bf16[128,768]{1,0:T(8,128)(2,1)S(1)}, bf16[128,768]{1,0:T(8,128)(2,1)S(1)}, u32[]{:S(2)}, u32[]{:S(2)}) collective-permute-start(bf16[128,768]{1,0:T(8,128)(2,1)S(1)} %get-tuple-element.335), channel_id=1, source_target_pairs={{0,2},{1,3},{2,0},{3,1},{4,6},{5,7},{6,4},{7,5},{8,10},{9,11},{10,... | collective-permute-start | bytes 589832 | tf_op jit(solution)/shard_map/ppermute | solution.py:545
  26.3 2.2 %mlp_forward.3 = (bf16[128,768]{1,0:T(8,128)(2,1)S(1)}, bf16[128,768]{1,0:T(8,128)(2,1)S(1)}, bf16[128,768]{1,0:T(8,128)(2,1)S(1)}, bf16[128,768]{1,0:T(8,128)(2...) custom-call(bf16[128,768]{1,0:T(8,128)(2,1)} %collective-permute-don, ...), custom_call_target="tpu_custom_call", output_to_operand_aliasing={{9}: (1, {}), {10}: (2, {}), {11}: (3, {}), {12}: (4, {}), ... | custom-call | tf_op jit(solution)/shard_map/mlp_forward/pallas_call | solution.py:121
  28.6 3.3 %collective-permute-done.7.refs_1_ = bf16[128,768]{1,0:T(8,128)(2,1)S(1)} collective-permute-done((bf16[128,768]{1,0:T(8,128)(2,1)S(1)}, bf16[128,768]{1,0:T(8,128)(2,1)S(1)}, u32[]{:S(2)}, u32[]{:S(2)}) %collective-permute-start.7) | collective-permute-done | bytes 196640 | tf_op jit(solution)/shard_map/ppermute | solution.py:545
  31.9 2.2 %mlp_backward.2 = (bf16[128,768]{1,0:T(8,128)(2,1)S(1)}, bf16[128,768]{1,0:T(8,128)(2,1)S(1)}, bf16[128,768]{1,0:T(8,128)(2,1)S(1)}, bf16[128,768]{1,0:T(8,128)(...) custom-call(s32[1]{0:T(128)S(6)} %copy.493.refs_0_, ...), custom_call_target="tpu_custom_call", output_to_operand_aliasing={{7}: (2, {}), {8}: (3, {}), {9}: (4, {}), {10}: (5, {}), {1... | custom-call | tf_op jit(solution)/shard_map/mlp_backward/pallas_call | solution.py:121
  34.0 1.7 %collective-permute-done.6.refs_1_ = bf16[128,768]{1,0:T(8,128)(2,1)S(1)} collective-permute-done((bf16[128,768]{1,0:T(8,128)(2,1)S(1)}, bf16[128,768]{1,0:T(8,128)(2,1)S(1)}, u32[]{:S(2)}, u32[]{:S(2)}) %collective-permute-start.6) | collective-permute-done | bytes 196640 | tf_op jit(solution)/shard_map/ppermute | solution.py:545
  35.7 2.7 %mlp_backward.3 = (bf16[128,768]{1,0:T(8,128)(2,1)S(1)}, bf16[128,768]{1,0:T(8,128)(2,1)S(1)}, bf16[128,768]{1,0:T(8,128)(2,1)S(1)}, bf16[128,768]{1,0:T(8,128)(...) custom-call(s32[1]{0:T(128)S(6)} %copy.493.refs_0_, ...), custom_call_target="tpu_custom_call", output_to_operand_aliasing={{11}: (2, {}), {12}: (3, {}), {13}: (4, {}), {14}: (5, {}),... | custom-call | tf_op jit(solution)/shard_map/mlp_backward/pallas_call | solution.py:121
  39.5 1.7 %collective-permute-start.8 = (bf16[256,768]{1,0:T(8,128)(2,1)S(1)}, bf16[256,768]{1,0:T(8,128)(2,1)S(1)}, u32[]{:S(2)}, u32[]{:S(2)}) collective-permute-start(bf16[256,768]{1,0:T(8,128)(2,1)S(1)} %get-tuple-element.387), channel_id=1, source_target_pairs={{0,2},{1,3},{2,0},{3,1},{4,6},{5,7},{6,4},{7,5},{8,10},{9,11},{10,... | collective-permute-start | bytes 1179656 | tf_op jit(solution)/shard_map/ppermute | solution.py:545
  43.2 1.5 %collective-permute-start.17 = (bf16[2,96,768]{2,1,0:T(8,128)(2,1)S(1)}, bf16[2,96,768]{2,1,0:T(8,128)(2,1)S(1)}, u32[]{:S(2)}, u32[]{:S(2)}) collective-permute-start(bf16[2,96,768]{2,1,0:T(8,128)(2,1)S(1)} %get-tuple-element.467), channel_id=1, source_target_pairs={{0,4},{1,9},{2,6},{3,11},{4,0},{5,13},{6,2},{7,15},{8,12},{9,1},{1... | collective-permute-start | bytes 884744 | tf_op jit(solution)/shard_map/ppermute | solution.py:561
  46.2 1.6 %collective-permute-start.24 = (bf16[4,96,768]{2,1,0:T(8,128)(2,1)S(1)}, bf16[4,96,768]{2,1,0:T(8,128)(2,1)S(1)}, u32[]{:S(2)}, u32[]{:S(2)}) collective-permute-start(bf16[4,96,768]{2,1,0:T(8,128)(2,1)S(1)} %get-tuple-element.511), channel_id=1, source_target_pairs={{0,4},{1,9},{2,6},{3,11},{4,0},{5,13},{6,2},{7,15},{8,12},{9,1},{1... | collective-permute-start | bytes 1769480 | tf_op jit(solution)/shard_map/ppermute | solution.py:561
  47.8 2.7 %collective-permute-done.8.refs_0_ = bf16[256,768]{1,0:T(8,128)(2,1)S(1)} collective-permute-done((bf16[256,768]{1,0:T(8,128)(2,1)S(1)}, bf16[256,768]{1,0:T(8,128)(2,1)S(1)}, u32[]{:S(2)}, u32[]{:S(2)}) %collective-permute-start.8) | collective-permute-done | bytes 393248 | tf_op jit(solution)/shard_map/ppermute | solution.py:545
  51.2 1.9 %collective-permute-done.18.refs_1_ = bf16[2,96,768]{2,1,0:T(8,128)(2,1)S(1)} collective-permute-done((bf16[2,96,768]{2,1,0:T(8,128)(2,1)S(1)}, bf16[2,96,768]{2,1,0:T(8,128)(2,1)S(1)}, u32[]{:S(2)}, u32[]{:S(2)}) %collective-permute-start.18) | collective-permute-done | bytes 294944 | tf_op jit(solution)/shard_map/ppermute | solution.py:561
  53.2 1.7 %collective-permute-start.25 = (bf16[2,96,768]{2,1,0:T(8,128)(2,1)S(1)}, bf16[2,96,768]{2,1,0:T(8,128)(2,1)S(1)}, u32[]{:S(2)}, u32[]{:S(2)}) collective-permute-start(bf16[2,96,768]{2,1,0:T(8,128)(2,1)S(1)} %get-tuple-element.512), channel_id=1, source_target_pairs={{0,8},{1,5},{2,10},{3,7},{4,12},{5,1},{6,14},{7,3},{8,0},{9,13},{1... | collective-permute-start | bytes 884744 | tf_op jit(solution)/shard_map/ppermute | solution.py:561
  54.9 4.6 %attn_backward.1 = (bf16[4,104,768]{2,1,0:T(8,128)(2,1)S(1)}, f32[4,104,768]{2,1,0:T(8,128)S(1)}, bf16[512,192]{1,0:T(8,128)(2,1)S(1)}, bf16[512,192]{1,0:T(8,12...) custom-call(s32[1]{0:T(128)S(6)} %copy.493.refs_0_, ...), custom_call_target="tpu_custom_call", output_to_operand_aliasing={{5}: (4, {}), {6}: (5, {}), {7}: (6, {}), {8}: (7, {}), {9}... | custom-call | tf_op jit(solution)/shard_map/attn_backward/pallas_call | solution.py:121
  59.5 1.6 %collective-permute-start.19 = (bf16[4,104,768]{2,1,0:T(8,128)(2,1)S(1)}, bf16[4,104,768]{2,1,0:T(8,128)(2,1)S(1)}, u32[]{:S(2)}, u32[]{:S(2)}) collective-permute-start(bf16[4,104,768]{2,1,0:T(8,128)(2,1)S(1)} %get-tuple-element.495), channel_id=1, source_target_pairs={{0,4},{1,9},{2,6},{3,11},{4,0},{5,13},{6,2},{7,15},{8,12},{9,1},{1... | collective-permute-start | bytes 1916936 | tf_op jit(solution)/shard_map/ppermute | solution.py:561
  65.0 1.6 %collective-permute-start.29 = (bf16[2,96,768]{2,1,0:T(8,128)(2,1)S(1)}, bf16[2,96,768]{2,1,0:T(8,128)(2,1)S(1)}, u32[]{:S(2)}, u32[]{:S(2)}) collective-permute-start(bf16[2,96,768]{2,1,0:T(8,128)(2,1)S(1)} %get-tuple-element.534), channel_id=1, source_target_pairs={{0,8},{1,5},{2,10},{3,7},{4,12},{5,1},{6,14},{7,3},{8,0},{9,13},{1... | collective-permute-start | bytes 884744 | tf_op jit(solution)/shard_map/ppermute | solution.py:561
  66.6 2.6 %collective-permute-start.28 = (bf16[1,96,768]{2,1,0:T(8,128)(2,1)S(1)}, bf16[1,96,768]{2,1,0:T(8,128)(2,1)S(1)}, u32[]{:S(2)}, u32[]{:S(2)}) collective-permute-start(bf16[1,96,768]{2,1,0:T(8,128)(2,1)S(1)} %get-tuple-element.533), channel_id=1, source_target_pairs={{0,16},{1,17},{2,18},{3,19},{4,20},{5,21},{6,22},{7,23},{8,24},{9,... | collective-permute-start | bytes 442376 | tf_op jit(solution)/shard_map/ppermute | solution.py:561
  69.2 3.0 %collective-permute-done.19.refs_0_ = bf16[4,104,768]{2,1,0:T(8,128)(2,1)S(1)} collective-permute-done((bf16[4,104,768]{2,1,0:T(8,128)(2,1)S(1)}, bf16[4,104,768]{2,1,0:T(8,128)(2,1)S(1)}, u32[]{:S(2)}, u32[]{:S(2)}) %collective-permute-start.19) | collective-permute-done | bytes 639008 | tf_op jit(solution)/shard_map/ppermute | solution.py:561
  73.0 1.6 %collective-permute-done.28.refs_0_ = bf16[1,96,768]{2,1,0:T(8,128)(2,1)S(1)} collective-permute-done((bf16[1,96,768]{2,1,0:T(8,128)(2,1)S(1)}, bf16[1,96,768]{2,1,0:T(8,128)(2,1)S(1)}, u32[]{:S(2)}, u32[]{:S(2)}) %collective-permute-start.28) | collective-permute-done | bytes 147488 | tf_op jit(solution)/shard_map/ppermute | solution.py:561
  75.9 2.7 %collective-permute-start.31 = (bf16[1,96,768]{2,1,0:T(8,128)(2,1)S(1)}, bf16[1,96,768]{2,1,0:T(8,128)(2,1)S(1)}, u32[]{:S(2)}, u32[]{:S(2)}) collective-permute-start(bf16[1,96,768]{2,1,0:T(8,128)(2,1)S(1)} %get-tuple-element.559), channel_id=1, source_target_pairs={{0,16},{1,17},{2,18},{3,19},{4,20},{5,21},{6,22},{7,23},{8,24},{9,... | collective-permute-start | bytes 442376 | tf_op jit(solution)/shard_map/ppermute | solution.py:561
  79.4 2.7 %collective-permute-start.33 = (bf16[1,56,768]{2,1,0:T(8,128)(2,1)S(1)}, bf16[1,56,768]{2,1,0:T(8,128)(2,1)S(1)}, u32[]{:S(2)}, u32[]{:S(2)}) collective-permute-start(bf16[1,56,768]{2,1,0:T(8,128)(2,1)S(1)} %get-tuple-element.561), channel_id=1, source_target_pairs={{0,16},{1,17},{2,18},{3,19},{4,20},{5,21},{6,22},{7,23},{8,24},{9,... | collective-permute-start | bytes 258056 | tf_op jit(solution)/shard_map/ppermute | solution.py:561
  84.3 5.8 %collective-permute-done.31.refs_0_ = bf16[1,96,768]{2,1,0:T(8,128)(2,1)S(1)} collective-permute-done((bf16[1,96,768]{2,1,0:T(8,128)(2,1)S(1)}, bf16[1,96,768]{2,1,0:T(8,128)(2,1)S(1)}, u32[]{:S(2)}, u32[]{:S(2)}) %collective-permute-start.31) | collective-permute-done | bytes 147488 | tf_op jit(solution)/shard_map/ppermute | solution.py:561
  90.1 3.0 %collective-permute-done.32.refs_1_ = bf16[1,48,768]{2,1,0:T(8,128)(2,1)S(1)} collective-permute-done((bf16[1,48,768]{2,1,0:T(8,128)(2,1)S(1)}, bf16[1,48,768]{2,1,0:T(8,128)(2,1)S(1)}, u32[]{:S(2)}, u32[]{:S(2)}) %collective-permute-start.32) | collective-permute-done | bytes 73760 | tf_op jit(solution)/shard_map/ppermute | solution.py:561
  (100 shorter events, 20.5 us)
Async XLA Ops:
  0.6 15.1 %collective-permute-start.3 = (bf16[768,768]{1,0:T(8,128)(2,1)}, bf16[768,768]{1,0:T(8,128)(2,1)}, u32[]{:S(2)}, u32[]{:S(2)}) collective-permute-start(bf16[768,768]{1,0:T(8,128)(2,1)} %refs_4_.3), channel_id=1, source_target_pairs={{0,1},{1,0},{2,3},{3,2},{4,5},{5,4},{6,7},{7,6},{8,9},{9,8},{10,11... | collective-permute-start | bytes 3538952 | tf_op jit(solution)/shard_map/ppermute | solution.py:541
  1.2 14.6 %collective-permute-start.4 = (bf16[768,768]{1,0:T(8,128)(2,1)}, bf16[768,768]{1,0:T(8,128)(2,1)}, u32[]{:S(2)}, u32[]{:S(2)}) collective-permute-start(bf16[768,768]{1,0:T(8,128)(2,1)} %refs_6_.1), channel_id=1, source_target_pairs={{0,1},{1,0},{2,3},{3,2},{4,5},{5,4},{6,7},{7,6},{8,9},{9,8},{10,11... | collective-permute-start | bytes 3538952 | tf_op jit(solution)/shard_map/ppermute | solution.py:541
  8.8 1.8 %collective-permute-start = (bf16[256,768]{1,0:T(8,128)(2,1)S(1)}, bf16[256,768]{1,0:T(8,128)(2,1)S(1)}, u32[]{:S(2)}, u32[]{:S(2)}) collective-permute-start(bf16[256,768]{1,0:T(8,128)(2,1)S(1)} %get-tuple-element.296), channel_id=1, source_target_pairs={{0,1},{1,0},{2,3},{3,2},{4,5},{5,4},{6,7},{7,6},{8,9},{9,8},{10,11... | collective-permute-start | bytes 1179656 | tf_op jit(solution)/shard_map/ppermute | solution.py:541
  11.4 10.5 %collective-permute-start.2 = (bf16[128,768]{1,0:T(8,128)(2,1)}, bf16[128,768]{1,0:T(8,128)(2,1)}, u32[]{:S(2)}, u32[]{:S(2)}) collective-permute-start(bf16[128,768]{1,0:T(8,128)(2,1)} %get-tuple-element.299), channel_id=1, source_target_pairs={{0,2},{1,3},{2,0},{3,1},{4,6},{5,7},{6,4},{7,5},{8,10},{9,11},{10,... | collective-permute-start | bytes 589832 | tf_op jit(solution)/shard_map/ppermute | solution.py:545
  14.3 12.0 %collective-permute-start.1 = (bf16[128,768]{1,0:T(8,128)(2,1)}, bf16[128,768]{1,0:T(8,128)(2,1)}, u32[]{:S(2)}, u32[]{:S(2)}) collective-permute-start(bf16[128,768]{1,0:T(8,128)(2,1)} %get-tuple-element.298), channel_id=1, source_target_pairs={{0,2},{1,3},{2,0},{3,1},{4,6},{5,7},{6,4},{7,5},{8,10},{9,11},{10,... | collective-permute-start | bytes 589832 | tf_op jit(solution)/shard_map/ppermute | solution.py:545
  24.2 7.7 %collective-permute-start.7 = (bf16[128,768]{1,0:T(8,128)(2,1)S(1)}, bf16[128,768]{1,0:T(8,128)(2,1)S(1)}, u32[]{:S(2)}, u32[]{:S(2)}) collective-permute-start(bf16[128,768]{1,0:T(8,128)(2,1)S(1)} %get-tuple-element.335), channel_id=1, source_target_pairs={{0,2},{1,3},{2,0},{3,1},{4,6},{5,7},{6,4},{7,5},{8,10},{9,11},{10,... | collective-permute-start | bytes 589832 | tf_op jit(solution)/shard_map/ppermute | solution.py:545
  28.5 7.2 %collective-permute-start.6 = (bf16[128,768]{1,0:T(8,128)(2,1)S(1)}, bf16[128,768]{1,0:T(8,128)(2,1)S(1)}, u32[]{:S(2)}, u32[]{:S(2)}) collective-permute-start(bf16[128,768]{1,0:T(8,128)(2,1)S(1)} %get-tuple-element.334), channel_id=1, source_target_pairs={{0,2},{1,3},{2,0},{3,1},{4,6},{5,7},{6,4},{7,5},{8,10},{9,11},{10,... | collective-permute-start | bytes 589832 | tf_op jit(solution)/shard_map/ppermute | solution.py:545
  38.4 3.3 %collective-permute-start.12 = (bf16[256,768]{1,0:T(8,128)(2,1)S(1)}, bf16[256,768]{1,0:T(8,128)(2,1)S(1)}, u32[]{:S(2)}, u32[]{:S(2)}) collective-permute-start(bf16[256,768]{1,0:T(8,128)(2,1)S(1)} %get-tuple-element.391), channel_id=1, source_target_pairs={{0,1},{1,0},{2,3},{3,2},{4,5},{5,4},{6,7},{7,6},{8,9},{9,8},{10,11... | collective-permute-start | bytes 1179656 | tf_op jit(solution)/shard_map/ppermute | solution.py:541
  38.4 2.8 %collective-permute-start.13 = (bf16[128,768]{1,0:T(8,128)(2,1)S(1)}, bf16[128,768]{1,0:T(8,128)(2,1)S(1)}, u32[]{:S(2)}, u32[]{:S(2)}) collective-permute-start(bf16[128,768]{1,0:T(8,128)(2,1)S(1)} %get-tuple-element.392), channel_id=1, source_target_pairs={{0,1},{1,0},{2,3},{3,2},{4,5},{5,4},{6,7},{7,6},{8,9},{9,8},{10,11... | collective-permute-start | bytes 589832 | tf_op jit(solution)/shard_map/ppermute | solution.py:541
  38.9 2.3 %collective-permute-start.14 = (bf16[128,768]{1,0:T(8,128)(2,1)S(1)}, bf16[128,768]{1,0:T(8,128)(2,1)S(1)}, u32[]{:S(2)}, u32[]{:S(2)}) collective-permute-start(bf16[128,768]{1,0:T(8,128)(2,1)S(1)} %get-tuple-element.393), channel_id=1, source_target_pairs={{0,1},{1,0},{2,3},{3,2},{4,5},{5,4},{6,7},{7,6},{8,9},{9,8},{10,11... | collective-permute-start | bytes 589832 | tf_op jit(solution)/shard_map/ppermute | solution.py:541
  39.0 6.3 %collective-permute-start.11 = (bf16[256,768]{1,0:T(8,128)(2,1)S(1)}, bf16[256,768]{1,0:T(8,128)(2,1)S(1)}, u32[]{:S(2)}, u32[]{:S(2)}) collective-permute-start(bf16[256,768]{1,0:T(8,128)(2,1)S(1)} %get-tuple-element.390), channel_id=1, source_target_pairs={{0,1},{1,0},{2,3},{3,2},{4,5},{5,4},{6,7},{7,6},{8,9},{9,8},{10,11... | collective-permute-start | bytes 1179656 | tf_op jit(solution)/shard_map/ppermute | solution.py:541
  39.5 11.0 %collective-permute-start.8 = (bf16[256,768]{1,0:T(8,128)(2,1)S(1)}, bf16[256,768]{1,0:T(8,128)(2,1)S(1)}, u32[]{:S(2)}, u32[]{:S(2)}) collective-permute-start(bf16[256,768]{1,0:T(8,128)(2,1)S(1)} %get-tuple-element.387), channel_id=1, source_target_pairs={{0,2},{1,3},{2,0},{3,1},{4,6},{5,7},{6,4},{7,5},{8,10},{9,11},{10,... | collective-permute-start | bytes 1179656 | tf_op jit(solution)/shard_map/ppermute | solution.py:545
  41.2 9.3 %collective-permute-start.15 = (bf16[256,768]{1,0:T(8,128)(2,1)S(1)}, bf16[256,768]{1,0:T(8,128)(2,1)S(1)}, u32[]{:S(2)}, u32[]{:S(2)}) collective-permute-start(bf16[256,768]{1,0:T(8,128)(2,1)S(1)} %get-tuple-element.464.refs_21_), channel_id=1, source_target_pairs={{0,1},{1,0},{2,3},{3,2},{4,5},{5,4},{6,7},{7,6},{8,9},{9,8},{10,11... | collective-permute-start | bytes 1179656 | tf_op jit(solution)/shard_map/ppermute | solution.py:541
  41.2 2.0 %collective-permute-start.9 = (bf16[128,768]{1,0:T(8,128)(2,1)S(1)}, bf16[128,768]{1,0:T(8,128)(2,1)S(1)}, u32[]{:S(2)}, u32[]{:S(2)}) collective-permute-start(bf16[128,768]{1,0:T(8,128)(2,1)S(1)} %get-tuple-element.388), channel_id=1, source_target_pairs={{0,1},{1,0},{2,3},{3,2},{4,5},{5,4},{6,7},{7,6},{8,9},{9,8},{10,11... | collective-permute-start | bytes 589832 | tf_op jit(solution)/shard_map/ppermute | solution.py:541
  41.7 3.0 %collective-permute-start.10 = (bf16[128,768]{1,0:T(8,128)(2,1)S(1)}, bf16[128,768]{1,0:T(8,128)(2,1)S(1)}, u32[]{:S(2)}, u32[]{:S(2)}) collective-permute-start(bf16[128,768]{1,0:T(8,128)(2,1)S(1)} %get-tuple-element.389), channel_id=1, source_target_pairs={{0,1},{1,0},{2,3},{3,2},{4,5},{5,4},{6,7},{7,6},{8,9},{9,8},{10,11... | collective-permute-start | bytes 589832 | tf_op jit(solution)/shard_map/ppermute | solution.py:541
  43.2 8.0 %collective-permute-start.17 = (bf16[2,96,768]{2,1,0:T(8,128)(2,1)S(1)}, bf16[2,96,768]{2,1,0:T(8,128)(2,1)S(1)}, u32[]{:S(2)}, u32[]{:S(2)}) collective-permute-start(bf16[2,96,768]{2,1,0:T(8,128)(2,1)S(1)} %get-tuple-element.467), channel_id=1, source_target_pairs={{0,4},{1,9},{2,6},{3,11},{4,0},{5,13},{6,2},{7,15},{8,12},{9,1},{1... | collective-permute-start | bytes 884744 | tf_op jit(solution)/shard_map/ppermute | solution.py:561
  44.8 8.3 %collective-permute-start.18 = (bf16[2,96,768]{2,1,0:T(8,128)(2,1)S(1)}, bf16[2,96,768]{2,1,0:T(8,128)(2,1)S(1)}, u32[]{:S(2)}, u32[]{:S(2)}) collective-permute-start(bf16[2,96,768]{2,1,0:T(8,128)(2,1)S(1)} %get-tuple-element.468), channel_id=1, source_target_pairs={{0,4},{1,9},{2,6},{3,11},{4,0},{5,13},{6,2},{7,15},{8,12},{9,1},{1... | collective-permute-start | bytes 884744 | tf_op jit(solution)/shard_map/ppermute | solution.py:561
  46.2 16.4 %collective-permute-start.24 = (bf16[4,96,768]{2,1,0:T(8,128)(2,1)S(1)}, bf16[4,96,768]{2,1,0:T(8,128)(2,1)S(1)}, u32[]{:S(2)}, u32[]{:S(2)}) collective-permute-start(bf16[4,96,768]{2,1,0:T(8,128)(2,1)S(1)} %get-tuple-element.511), channel_id=1, source_target_pairs={{0,4},{1,9},{2,6},{3,11},{4,0},{5,13},{6,2},{7,15},{8,12},{9,1},{1... | collective-permute-start | bytes 1769480 | tf_op jit(solution)/shard_map/ppermute | solution.py:561
  51.1 3.8 %collective-permute-start.16 = (bf16[272,768]{1,0:T(8,128)(2,1)S(1)}, bf16[272,768]{1,0:T(8,128)(2,1)S(1)}, u32[]{:S(2)}, u32[]{:S(2)}) collective-permute-start(bf16[272,768]{1,0:T(8,128)(2,1)S(1)} %get-tuple-element.465.refs_1_), channel_id=1, source_target_pairs={{0,1},{1,0},{2,3},{3,2},{4,5},{5,4},{6,7},{7,6},{8,9},{9,8},{10,11... | collective-permute-start | bytes 1253384 | tf_op jit(solution)/shard_map/ppermute | solution.py:541
  53.2 9.2 %collective-permute-start.25 = (bf16[2,96,768]{2,1,0:T(8,128)(2,1)S(1)}, bf16[2,96,768]{2,1,0:T(8,128)(2,1)S(1)}, u32[]{:S(2)}, u32[]{:S(2)}) collective-permute-start(bf16[2,96,768]{2,1,0:T(8,128)(2,1)S(1)} %get-tuple-element.512), channel_id=1, source_target_pairs={{0,8},{1,5},{2,10},{3,7},{4,12},{5,1},{6,14},{7,3},{8,0},{9,13},{1... | collective-permute-start | bytes 884744 | tf_op jit(solution)/shard_map/ppermute | solution.py:561
  59.5 12.7 %collective-permute-start.19 = (bf16[4,104,768]{2,1,0:T(8,128)(2,1)S(1)}, bf16[4,104,768]{2,1,0:T(8,128)(2,1)S(1)}, u32[]{:S(2)}, u32[]{:S(2)}) collective-permute-start(bf16[4,104,768]{2,1,0:T(8,128)(2,1)S(1)} %get-tuple-element.495), channel_id=1, source_target_pairs={{0,4},{1,9},{2,6},{3,11},{4,0},{5,13},{6,2},{7,15},{8,12},{9,1},{1... | collective-permute-start | bytes 1916936 | tf_op jit(solution)/shard_map/ppermute | solution.py:561
  61.8 1.4 %collective-permute-start.20 = (bf16[64,768]{1,0:T(8,128)(2,1)S(1)}, bf16[64,768]{1,0:T(8,128)(2,1)S(1)}, u32[]{:S(2)}, u32[]{:S(2)}) collective-permute-start(bf16[64,768]{1,0:T(8,128)(2,1)S(1)} %get-tuple-element.507), channel_id=1, source_target_pairs={{0,1},{1,0},{2,3},{3,2},{4,5},{5,4},{6,7},{7,6},{8,9},{9,8},{10,11... | collective-permute-start | bytes 294920 | tf_op jit(solution)/shard_map/ppermute | solution.py:541
  61.9 1.4 %collective-permute-start.21 = (bf16[64,768]{1,0:T(8,128)(2,1)S(1)}, bf16[64,768]{1,0:T(8,128)(2,1)S(1)}, u32[]{:S(2)}, u32[]{:S(2)}) collective-permute-start(bf16[64,768]{1,0:T(8,128)(2,1)S(1)} %get-tuple-element.508), channel_id=1, source_target_pairs={{0,1},{1,0},{2,3},{3,2},{4,5},{5,4},{6,7},{7,6},{8,9},{9,8},{10,11... | collective-permute-start | bytes 294920 | tf_op jit(solution)/shard_map/ppermute | solution.py:541
  62.4 1.3 %collective-permute-start.22 = (bf16[64,768]{1,0:T(8,128)(2,1)S(1)}, bf16[64,768]{1,0:T(8,128)(2,1)S(1)}, u32[]{:S(2)}, u32[]{:S(2)}) collective-permute-start(bf16[64,768]{1,0:T(8,128)(2,1)S(1)} %get-tuple-element.509), channel_id=1, source_target_pairs={{0,1},{1,0},{2,3},{3,2},{4,5},{5,4},{6,7},{7,6},{8,9},{9,8},{10,11... | collective-permute-start | bytes 294920 | tf_op jit(solution)/shard_map/ppermute | solution.py:541
  64.0 11.7 %collective-permute-start.27 = (bf16[256,768]{1,0:T(8,128)(2,1)S(1)}, bf16[256,768]{1,0:T(8,128)(2,1)S(1)}, u32[]{:S(2)}, u32[]{:S(2)}) collective-permute-start(bf16[256,768]{1,0:T(8,128)(2,1)S(1)} %get-tuple-element.532.refs_0_), channel_id=1, source_target_pairs={{0,2},{1,3},{2,0},{3,1},{4,6},{5,7},{6,4},{7,5},{8,10},{9,11},{10,... | collective-permute-start | bytes 1179656 | tf_op jit(solution)/shard_map/ppermute | solution.py:545
  65.0 9.9 %collective-permute-start.29 = (bf16[2,96,768]{2,1,0:T(8,128)(2,1)S(1)}, bf16[2,96,768]{2,1,0:T(8,128)(2,1)S(1)}, u32[]{:S(2)}, u32[]{:S(2)}) collective-permute-start(bf16[2,96,768]{2,1,0:T(8,128)(2,1)S(1)} %get-tuple-element.534), channel_id=1, source_target_pairs={{0,8},{1,5},{2,10},{3,7},{4,12},{5,1},{6,14},{7,3},{8,0},{9,13},{1... | collective-permute-start | bytes 884744 | tf_op jit(solution)/shard_map/ppermute | solution.py:561
  66.6 8.0 %collective-permute-start.28 = (bf16[1,96,768]{2,1,0:T(8,128)(2,1)S(1)}, bf16[1,96,768]{2,1,0:T(8,128)(2,1)S(1)}, u32[]{:S(2)}, u32[]{:S(2)}) collective-permute-start(bf16[1,96,768]{2,1,0:T(8,128)(2,1)S(1)} %get-tuple-element.533), channel_id=1, source_target_pairs={{0,16},{1,17},{2,18},{3,19},{4,20},{5,21},{6,22},{7,23},{8,24},{9,... | collective-permute-start | bytes 442376 | tf_op jit(solution)/shard_map/ppermute | solution.py:561
  72.3 7.1 %collective-permute-start.26 = (bf16[2,104,768]{2,1,0:T(8,128)(2,1)S(1)}, bf16[2,104,768]{2,1,0:T(8,128)(2,1)S(1)}, u32[]{:S(2)}, u32[]{:S(2)}) collective-permute-start(bf16[2,104,768]{2,1,0:T(8,128)(2,1)S(1)} %get-tuple-element.531), channel_id=1, source_target_pairs={{0,8},{1,5},{2,10},{3,7},{4,12},{5,1},{6,14},{7,3},{8,0},{9,13},{1... | collective-permute-start | bytes 958472 | tf_op jit(solution)/shard_map/ppermute | solution.py:561
  75.8 7.5 %collective-permute-start.30 = (bf16[256,768]{1,0:T(8,128)(2,1)S(1)}, bf16[256,768]{1,0:T(8,128)(2,1)S(1)}, u32[]{:S(2)}, u32[]{:S(2)}) collective-permute-start(bf16[256,768]{1,0:T(8,128)(2,1)S(1)} %get-tuple-element.555.refs_0_), channel_id=1, source_target_pairs={{0,1},{1,0},{2,3},{3,2},{4,5},{5,4},{6,7},{7,6},{8,9},{9,8},{10,11... | collective-permute-start | bytes 1179656 | tf_op jit(solution)/shard_map/ppermute | solution.py:541
  75.9 14.2 %collective-permute-start.31 = (bf16[1,96,768]{2,1,0:T(8,128)(2,1)S(1)}, bf16[1,96,768]{2,1,0:T(8,128)(2,1)S(1)}, u32[]{:S(2)}, u32[]{:S(2)}) collective-permute-start(bf16[1,96,768]{2,1,0:T(8,128)(2,1)S(1)} %get-tuple-element.559), channel_id=1, source_target_pairs={{0,16},{1,17},{2,18},{3,19},{4,20},{5,21},{6,22},{7,23},{8,24},{9,... | collective-permute-start | bytes 442376 | tf_op jit(solution)/shard_map/ppermute | solution.py:561
  79.4 13.7 %collective-permute-start.33 = (bf16[1,56,768]{2,1,0:T(8,128)(2,1)S(1)}, bf16[1,56,768]{2,1,0:T(8,128)(2,1)S(1)}, u32[]{:S(2)}, u32[]{:S(2)}) collective-permute-start(bf16[1,56,768]{2,1,0:T(8,128)(2,1)S(1)} %get-tuple-element.561), channel_id=1, source_target_pairs={{0,16},{1,17},{2,18},{3,19},{4,20},{5,21},{6,22},{7,23},{8,24},{9,... | collective-permute-start | bytes 258056 | tf_op jit(solution)/shard_map/ppermute | solution.py:561
  82.1 11.0 %collective-permute-start.32 = (bf16[1,48,768]{2,1,0:T(8,128)(2,1)S(1)}, bf16[1,48,768]{2,1,0:T(8,128)(2,1)S(1)}, u32[]{:S(2)}, u32[]{:S(2)}) collective-permute-start(bf16[1,48,768]{2,1,0:T(8,128)(2,1)S(1)} %get-tuple-element.560), channel_id=1, source_target_pairs={{0,16},{1,17},{2,18},{3,19},{4,20},{5,21},{6,22},{7,23},{8,24},{9,... | collective-permute-start | bytes 221192 | tf_op jit(solution)/shard_map/ppermute | solution.py:561
  (19 other events, 71.0 us)

commit v6 on v5

--- a/solution.py
+++ b/solution.py
@@ -54,6 +54,8 @@
     H_ACT,
     H_ACT_PASS,
     H_ATTN,
+    H_ATT_OWN,
+    H_ATT_OTHER,
     H_ATTN_KEEP,
     H_BACK,
     H_COTANGENT,
@@ -86,7 +88,7 @@
     H_UP_OWN,
     H_W_OUT,
     H_W_QKV,
-) = range(35)
+) = range(37)
 
 
 class State:
@@ -157,34 +159,47 @@
     return packed[index : index + 1, :]
 
 
-def attn_forward(lengths, tokens, w_qkv, bias_qv, w_out, saved_o, send_o, keep_o):
-    core, length = my_core(), lengths[0]
-    rows, width = saved_o.shape[1:]
-    half = rows // 2
-    x = tokens[...]
-    query = (nt(x, w_qkv[0]) + bias_qv[0:1, :]).astype(LOW)
-    keys = nt(x, w_qkv[1]).astype(LOW)
-    values = (nt(x, w_qkv[2]) + bias_qv[1:2, :]).astype(LOW)
-    saved_o[0] = query
-    saved_o[1] = keys
-    saved_o[2] = values
+def attend(start, rows_here, length, query, keys, values, saved_o):
+    rows, width = keys.shape
     head_of = lax.broadcasted_iota(jnp.int32, (rows, width), 1) // HEAD_DIM
-    key_valid = lax.broadcasted_iota(jnp.int32, (rows, rows), 1) < length
+    head_here = lax.broadcasted_iota(jnp.int32, (rows_here, width), 1) // HEAD_DIM
+    key_valid = lax.broadcasted_iota(jnp.int32, (rows_here, rows), 1) < length
     scaled = query.astype(F32) * HEAD_DIM ** -0.5
     value_full = values.astype(F32)
-    total = jnp.zeros((rows, width), F32)
+    total = jnp.zeros((rows_here, width), F32)
     for head in range(width // HEAD_DIM):
-        here = head_of == head
-        scores = nt(jnp.where(here, scaled, 0.0).astype(LOW), keys)
+        scores = nt(jnp.where(head_here == head, scaled, 0.0).astype(LOW), keys)
         scores = jnp.where(key_valid, scores, -1e30)
         expo = jnp.exp(scores - jnp.max(scores, -1, keepdims=True))
         probs = (expo * (1.0 / jnp.sum(expo, -1, keepdims=True))).astype(LOW)
-        total = total + nn(probs, jnp.where(here, value_full, 0.0).astype(LOW))
-    saved_o[3] = total.astype(LOW)
-    other_start = pl.multiple_of((1 - core) * half, half)
-    own_start = pl.multiple_of(core * half, half)
-    send_o[...] = nn(saved_o[3, pl.ds(other_start, half), :], w_out[...]).astype(LOW)
-    keep_o[...] = nn(saved_o[3, pl.ds(own_start, half), :], w_out[...])
+        total = total + nn(probs, jnp.where(head_of == head, value_full, 0.0).astype(LOW))
+    attended = total.astype(LOW)
+    saved_o[...] = attended
+    return attended
+
+
+def attn_forward_other(lengths, tokens, w_qkv, bias_qv, w_out, saved_o, att_o, send_o):
+    rows = saved_o.shape[1]
+    half = rows // 2
+    x = tokens[...]
+    saved_o[0] = (nt(x, w_qkv[0]) + bias_qv[0:1, :]).astype(LOW)
+    keys = nt(x, w_qkv[1]).astype(LOW)
+    values = (nt(x, w_qkv[2]) + bias_qv[1:2, :]).astype(LOW)
+    saved_o[1] = keys
+    saved_o[2] = values
+    start = pl.multiple_of((1 - my_core()) * half, half)
+    query = saved_o[0, pl.ds(start, half), :]
+    attended = attend(start, half, lengths[0], query, keys, values, att_o)
+    send_o[...] = nn(attended, w_out[...]).astype(LOW)
+
+
+def attn_forward_own(lengths, w_out, saved, att_o, keep_o):
+    rows = saved.shape[1]
+    half = rows // 2
+    start = pl.multiple_of(my_core() * half, half)
+    query = saved[0, pl.ds(start, half), :]
+    attended = attend(start, half, lengths[0], query, saved[1], saved[2], att_o)
+    keep_o[...] = nn(attended, w_out[...])
 
 
 def add_chunks(kept, received, *outs):
@@ -378,12 +393,13 @@
     lengths, *refs,
 ):
     pieces, refs = refs[:2], refs[2:]
-    sums_own, w_out, saved, tokens, sum_down, sum_up = refs[:6]
-    send_o, keep_o, gq_o, gk_o, gv_o, grad_attn, blocks, sums = refs[6:]
+    sums_own, w_out, saved, att_own, att_other, tokens, sum_down, sum_up = refs[:8]
+    send_o, keep_o, gq_o, gk_o, gv_o, grad_attn, attended, blocks, sums = refs[8:]
     length = lengths[0]
     rows, width = saved.shape[1:]
     half = rows // 2
     place_rows(*[piece.at[pl.ds(0, half)] for piece in pieces], grad_attn)
+    place_rows(att_own, att_other, attended)
     grad_rows = grad_attn[...]
     grad_att = nt(grad_rows, w_out[...]).astype(LOW)
     scale = HEAD_DIM ** -0.5
@@ -415,7 +431,7 @@
     gv_o[...] = low_v
     x = tokens[...]
     weight = jnp.concatenate(
-        [tn(x, low_q), tn(x, low_k), tn(x, low_v), tn(grad_rows, saved[3])], 1
+        [tn(x, low_q), tn(x, low_k), tn(x, low_v), tn(grad_rows, attended[...])], 1
     )
     spread(blocks, weight)
     others = pieces[1][half:, :].astype(F32)
@@ -597,10 +613,19 @@
     packed_other = to_core(packed)
 
     state = State()
-    attn_send, attn_keep = state.call(
-        attn_forward,
-        [((4, rows, width), LOW, (H_SAVED,)), ((half, model), LOW), ((half, model), F32)],
+    (attn_send,) = state.call(
+        attn_forward_other,
+        [
+            ((3, rows, width), LOW, (H_SAVED,)), ((half, width), LOW, (H_ATT_OTHER,)),
+            ((half, model), LOW),
+        ],
         lengths, tokens, w_turned, bias_qv, w_out,
+        mib=20,
+    )
+    (attn_keep,) = state.call(
+        attn_forward_own,
+        [((half, width), LOW, (H_ATT_OWN,)), ((half, model), F32)],
+        lengths, w_out, (H_SAVED,),
         mib=20,
     )
     attn_parts = state.call(
@@ -610,17 +635,19 @@
     )
     received = [to_chip(part) for part in attn_parts]
     held = {
-        (H_TOKENS,): tokens, (H_W_OUT,): w_out, (H_W_QKV,): w_turned, (H_COTANGENT,): cotangent,
+        (H_TOKENS,): tokens, (H_W_OUT,): w_out, (H_W_QKV,): w_turned,
         (H_UP_OWN,): w_up, (H_UP_OTHER,): up_other, (H_DOWN_OWN,): w_down, (H_DOWN_OTHER,): down_other,
         (H_PACKED,): packed, (H_PACKED_OTHER,): packed_other,
     }
-    state.call(
-        hold,
-        [(array.shape, array.dtype, name) for name, array in held.items()],
-        *held.values(),
-        scratch=[pltpu.SemaphoreType.DMA((len(held),))], loose=range(len(held)),
-    )
-
+    def hold_on(arrays):
+        state.call(
+            hold,
+            [(array.shape, array.dtype, name) for name, array in arrays.items()],
+            *arrays.values(),
+            scratch=[pltpu.SemaphoreType.DMA((len(arrays),))], loose=range(len(arrays)),
+        )
+
+    hold_on(held)
     last = CHUNKS - 1
     passed, hidden_other, act_other = [], [], []
     for c in chunks:
@@ -641,8 +668,13 @@
         hidden_other.append(to_core(hidden_pass))
         act_other.append(to_core(act_pass))
     received = passed
+    hold_on({(H_COTANGENT,): cotangent})
 
     for c in chunks:
+        if c == last:
+            for early in chunks:
+                state.arrays[(H_FWD_OTHER, early)] = hidden_other[early]
+                state.arrays[(H_ACT_PASS, early)] = act_other[early]
         sends = state.call(
             partial(mlp_backward, c),
             [
@@ -687,14 +719,15 @@
 
     down_got = weight_parts(
         DOWN_PARTS, H_DOWN_KEEP, (1, model), H_SUM_DOWN,
-        held_chunks(H_GRAD) + [grad_other], held_chunks(H_ACT) + act_other,
+        held_chunks(H_GRAD) + [grad_other], held_chunks(H_ACT) + held_chunks(H_ACT_PASS),
     )
     up_got = weight_parts(
         UP_PARTS, H_UP_KEEP, (2, units), H_SUM_UP,
-        held_chunks(H_HID) + hidden_other, held_chunks(H_PRE) + [pre_other],
+        held_chunks(H_HID) + held_chunks(H_FWD_OTHER), held_chunks(H_PRE) + [pre_other],
     )
     for c in chunks:
         state.drop((H_HID, c), (H_ACT, c), (H_GRAD, c), (H_PRE, c))
+        state.drop((H_FWD_OTHER, c), (H_ACT_PASS, c))
     state.arrays[(H_OUT_HALF,)] = out_half
     state.arrays[(H_OUT_OTHER,)] = out_other
 
@@ -771,15 +804,17 @@
         ]
         + [((rows, width), LOW)] * 3,
         lengths, grad_attn, grad_attn_other, sums,
-        (H_W_OUT,), (H_SAVED,), (H_TOKENS,), (H_SUM_DOWN,), (H_SUM_UP,),
+        (H_W_OUT,), (H_SAVED,), (H_ATT_OWN,), (H_ATT_OTHER,), (H_TOKENS,), (H_SUM_DOWN,), (H_SUM_UP,),
         scratch=[
             pltpu.VMEM((rows, model), LOW),
+            pltpu.VMEM((rows, width), LOW),
             pltpu.VMEM((dp_size, block, model), F32),
             pltpu.VMEM((VECTOR_ROWS, model), F32),
         ],
         mib=24,
     )
-    state.drop((H_SAVED,), (H_SUM_DOWN,), (H_SUM_UP,), (H_W_OUT,), (H_TOKENS,))
+    state.drop((H_SAVED,), (H_ATT_OWN,), (H_ATT_OTHER,))
+    state.drop((H_SUM_DOWN,), (H_SUM_UP,), (H_W_OUT,), (H_TOKENS,))
     state.drop((H_PACKED,), (H_PACKED_OTHER,))
     running_attn = ([to_dp(attn_w_send, 0, dp_size, tensor_size)], 1)
     *token_parts, token_keep = state.call(

time: 94.5 us -> 91 us (0.963)
  waiting for transfers between devices: 27.7 us -> 25.4 us
    ppermute x11, waiting for transfers between devices: 16.4 us -> 14.7 us  [to_dp(): return lax.ppermute(block, ('dp', 'tensor'), pairs)]
    ppermute x17, waiting for transfers between devices: 3.78 us -> 2.17 us  [to_core(): return lax.ppermute(block, 'tensor', CORE_PAIRS)]
    ppermute x6, waiting for transfers between devices: 7.59 us -> 8.57 us  [to_chip(): return lax.ppermute(block, 'tensor', CHIP_PAIRS)]
    unnamed x34 -> x36, local copies, waits for them, and re-layouts: 7.67 us -> 7.21 us
    pallas_call x22 -> x24, Pallas kernels: 27.6 us -> 27.5 us  [call(): pl.pallas_call(body, name=getattr(kernel, 'func', kernel).__name__, out_s...]
  transfers between devices with their start and end apart: 34 -> 34, of which waited for: 18 -> 17; matrix products, arithmetic and copies ran while one was open for 0% -> 0% of each run, Pallas kernels for 25% -> 26%
where the time goes in v6:
time: 91 us; the launch traced here: 90.6 us
  starting transfers between devices  28.6 us (31%)
  Pallas kernels  27.5 us (30%)
  waiting for transfers between devices  25.4 us (28%)
  local copies, waits for them, and re-layouts  7.29 us (8%)
  between operations  1.69 us (2%)
    pallas_call x24, Pallas kernels, call(): pl.pallas_call(body, name=getattr(kernel, 'func', kernel).__name__, out_s...  27.5 us
    ppermute x11, starting transfers between devices, to_dp(): return lax.ppermute(block, ('dp', 'tensor'), pairs)  17.9 us
    ppermute x11, waiting for transfers between devices, to_dp(): return lax.ppermute(block, ('dp', 'tensor'), pairs)  14.7 us
    ppermute x6, waiting for transfers between devices, to_chip(): return lax.ppermute(block, 'tensor', CHIP_PAIRS)  8.57 us
    ppermute x6, starting transfers between devices, to_chip(): return lax.ppermute(block, 'tensor', CHIP_PAIRS)  7.32 us
    unnamed x36, local copies, waits for them, and re-layouts  7.21 us
    ppermute x17, starting transfers between devices, to_core(): return lax.ppermute(block, 'tensor', CORE_PAIRS)  3.46 us
    ppermute x17, waiting for transfers between devices, to_core(): return lax.ppermute(block, 'tensor', CORE_PAIRS)  2.17 us
  transfers between devices with their start and end apart: 34, of which 17 were waited for; matrix products, arithmetic and copies ran while one was open for 0% of the time, Pallas kernels for 26%

profile of v6, /device:TPU:0, one launch (start us, length us, event | category | flops | bytes accessed | tf_op | source)
XLA Modules:
  0.0 90.6 jit_solution(18350787768206033596)
XLA Ops:
  1.9 1.2 %copy-done = bf16[3,768,192]{1,2,0:T(8,128)(2,1)S(1)} copy-done((bf16[3,768,192]{1,2,0:T(8,128)(2,1)S(1)}, bf16[3,768,192]{1,2,0:T(8,128)(2,1)}, u32[]{:S(2)}) %copy-start) | copy-done | bytes 884760
  3.1 1.1 %copy-done.2 = bf16[512,768]{1,0:T(8,128)(2,1)S(1)} copy-done((bf16[512,768]{1,0:T(8,128)(2,1)S(1)}, bf16[512,768]{1,0:T(8,128)(2,1)}, u32[]{:S(2)}) %copy-start.2) | copy-done | bytes 786456
  5.8 2.2 %attn_forward_other.1 = (bf16[3,512,192]{2,1,0:T(8,128)(2,1)S(1)}, bf16[256,192]{1,0:T(8,128)(2,1)S(1)}, bf16[256,768]{1,0:T(8,128)(2,1)S(1)}) custom-call(s32[1]{0:T(128)S(6)} %copy.609.refs_0_, bf16[512,768]{1,0:T(8,128)(2,1)S(1)} %copy-done.2, bf16[3,192,768]{2,1,0:T(8,128)(2,1)S(1)} %bitcast.2, f32[2,192]{1,0:T(2,128)S(1)} %copy-done.9, ...), custom_call_target="tpu_custom_call" | custom-call | tf_op jit(solution)/shard_map/attn_forward_other/pallas_call | solution.py:123
  8.5 1.6 %attn_forward_own.1 = (bf16[256,192]{1,0:T(8,128)(2,1)S(1)}, f32[256,768]{1,0:T(8,128)S(1)}, bf16[3,512,192]{2,1,0:T(8,128)(2,1)S(1)}, bf16[256,192]{1,0:T(8,128)(2,1)S(1)}) custom-call(s32[1]{0:T(128)S(6)} %copy.609.refs_0_, bf16[192,768]{1,0:T(8,128)(2,1)S(1)} %copy-done.5, ...), custom_call_target="tpu_custom_call", output_to_operand_aliasing={{2}: (2, {}), {3}: (3, {})} | custom-call | tf_op jit(solution)/shard_map/attn_forward_own/pallas_call | solution.py:123
  11.7 2.6 %collective-permute-start.2 = (bf16[128,768]{1,0:T(8,128)(2,1)}, bf16[128,768]{1,0:T(8,128)(2,1)}, u32[]{:S(2)}, u32[]{:S(2)}) collective-permute-start(bf16[128,768]{1,0:T(8,128)(2,1)} %get-tuple-element.357), channel_id=1, source_target_pairs={{0,2},{1,3},{2,0},{3,1},{4,6},{5,7},{6,4},{7,5},{8,10},{9,11},{10,... | collective-permute-start | bytes 589832 | tf_op jit(solution)/shard_map/ppermute | solution.py:561
  15.7 1.3 %copy-done.6 = bf16[768,768]{1,0:T(8,128)(2,1)S(1)} copy-done((bf16[768,768]{1,0:T(8,128)(2,1)S(1)}, bf16[768,768]{1,0:T(8,128)(2,1)}, u32[]{:S(2)}) %copy-start.6) | copy-done | bytes 1179672
  17.0 1.3 %copy-done.7 = bf16[768,768]{1,0:T(8,128)(2,1)S(1)} copy-done((bf16[768,768]{1,0:T(8,128)(2,1)S(1)}, bf16[768,768]{1,0:T(8,128)(2,1)}, u32[]{:S(2)}) %copy-start.7) | copy-done | bytes 1179672
  18.3 2.4 %hold.2 = (bf16[512,768]{1,0:T(8,128)(2,1)S(1)}, bf16[192,768]{1,0:T(8,128)(2,1)S(1)}, bf16[3,192,768]{2,1,0:T(8,128)(2,1)S(1)}, bf16[768,768]{1,0:T(8,128)(2,1)...) custom-call(bf16[512,768]{1,0:T(8,128)(2,1)S(1)} %copy-done.3, ...), custom_call_target="tpu_custom_call", output_to_operand_aliasing={{9}: (9, {}), {10}: (10, {}), {11}: (11, {}), {12}: (12, {}... | custom-call | tf_op jit(solution)/shard_map/hold/pallas_call | solution.py:123
  20.7 2.2 %mlp_forward.2 = (bf16[128,768]{1,0:T(8,128)(2,1)S(1)}, bf16[128,768]{1,0:T(8,128)(2,1)S(1)}, bf16[128,768]{1,0:T(8,128)(2,1)S(1)}, bf16[128,768]{1,0:T(8,128)(2...) custom-call(bf16[128,768]{1,0:T(8,128)(2,1)} %collective-permute-don, ...), custom_call_target="tpu_custom_call", output_to_operand_aliasing={{9}: (1, {}), {10}: (2, {}), {11}: (3, {}), {12}: (4, {}), ... | custom-call | tf_op jit(solution)/shard_map/mlp_forward/pallas_call | solution.py:123
  22.9 1.6 %collective-permute-start.7 = (bf16[128,768]{1,0:T(8,128)(2,1)S(1)}, bf16[128,768]{1,0:T(8,128)(2,1)S(1)}, u32[]{:S(2)}, u32[]{:S(2)}) collective-permute-start(bf16[128,768]{1,0:T(8,128)(2,1)S(1)} %get-tuple-element.397), channel_id=1, source_target_pairs={{0,2},{1,3},{2,0},{3,1},{4,6},{5,7},{6,4},{7,5},{8,10},{9,11},{10,... | collective-permute-start | bytes 589832 | tf_op jit(solution)/shard_map/ppermute | solution.py:561
  25.1 1.3 %mlp_forward.3 = (bf16[128,768]{1,0:T(8,128)(2,1)S(1)}, bf16[128,768]{1,0:T(8,128)(2,1)S(1)}, bf16[128,768]{1,0:T(8,128)(2,1)S(1)}, bf16[128,768]{1,0:T(8,128)(2...) custom-call(bf16[128,768]{1,0:T(8,128)(2,1)S(1)} %collective-permute, ...), custom_call_target="tpu_custom_call", output_to_operand_aliasing={{9}: (1, {}), {10}: (2, {}), {11}: (3, {}), {12}: (4, {}), ... | custom-call | tf_op jit(solution)/shard_map/mlp_forward/pallas_call | solution.py:123
  27.3 3.4 %collective-permute-done.7.refs_1_ = bf16[128,768]{1,0:T(8,128)(2,1)S(1)} collective-permute-done((bf16[128,768]{1,0:T(8,128)(2,1)S(1)}, bf16[128,768]{1,0:T(8,128)(2,1)S(1)}, u32[]{:S(2)}, u32[]{:S(2)}) %collective-permute-start.7) | collective-permute-done | bytes 196640 | tf_op jit(solution)/shard_map/ppermute | solution.py:561
  31.0 2.2 %mlp_backward.2 = (bf16[128,768]{1,0:T(8,128)(2,1)S(1)}, bf16[128,768]{1,0:T(8,128)(2,1)S(1)}, bf16[128,768]{1,0:T(8,128)(2,1)S(1)}, bf16[128,768]{1,0:T(8,128)(...) custom-call(s32[1]{0:T(128)S(6)} %copy.609.refs_0_, ...), custom_call_target="tpu_custom_call", output_to_operand_aliasing={{7}: (2, {}), {8}: (3, {}), {9}: (4, {}), {10}: (5, {}), {1... | custom-call | tf_op jit(solution)/shard_map/mlp_backward/pallas_call | solution.py:123
  33.2 1.0 %collective-permute-done.6.refs_1_ = bf16[128,768]{1,0:T(8,128)(2,1)S(1)} collective-permute-done((bf16[128,768]{1,0:T(8,128)(2,1)S(1)}, bf16[128,768]{1,0:T(8,128)(2,1)S(1)}, u32[]{:S(2)}, u32[]{:S(2)}) %collective-permute-start.6) | collective-permute-done | bytes 196640 | tf_op jit(solution)/shard_map/ppermute | solution.py:561
  34.2 2.7 %mlp_backward.3 = (bf16[128,768]{1,0:T(8,128)(2,1)S(1)}, bf16[128,768]{1,0:T(8,128)(2,1)S(1)}, bf16[128,768]{1,0:T(8,128)(2,1)S(1)}, bf16[128,768]{1,0:T(8,128)(...) custom-call(s32[1]{0:T(128)S(6)} %copy.609.refs_0_, ...), custom_call_target="tpu_custom_call", output_to_operand_aliasing={{11}: (2, {}), {12}: (3, {}), {13}: (4, {}), {14}: (5, {}),... | custom-call | tf_op jit(solution)/shard_map/mlp_backward/pallas_call | solution.py:123
  38.6 1.0 %weight_grad.2 = (bf16[2,96,768]{2,1,0:T(8,128)(2,1)S(1)}, bf16[2,96,768]{2,1,0:T(8,128)(2,1)S(1)}, f32[4,96,768]{2,1,0:T(8,128)S(1)}, f32[1,768]{1,0:T(1,128)S(...) custom-call(bf16[256,768]{1,0:T(8,128)(2,1)S(1)} %collective-permute, ...), custom_call_target="tpu_custom_call", output_to_operand_aliasing={{4}: (1, {}), {5}: (2, {}), {6}: (3, {}), {7}: (4, {}), {8}... | custom-call | tf_op jit(solution)/shard_map/weight_grad/pallas_call | solution.py:123
  39.6 1.6 %collective-permute-start.17 = (bf16[2,96,768]{2,1,0:T(8,128)(2,1)S(1)}, bf16[2,96,768]{2,1,0:T(8,128)(2,1)S(1)}, u32[]{:S(2)}, u32[]{:S(2)}) collective-permute-start(bf16[2,96,768]{2,1,0:T(8,128)(2,1)S(1)} %get-tuple-element.571), channel_id=1, source_target_pairs={{0,4},{1,9},{2,6},{3,11},{4,0},{5,13},{6,2},{7,15},{8,12},{9,1},{1... | collective-permute-start | bytes 884744 | tf_op jit(solution)/shard_map/ppermute | solution.py:577
  42.6 1.6 %collective-permute-start.24 = (bf16[4,96,768]{2,1,0:T(8,128)(2,1)S(1)}, bf16[4,96,768]{2,1,0:T(8,128)(2,1)S(1)}, u32[]{:S(2)}, u32[]{:S(2)}) collective-permute-start(bf16[4,96,768]{2,1,0:T(8,128)(2,1)S(1)} %get-tuple-element.619), channel_id=1, source_target_pairs={{0,4},{1,9},{2,6},{3,11},{4,0},{5,13},{6,2},{7,15},{8,12},{9,1},{1... | collective-permute-start | bytes 1769480 | tf_op jit(solution)/shard_map/ppermute | solution.py:577
  44.2 4.2 %collective-permute-done.12.refs_0_ = bf16[256,768]{1,0:T(8,128)(2,1)S(1)} collective-permute-done((bf16[256,768]{1,0:T(8,128)(2,1)S(1)}, bf16[256,768]{1,0:T(8,128)(2,1)S(1)}, u32[]{:S(2)}, u32[]{:S(2)}) %collective-permute-start.12) | collective-permute-done | bytes 393248 | tf_op jit(solution)/shard_map/ppermute | solution.py:561
  49.6 1.6 %collective-permute-start.25 = (bf16[2,96,768]{2,1,0:T(8,128)(2,1)S(1)}, bf16[2,96,768]{2,1,0:T(8,128)(2,1)S(1)}, u32[]{:S(2)}, u32[]{:S(2)}) collective-permute-start(bf16[2,96,768]{2,1,0:T(8,128)(2,1)S(1)} %get-tuple-element.620), channel_id=1, source_target_pairs={{0,8},{1,5},{2,10},{3,7},{4,12},{5,1},{6,14},{7,3},{8,0},{9,13},{1... | collective-permute-start | bytes 884744 | tf_op jit(solution)/shard_map/ppermute | solution.py:577
  51.3 4.4 %attn_backward.1 = (bf16[4,104,768]{2,1,0:T(8,128)(2,1)S(1)}, f32[4,104,768]{2,1,0:T(8,128)S(1)}, bf16[512,192]{1,0:T(8,128)(2,1)S(1)}, bf16[512,192]{1,0:T(8,12...) custom-call(s32[1]{0:T(128)S(6)} %copy.609.refs_0_, ...), custom_call_target="tpu_custom_call", output_to_operand_aliasing={{5}: (4, {}), {6}: (5, {}), {7}: (6, {}), {8}: (7, {}), {9}... | custom-call | tf_op jit(solution)/shard_map/attn_backward/pallas_call | solution.py:123
  55.6 1.6 %collective-permute-start.19 = (bf16[4,104,768]{2,1,0:T(8,128)(2,1)S(1)}, bf16[4,104,768]{2,1,0:T(8,128)(2,1)S(1)}, u32[]{:S(2)}, u32[]{:S(2)}) collective-permute-start(bf16[4,104,768]{2,1,0:T(8,128)(2,1)S(1)} %get-tuple-element.603), channel_id=1, source_target_pairs={{0,4},{1,9},{2,6},{3,11},{4,0},{5,13},{6,2},{7,15},{8,12},{9,1},{1... | collective-permute-start | bytes 1916936 | tf_op jit(solution)/shard_map/ppermute | solution.py:577
  60.4 1.0 %collective-permute-start.27 = (bf16[256,768]{1,0:T(8,128)(2,1)S(1)}, bf16[256,768]{1,0:T(8,128)(2,1)S(1)}, u32[]{:S(2)}, u32[]{:S(2)}) collective-permute-start(bf16[256,768]{1,0:T(8,128)(2,1)S(1)} %get-tuple-element.640.refs_0_), channel_id=1, source_target_pairs={{0,2},{1,3},{2,0},{3,1},{4,6},{5,7},{6,4},{7,5},{8,10},{9,11},{10,... | collective-permute-start | bytes 1179656 | tf_op jit(solution)/shard_map/ppermute | solution.py:561
  61.4 1.6 %collective-permute-start.29 = (bf16[2,96,768]{2,1,0:T(8,128)(2,1)S(1)}, bf16[2,96,768]{2,1,0:T(8,128)(2,1)S(1)}, u32[]{:S(2)}, u32[]{:S(2)}) collective-permute-start(bf16[2,96,768]{2,1,0:T(8,128)(2,1)S(1)} %get-tuple-element.642), channel_id=1, source_target_pairs={{0,8},{1,5},{2,10},{3,7},{4,12},{5,1},{6,14},{7,3},{8,0},{9,13},{1... | collective-permute-start | bytes 884744 | tf_op jit(solution)/shard_map/ppermute | solution.py:577
  62.9 2.6 %collective-permute-start.28 = (bf16[1,96,768]{2,1,0:T(8,128)(2,1)S(1)}, bf16[1,96,768]{2,1,0:T(8,128)(2,1)S(1)}, u32[]{:S(2)}, u32[]{:S(2)}) collective-permute-start(bf16[1,96,768]{2,1,0:T(8,128)(2,1)S(1)} %get-tuple-element.641), channel_id=1, source_target_pairs={{0,16},{1,17},{2,18},{3,19},{4,20},{5,21},{6,22},{7,23},{8,24},{9,... | collective-permute-start | bytes 442376 | tf_op jit(solution)/shard_map/ppermute | solution.py:577
  65.5 2.7 %collective-permute-done.19.refs_0_ = bf16[4,104,768]{2,1,0:T(8,128)(2,1)S(1)} collective-permute-done((bf16[4,104,768]{2,1,0:T(8,128)(2,1)S(1)}, bf16[4,104,768]{2,1,0:T(8,128)(2,1)S(1)}, u32[]{:S(2)}, u32[]{:S(2)}) %collective-permute-start.19) | collective-permute-done | bytes 639008 | tf_op jit(solution)/shard_map/ppermute | solution.py:577
  68.4 1.1 %collective-permute-start.26 = (bf16[2,104,768]{2,1,0:T(8,128)(2,1)S(1)}, bf16[2,104,768]{2,1,0:T(8,128)(2,1)S(1)}, u32[]{:S(2)}, u32[]{:S(2)}) collective-permute-start(bf16[2,104,768]{2,1,0:T(8,128)(2,1)S(1)} %get-tuple-element.639), channel_id=1, source_target_pairs={{0,8},{1,5},{2,10},{3,7},{4,12},{5,1},{6,14},{7,3},{8,0},{9,13},{1... | collective-permute-start | bytes 958472 | tf_op jit(solution)/shard_map/ppermute | solution.py:577
  69.5 1.4 %collective-permute-done.28.refs_0_ = bf16[1,96,768]{2,1,0:T(8,128)(2,1)S(1)} collective-permute-done((bf16[1,96,768]{2,1,0:T(8,128)(2,1)S(1)}, bf16[1,96,768]{2,1,0:T(8,128)(2,1)S(1)}, u32[]{:S(2)}, u32[]{:S(2)}) %collective-permute-start.28) | collective-permute-done | bytes 147488 | tf_op jit(solution)/shard_map/ppermute | solution.py:577
  72.4 2.6 %collective-permute-start.31 = (bf16[1,96,768]{2,1,0:T(8,128)(2,1)S(1)}, bf16[1,96,768]{2,1,0:T(8,128)(2,1)S(1)}, u32[]{:S(2)}, u32[]{:S(2)}) collective-permute-start(bf16[1,96,768]{2,1,0:T(8,128)(2,1)S(1)} %get-tuple-element.667), channel_id=1, source_target_pairs={{0,16},{1,17},{2,18},{3,19},{4,20},{5,21},{6,22},{7,23},{8,24},{9,... | collective-permute-start | bytes 442376 | tf_op jit(solution)/shard_map/ppermute | solution.py:577
  75.5 2.7 %collective-permute-start.33 = (bf16[1,56,768]{2,1,0:T(8,128)(2,1)S(1)}, bf16[1,56,768]{2,1,0:T(8,128)(2,1)S(1)}, u32[]{:S(2)}, u32[]{:S(2)}) collective-permute-start(bf16[1,56,768]{2,1,0:T(8,128)(2,1)S(1)} %get-tuple-element.669), channel_id=1, source_target_pairs={{0,16},{1,17},{2,18},{3,19},{4,20},{5,21},{6,22},{7,23},{8,24},{9,... | collective-permute-start | bytes 258056 | tf_op jit(solution)/shard_map/ppermute | solution.py:577
  80.4 6.2 %collective-permute-done.31.refs_0_ = bf16[1,96,768]{2,1,0:T(8,128)(2,1)S(1)} collective-permute-done((bf16[1,96,768]{2,1,0:T(8,128)(2,1)S(1)}, bf16[1,96,768]{2,1,0:T(8,128)(2,1)S(1)}, u32[]{:S(2)}, u32[]{:S(2)}) %collective-permute-start.31) | collective-permute-done | bytes 147488 | tf_op jit(solution)/shard_map/ppermute | solution.py:577
  86.6 3.0 %collective-permute-done.32.refs_1_ = bf16[1,48,768]{2,1,0:T(8,128)(2,1)S(1)} collective-permute-done((bf16[1,48,768]{2,1,0:T(8,128)(2,1)S(1)}, bf16[1,48,768]{2,1,0:T(8,128)(2,1)S(1)}, u32[]{:S(2)}, u32[]{:S(2)}) %collective-permute-start.32) | collective-permute-done | bytes 73760 | tf_op jit(solution)/shard_map/ppermute | solution.py:577
  (104 shorter events, 20.1 us)
Async XLA Ops:
  0.6 15.1 %collective-permute-start.3 = (bf16[768,768]{1,0:T(8,128)(2,1)}, bf16[768,768]{1,0:T(8,128)(2,1)}, u32[]{:S(2)}, u32[]{:S(2)}) collective-permute-start(bf16[768,768]{1,0:T(8,128)(2,1)} %refs_3_.3), channel_id=1, source_target_pairs={{0,1},{1,0},{2,3},{3,2},{4,5},{5,4},{6,7},{7,6},{8,9},{9,8},{10,11... | collective-permute-start | bytes 3538952 | tf_op jit(solution)/shard_map/ppermute | solution.py:557
  1.2 14.6 %collective-permute-start.4 = (bf16[768,768]{1,0:T(8,128)(2,1)}, bf16[768,768]{1,0:T(8,128)(2,1)}, u32[]{:S(2)}, u32[]{:S(2)}) collective-permute-start(bf16[768,768]{1,0:T(8,128)(2,1)} %refs_5_.1), channel_id=1, source_target_pairs={{0,1},{1,0},{2,3},{3,2},{4,5},{5,4},{6,7},{7,6},{8,9},{9,8},{10,11... | collective-permute-start | bytes 3538952 | tf_op jit(solution)/shard_map/ppermute | solution.py:557
  8.0 2.2 %collective-permute-start = (bf16[256,768]{1,0:T(8,128)(2,1)S(1)}, bf16[256,768]{1,0:T(8,128)(2,1)S(1)}, u32[]{:S(2)}, u32[]{:S(2)}) collective-permute-start(bf16[256,768]{1,0:T(8,128)(2,1)S(1)} %get-tuple-element.352), channel_id=1, source_target_pairs={{0,1},{1,0},{2,3},{3,2},{4,5},{5,4},{6,7},{7,6},{8,9},{9,8},{10,11... | collective-permute-start | bytes 1179656 | tf_op jit(solution)/shard_map/ppermute | solution.py:557
  11.7 9.0 %collective-permute-start.2 = (bf16[128,768]{1,0:T(8,128)(2,1)}, bf16[128,768]{1,0:T(8,128)(2,1)}, u32[]{:S(2)}, u32[]{:S(2)}) collective-permute-start(bf16[128,768]{1,0:T(8,128)(2,1)} %get-tuple-element.357), channel_id=1, source_target_pairs={{0,2},{1,3},{2,0},{3,1},{4,6},{5,7},{6,4},{7,5},{8,10},{9,11},{10,... | collective-permute-start | bytes 589832 | tf_op jit(solution)/shard_map/ppermute | solution.py:561
  14.7 10.4 %collective-permute-start.1 = (bf16[128,768]{1,0:T(8,128)(2,1)}, bf16[128,768]{1,0:T(8,128)(2,1)S(1)}, u32[]{:S(2)}, u32[]{:S(2)}) collective-permute-start(bf16[128,768]{1,0:T(8,128)(2,1)} %copy-done.10), channel_id=1, source_target_pairs={{0,2},{1,3},{2,0},{3,1},{4,6},{5,7},{6,4},{7,5},{8,10},{9,11},{10,... | collective-permute-start | bytes 589832 | tf_op jit(solution)/shard_map/ppermute | solution.py:561
  22.9 7.8 %collective-permute-start.7 = (bf16[128,768]{1,0:T(8,128)(2,1)S(1)}, bf16[128,768]{1,0:T(8,128)(2,1)S(1)}, u32[]{:S(2)}, u32[]{:S(2)}) collective-permute-start(bf16[128,768]{1,0:T(8,128)(2,1)S(1)} %get-tuple-element.397), channel_id=1, source_target_pairs={{0,2},{1,3},{2,0},{3,1},{4,6},{5,7},{6,4},{7,5},{8,10},{9,11},{10,... | collective-permute-start | bytes 589832 | tf_op jit(solution)/shard_map/ppermute | solution.py:561
  24.5 8.6 %collective-permute-start.8 = (bf16[128,768]{1,0:T(8,128)(2,1)S(1)}, bf16[128,768]{1,0:T(8,128)(2,1)S(1)}, u32[]{:S(2)}, u32[]{:S(2)}) collective-permute-start(bf16[128,768]{1,0:T(8,128)(2,1)S(1)} %get-tuple-element.477), channel_id=1, source_target_pairs={{0,1},{1,0},{2,3},{3,2},{4,5},{5,4},{6,7},{7,6},{8,9},{9,8},{10,11... | collective-permute-start | bytes 589832 | tf_op jit(solution)/shard_map/ppermute | solution.py:557
  24.5 8.6 %collective-permute-start.9 = (bf16[128,768]{1,0:T(8,128)(2,1)S(1)}, bf16[128,768]{1,0:T(8,128)(2,1)S(1)}, u32[]{:S(2)}, u32[]{:S(2)}) collective-permute-start(bf16[128,768]{1,0:T(8,128)(2,1)S(1)} %get-tuple-element.478), channel_id=1, source_target_pairs={{0,1},{1,0},{2,3},{3,2},{4,5},{5,4},{6,7},{7,6},{8,9},{9,8},{10,11... | collective-permute-start | bytes 589832 | tf_op jit(solution)/shard_map/ppermute | solution.py:557
  26.3 7.8 %collective-permute-start.6 = (bf16[128,768]{1,0:T(8,128)(2,1)S(1)}, bf16[128,768]{1,0:T(8,128)(2,1)S(1)}, u32[]{:S(2)}, u32[]{:S(2)}) collective-permute-start(bf16[128,768]{1,0:T(8,128)(2,1)S(1)} %get-tuple-element.396), channel_id=1, source_target_pairs={{0,2},{1,3},{2,0},{3,1},{4,6},{5,7},{6,4},{7,5},{8,10},{9,11},{10,... | collective-permute-start | bytes 589832 | tf_op jit(solution)/shard_map/ppermute | solution.py:561
  27.3 6.9 %collective-permute-start.10 = (bf16[128,768]{1,0:T(8,128)(2,1)S(1)}, bf16[128,768]{1,0:T(8,128)(2,1)S(1)}, u32[]{:S(2)}, u32[]{:S(2)}) collective-permute-start(bf16[128,768]{1,0:T(8,128)(2,1)S(1)} %get-tuple-element.479), channel_id=1, source_target_pairs={{0,1},{1,0},{2,3},{3,2},{4,5},{5,4},{6,7},{7,6},{8,9},{9,8},{10,11... | collective-permute-start | bytes 589832 | tf_op jit(solution)/shard_map/ppermute | solution.py:557
  30.7 3.5 %collective-permute-start.11 = (bf16[128,768]{1,0:T(8,128)(2,1)S(1)}, bf16[128,768]{1,0:T(8,128)(2,1)S(1)}, u32[]{:S(2)}, u32[]{:S(2)}) collective-permute-start(bf16[128,768]{1,0:T(8,128)(2,1)S(1)} %get-tuple-element.480), channel_id=1, source_target_pairs={{0,1},{1,0},{2,3},{3,2},{4,5},{5,4},{6,7},{7,6},{8,9},{9,8},{10,11... | collective-permute-start | bytes 589832 | tf_op jit(solution)/shard_map/ppermute | solution.py:557
  36.9 1.7 %collective-permute-start.14 = (bf16[256,768]{1,0:T(8,128)(2,1)S(1)}, bf16[256,768]{1,0:T(8,128)(2,1)S(1)}, u32[]{:S(2)}, u32[]{:S(2)}) collective-permute-start(bf16[256,768]{1,0:T(8,128)(2,1)S(1)} %get-tuple-element.483), channel_id=1, source_target_pairs={{0,1},{1,0},{2,3},{3,2},{4,5},{5,4},{6,7},{7,6},{8,9},{9,8},{10,11... | collective-permute-start | bytes 1179656 | tf_op jit(solution)/shard_map/ppermute | solution.py:557
  36.9 4.8 %collective-permute-start.13 = (bf16[256,768]{1,0:T(8,128)(2,1)S(1)}, bf16[256,768]{1,0:T(8,128)(2,1)S(1)}, u32[]{:S(2)}, u32[]{:S(2)}) collective-permute-start(bf16[256,768]{1,0:T(8,128)(2,1)S(1)} %get-tuple-element.482), channel_id=1, source_target_pairs={{0,1},{1,0},{2,3},{3,2},{4,5},{5,4},{6,7},{7,6},{8,9},{9,8},{10,11... | collective-permute-start | bytes 1179656 | tf_op jit(solution)/shard_map/ppermute | solution.py:557
  37.4 11.0 %collective-permute-start.12 = (bf16[256,768]{1,0:T(8,128)(2,1)S(1)}, bf16[256,768]{1,0:T(8,128)(2,1)S(1)}, u32[]{:S(2)}, u32[]{:S(2)}) collective-permute-start(bf16[256,768]{1,0:T(8,128)(2,1)S(1)} %get-tuple-element.481), channel_id=1, source_target_pairs={{0,2},{1,3},{2,0},{3,1},{4,6},{5,7},{6,4},{7,5},{8,10},{9,11},{10,... | collective-permute-start | bytes 1179656 | tf_op jit(solution)/shard_map/ppermute | solution.py:561
  38.3 10.1 %collective-permute-start.15 = (bf16[256,768]{1,0:T(8,128)(2,1)S(1)}, bf16[256,768]{1,0:T(8,128)(2,1)S(1)}, u32[]{:S(2)}, u32[]{:S(2)}) collective-permute-start(bf16[256,768]{1,0:T(8,128)(2,1)S(1)} %get-tuple-element.568.refs_23_), channel_id=1, source_target_pairs={{0,1},{1,0},{2,3},{3,2},{4,5},{5,4},{6,7},{7,6},{8,9},{9,8},{10,11... | collective-permute-start | bytes 1179656 | tf_op jit(solution)/shard_map/ppermute | solution.py:557
  39.6 9.5 %collective-permute-start.17 = (bf16[2,96,768]{2,1,0:T(8,128)(2,1)S(1)}, bf16[2,96,768]{2,1,0:T(8,128)(2,1)S(1)}, u32[]{:S(2)}, u32[]{:S(2)}) collective-permute-start(bf16[2,96,768]{2,1,0:T(8,128)(2,1)S(1)} %get-tuple-element.571), channel_id=1, source_target_pairs={{0,4},{1,9},{2,6},{3,11},{4,0},{5,13},{6,2},{7,15},{8,12},{9,1},{1... | collective-permute-start | bytes 884744 | tf_op jit(solution)/shard_map/ppermute | solution.py:577
  41.2 8.4 %collective-permute-start.18 = (bf16[2,96,768]{2,1,0:T(8,128)(2,1)S(1)}, bf16[2,96,768]{2,1,0:T(8,128)(2,1)S(1)}, u32[]{:S(2)}, u32[]{:S(2)}) collective-permute-start(bf16[2,96,768]{2,1,0:T(8,128)(2,1)S(1)} %get-tuple-element.572), channel_id=1, source_target_pairs={{0,4},{1,9},{2,6},{3,11},{4,0},{5,13},{6,2},{7,15},{8,12},{9,1},{1... | collective-permute-start | bytes 884744 | tf_op jit(solution)/shard_map/ppermute | solution.py:577
  42.6 16.4 %collective-permute-start.24 = (bf16[4,96,768]{2,1,0:T(8,128)(2,1)S(1)}, bf16[4,96,768]{2,1,0:T(8,128)(2,1)S(1)}, u32[]{:S(2)}, u32[]{:S(2)}) collective-permute-start(bf16[4,96,768]{2,1,0:T(8,128)(2,1)S(1)} %get-tuple-element.619), channel_id=1, source_target_pairs={{0,4},{1,9},{2,6},{3,11},{4,0},{5,13},{6,2},{7,15},{8,12},{9,1},{1... | collective-permute-start | bytes 1769480 | tf_op jit(solution)/shard_map/ppermute | solution.py:577
  49.1 2.2 %collective-permute-start.16 = (bf16[272,768]{1,0:T(8,128)(2,1)S(1)}, bf16[272,768]{1,0:T(8,128)(2,1)S(1)}, u32[]{:S(2)}, u32[]{:S(2)}) collective-permute-start(bf16[272,768]{1,0:T(8,128)(2,1)S(1)} %get-tuple-element.569.refs_1_), channel_id=1, source_target_pairs={{0,1},{1,0},{2,3},{3,2},{4,5},{5,4},{6,7},{7,6},{8,9},{9,8},{10,11... | collective-permute-start | bytes 1253384 | tf_op jit(solution)/shard_map/ppermute | solution.py:557
  49.6 8.9 %collective-permute-start.25 = (bf16[2,96,768]{2,1,0:T(8,128)(2,1)S(1)}, bf16[2,96,768]{2,1,0:T(8,128)(2,1)S(1)}, u32[]{:S(2)}, u32[]{:S(2)}) collective-permute-start(bf16[2,96,768]{2,1,0:T(8,128)(2,1)S(1)} %get-tuple-element.620), channel_id=1, source_target_pairs={{0,8},{1,5},{2,10},{3,7},{4,12},{5,1},{6,14},{7,3},{8,0},{9,13},{1... | collective-permute-start | bytes 884744 | tf_op jit(solution)/shard_map/ppermute | solution.py:577
  55.6 12.6 %collective-permute-start.19 = (bf16[4,104,768]{2,1,0:T(8,128)(2,1)S(1)}, bf16[4,104,768]{2,1,0:T(8,128)(2,1)S(1)}, u32[]{:S(2)}, u32[]{:S(2)}) collective-permute-start(bf16[4,104,768]{2,1,0:T(8,128)(2,1)S(1)} %get-tuple-element.603), channel_id=1, source_target_pairs={{0,4},{1,9},{2,6},{3,11},{4,0},{5,13},{6,2},{7,15},{8,12},{9,1},{1... | collective-permute-start | bytes 1916936 | tf_op jit(solution)/shard_map/ppermute | solution.py:577
  58.0 1.4 %collective-permute-start.20 = (bf16[64,768]{1,0:T(8,128)(2,1)S(1)}, bf16[64,768]{1,0:T(8,128)(2,1)S(1)}, u32[]{:S(2)}, u32[]{:S(2)}) collective-permute-start(bf16[64,768]{1,0:T(8,128)(2,1)S(1)} %get-tuple-element.615), channel_id=1, source_target_pairs={{0,1},{1,0},{2,3},{3,2},{4,5},{5,4},{6,7},{7,6},{8,9},{9,8},{10,11... | collective-permute-start | bytes 294920 | tf_op jit(solution)/shard_map/ppermute | solution.py:557
  58.1 1.4 %collective-permute-start.21 = (bf16[64,768]{1,0:T(8,128)(2,1)S(1)}, bf16[64,768]{1,0:T(8,128)(2,1)S(1)}, u32[]{:S(2)}, u32[]{:S(2)}) collective-permute-start(bf16[64,768]{1,0:T(8,128)(2,1)S(1)} %get-tuple-element.616), channel_id=1, source_target_pairs={{0,1},{1,0},{2,3},{3,2},{4,5},{5,4},{6,7},{7,6},{8,9},{9,8},{10,11... | collective-permute-start | bytes 294920 | tf_op jit(solution)/shard_map/ppermute | solution.py:557
  58.6 1.3 %collective-permute-start.22 = (bf16[64,768]{1,0:T(8,128)(2,1)S(1)}, bf16[64,768]{1,0:T(8,128)(2,1)S(1)}, u32[]{:S(2)}, u32[]{:S(2)}) collective-permute-start(bf16[64,768]{1,0:T(8,128)(2,1)S(1)} %get-tuple-element.617), channel_id=1, source_target_pairs={{0,1},{1,0},{2,3},{3,2},{4,5},{5,4},{6,7},{7,6},{8,9},{9,8},{10,11... | collective-permute-start | bytes 294920 | tf_op jit(solution)/shard_map/ppermute | solution.py:557
  60.4 11.8 %collective-permute-start.27 = (bf16[256,768]{1,0:T(8,128)(2,1)S(1)}, bf16[256,768]{1,0:T(8,128)(2,1)S(1)}, u32[]{:S(2)}, u32[]{:S(2)}) collective-permute-start(bf16[256,768]{1,0:T(8,128)(2,1)S(1)} %get-tuple-element.640.refs_0_), channel_id=1, source_target_pairs={{0,2},{1,3},{2,0},{3,1},{4,6},{5,7},{6,4},{7,5},{8,10},{9,11},{10,... | collective-permute-start | bytes 1179656 | tf_op jit(solution)/shard_map/ppermute | solution.py:561
  61.4 10.1 %collective-permute-start.29 = (bf16[2,96,768]{2,1,0:T(8,128)(2,1)S(1)}, bf16[2,96,768]{2,1,0:T(8,128)(2,1)S(1)}, u32[]{:S(2)}, u32[]{:S(2)}) collective-permute-start(bf16[2,96,768]{2,1,0:T(8,128)(2,1)S(1)} %get-tuple-element.642), channel_id=1, source_target_pairs={{0,8},{1,5},{2,10},{3,7},{4,12},{5,1},{6,14},{7,3},{8,0},{9,13},{1... | collective-permute-start | bytes 884744 | tf_op jit(solution)/shard_map/ppermute | solution.py:577
  62.9 8.0 %collective-permute-start.28 = (bf16[1,96,768]{2,1,0:T(8,128)(2,1)S(1)}, bf16[1,96,768]{2,1,0:T(8,128)(2,1)S(1)}, u32[]{:S(2)}, u32[]{:S(2)}) collective-permute-start(bf16[1,96,768]{2,1,0:T(8,128)(2,1)S(1)} %get-tuple-element.641), channel_id=1, source_target_pairs={{0,16},{1,17},{2,18},{3,19},{4,20},{5,21},{6,22},{7,23},{8,24},{9,... | collective-permute-start | bytes 442376 | tf_op jit(solution)/shard_map/ppermute | solution.py:577
  68.4 7.1 %collective-permute-start.26 = (bf16[2,104,768]{2,1,0:T(8,128)(2,1)S(1)}, bf16[2,104,768]{2,1,0:T(8,128)(2,1)S(1)}, u32[]{:S(2)}, u32[]{:S(2)}) collective-permute-start(bf16[2,104,768]{2,1,0:T(8,128)(2,1)S(1)} %get-tuple-element.639), channel_id=1, source_target_pairs={{0,8},{1,5},{2,10},{3,7},{4,12},{5,1},{6,14},{7,3},{8,0},{9,13},{1... | collective-permute-start | bytes 958472 | tf_op jit(solution)/shard_map/ppermute | solution.py:577
  72.3 7.1 %collective-permute-start.30 = (bf16[256,768]{1,0:T(8,128)(2,1)S(1)}, bf16[256,768]{1,0:T(8,128)(2,1)S(1)}, u32[]{:S(2)}, u32[]{:S(2)}) collective-permute-start(bf16[256,768]{1,0:T(8,128)(2,1)S(1)} %get-tuple-element.663.refs_0_), channel_id=1, source_target_pairs={{0,1},{1,0},{2,3},{3,2},{4,5},{5,4},{6,7},{7,6},{8,9},{9,8},{10,11... | collective-permute-start | bytes 1179656 | tf_op jit(solution)/shard_map/ppermute | solution.py:557
  72.4 14.2 %collective-permute-start.31 = (bf16[1,96,768]{2,1,0:T(8,128)(2,1)S(1)}, bf16[1,96,768]{2,1,0:T(8,128)(2,1)S(1)}, u32[]{:S(2)}, u32[]{:S(2)}) collective-permute-start(bf16[1,96,768]{2,1,0:T(8,128)(2,1)S(1)} %get-tuple-element.667), channel_id=1, source_target_pairs={{0,16},{1,17},{2,18},{3,19},{4,20},{5,21},{6,22},{7,23},{8,24},{9,... | collective-permute-start | bytes 442376 | tf_op jit(solution)/shard_map/ppermute | solution.py:577
  75.5 14.1 %collective-permute-start.33 = (bf16[1,56,768]{2,1,0:T(8,128)(2,1)S(1)}, bf16[1,56,768]{2,1,0:T(8,128)(2,1)S(1)}, u32[]{:S(2)}, u32[]{:S(2)}) collective-permute-start(bf16[1,56,768]{2,1,0:T(8,128)(2,1)S(1)} %get-tuple-element.669), channel_id=1, source_target_pairs={{0,16},{1,17},{2,18},{3,19},{4,20},{5,21},{6,22},{7,23},{8,24},{9,... | collective-permute-start | bytes 258056 | tf_op jit(solution)/shard_map/ppermute | solution.py:577
  78.2 11.4 %collective-permute-start.32 = (bf16[1,48,768]{2,1,0:T(8,128)(2,1)S(1)}, bf16[1,48,768]{2,1,0:T(8,128)(2,1)S(1)}, u32[]{:S(2)}, u32[]{:S(2)}) collective-permute-start(bf16[1,48,768]{2,1,0:T(8,128)(2,1)S(1)} %get-tuple-element.668), channel_id=1, source_target_pairs={{0,16},{1,17},{2,18},{3,19},{4,20},{5,21},{6,22},{7,23},{8,24},{9,... | collective-permute-start | bytes 221192 | tf_op jit(solution)/shard_map/ppermute | solution.py:577
  (20 other events, 57.8 us)

commit v7 on v6

--- a/solution.py
+++ b/solution.py
@@ -12,7 +12,7 @@
 NORM_EPSILON = 1e-05
 CORES = 2
 CHUNKS = 2
-DOWN_PARTS = 2
+DOWN_PARTS = 1
 UP_PARTS = 1
 PIECES = 4
 F32 = jnp.float32
@@ -203,13 +203,13 @@
 
 
 def add_chunks(kept, received, *outs):
-    rows = outs[0].shape[0]
-    count = len(outs) // 2
-    for index in range(count):
+    *parts, whole = outs
+    rows = parts[0].shape[0]
+    for index, part in enumerate(parts):
         picked = slice(index * rows, (index + 1) * rows)
         total = (kept[picked, :] + received[picked, :].astype(F32)).astype(LOW)
-        outs[index][...] = total
-        outs[count + index][...] = total
+        part[...] = total
+        whole[picked, :] = total
 
 
 def hold(*refs):
@@ -264,7 +264,8 @@
     rows, width = part_o.shape
     start = pl.multiple_of((my_core() * CHUNKS + index) * rows, rows)
     resid = tokens[pl.ds(start, rows), :].astype(F32) + row(packed, BIAS_OUT)
-    resid = resid + (own[...].astype(F32) + received[...].astype(F32))
+    own_rows = own[index * rows : (index + 1) * rows, :].astype(F32)
+    resid = resid + (own_rows + received[...].astype(F32))
     normed, inverse = normalize(resid)
     normed_o[...] = normed
     inverse_o[...] = inverse
@@ -630,7 +631,7 @@
     )
     attn_parts = state.call(
         add_chunks,
-        [((chunk, model), LOW)] * CHUNKS + [((chunk, model), LOW, (H_ATTN, c)) for c in chunks],
+        [((chunk, model), LOW)] * CHUNKS + [((half, model), LOW, (H_ATTN,))],
         attn_keep, to_core(attn_send),
     )
     received = [to_chip(part) for part in attn_parts]
@@ -660,13 +661,13 @@
                 ((2, chunk, units), F32, (H_SLOPES, c)),
                 ((chunk, model), F32, (H_NORMED, c)), ((chunk, 1), F32, (H_INVERSE, c)),
             ],
-            received[c], (H_TOKENS,), (H_ATTN, c), (H_PACKED,), (H_PACKED_OTHER,),
+            received[c], (H_TOKENS,), (H_ATTN,), (H_PACKED,), (H_PACKED_OTHER,),
             (H_UP_OWN,), (H_UP_OTHER,), (H_DOWN_OWN,), (H_DOWN_OTHER,),
         )
-        state.drop((H_ATTN, c))
         passed.append(to_chip(part))
         hidden_other.append(to_core(hidden_pass))
         act_other.append(to_core(act_pass))
+    state.drop((H_ATTN,))
     received = passed
     hold_on({(H_COTANGENT,): cotangent})
 
@@ -838,7 +839,8 @@
         advance((H_ATTN_KEEP,))
         left = [name for name in others if name in running]
         if left != [(H_UP_KEEP,)]:
-            advance(*left)
+            for name in reversed(left):
+                advance(name)
     (output_low,) = state.call(
         place_rows, [((rows, model), LOW)], (H_OUT_HALF,), (H_OUT_OTHER,)
     )

time: 91 us -> 90.4 us (level)
  starting transfers between devices: 28.6 us -> 27.5 us
  waiting for transfers between devices: 25.4 us -> 26.5 us
    ppermute x11 -> x10, starting transfers between devices: 17.9 us -> 16.1 us  [to_dp(): return lax.ppermute(block, ('dp', 'tensor'), pairs)]
    ppermute x6, waiting for transfers between devices: 8.57 us -> 10.1 us  [to_chip(): return lax.ppermute(block, 'tensor', CHIP_PAIRS)]
    ppermute x11 -> x10, waiting for transfers between devices: 14.7 us -> 15 us  [to_dp(): return lax.ppermute(block, ('dp', 'tensor'), pairs)]
    pallas_call x24 -> x25, Pallas kernels: 27.5 us -> 27.7 us  [call(): pl.pallas_call(body, name=getattr(kernel, 'func', kernel).__name__, out_s...]
  transfers between devices with their start and end apart: 34 -> 33, of which waited for: 17 -> 14; matrix products, arithmetic and copies ran while one was open for 0% -> 0% of each run, Pallas kernels for 26% -> 27%
where the time goes in v7:
time: 90.4 us; the launch traced here: 90 us
  Pallas kernels  27.7 us (31%)
  starting transfers between devices  27.5 us (30%)
  waiting for transfers between devices  26.5 us (29%)
  local copies, waits for them, and re-layouts  6.62 us (7%)
  between operations  1.71 us (2%)
    pallas_call x25, Pallas kernels, call(): pl.pallas_call(body, name=getattr(kernel, 'func', kernel).__name__, out_s...  27.7 us
    ppermute x10, starting transfers between devices, to_dp(): return lax.ppermute(block, ('dp', 'tensor'), pairs)  16.1 us
    ppermute x10, waiting for transfers between devices, to_dp(): return lax.ppermute(block, ('dp', 'tensor'), pairs)  15 us
    ppermute x6, waiting for transfers between devices, to_chip(): return lax.ppermute(block, 'tensor', CHIP_PAIRS)  10.1 us
    ppermute x6, starting transfers between devices, to_chip(): return lax.ppermute(block, 'tensor', CHIP_PAIRS)  7.81 us
    unnamed x36, local copies, waits for them, and re-layouts  6.54 us
    ppermute x17, starting transfers between devices, to_core(): return lax.ppermute(block, 'tensor', CORE_PAIRS)  3.57 us
  transfers between devices with their start and end apart: 33, of which 14 were waited for; matrix products, arithmetic and copies ran while one was open for 0% of the time, Pallas kernels for 27%

profile of v7, /device:TPU:0, one launch (start us, length us, event | category | flops | bytes accessed | tf_op | source)
XLA Modules:
  0.0 90.0 jit_solution(12016707287733639510)
XLA Ops:
  1.9 1.2 %copy-done = bf16[3,768,192]{1,2,0:T(8,128)(2,1)S(1)} copy-done((bf16[3,768,192]{1,2,0:T(8,128)(2,1)S(1)}, bf16[3,768,192]{1,2,0:T(8,128)(2,1)}, u32[]{:S(2)}) %copy-start) | copy-done | bytes 884760
  3.1 1.1 %copy-done.2 = bf16[512,768]{1,0:T(8,128)(2,1)S(1)} copy-done((bf16[512,768]{1,0:T(8,128)(2,1)S(1)}, bf16[512,768]{1,0:T(8,128)(2,1)}, u32[]{:S(2)}) %copy-start.2) | copy-done | bytes 786456
  4.2 1.0 %copy-done.4 = bf16[192,768]{1,0:T(8,128)(2,1)S(1)} copy-done((bf16[192,768]{1,0:T(8,128)(2,1)S(1)}, bf16[192,768]{1,0:T(8,128)(2,1)}, u32[]{:S(2)}) %copy-start.4) | copy-done | bytes 294936
  5.8 2.2 %attn_forward_other.1 = (bf16[3,512,192]{2,1,0:T(8,128)(2,1)S(1)}, bf16[256,192]{1,0:T(8,128)(2,1)S(1)}, bf16[256,768]{1,0:T(8,128)(2,1)S(1)}) custom-call(s32[1]{0:T(128)S(6)} %copy.617.refs_0_, bf16[512,768]{1,0:T(8,128)(2,1)S(1)} %copy-done.2, bf16[3,192,768]{2,1,0:T(8,128)(2,1)S(1)} %bitcast.2, f32[2,192]{1,0:T(2,128)S(1)} %copy-done.9, ...), custom_call_target="tpu_custom_call" | custom-call | tf_op jit(solution)/shard_map/attn_forward_other/pallas_call | solution.py:123
  8.5 1.6 %attn_forward_own.1 = (bf16[256,192]{1,0:T(8,128)(2,1)S(1)}, f32[256,768]{1,0:T(8,128)S(1)}, bf16[3,512,192]{2,1,0:T(8,128)(2,1)S(1)}, bf16[256,192]{1,0:T(8,128)(2,1)S(1)}) custom-call(s32[1]{0:T(128)S(6)} %copy.617.refs_0_, bf16[192,768]{1,0:T(8,128)(2,1)S(1)} %copy-done.5, ...), custom_call_target="tpu_custom_call", output_to_operand_aliasing={{2}: (2, {}), {3}: (3, {})} | custom-call | tf_op jit(solution)/shard_map/attn_forward_own/pallas_call | solution.py:123
  11.0 2.6 %collective-permute-start.2 = (bf16[128,768]{1,0:T(8,128)(2,1)}, bf16[128,768]{1,0:T(8,128)(2,1)}, u32[]{:S(2)}, u32[]{:S(2)}) collective-permute-start(bf16[128,768]{1,0:T(8,128)(2,1)} %get-tuple-element.360), channel_id=1, source_target_pairs={{0,2},{1,3},{2,0},{3,1},{4,6},{5,7},{6,4},{7,5},{8,10},{9,11},{10,... | collective-permute-start | bytes 589832 | tf_op jit(solution)/shard_map/ppermute | solution.py:562
  15.1 1.3 %copy-done.6 = bf16[768,768]{1,0:T(8,128)(2,1)S(1)} copy-done((bf16[768,768]{1,0:T(8,128)(2,1)S(1)}, bf16[768,768]{1,0:T(8,128)(2,1)}, u32[]{:S(2)}) %copy-start.6) | copy-done | bytes 1179672
  16.4 1.3 %copy-done.7 = bf16[768,768]{1,0:T(8,128)(2,1)S(1)} copy-done((bf16[768,768]{1,0:T(8,128)(2,1)S(1)}, bf16[768,768]{1,0:T(8,128)(2,1)}, u32[]{:S(2)}) %copy-start.7) | copy-done | bytes 1179672
  17.6 2.4 %hold.2 = (bf16[512,768]{1,0:T(8,128)(2,1)S(1)}, bf16[192,768]{1,0:T(8,128)(2,1)S(1)}, bf16[3,192,768]{2,1,0:T(8,128)(2,1)S(1)}, bf16[768,768]{1,0:T(8,128)(2,1)...) custom-call(bf16[512,768]{1,0:T(8,128)(2,1)S(1)} %copy-done.3, ...), custom_call_target="tpu_custom_call", output_to_operand_aliasing={{9}: (9, {}), {10}: (10, {}), {11}: (11, {}), {12}: (12, {})} | custom-call | tf_op jit(solution)/shard_map/hold/pallas_call | solution.py:123
  20.0 2.2 %mlp_forward.2 = (bf16[128,768]{1,0:T(8,128)(2,1)S(1)}, bf16[128,768]{1,0:T(8,128)(2,1)S(1)}, bf16[128,768]{1,0:T(8,128)(2,1)S(1)}, bf16[128,768]{1,0:T(8,128)(2...) custom-call(bf16[128,768]{1,0:T(8,128)(2,1)} %collective-permute-don, ...), custom_call_target="tpu_custom_call", output_to_operand_aliasing={{9}: (1, {}), {10}: (2, {}), {11}: (3, {}), {12}: (4, {}), ... | custom-call | tf_op jit(solution)/shard_map/mlp_forward/pallas_call | solution.py:123
  22.3 1.6 %collective-permute-start.7 = (bf16[128,768]{1,0:T(8,128)(2,1)S(1)}, bf16[128,768]{1,0:T(8,128)(2,1)S(1)}, u32[]{:S(2)}, u32[]{:S(2)}) collective-permute-start(bf16[128,768]{1,0:T(8,128)(2,1)S(1)} %get-tuple-element.398), channel_id=1, source_target_pairs={{0,2},{1,3},{2,0},{3,1},{4,6},{5,7},{6,4},{7,5},{8,10},{9,11},{10,... | collective-permute-start | bytes 589832 | tf_op jit(solution)/shard_map/ppermute | solution.py:562
  24.4 1.3 %mlp_forward.3 = (bf16[128,768]{1,0:T(8,128)(2,1)S(1)}, bf16[128,768]{1,0:T(8,128)(2,1)S(1)}, bf16[128,768]{1,0:T(8,128)(2,1)S(1)}, bf16[128,768]{1,0:T(8,128)(2...) custom-call(bf16[128,768]{1,0:T(8,128)(2,1)S(1)} %collective-permute, ...), custom_call_target="tpu_custom_call", output_to_operand_aliasing={{9}: (1, {}), {10}: (2, {}), {11}: (3, {}), {12}: (4, {}), ... | custom-call | tf_op jit(solution)/shard_map/mlp_forward/pallas_call | solution.py:123
  26.6 3.4 %collective-permute-done.7.refs_1_ = bf16[128,768]{1,0:T(8,128)(2,1)S(1)} collective-permute-done((bf16[128,768]{1,0:T(8,128)(2,1)S(1)}, bf16[128,768]{1,0:T(8,128)(2,1)S(1)}, u32[]{:S(2)}, u32[]{:S(2)}) %collective-permute-start.7) | collective-permute-done | bytes 196640 | tf_op jit(solution)/shard_map/ppermute | solution.py:562
  30.3 2.2 %mlp_backward.2 = (bf16[128,768]{1,0:T(8,128)(2,1)S(1)}, bf16[128,768]{1,0:T(8,128)(2,1)S(1)}, bf16[128,768]{1,0:T(8,128)(2,1)S(1)}, bf16[128,768]{1,0:T(8,128)(...) custom-call(s32[1]{0:T(128)S(6)} %copy.617.refs_0_, ...), custom_call_target="tpu_custom_call", output_to_operand_aliasing={{7}: (2, {}), {8}: (3, {}), {9}: (4, {}), {10}: (5, {}), {1... | custom-call | tf_op jit(solution)/shard_map/mlp_backward/pallas_call | solution.py:123
  33.5 2.7 %mlp_backward.3 = (bf16[128,768]{1,0:T(8,128)(2,1)S(1)}, bf16[128,768]{1,0:T(8,128)(2,1)S(1)}, bf16[128,768]{1,0:T(8,128)(2,1)S(1)}, bf16[128,768]{1,0:T(8,128)(...) custom-call(s32[1]{0:T(128)S(6)} %copy.617.refs_0_, ...), custom_call_target="tpu_custom_call", output_to_operand_aliasing={{11}: (2, {}), {12}: (3, {}), {13}: (4, {}), {14}: (5, {}),... | custom-call | tf_op jit(solution)/shard_map/mlp_backward/pallas_call | solution.py:123
  38.0 1.0 %weight_grad.2 = (bf16[4,96,768]{2,1,0:T(8,128)(2,1)S(1)}, f32[4,96,768]{2,1,0:T(8,128)S(1)}, f32[1,768]{1,0:T(1,128)S(1)}, bf16[3,512,192]{2,1,0:T(8,128)(2,1)S...) custom-call(bf16[256,768]{1,0:T(8,128)(2,1)S(1)} %collective-permute, ...), custom_call_target="tpu_custom_call", output_to_operand_aliasing={{3}: (1, {}), {4}: (2, {}), {5}: (3, {}), {6}: (4, {}), {7}... | custom-call | tf_op jit(solution)/shard_map/weight_grad/pallas_call | solution.py:123
  39.0 1.6 %collective-permute-start.17 = (bf16[4,96,768]{2,1,0:T(8,128)(2,1)S(1)}, bf16[4,96,768]{2,1,0:T(8,128)(2,1)S(1)}, u32[]{:S(2)}, u32[]{:S(2)}) collective-permute-start(bf16[4,96,768]{2,1,0:T(8,128)(2,1)S(1)} %get-tuple-element.572), channel_id=1, source_target_pairs={{0,4},{1,9},{2,6},{3,11},{4,0},{5,13},{6,2},{7,15},{8,12},{9,1},{1... | collective-permute-start | bytes 1769480 | tf_op jit(solution)/shard_map/ppermute | solution.py:578
  42.1 5.7 %collective-permute-done.12.refs_0_ = bf16[256,768]{1,0:T(8,128)(2,1)S(1)} collective-permute-done((bf16[256,768]{1,0:T(8,128)(2,1)S(1)}, bf16[256,768]{1,0:T(8,128)(2,1)S(1)}, u32[]{:S(2)}, u32[]{:S(2)}) %collective-permute-start.12) | collective-permute-done | bytes 393248 | tf_op jit(solution)/shard_map/ppermute | solution.py:562
  49.1 1.6 %collective-permute-start.24 = (bf16[2,96,768]{2,1,0:T(8,128)(2,1)S(1)}, bf16[2,96,768]{2,1,0:T(8,128)(2,1)S(1)}, u32[]{:S(2)}, u32[]{:S(2)}) collective-permute-start(bf16[2,96,768]{2,1,0:T(8,128)(2,1)S(1)} %get-tuple-element.620), channel_id=1, source_target_pairs={{0,8},{1,5},{2,10},{3,7},{4,12},{5,1},{6,14},{7,3},{8,0},{9,13},{1... | collective-permute-start | bytes 884744 | tf_op jit(solution)/shard_map/ppermute | solution.py:578
  50.7 4.4 %attn_backward.1 = (bf16[4,104,768]{2,1,0:T(8,128)(2,1)S(1)}, f32[4,104,768]{2,1,0:T(8,128)S(1)}, bf16[512,192]{1,0:T(8,128)(2,1)S(1)}, bf16[512,192]{1,0:T(8,12...) custom-call(s32[1]{0:T(128)S(6)} %copy.617.refs_0_, ...), custom_call_target="tpu_custom_call", output_to_operand_aliasing={{5}: (4, {}), {6}: (5, {}), {7}: (6, {}), {8}: (7, {}), {9}... | custom-call | tf_op jit(solution)/shard_map/attn_backward/pallas_call | solution.py:123
  55.1 1.6 %collective-permute-start.18 = (bf16[4,104,768]{2,1,0:T(8,128)(2,1)S(1)}, bf16[4,104,768]{2,1,0:T(8,128)(2,1)S(1)}, u32[]{:S(2)}, u32[]{:S(2)}) collective-permute-start(bf16[4,104,768]{2,1,0:T(8,128)(2,1)S(1)} %get-tuple-element.603), channel_id=1, source_target_pairs={{0,4},{1,9},{2,6},{3,11},{4,0},{5,13},{6,2},{7,15},{8,12},{9,1},{1... | collective-permute-start | bytes 1916936 | tf_op jit(solution)/shard_map/ppermute | solution.py:578
  59.9 1.0 %collective-permute-start.26 = (bf16[256,768]{1,0:T(8,128)(2,1)S(1)}, bf16[256,768]{1,0:T(8,128)(2,1)S(1)}, u32[]{:S(2)}, u32[]{:S(2)}) collective-permute-start(bf16[256,768]{1,0:T(8,128)(2,1)S(1)} %get-tuple-element.640.refs_0_), channel_id=1, source_target_pairs={{0,2},{1,3},{2,0},{3,1},{4,6},{5,7},{6,4},{7,5},{8,10},{9,11},{10,... | collective-permute-start | bytes 1179656 | tf_op jit(solution)/shard_map/ppermute | solution.py:562
  60.9 1.6 %collective-permute-start.28 = (bf16[2,96,768]{2,1,0:T(8,128)(2,1)S(1)}, bf16[2,96,768]{2,1,0:T(8,128)(2,1)S(1)}, u32[]{:S(2)}, u32[]{:S(2)}) collective-permute-start(bf16[2,96,768]{2,1,0:T(8,128)(2,1)S(1)} %get-tuple-element.642), channel_id=1, source_target_pairs={{0,8},{1,5},{2,10},{3,7},{4,12},{5,1},{6,14},{7,3},{8,0},{9,13},{1... | collective-permute-start | bytes 884744 | tf_op jit(solution)/shard_map/ppermute | solution.py:578
  62.5 2.6 %collective-permute-start.27 = (bf16[1,96,768]{2,1,0:T(8,128)(2,1)S(1)}, bf16[1,96,768]{2,1,0:T(8,128)(2,1)S(1)}, u32[]{:S(2)}, u32[]{:S(2)}) collective-permute-start(bf16[1,96,768]{2,1,0:T(8,128)(2,1)S(1)} %get-tuple-element.641), channel_id=1, source_target_pairs={{0,16},{1,17},{2,18},{3,19},{4,20},{5,21},{6,22},{7,23},{8,24},{9,... | collective-permute-start | bytes 442376 | tf_op jit(solution)/shard_map/ppermute | solution.py:578
  65.1 2.4 %collective-permute-done.18.refs_0_ = bf16[4,104,768]{2,1,0:T(8,128)(2,1)S(1)} collective-permute-done((bf16[4,104,768]{2,1,0:T(8,128)(2,1)S(1)}, bf16[4,104,768]{2,1,0:T(8,128)(2,1)S(1)}, u32[]{:S(2)}, u32[]{:S(2)}) %collective-permute-start.18) | collective-permute-done | bytes 639008 | tf_op jit(solution)/shard_map/ppermute | solution.py:578
  67.6 1.0 %collective-permute-start.25 = (bf16[2,104,768]{2,1,0:T(8,128)(2,1)S(1)}, bf16[2,104,768]{2,1,0:T(8,128)(2,1)S(1)}, u32[]{:S(2)}, u32[]{:S(2)}) collective-permute-start(bf16[2,104,768]{2,1,0:T(8,128)(2,1)S(1)} %get-tuple-element.639), channel_id=1, source_target_pairs={{0,8},{1,5},{2,10},{3,7},{4,12},{5,1},{6,14},{7,3},{8,0},{9,13},{1... | collective-permute-start | bytes 958472 | tf_op jit(solution)/shard_map/ppermute | solution.py:578
  68.6 2.2 %collective-permute-done.28.refs_0_ = bf16[2,96,768]{2,1,0:T(8,128)(2,1)S(1)} collective-permute-done((bf16[2,96,768]{2,1,0:T(8,128)(2,1)S(1)}, bf16[2,96,768]{2,1,0:T(8,128)(2,1)S(1)}, u32[]{:S(2)}, u32[]{:S(2)}) %collective-permute-start.28) | collective-permute-done | bytes 294944 | tf_op jit(solution)/shard_map/ppermute | solution.py:578
  71.8 2.6 %collective-permute-start.30 = (bf16[1,96,768]{2,1,0:T(8,128)(2,1)S(1)}, bf16[1,96,768]{2,1,0:T(8,128)(2,1)S(1)}, u32[]{:S(2)}, u32[]{:S(2)}) collective-permute-start(bf16[1,96,768]{2,1,0:T(8,128)(2,1)S(1)} %get-tuple-element.673), channel_id=1, source_target_pairs={{0,16},{1,17},{2,18},{3,19},{4,20},{5,21},{6,22},{7,23},{8,24},{9,... | collective-permute-start | bytes 442376 | tf_op jit(solution)/shard_map/ppermute | solution.py:578
  74.7 2.7 %collective-permute-start.32 = (bf16[1,56,768]{2,1,0:T(8,128)(2,1)S(1)}, bf16[1,56,768]{2,1,0:T(8,128)(2,1)S(1)}, u32[]{:S(2)}, u32[]{:S(2)}) collective-permute-start(bf16[1,56,768]{2,1,0:T(8,128)(2,1)S(1)} %get-tuple-element.675), channel_id=1, source_target_pairs={{0,16},{1,17},{2,18},{3,19},{4,20},{5,21},{6,22},{7,23},{8,24},{9,... | collective-permute-start | bytes 258056 | tf_op jit(solution)/shard_map/ppermute | solution.py:578
  79.6 6.5 %collective-permute-done.30.refs_0_ = bf16[1,96,768]{2,1,0:T(8,128)(2,1)S(1)} collective-permute-done((bf16[1,96,768]{2,1,0:T(8,128)(2,1)S(1)}, bf16[1,96,768]{2,1,0:T(8,128)(2,1)S(1)}, u32[]{:S(2)}, u32[]{:S(2)}) %collective-permute-start.30) | collective-permute-done | bytes 147488 | tf_op jit(solution)/shard_map/ppermute | solution.py:578
  86.0 3.0 %collective-permute-done.31.refs_1_ = bf16[1,48,768]{2,1,0:T(8,128)(2,1)S(1)} collective-permute-done((bf16[1,48,768]{2,1,0:T(8,128)(2,1)S(1)}, bf16[1,48,768]{2,1,0:T(8,128)(2,1)S(1)}, u32[]{:S(2)}, u32[]{:S(2)}) %collective-permute-start.31) | collective-permute-done | bytes 73760 | tf_op jit(solution)/shard_map/ppermute | solution.py:578
  89.0 1.0 %run_parts.13 = (f32[96,768]{1,0:T(8,128)}, f32[3,96,192]{2,1,0:T(8,128)}, f32[192,96]{1,0:T(8,128)}, f32[2,24]{1,0:T(2,128)}, f32[96]{0:T(128)}, /*index=5*/f32...) custom-call(bf16[1,96,768]{2,1,0:T(8,128)(2,1)S(1)} %collective-perm, ...), custom_call_target="tpu_custom_call", output_to_operand_aliasing={{11}: (3, {}), {12}: (4, {})} | custom-call | tf_op jit(solution)/shard_map/run_parts/pallas_call | solution.py:123
  (103 shorter events, 17.9 us)
Async XLA Ops:
  0.6 14.4 %collective-permute-start.3 = (bf16[768,768]{1,0:T(8,128)(2,1)}, bf16[768,768]{1,0:T(8,128)(2,1)}, u32[]{:S(2)}, u32[]{:S(2)}) collective-permute-start(bf16[768,768]{1,0:T(8,128)(2,1)} %refs_3_.3), channel_id=1, source_target_pairs={{0,1},{1,0},{2,3},{3,2},{4,5},{5,4},{6,7},{7,6},{8,9},{9,8},{10,11... | collective-permute-start | bytes 3538952 | tf_op jit(solution)/shard_map/ppermute | solution.py:558
  1.2 13.9 %collective-permute-start.4 = (bf16[768,768]{1,0:T(8,128)(2,1)}, bf16[768,768]{1,0:T(8,128)(2,1)}, u32[]{:S(2)}, u32[]{:S(2)}) collective-permute-start(bf16[768,768]{1,0:T(8,128)(2,1)} %refs_5_.1), channel_id=1, source_target_pairs={{0,1},{1,0},{2,3},{3,2},{4,5},{5,4},{6,7},{7,6},{8,9},{9,8},{10,11... | collective-permute-start | bytes 3538952 | tf_op jit(solution)/shard_map/ppermute | solution.py:558
  8.0 2.2 %collective-permute-start = (bf16[256,768]{1,0:T(8,128)(2,1)S(1)}, bf16[256,768]{1,0:T(8,128)(2,1)S(1)}, u32[]{:S(2)}, u32[]{:S(2)}) collective-permute-start(bf16[256,768]{1,0:T(8,128)(2,1)S(1)} %get-tuple-element.355), channel_id=1, source_target_pairs={{0,1},{1,0},{2,3},{3,2},{4,5},{5,4},{6,7},{7,6},{8,9},{9,8},{10,11... | collective-permute-start | bytes 1179656 | tf_op jit(solution)/shard_map/ppermute | solution.py:558
  11.0 9.0 %collective-permute-start.2 = (bf16[128,768]{1,0:T(8,128)(2,1)}, bf16[128,768]{1,0:T(8,128)(2,1)}, u32[]{:S(2)}, u32[]{:S(2)}) collective-permute-start(bf16[128,768]{1,0:T(8,128)(2,1)} %get-tuple-element.360), channel_id=1, source_target_pairs={{0,2},{1,3},{2,0},{3,1},{4,6},{5,7},{6,4},{7,5},{8,10},{9,11},{10,... | collective-permute-start | bytes 589832 | tf_op jit(solution)/shard_map/ppermute | solution.py:562
  14.0 10.4 %collective-permute-start.1 = (bf16[128,768]{1,0:T(8,128)(2,1)}, bf16[128,768]{1,0:T(8,128)(2,1)S(1)}, u32[]{:S(2)}, u32[]{:S(2)}) collective-permute-start(bf16[128,768]{1,0:T(8,128)(2,1)} %copy-done.10), channel_id=1, source_target_pairs={{0,2},{1,3},{2,0},{3,1},{4,6},{5,7},{6,4},{7,5},{8,10},{9,11},{10,... | collective-permute-start | bytes 589832 | tf_op jit(solution)/shard_map/ppermute | solution.py:562
  22.3 7.8 %collective-permute-start.7 = (bf16[128,768]{1,0:T(8,128)(2,1)S(1)}, bf16[128,768]{1,0:T(8,128)(2,1)S(1)}, u32[]{:S(2)}, u32[]{:S(2)}) collective-permute-start(bf16[128,768]{1,0:T(8,128)(2,1)S(1)} %get-tuple-element.398), channel_id=1, source_target_pairs={{0,2},{1,3},{2,0},{3,1},{4,6},{5,7},{6,4},{7,5},{8,10},{9,11},{10,... | collective-permute-start | bytes 589832 | tf_op jit(solution)/shard_map/ppermute | solution.py:562
  23.9 8.6 %collective-permute-start.8 = (bf16[128,768]{1,0:T(8,128)(2,1)S(1)}, bf16[128,768]{1,0:T(8,128)(2,1)S(1)}, u32[]{:S(2)}, u32[]{:S(2)}) collective-permute-start(bf16[128,768]{1,0:T(8,128)(2,1)S(1)} %get-tuple-element.478), channel_id=1, source_target_pairs={{0,1},{1,0},{2,3},{3,2},{4,5},{5,4},{6,7},{7,6},{8,9},{9,8},{10,11... | collective-permute-start | bytes 589832 | tf_op jit(solution)/shard_map/ppermute | solution.py:558
  23.9 8.6 %collective-permute-start.9 = (bf16[128,768]{1,0:T(8,128)(2,1)S(1)}, bf16[128,768]{1,0:T(8,128)(2,1)S(1)}, u32[]{:S(2)}, u32[]{:S(2)}) collective-permute-start(bf16[128,768]{1,0:T(8,128)(2,1)S(1)} %get-tuple-element.479), channel_id=1, source_target_pairs={{0,1},{1,0},{2,3},{3,2},{4,5},{5,4},{6,7},{7,6},{8,9},{9,8},{10,11... | collective-permute-start | bytes 589832 | tf_op jit(solution)/shard_map/ppermute | solution.py:558
  25.7 7.8 %collective-permute-start.6 = (bf16[128,768]{1,0:T(8,128)(2,1)S(1)}, bf16[128,768]{1,0:T(8,128)(2,1)S(1)}, u32[]{:S(2)}, u32[]{:S(2)}) collective-permute-start(bf16[128,768]{1,0:T(8,128)(2,1)S(1)} %get-tuple-element.397), channel_id=1, source_target_pairs={{0,2},{1,3},{2,0},{3,1},{4,6},{5,7},{6,4},{7,5},{8,10},{9,11},{10,... | collective-permute-start | bytes 589832 | tf_op jit(solution)/shard_map/ppermute | solution.py:562
  26.6 6.9 %collective-permute-start.10 = (bf16[128,768]{1,0:T(8,128)(2,1)S(1)}, bf16[128,768]{1,0:T(8,128)(2,1)S(1)}, u32[]{:S(2)}, u32[]{:S(2)}) collective-permute-start(bf16[128,768]{1,0:T(8,128)(2,1)S(1)} %get-tuple-element.480), channel_id=1, source_target_pairs={{0,1},{1,0},{2,3},{3,2},{4,5},{5,4},{6,7},{7,6},{8,9},{9,8},{10,11... | collective-permute-start | bytes 589832 | tf_op jit(solution)/shard_map/ppermute | solution.py:558
  30.1 3.4 %collective-permute-start.11 = (bf16[128,768]{1,0:T(8,128)(2,1)S(1)}, bf16[128,768]{1,0:T(8,128)(2,1)S(1)}, u32[]{:S(2)}, u32[]{:S(2)}) collective-permute-start(bf16[128,768]{1,0:T(8,128)(2,1)S(1)} %get-tuple-element.481), channel_id=1, source_target_pairs={{0,1},{1,0},{2,3},{3,2},{4,5},{5,4},{6,7},{7,6},{8,9},{9,8},{10,11... | collective-permute-start | bytes 589832 | tf_op jit(solution)/shard_map/ppermute | solution.py:558
  36.3 1.7 %collective-permute-start.14 = (bf16[256,768]{1,0:T(8,128)(2,1)S(1)}, bf16[256,768]{1,0:T(8,128)(2,1)S(1)}, u32[]{:S(2)}, u32[]{:S(2)}) collective-permute-start(bf16[256,768]{1,0:T(8,128)(2,1)S(1)} %get-tuple-element.484), channel_id=1, source_target_pairs={{0,1},{1,0},{2,3},{3,2},{4,5},{5,4},{6,7},{7,6},{8,9},{9,8},{10,11... | collective-permute-start | bytes 1179656 | tf_op jit(solution)/shard_map/ppermute | solution.py:558
  36.3 4.3 %collective-permute-start.13 = (bf16[256,768]{1,0:T(8,128)(2,1)S(1)}, bf16[256,768]{1,0:T(8,128)(2,1)S(1)}, u32[]{:S(2)}, u32[]{:S(2)}) collective-permute-start(bf16[256,768]{1,0:T(8,128)(2,1)S(1)} %get-tuple-element.483), channel_id=1, source_target_pairs={{0,1},{1,0},{2,3},{3,2},{4,5},{5,4},{6,7},{7,6},{8,9},{9,8},{10,11... | collective-permute-start | bytes 1179656 | tf_op jit(solution)/shard_map/ppermute | solution.py:558
  36.8 11.0 %collective-permute-start.12 = (bf16[256,768]{1,0:T(8,128)(2,1)S(1)}, bf16[256,768]{1,0:T(8,128)(2,1)S(1)}, u32[]{:S(2)}, u32[]{:S(2)}) collective-permute-start(bf16[256,768]{1,0:T(8,128)(2,1)S(1)} %get-tuple-element.482), channel_id=1, source_target_pairs={{0,2},{1,3},{2,0},{3,1},{4,6},{5,7},{6,4},{7,5},{8,10},{9,11},{10,... | collective-permute-start | bytes 1179656 | tf_op jit(solution)/shard_map/ppermute | solution.py:562
  37.7 10.1 %collective-permute-start.15 = (bf16[256,768]{1,0:T(8,128)(2,1)S(1)}, bf16[256,768]{1,0:T(8,128)(2,1)S(1)}, u32[]{:S(2)}, u32[]{:S(2)}) collective-permute-start(bf16[256,768]{1,0:T(8,128)(2,1)S(1)} %get-tuple-element.569.refs_23_), channel_id=1, source_target_pairs={{0,1},{1,0},{2,3},{3,2},{4,5},{5,4},{6,7},{7,6},{8,9},{9,8},{10,11... | collective-permute-start | bytes 1179656 | tf_op jit(solution)/shard_map/ppermute | solution.py:558
  39.0 9.9 %collective-permute-start.17 = (bf16[4,96,768]{2,1,0:T(8,128)(2,1)S(1)}, bf16[4,96,768]{2,1,0:T(8,128)(2,1)S(1)}, u32[]{:S(2)}, u32[]{:S(2)}) collective-permute-start(bf16[4,96,768]{2,1,0:T(8,128)(2,1)S(1)} %get-tuple-element.572), channel_id=1, source_target_pairs={{0,4},{1,9},{2,6},{3,11},{4,0},{5,13},{6,2},{7,15},{8,12},{9,1},{1... | collective-permute-start | bytes 1769480 | tf_op jit(solution)/shard_map/ppermute | solution.py:578
  41.5 16.9 %collective-permute-start.23 = (bf16[4,96,768]{2,1,0:T(8,128)(2,1)S(1)}, bf16[4,96,768]{2,1,0:T(8,128)(2,1)S(1)}, u32[]{:S(2)}, u32[]{:S(2)}) collective-permute-start(bf16[4,96,768]{2,1,0:T(8,128)(2,1)S(1)} %get-tuple-element.619), channel_id=1, source_target_pairs={{0,4},{1,9},{2,6},{3,11},{4,0},{5,13},{6,2},{7,15},{8,12},{9,1},{1... | collective-permute-start | bytes 1769480 | tf_op jit(solution)/shard_map/ppermute | solution.py:578
  48.4 2.3 %collective-permute-start.16 = (bf16[272,768]{1,0:T(8,128)(2,1)S(1)}, bf16[272,768]{1,0:T(8,128)(2,1)S(1)}, u32[]{:S(2)}, u32[]{:S(2)}) collective-permute-start(bf16[272,768]{1,0:T(8,128)(2,1)S(1)} %get-tuple-element.570.refs_1_), channel_id=1, source_target_pairs={{0,1},{1,0},{2,3},{3,2},{4,5},{5,4},{6,7},{7,6},{8,9},{9,8},{10,11... | collective-permute-start | bytes 1253384 | tf_op jit(solution)/shard_map/ppermute | solution.py:558
  49.1 9.3 %collective-permute-start.24 = (bf16[2,96,768]{2,1,0:T(8,128)(2,1)S(1)}, bf16[2,96,768]{2,1,0:T(8,128)(2,1)S(1)}, u32[]{:S(2)}, u32[]{:S(2)}) collective-permute-start(bf16[2,96,768]{2,1,0:T(8,128)(2,1)S(1)} %get-tuple-element.620), channel_id=1, source_target_pairs={{0,8},{1,5},{2,10},{3,7},{4,12},{5,1},{6,14},{7,3},{8,0},{9,13},{1... | collective-permute-start | bytes 884744 | tf_op jit(solution)/shard_map/ppermute | solution.py:578
  55.1 12.4 %collective-permute-start.18 = (bf16[4,104,768]{2,1,0:T(8,128)(2,1)S(1)}, bf16[4,104,768]{2,1,0:T(8,128)(2,1)S(1)}, u32[]{:S(2)}, u32[]{:S(2)}) collective-permute-start(bf16[4,104,768]{2,1,0:T(8,128)(2,1)S(1)} %get-tuple-element.603), channel_id=1, source_target_pairs={{0,4},{1,9},{2,6},{3,11},{4,0},{5,13},{6,2},{7,15},{8,12},{9,1},{1... | collective-permute-start | bytes 1916936 | tf_op jit(solution)/shard_map/ppermute | solution.py:578
  57.4 1.6 %collective-permute-start.19 = (bf16[64,768]{1,0:T(8,128)(2,1)S(1)}, bf16[64,768]{1,0:T(8,128)(2,1)S(1)}, u32[]{:S(2)}, u32[]{:S(2)}) collective-permute-start(bf16[64,768]{1,0:T(8,128)(2,1)S(1)} %get-tuple-element.615), channel_id=1, source_target_pairs={{0,1},{1,0},{2,3},{3,2},{4,5},{5,4},{6,7},{7,6},{8,9},{9,8},{10,11... | collective-permute-start | bytes 294920 | tf_op jit(solution)/shard_map/ppermute | solution.py:558
  57.5 1.6 %collective-permute-start.20 = (bf16[64,768]{1,0:T(8,128)(2,1)S(1)}, bf16[64,768]{1,0:T(8,128)(2,1)S(1)}, u32[]{:S(2)}, u32[]{:S(2)}) collective-permute-start(bf16[64,768]{1,0:T(8,128)(2,1)S(1)} %get-tuple-element.616), channel_id=1, source_target_pairs={{0,1},{1,0},{2,3},{3,2},{4,5},{5,4},{6,7},{7,6},{8,9},{9,8},{10,11... | collective-permute-start | bytes 294920 | tf_op jit(solution)/shard_map/ppermute | solution.py:558
  58.4 1.3 %collective-permute-start.21 = (bf16[64,768]{1,0:T(8,128)(2,1)S(1)}, bf16[64,768]{1,0:T(8,128)(2,1)S(1)}, u32[]{:S(2)}, u32[]{:S(2)}) collective-permute-start(bf16[64,768]{1,0:T(8,128)(2,1)S(1)} %get-tuple-element.617), channel_id=1, source_target_pairs={{0,1},{1,0},{2,3},{3,2},{4,5},{5,4},{6,7},{7,6},{8,9},{9,8},{10,11... | collective-permute-start | bytes 294920 | tf_op jit(solution)/shard_map/ppermute | solution.py:558
  58.4 1.5 %collective-permute-start.22 = (bf16[64,768]{1,0:T(8,128)(2,1)S(1)}, bf16[64,768]{1,0:T(8,128)(2,1)S(1)}, u32[]{:S(2)}, u32[]{:S(2)}) collective-permute-start(bf16[64,768]{1,0:T(8,128)(2,1)S(1)} %get-tuple-element.618), channel_id=1, source_target_pairs={{0,1},{1,0},{2,3},{3,2},{4,5},{5,4},{6,7},{7,6},{8,9},{9,8},{10,11... | collective-permute-start | bytes 294920 | tf_op jit(solution)/shard_map/ppermute | solution.py:558
  59.9 11.7 %collective-permute-start.26 = (bf16[256,768]{1,0:T(8,128)(2,1)S(1)}, bf16[256,768]{1,0:T(8,128)(2,1)S(1)}, u32[]{:S(2)}, u32[]{:S(2)}) collective-permute-start(bf16[256,768]{1,0:T(8,128)(2,1)S(1)} %get-tuple-element.640.refs_0_), channel_id=1, source_target_pairs={{0,2},{1,3},{2,0},{3,1},{4,6},{5,7},{6,4},{7,5},{8,10},{9,11},{10,... | collective-permute-start | bytes 1179656 | tf_op jit(solution)/shard_map/ppermute | solution.py:562
  60.9 9.9 %collective-permute-start.28 = (bf16[2,96,768]{2,1,0:T(8,128)(2,1)S(1)}, bf16[2,96,768]{2,1,0:T(8,128)(2,1)S(1)}, u32[]{:S(2)}, u32[]{:S(2)}) collective-permute-start(bf16[2,96,768]{2,1,0:T(8,128)(2,1)S(1)} %get-tuple-element.642), channel_id=1, source_target_pairs={{0,8},{1,5},{2,10},{3,7},{4,12},{5,1},{6,14},{7,3},{8,0},{9,13},{1... | collective-permute-start | bytes 884744 | tf_op jit(solution)/shard_map/ppermute | solution.py:578
  62.5 8.4 %collective-permute-start.27 = (bf16[1,96,768]{2,1,0:T(8,128)(2,1)S(1)}, bf16[1,96,768]{2,1,0:T(8,128)(2,1)S(1)}, u32[]{:S(2)}, u32[]{:S(2)}) collective-permute-start(bf16[1,96,768]{2,1,0:T(8,128)(2,1)S(1)} %get-tuple-element.641), channel_id=1, source_target_pairs={{0,16},{1,17},{2,18},{3,19},{4,20},{5,21},{6,22},{7,23},{8,24},{9,... | collective-permute-start | bytes 442376 | tf_op jit(solution)/shard_map/ppermute | solution.py:578
  67.6 7.1 %collective-permute-start.25 = (bf16[2,104,768]{2,1,0:T(8,128)(2,1)S(1)}, bf16[2,104,768]{2,1,0:T(8,128)(2,1)S(1)}, u32[]{:S(2)}, u32[]{:S(2)}) collective-permute-start(bf16[2,104,768]{2,1,0:T(8,128)(2,1)S(1)} %get-tuple-element.639), channel_id=1, source_target_pairs={{0,8},{1,5},{2,10},{3,7},{4,12},{5,1},{6,14},{7,3},{8,0},{9,13},{1... | collective-permute-start | bytes 958472 | tf_op jit(solution)/shard_map/ppermute | solution.py:578
  71.8 6.9 %collective-permute-start.29 = (bf16[256,768]{1,0:T(8,128)(2,1)S(1)}, bf16[256,768]{1,0:T(8,128)(2,1)S(1)}, u32[]{:S(2)}, u32[]{:S(2)}) collective-permute-start(bf16[256,768]{1,0:T(8,128)(2,1)S(1)} %get-tuple-element.669.refs_0_), channel_id=1, source_target_pairs={{0,1},{1,0},{2,3},{3,2},{4,5},{5,4},{6,7},{7,6},{8,9},{9,8},{10,11... | collective-permute-start | bytes 1179656 | tf_op jit(solution)/shard_map/ppermute | solution.py:558
  71.8 14.2 %collective-permute-start.30 = (bf16[1,96,768]{2,1,0:T(8,128)(2,1)S(1)}, bf16[1,96,768]{2,1,0:T(8,128)(2,1)S(1)}, u32[]{:S(2)}, u32[]{:S(2)}) collective-permute-start(bf16[1,96,768]{2,1,0:T(8,128)(2,1)S(1)} %get-tuple-element.673), channel_id=1, source_target_pairs={{0,16},{1,17},{2,18},{3,19},{4,20},{5,21},{6,22},{7,23},{8,24},{9,... | collective-permute-start | bytes 442376 | tf_op jit(solution)/shard_map/ppermute | solution.py:578
  74.7 14.3 %collective-permute-start.32 = (bf16[1,56,768]{2,1,0:T(8,128)(2,1)S(1)}, bf16[1,56,768]{2,1,0:T(8,128)(2,1)S(1)}, u32[]{:S(2)}, u32[]{:S(2)}) collective-permute-start(bf16[1,56,768]{2,1,0:T(8,128)(2,1)S(1)} %get-tuple-element.675), channel_id=1, source_target_pairs={{0,16},{1,17},{2,18},{3,19},{4,20},{5,21},{6,22},{7,23},{8,24},{9,... | collective-permute-start | bytes 258056 | tf_op jit(solution)/shard_map/ppermute | solution.py:578
  77.3 11.7 %collective-permute-start.31 = (bf16[1,48,768]{2,1,0:T(8,128)(2,1)S(1)}, bf16[1,48,768]{2,1,0:T(8,128)(2,1)S(1)}, u32[]{:S(2)}, u32[]{:S(2)}) collective-permute-start(bf16[1,48,768]{2,1,0:T(8,128)(2,1)S(1)} %get-tuple-element.674), channel_id=1, source_target_pairs={{0,16},{1,17},{2,18},{3,19},{4,20},{5,21},{6,22},{7,23},{8,24},{9,... | collective-permute-start | bytes 221192 | tf_op jit(solution)/shard_map/ppermute | solution.py:578
  (19 other events, 52.5 us)

commit v8 on v7

--- a/solution.py
+++ b/solution.py
@@ -233,13 +233,12 @@
         out[picked, :] = (kept[picked, :] + part[...].astype(F32)).astype(LOW)
 
 
-def final_rows(*refs):
-    resids, (own, received, out) = refs[:-3], refs[-3:]
-    rows = resids[0].shape[0]
-    for index, resid in enumerate(resids):
+def final_rows(resid, own, received, *outs):
+    rows = outs[0].shape[0]
+    for index, out in enumerate(outs):
         picked = slice(index * rows, (index + 1) * rows)
-        out[picked, :] = (
-            resid[...] + (own[picked, :].astype(F32) + received[picked, :].astype(F32))
+        out[...] = (
+            resid[picked, :] + (own[picked, :].astype(F32) + received[picked, :].astype(F32))
         ).astype(LOW)
 
 
@@ -832,8 +831,9 @@
     others = [(H_DOWN_KEEP,), (H_UP_KEEP,)]
     while running[(H_ATTN_KEEP,)][1] < steps:
         if running[(H_ATTN_KEEP,)][1] == steps - 1:
-            (token_half,) = state.call(
-                final_rows, [((half, model), LOW)], (H_LAST,), token_own, token_received
+            token_half = state.call(
+                final_rows, [((half // PIECES, model), LOW)] * PIECES, (H_LAST,),
+                token_own, token_received,
             )
             state.drop((H_LAST,))
         advance((H_ATTN_KEEP,))
@@ -846,7 +846,7 @@
     )
     state.drop((H_OUT_HALF,), (H_OUT_OTHER,))
     (token_total,) = state.call(
-        place_rows, [((rows, model), LOW)], token_half, to_core(token_half),
+        place_rows, [((rows, model), LOW)], *token_half, *[to_core(part) for part in token_half],
     )
     advance(*[name for name in others if name in running], (H_ATTN_KEEP,))
     sum_w_down, sum_w_up = finished[(H_DOWN_KEEP,)], finished[(H_UP_KEEP,)]

time: 90.4 us -> 101 us (1.12)
  waiting for transfers between devices: 26.5 us -> 35.5 us
  starting transfers between devices: 27.5 us -> 29.4 us
    ppermute x10, waiting for transfers between devices: 15 us -> 23.1 us  [to_dp(): return lax.ppermute(block, ('dp', 'tensor'), pairs)]
    ppermute x10, starting transfers between devices: 16.1 us -> 17.4 us  [to_dp(): return lax.ppermute(block, ('dp', 'tensor'), pairs)]
    ppermute x17 -> x20, starting transfers between devices: 3.57 us -> 4.15 us  [to_core(): return lax.ppermute(block, 'tensor', CORE_PAIRS)]
  transfers between devices with their start and end apart: 33 -> 36, of which waited for: 14 -> 11; matrix products, arithmetic and copies ran while one was open for 0% -> 0% of each run, Pallas kernels for 27% -> 24%
where the time goes in v8:
time: 101 us
  waiting for transfers between devices  35.5 us (35%)
  starting transfers between devices  29.4 us (29%)
  Pallas kernels  27.6 us (27%)
  local copies, waits for them, and re-layouts  6.62 us (7%)
  between operations  1.73 us (2%)
    pallas_call x25, Pallas kernels, call(): pl.pallas_call(body, name=getattr(kernel, 'func', kernel).__name__, out_s...  27.6 us
    ppermute x10, waiting for transfers between devices, to_dp(): return lax.ppermute(block, ('dp', 'tensor'), pairs)  23.1 us
    ppermute x10, starting transfers between devices, to_dp(): return lax.ppermute(block, ('dp', 'tensor'), pairs)  17.4 us
    ppermute x6, waiting for transfers between devices, to_chip(): return lax.ppermute(block, 'tensor', CHIP_PAIRS)  10.7 us
    ppermute x6, starting transfers between devices, to_chip(): return lax.ppermute(block, 'tensor', CHIP_PAIRS)  7.85 us
    unnamed x36, local copies, waits for them, and re-layouts  6.54 us
    ppermute x20, starting transfers between devices, to_core(): return lax.ppermute(block, 'tensor', CORE_PAIRS)  4.15 us
  transfers between devices with their start and end apart: 36, of which 11 were waited for; matrix products, arithmetic and copies ran while one was open for 0% of the time, Pallas kernels for 24%

profile of v8, /device:TPU:0, one launch (start us, length us, event | category | flops | bytes accessed | tf_op | source)
XLA Modules:
  0.0 100.9 jit_solution(344923197785386404)
XLA Ops:
  1.9 1.2 %copy-done = bf16[3,768,192]{1,2,0:T(8,128)(2,1)S(1)} copy-done((bf16[3,768,192]{1,2,0:T(8,128)(2,1)S(1)}, bf16[3,768,192]{1,2,0:T(8,128)(2,1)}, u32[]{:S(2)}) %copy-start) | copy-done | bytes 884760
  3.1 1.1 %copy-done.2 = bf16[512,768]{1,0:T(8,128)(2,1)S(1)} copy-done((bf16[512,768]{1,0:T(8,128)(2,1)S(1)}, bf16[512,768]{1,0:T(8,128)(2,1)}, u32[]{:S(2)}) %copy-start.2) | copy-done | bytes 786456
  5.8 2.2 %attn_forward_other.1 = (bf16[3,512,192]{2,1,0:T(8,128)(2,1)S(1)}, bf16[256,192]{1,0:T(8,128)(2,1)S(1)}, bf16[256,768]{1,0:T(8,128)(2,1)S(1)}) custom-call(s32[1]{0:T(128)S(6)} %copy.617.refs_0_, bf16[512,768]{1,0:T(8,128)(2,1)S(1)} %copy-done.2, bf16[3,192,768]{2,1,0:T(8,128)(2,1)S(1)} %bitcast.2, f32[2,192]{1,0:T(2,128)S(1)} %copy-done.9, ...), custom_call_target="tpu_custom_call" | custom-call | tf_op jit(solution)/shard_map/attn_forward_other/pallas_call | solution.py:123
  8.5 1.6 %attn_forward_own.1 = (bf16[256,192]{1,0:T(8,128)(2,1)S(1)}, f32[256,768]{1,0:T(8,128)S(1)}, bf16[3,512,192]{2,1,0:T(8,128)(2,1)S(1)}, bf16[256,192]{1,0:T(8,128)(2,1)S(1)}) custom-call(s32[1]{0:T(128)S(6)} %copy.617.refs_0_, bf16[192,768]{1,0:T(8,128)(2,1)S(1)} %copy-done.5, ...), custom_call_target="tpu_custom_call", output_to_operand_aliasing={{2}: (2, {}), {3}: (3, {})} | custom-call | tf_op jit(solution)/shard_map/attn_forward_own/pallas_call | solution.py:123
  11.0 2.6 %collective-permute-start.2 = (bf16[128,768]{1,0:T(8,128)(2,1)}, bf16[128,768]{1,0:T(8,128)(2,1)}, u32[]{:S(2)}, u32[]{:S(2)}) collective-permute-start(bf16[128,768]{1,0:T(8,128)(2,1)} %get-tuple-element.363), channel_id=1, source_target_pairs={{0,2},{1,3},{2,0},{3,1},{4,6},{5,7},{6,4},{7,5},{8,10},{9,11},{10,... | collective-permute-start | bytes 589832 | tf_op jit(solution)/shard_map/ppermute | solution.py:561
  15.1 1.3 %copy-done.6 = bf16[768,768]{1,0:T(8,128)(2,1)S(1)} copy-done((bf16[768,768]{1,0:T(8,128)(2,1)S(1)}, bf16[768,768]{1,0:T(8,128)(2,1)}, u32[]{:S(2)}) %copy-start.6) | copy-done | bytes 1179672
  16.4 1.3 %copy-done.7 = bf16[768,768]{1,0:T(8,128)(2,1)S(1)} copy-done((bf16[768,768]{1,0:T(8,128)(2,1)S(1)}, bf16[768,768]{1,0:T(8,128)(2,1)}, u32[]{:S(2)}) %copy-start.7) | copy-done | bytes 1179672
  17.6 2.4 %hold.2 = (bf16[512,768]{1,0:T(8,128)(2,1)S(1)}, bf16[192,768]{1,0:T(8,128)(2,1)S(1)}, bf16[3,192,768]{2,1,0:T(8,128)(2,1)S(1)}, bf16[768,768]{1,0:T(8,128)(2,1)...) custom-call(bf16[512,768]{1,0:T(8,128)(2,1)S(1)} %copy-done.3, ...), custom_call_target="tpu_custom_call", output_to_operand_aliasing={{9}: (9, {}), {10}: (10, {}), {11}: (11, {}), {12}: (12, {})} | custom-call | tf_op jit(solution)/shard_map/hold/pallas_call | solution.py:123
  20.0 2.2 %mlp_forward.2 = (bf16[128,768]{1,0:T(8,128)(2,1)S(1)}, bf16[128,768]{1,0:T(8,128)(2,1)S(1)}, bf16[128,768]{1,0:T(8,128)(2,1)S(1)}, bf16[128,768]{1,0:T(8,128)(2...) custom-call(bf16[128,768]{1,0:T(8,128)(2,1)} %collective-permute-don, ...), custom_call_target="tpu_custom_call", output_to_operand_aliasing={{9}: (1, {}), {10}: (2, {}), {11}: (3, {}), {12}: (4, {}), ... | custom-call | tf_op jit(solution)/shard_map/mlp_forward/pallas_call | solution.py:123
  22.3 1.6 %collective-permute-start.7 = (bf16[128,768]{1,0:T(8,128)(2,1)S(1)}, bf16[128,768]{1,0:T(8,128)(2,1)S(1)}, u32[]{:S(2)}, u32[]{:S(2)}) collective-permute-start(bf16[128,768]{1,0:T(8,128)(2,1)S(1)} %get-tuple-element.401), channel_id=1, source_target_pairs={{0,2},{1,3},{2,0},{3,1},{4,6},{5,7},{6,4},{7,5},{8,10},{9,11},{10,... | collective-permute-start | bytes 589832 | tf_op jit(solution)/shard_map/ppermute | solution.py:561
  24.4 1.3 %mlp_forward.3 = (bf16[128,768]{1,0:T(8,128)(2,1)S(1)}, bf16[128,768]{1,0:T(8,128)(2,1)S(1)}, bf16[128,768]{1,0:T(8,128)(2,1)S(1)}, bf16[128,768]{1,0:T(8,128)(2...) custom-call(bf16[128,768]{1,0:T(8,128)(2,1)S(1)} %collective-permute, ...), custom_call_target="tpu_custom_call", output_to_operand_aliasing={{9}: (1, {}), {10}: (2, {}), {11}: (3, {}), {12}: (4, {}), ... | custom-call | tf_op jit(solution)/shard_map/mlp_forward/pallas_call | solution.py:123
  26.6 3.4 %collective-permute-done.7.refs_1_ = bf16[128,768]{1,0:T(8,128)(2,1)S(1)} collective-permute-done((bf16[128,768]{1,0:T(8,128)(2,1)S(1)}, bf16[128,768]{1,0:T(8,128)(2,1)S(1)}, u32[]{:S(2)}, u32[]{:S(2)}) %collective-permute-start.7) | collective-permute-done | bytes 196640 | tf_op jit(solution)/shard_map/ppermute | solution.py:561
  30.3 2.2 %mlp_backward.2 = (bf16[128,768]{1,0:T(8,128)(2,1)S(1)}, bf16[128,768]{1,0:T(8,128)(2,1)S(1)}, bf16[128,768]{1,0:T(8,128)(2,1)S(1)}, bf16[128,768]{1,0:T(8,128)(...) custom-call(s32[1]{0:T(128)S(6)} %copy.617.refs_0_, ...), custom_call_target="tpu_custom_call", output_to_operand_aliasing={{7}: (2, {}), {8}: (3, {}), {9}: (4, {}), {10}: (5, {}), {1... | custom-call | tf_op jit(solution)/shard_map/mlp_backward/pallas_call | solution.py:123
  33.5 2.7 %mlp_backward.3 = (bf16[128,768]{1,0:T(8,128)(2,1)S(1)}, bf16[128,768]{1,0:T(8,128)(2,1)S(1)}, bf16[128,768]{1,0:T(8,128)(2,1)S(1)}, bf16[128,768]{1,0:T(8,128)(...) custom-call(s32[1]{0:T(128)S(6)} %copy.617.refs_0_, ...), custom_call_target="tpu_custom_call", output_to_operand_aliasing={{11}: (2, {}), {12}: (3, {}), {13}: (4, {}), {14}: (5, {}),... | custom-call | tf_op jit(solution)/shard_map/mlp_backward/pallas_call | solution.py:123
  38.0 1.0 weight_grad.2
  39.0 1.6 %collective-permute-start.17 = (bf16[4,96,768]{2,1,0:T(8,128)(2,1)S(1)}, bf16[4,96,768]{2,1,0:T(8,128)(2,1)S(1)}, u32[]{:S(2)}, u32[]{:S(2)}) collective-permute-start(bf16[4,96,768]{2,1,0:T(8,128)(2,1)S(1)} %get-tuple-element.575), channel_id=1, source_target_pairs={{0,4},{1,9},{2,6},{3,11},{4,0},{5,13},{6,2},{7,15},{8,12},{9,1},{1... | collective-permute-start | bytes 1769480 | tf_op jit(solution)/shard_map/ppermute | solution.py:577
  41.5 6.3 %collective-permute-done.12.refs_0_ = bf16[256,768]{1,0:T(8,128)(2,1)S(1)} collective-permute-done((bf16[256,768]{1,0:T(8,128)(2,1)S(1)}, bf16[256,768]{1,0:T(8,128)(2,1)S(1)}, u32[]{:S(2)}, u32[]{:S(2)}) %collective-permute-start.12) | collective-permute-done | bytes 393248 | tf_op jit(solution)/shard_map/ppermute | solution.py:561
  48.5 1.6 %collective-permute-start.23 = (bf16[4,96,768]{2,1,0:T(8,128)(2,1)S(1)}, bf16[4,96,768]{2,1,0:T(8,128)(2,1)S(1)}, u32[]{:S(2)}, u32[]{:S(2)}) collective-permute-start(bf16[4,96,768]{2,1,0:T(8,128)(2,1)S(1)} %get-tuple-element.622), channel_id=1, source_target_pairs={{0,4},{1,9},{2,6},{3,11},{4,0},{5,13},{6,2},{7,15},{8,12},{9,1},{1... | collective-permute-start | bytes 1769480 | tf_op jit(solution)/shard_map/ppermute | solution.py:577
  50.3 4.4 %attn_backward.1 = (bf16[4,104,768]{2,1,0:T(8,128)(2,1)S(1)}, f32[4,104,768]{2,1,0:T(8,128)S(1)}, bf16[512,192]{1,0:T(8,128)(2,1)S(1)}, bf16[512,192]{1,0:T(8,12...) custom-call(s32[1]{0:T(128)S(6)} %copy.617.refs_0_, ...), custom_call_target="tpu_custom_call", output_to_operand_aliasing={{5}: (4, {}), {6}: (5, {}), {7}: (6, {}), {8}: (7, {}), {9}... | custom-call | tf_op jit(solution)/shard_map/attn_backward/pallas_call | solution.py:123
  54.7 1.6 %collective-permute-start.18 = (bf16[4,104,768]{2,1,0:T(8,128)(2,1)S(1)}, bf16[4,104,768]{2,1,0:T(8,128)(2,1)S(1)}, u32[]{:S(2)}, u32[]{:S(2)}) collective-permute-start(bf16[4,104,768]{2,1,0:T(8,128)(2,1)S(1)} %get-tuple-element.606), channel_id=1, source_target_pairs={{0,4},{1,9},{2,6},{3,11},{4,0},{5,13},{6,2},{7,15},{8,12},{9,1},{1... | collective-permute-start | bytes 1916936 | tf_op jit(solution)/shard_map/ppermute | solution.py:577
  56.2 1.6 %collective-permute-start.24 = (bf16[2,96,768]{2,1,0:T(8,128)(2,1)S(1)}, bf16[2,96,768]{2,1,0:T(8,128)(2,1)S(1)}, u32[]{:S(2)}, u32[]{:S(2)}) collective-permute-start(bf16[2,96,768]{2,1,0:T(8,128)(2,1)S(1)} %get-tuple-element.623), channel_id=1, source_target_pairs={{0,8},{1,5},{2,10},{3,7},{4,12},{5,1},{6,14},{7,3},{8,0},{9,13},{1... | collective-permute-start | bytes 884744 | tf_op jit(solution)/shard_map/ppermute | solution.py:577
  59.2 6.9 %collective-permute-done.24.refs_1_ = bf16[2,96,768]{2,1,0:T(8,128)(2,1)S(1)} collective-permute-done((bf16[2,96,768]{2,1,0:T(8,128)(2,1)S(1)}, bf16[2,96,768]{2,1,0:T(8,128)(2,1)S(1)}, u32[]{:S(2)}, u32[]{:S(2)}) %collective-permute-start.24) | collective-permute-done | bytes 294944 | tf_op jit(solution)/shard_map/ppermute | solution.py:577
  66.3 1.1 %collective-permute-done.22.refs_4_ = bf16[64,768]{1,0:T(8,128)(2,1)S(1)} collective-permute-done((bf16[64,768]{1,0:T(8,128)(2,1)S(1)}, bf16[64,768]{1,0:T(8,128)(2,1)S(1)}, u32[]{:S(2)}, u32[]{:S(2)}) %collective-permute-start.22) | collective-permute-done | bytes 98336 | tf_op jit(solution)/shard_map/ppermute | solution.py:557
  67.6 1.0 %collective-permute-start.26 = (bf16[256,768]{1,0:T(8,128)(2,1)S(1)}, bf16[256,768]{1,0:T(8,128)(2,1)S(1)}, u32[]{:S(2)}, u32[]{:S(2)}) collective-permute-start(bf16[256,768]{1,0:T(8,128)(2,1)S(1)} %get-tuple-element.643.refs_0_), channel_id=1, source_target_pairs={{0,2},{1,3},{2,0},{3,1},{4,6},{5,7},{6,4},{7,5},{8,10},{9,11},{10,... | collective-permute-start | bytes 1179656 | tf_op jit(solution)/shard_map/ppermute | solution.py:561
  68.6 1.6 %collective-permute-start.28 = (bf16[2,96,768]{2,1,0:T(8,128)(2,1)S(1)}, bf16[2,96,768]{2,1,0:T(8,128)(2,1)S(1)}, u32[]{:S(2)}, u32[]{:S(2)}) collective-permute-start(bf16[2,96,768]{2,1,0:T(8,128)(2,1)S(1)} %get-tuple-element.645), channel_id=1, source_target_pairs={{0,8},{1,5},{2,10},{3,7},{4,12},{5,1},{6,14},{7,3},{8,0},{9,13},{1... | collective-permute-start | bytes 884744 | tf_op jit(solution)/shard_map/ppermute | solution.py:577
  70.8 2.6 %collective-permute-start.27 = (bf16[1,96,768]{2,1,0:T(8,128)(2,1)S(1)}, bf16[1,96,768]{2,1,0:T(8,128)(2,1)S(1)}, u32[]{:S(2)}, u32[]{:S(2)}) collective-permute-start(bf16[1,96,768]{2,1,0:T(8,128)(2,1)S(1)} %get-tuple-element.644), channel_id=1, source_target_pairs={{0,16},{1,17},{2,18},{3,19},{4,20},{5,21},{6,22},{7,23},{8,24},{9,... | collective-permute-start | bytes 442376 | tf_op jit(solution)/shard_map/ppermute | solution.py:577
  73.4 5.1 %collective-permute-done.28.refs_0_ = bf16[2,96,768]{2,1,0:T(8,128)(2,1)S(1)} collective-permute-done((bf16[2,96,768]{2,1,0:T(8,128)(2,1)S(1)}, bf16[2,96,768]{2,1,0:T(8,128)(2,1)S(1)}, u32[]{:S(2)}, u32[]{:S(2)}) %collective-permute-start.28) | collective-permute-done | bytes 294944 | tf_op jit(solution)/shard_map/ppermute | solution.py:577
  78.5 2.5 %collective-permute-done.27.refs_0_ = bf16[1,96,768]{2,1,0:T(8,128)(2,1)S(1)} collective-permute-done((bf16[1,96,768]{2,1,0:T(8,128)(2,1)S(1)}, bf16[1,96,768]{2,1,0:T(8,128)(2,1)S(1)}, u32[]{:S(2)}, u32[]{:S(2)}) %collective-permute-start.27) | collective-permute-done | bytes 147488 | tf_op jit(solution)/shard_map/ppermute | solution.py:577
  82.4 3.4 %collective-permute-start.33 = (bf16[1,96,768]{2,1,0:T(8,128)(2,1)S(1)}, bf16[1,96,768]{2,1,0:T(8,128)(2,1)S(1)}, u32[]{:S(2)}, u32[]{:S(2)}) collective-permute-start(bf16[1,96,768]{2,1,0:T(8,128)(2,1)S(1)} %get-tuple-element.679), channel_id=1, source_target_pairs={{0,16},{1,17},{2,18},{3,19},{4,20},{5,21},{6,22},{7,23},{8,24},{9,... | collective-permute-start | bytes 442376 | tf_op jit(solution)/shard_map/ppermute | solution.py:577
  86.6 2.8 %collective-permute-start.34 = (bf16[1,48,768]{2,1,0:T(8,128)(2,1)S(1)}, bf16[1,48,768]{2,1,0:T(8,128)(2,1)S(1)}, u32[]{:S(2)}, u32[]{:S(2)}) collective-permute-start(bf16[1,48,768]{2,1,0:T(8,128)(2,1)S(1)} %get-tuple-element.680), channel_id=1, source_target_pairs={{0,16},{1,17},{2,18},{3,19},{4,20},{5,21},{6,22},{7,23},{8,24},{9,... | collective-permute-start | bytes 221192 | tf_op jit(solution)/shard_map/ppermute | solution.py:577
  91.3 5.8 %collective-permute-done.33.refs_0_ = bf16[1,96,768]{2,1,0:T(8,128)(2,1)S(1)} collective-permute-done((bf16[1,96,768]{2,1,0:T(8,128)(2,1)S(1)}, bf16[1,96,768]{2,1,0:T(8,128)(2,1)S(1)}, u32[]{:S(2)}, u32[]{:S(2)}) %collective-permute-start.33) | collective-permute-done | bytes 147488 | tf_op jit(solution)/shard_map/ppermute | solution.py:577
  97.0 2.9 %collective-permute-done.34.refs_1_ = bf16[1,48,768]{2,1,0:T(8,128)(2,1)S(1)} collective-permute-done((bf16[1,48,768]{2,1,0:T(8,128)(2,1)S(1)}, bf16[1,48,768]{2,1,0:T(8,128)(2,1)S(1)}, u32[]{:S(2)}, u32[]{:S(2)}) %collective-permute-start.34) | collective-permute-done | bytes 73760 | tf_op jit(solution)/shard_map/ppermute | solution.py:577
  (109 shorter events, 18.5 us)
Async XLA Ops:
  0.6 14.4 %collective-permute-start.3 = (bf16[768,768]{1,0:T(8,128)(2,1)}, bf16[768,768]{1,0:T(8,128)(2,1)}, u32[]{:S(2)}, u32[]{:S(2)}) collective-permute-start(bf16[768,768]{1,0:T(8,128)(2,1)} %refs_3_.3), channel_id=1, source_target_pairs={{0,1},{1,0},{2,3},{3,2},{4,5},{5,4},{6,7},{7,6},{8,9},{9,8},{10,11... | collective-permute-start | bytes 3538952 | tf_op jit(solution)/shard_map/ppermute | solution.py:557
  1.2 13.9 %collective-permute-start.4 = (bf16[768,768]{1,0:T(8,128)(2,1)}, bf16[768,768]{1,0:T(8,128)(2,1)}, u32[]{:S(2)}, u32[]{:S(2)}) collective-permute-start(bf16[768,768]{1,0:T(8,128)(2,1)} %refs_5_.1), channel_id=1, source_target_pairs={{0,1},{1,0},{2,3},{3,2},{4,5},{5,4},{6,7},{7,6},{8,9},{9,8},{10,11... | collective-permute-start | bytes 3538952 | tf_op jit(solution)/shard_map/ppermute | solution.py:557
  8.0 2.2 %collective-permute-start = (bf16[256,768]{1,0:T(8,128)(2,1)S(1)}, bf16[256,768]{1,0:T(8,128)(2,1)S(1)}, u32[]{:S(2)}, u32[]{:S(2)}) collective-permute-start(bf16[256,768]{1,0:T(8,128)(2,1)S(1)} %get-tuple-element.358), channel_id=1, source_target_pairs={{0,1},{1,0},{2,3},{3,2},{4,5},{5,4},{6,7},{7,6},{8,9},{9,8},{10,11... | collective-permute-start | bytes 1179656 | tf_op jit(solution)/shard_map/ppermute | solution.py:557
  11.0 9.0 %collective-permute-start.2 = (bf16[128,768]{1,0:T(8,128)(2,1)}, bf16[128,768]{1,0:T(8,128)(2,1)}, u32[]{:S(2)}, u32[]{:S(2)}) collective-permute-start(bf16[128,768]{1,0:T(8,128)(2,1)} %get-tuple-element.363), channel_id=1, source_target_pairs={{0,2},{1,3},{2,0},{3,1},{4,6},{5,7},{6,4},{7,5},{8,10},{9,11},{10,... | collective-permute-start | bytes 589832 | tf_op jit(solution)/shard_map/ppermute | solution.py:561
  14.0 10.4 %collective-permute-start.1 = (bf16[128,768]{1,0:T(8,128)(2,1)}, bf16[128,768]{1,0:T(8,128)(2,1)S(1)}, u32[]{:S(2)}, u32[]{:S(2)}) collective-permute-start(bf16[128,768]{1,0:T(8,128)(2,1)} %copy-done.10), channel_id=1, source_target_pairs={{0,2},{1,3},{2,0},{3,1},{4,6},{5,7},{6,4},{7,5},{8,10},{9,11},{10,... | collective-permute-start | bytes 589832 | tf_op jit(solution)/shard_map/ppermute | solution.py:561
  22.3 7.8 %collective-permute-start.7 = (bf16[128,768]{1,0:T(8,128)(2,1)S(1)}, bf16[128,768]{1,0:T(8,128)(2,1)S(1)}, u32[]{:S(2)}, u32[]{:S(2)}) collective-permute-start(bf16[128,768]{1,0:T(8,128)(2,1)S(1)} %get-tuple-element.401), channel_id=1, source_target_pairs={{0,2},{1,3},{2,0},{3,1},{4,6},{5,7},{6,4},{7,5},{8,10},{9,11},{10,... | collective-permute-start | bytes 589832 | tf_op jit(solution)/shard_map/ppermute | solution.py:561
  23.9 8.6 %collective-permute-start.8 = (bf16[128,768]{1,0:T(8,128)(2,1)S(1)}, bf16[128,768]{1,0:T(8,128)(2,1)S(1)}, u32[]{:S(2)}, u32[]{:S(2)}) collective-permute-start(bf16[128,768]{1,0:T(8,128)(2,1)S(1)} %get-tuple-element.481), channel_id=1, source_target_pairs={{0,1},{1,0},{2,3},{3,2},{4,5},{5,4},{6,7},{7,6},{8,9},{9,8},{10,11... | collective-permute-start | bytes 589832 | tf_op jit(solution)/shard_map/ppermute | solution.py:557
  23.9 8.6 %collective-permute-start.9 = (bf16[128,768]{1,0:T(8,128)(2,1)S(1)}, bf16[128,768]{1,0:T(8,128)(2,1)S(1)}, u32[]{:S(2)}, u32[]{:S(2)}) collective-permute-start(bf16[128,768]{1,0:T(8,128)(2,1)S(1)} %get-tuple-element.482), channel_id=1, source_target_pairs={{0,1},{1,0},{2,3},{3,2},{4,5},{5,4},{6,7},{7,6},{8,9},{9,8},{10,11... | collective-permute-start | bytes 589832 | tf_op jit(solution)/shard_map/ppermute | solution.py:557
  25.7 7.8 %collective-permute-start.6 = (bf16[128,768]{1,0:T(8,128)(2,1)S(1)}, bf16[128,768]{1,0:T(8,128)(2,1)S(1)}, u32[]{:S(2)}, u32[]{:S(2)}) collective-permute-start(bf16[128,768]{1,0:T(8,128)(2,1)S(1)} %get-tuple-element.400), channel_id=1, source_target_pairs={{0,2},{1,3},{2,0},{3,1},{4,6},{5,7},{6,4},{7,5},{8,10},{9,11},{10,... | collective-permute-start | bytes 589832 | tf_op jit(solution)/shard_map/ppermute | solution.py:561
  26.6 6.9 %collective-permute-start.10 = (bf16[128,768]{1,0:T(8,128)(2,1)S(1)}, bf16[128,768]{1,0:T(8,128)(2,1)S(1)}, u32[]{:S(2)}, u32[]{:S(2)}) collective-permute-start(bf16[128,768]{1,0:T(8,128)(2,1)S(1)} %get-tuple-element.483), channel_id=1, source_target_pairs={{0,1},{1,0},{2,3},{3,2},{4,5},{5,4},{6,7},{7,6},{8,9},{9,8},{10,11... | collective-permute-start | bytes 589832 | tf_op jit(solution)/shard_map/ppermute | solution.py:557
  30.1 3.4 %collective-permute-start.11 = (bf16[128,768]{1,0:T(8,128)(2,1)S(1)}, bf16[128,768]{1,0:T(8,128)(2,1)S(1)}, u32[]{:S(2)}, u32[]{:S(2)}) collective-permute-start(bf16[128,768]{1,0:T(8,128)(2,1)S(1)} %get-tuple-element.484), channel_id=1, source_target_pairs={{0,1},{1,0},{2,3},{3,2},{4,5},{5,4},{6,7},{7,6},{8,9},{9,8},{10,11... | collective-permute-start | bytes 589832 | tf_op jit(solution)/shard_map/ppermute | solution.py:557
  36.3 4.3 %collective-permute-start.13 = (bf16[256,768]{1,0:T(8,128)(2,1)S(1)}, bf16[256,768]{1,0:T(8,128)(2,1)S(1)}, u32[]{:S(2)}, u32[]{:S(2)}) collective-permute-start(bf16[256,768]{1,0:T(8,128)(2,1)S(1)} %get-tuple-element.486), channel_id=1, source_target_pairs={{0,1},{1,0},{2,3},{3,2},{4,5},{5,4},{6,7},{7,6},{8,9},{9,8},{10,11... | collective-permute-start | bytes 1179656 | tf_op jit(solution)/shard_map/ppermute | solution.py:557
  36.8 11.0 %collective-permute-start.12 = (bf16[256,768]{1,0:T(8,128)(2,1)S(1)}, bf16[256,768]{1,0:T(8,128)(2,1)S(1)}, u32[]{:S(2)}, u32[]{:S(2)}) collective-permute-start(bf16[256,768]{1,0:T(8,128)(2,1)S(1)} %get-tuple-element.485), channel_id=1, source_target_pairs={{0,2},{1,3},{2,0},{3,1},{4,6},{5,7},{6,4},{7,5},{8,10},{9,11},{10,... | collective-permute-start | bytes 1179656 | tf_op jit(solution)/shard_map/ppermute | solution.py:561
  37.7 10.1 %collective-permute-start.15 = (bf16[256,768]{1,0:T(8,128)(2,1)S(1)}, bf16[256,768]{1,0:T(8,128)(2,1)S(1)}, u32[]{:S(2)}, u32[]{:S(2)}) collective-permute-start(bf16[256,768]{1,0:T(8,128)(2,1)S(1)} %get-tuple-element.572.refs_23_), channel_id=1, source_target_pairs={{0,1},{1,0},{2,3},{3,2},{4,5},{5,4},{6,7},{7,6},{8,9},{9,8},{10,11... | collective-permute-start | bytes 1179656 | tf_op jit(solution)/shard_map/ppermute | solution.py:557
  39.0 11.1 %collective-permute-start.17 = (bf16[4,96,768]{2,1,0:T(8,128)(2,1)S(1)}, bf16[4,96,768]{2,1,0:T(8,128)(2,1)S(1)}, u32[]{:S(2)}, u32[]{:S(2)}) collective-permute-start(bf16[4,96,768]{2,1,0:T(8,128)(2,1)S(1)} %get-tuple-element.575), channel_id=1, source_target_pairs={{0,4},{1,9},{2,6},{3,11},{4,0},{5,13},{6,2},{7,15},{8,12},{9,1},{1... | collective-permute-start | bytes 1769480 | tf_op jit(solution)/shard_map/ppermute | solution.py:577
  48.5 10.6 %collective-permute-start.23 = (bf16[4,96,768]{2,1,0:T(8,128)(2,1)S(1)}, bf16[4,96,768]{2,1,0:T(8,128)(2,1)S(1)}, u32[]{:S(2)}, u32[]{:S(2)}) collective-permute-start(bf16[4,96,768]{2,1,0:T(8,128)(2,1)S(1)} %get-tuple-element.622), channel_id=1, source_target_pairs={{0,4},{1,9},{2,6},{3,11},{4,0},{5,13},{6,2},{7,15},{8,12},{9,1},{1... | collective-permute-start | bytes 1769480 | tf_op jit(solution)/shard_map/ppermute | solution.py:577
  54.7 15.5 %collective-permute-start.18 = (bf16[4,104,768]{2,1,0:T(8,128)(2,1)S(1)}, bf16[4,104,768]{2,1,0:T(8,128)(2,1)S(1)}, u32[]{:S(2)}, u32[]{:S(2)}) collective-permute-start(bf16[4,104,768]{2,1,0:T(8,128)(2,1)S(1)} %get-tuple-element.606), channel_id=1, source_target_pairs={{0,4},{1,9},{2,6},{3,11},{4,0},{5,13},{6,2},{7,15},{8,12},{9,1},{1... | collective-permute-start | bytes 1916936 | tf_op jit(solution)/shard_map/ppermute | solution.py:577
  56.2 9.9 %collective-permute-start.24 = (bf16[2,96,768]{2,1,0:T(8,128)(2,1)S(1)}, bf16[2,96,768]{2,1,0:T(8,128)(2,1)S(1)}, u32[]{:S(2)}, u32[]{:S(2)}) collective-permute-start(bf16[2,96,768]{2,1,0:T(8,128)(2,1)S(1)} %get-tuple-element.623), channel_id=1, source_target_pairs={{0,8},{1,5},{2,10},{3,7},{4,12},{5,1},{6,14},{7,3},{8,0},{9,13},{1... | collective-permute-start | bytes 884744 | tf_op jit(solution)/shard_map/ppermute | solution.py:577
  58.6 7.8 %collective-permute-start.19 = (bf16[64,768]{1,0:T(8,128)(2,1)S(1)}, bf16[64,768]{1,0:T(8,128)(2,1)S(1)}, u32[]{:S(2)}, u32[]{:S(2)}) collective-permute-start(bf16[64,768]{1,0:T(8,128)(2,1)S(1)} %get-tuple-element.618), channel_id=1, source_target_pairs={{0,1},{1,0},{2,3},{3,2},{4,5},{5,4},{6,7},{7,6},{8,9},{9,8},{10,11... | collective-permute-start | bytes 294920 | tf_op jit(solution)/shard_map/ppermute | solution.py:557
  58.6 7.7 %collective-permute-start.20 = (bf16[64,768]{1,0:T(8,128)(2,1)S(1)}, bf16[64,768]{1,0:T(8,128)(2,1)S(1)}, u32[]{:S(2)}, u32[]{:S(2)}) collective-permute-start(bf16[64,768]{1,0:T(8,128)(2,1)S(1)} %get-tuple-element.619), channel_id=1, source_target_pairs={{0,1},{1,0},{2,3},{3,2},{4,5},{5,4},{6,7},{7,6},{8,9},{9,8},{10,11... | collective-permute-start | bytes 294920 | tf_op jit(solution)/shard_map/ppermute | solution.py:557
  59.1 7.2 %collective-permute-start.21 = (bf16[64,768]{1,0:T(8,128)(2,1)S(1)}, bf16[64,768]{1,0:T(8,128)(2,1)S(1)}, u32[]{:S(2)}, u32[]{:S(2)}) collective-permute-start(bf16[64,768]{1,0:T(8,128)(2,1)S(1)} %get-tuple-element.620), channel_id=1, source_target_pairs={{0,1},{1,0},{2,3},{3,2},{4,5},{5,4},{6,7},{7,6},{8,9},{9,8},{10,11... | collective-permute-start | bytes 294920 | tf_op jit(solution)/shard_map/ppermute | solution.py:557
  67.6 14.2 %collective-permute-start.26 = (bf16[256,768]{1,0:T(8,128)(2,1)S(1)}, bf16[256,768]{1,0:T(8,128)(2,1)S(1)}, u32[]{:S(2)}, u32[]{:S(2)}) collective-permute-start(bf16[256,768]{1,0:T(8,128)(2,1)S(1)} %get-tuple-element.643.refs_0_), channel_id=1, source_target_pairs={{0,2},{1,3},{2,0},{3,1},{4,6},{5,7},{6,4},{7,5},{8,10},{9,11},{10,... | collective-permute-start | bytes 1179656 | tf_op jit(solution)/shard_map/ppermute | solution.py:561
  68.6 9.9 %collective-permute-start.28 = (bf16[2,96,768]{2,1,0:T(8,128)(2,1)S(1)}, bf16[2,96,768]{2,1,0:T(8,128)(2,1)S(1)}, u32[]{:S(2)}, u32[]{:S(2)}) collective-permute-start(bf16[2,96,768]{2,1,0:T(8,128)(2,1)S(1)} %get-tuple-element.645), channel_id=1, source_target_pairs={{0,8},{1,5},{2,10},{3,7},{4,12},{5,1},{6,14},{7,3},{8,0},{9,13},{1... | collective-permute-start | bytes 884744 | tf_op jit(solution)/shard_map/ppermute | solution.py:577
  70.3 15.5 %collective-permute-start.25 = (bf16[2,104,768]{2,1,0:T(8,128)(2,1)S(1)}, bf16[2,104,768]{2,1,0:T(8,128)(2,1)S(1)}, u32[]{:S(2)}, u32[]{:S(2)}) collective-permute-start(bf16[2,104,768]{2,1,0:T(8,128)(2,1)S(1)} %get-tuple-element.642), channel_id=1, source_target_pairs={{0,8},{1,5},{2,10},{3,7},{4,12},{5,1},{6,14},{7,3},{8,0},{9,13},{1... | collective-permute-start | bytes 958472 | tf_op jit(solution)/shard_map/ppermute | solution.py:577
  70.8 10.2 %collective-permute-start.27 = (bf16[1,96,768]{2,1,0:T(8,128)(2,1)S(1)}, bf16[1,96,768]{2,1,0:T(8,128)(2,1)S(1)}, u32[]{:S(2)}, u32[]{:S(2)}) collective-permute-start(bf16[1,96,768]{2,1,0:T(8,128)(2,1)S(1)} %get-tuple-element.644), channel_id=1, source_target_pairs={{0,16},{1,17},{2,18},{3,19},{4,20},{5,21},{6,22},{7,23},{8,24},{9,... | collective-permute-start | bytes 442376 | tf_op jit(solution)/shard_map/ppermute | solution.py:577
  81.8 4.5 %collective-permute-start.29 = (bf16[64,768]{1,0:T(8,128)(2,1)S(1)}, bf16[64,768]{1,0:T(8,128)(2,1)S(1)}, u32[]{:S(2)}, u32[]{:S(2)}) collective-permute-start(bf16[64,768]{1,0:T(8,128)(2,1)S(1)} %get-tuple-element.672.refs_0_), channel_id=1, source_target_pairs={{0,1},{1,0},{2,3},{3,2},{4,5},{5,4},{6,7},{7,6},{8,9},{9,8},{10,11... | collective-permute-start | bytes 294920 | tf_op jit(solution)/shard_map/ppermute | solution.py:557
  81.9 4.7 %collective-permute-start.30 = (bf16[64,768]{1,0:T(8,128)(2,1)S(1)}, bf16[64,768]{1,0:T(8,128)(2,1)S(1)}, u32[]{:S(2)}, u32[]{:S(2)}) collective-permute-start(bf16[64,768]{1,0:T(8,128)(2,1)S(1)} %get-tuple-element.673.refs_1_), channel_id=1, source_target_pairs={{0,1},{1,0},{2,3},{3,2},{4,5},{5,4},{6,7},{7,6},{8,9},{9,8},{10,11... | collective-permute-start | bytes 294920 | tf_op jit(solution)/shard_map/ppermute | solution.py:557
  82.4 14.6 %collective-permute-start.33 = (bf16[1,96,768]{2,1,0:T(8,128)(2,1)S(1)}, bf16[1,96,768]{2,1,0:T(8,128)(2,1)S(1)}, u32[]{:S(2)}, u32[]{:S(2)}) collective-permute-start(bf16[1,96,768]{2,1,0:T(8,128)(2,1)S(1)} %get-tuple-element.679), channel_id=1, source_target_pairs={{0,16},{1,17},{2,18},{3,19},{4,20},{5,21},{6,22},{7,23},{8,24},{9,... | collective-permute-start | bytes 442376 | tf_op jit(solution)/shard_map/ppermute | solution.py:577
  85.8 4.5 %collective-permute-start.31 = (bf16[64,768]{1,0:T(8,128)(2,1)S(1)}, bf16[64,768]{1,0:T(8,128)(2,1)S(1)}, u32[]{:S(2)}, u32[]{:S(2)}) collective-permute-start(bf16[64,768]{1,0:T(8,128)(2,1)S(1)} %get-tuple-element.674.refs_2_), channel_id=1, source_target_pairs={{0,1},{1,0},{2,3},{3,2},{4,5},{5,4},{6,7},{7,6},{8,9},{9,8},{10,11... | collective-permute-start | bytes 294920 | tf_op jit(solution)/shard_map/ppermute | solution.py:557
  85.8 4.5 %collective-permute-start.32 = (bf16[64,768]{1,0:T(8,128)(2,1)S(1)}, bf16[64,768]{1,0:T(8,128)(2,1)S(1)}, u32[]{:S(2)}, u32[]{:S(2)}) collective-permute-start(bf16[64,768]{1,0:T(8,128)(2,1)S(1)} %get-tuple-element.675.refs_3_), channel_id=1, source_target_pairs={{0,1},{1,0},{2,3},{3,2},{4,5},{5,4},{6,7},{7,6},{8,9},{9,8},{10,11... | collective-permute-start | bytes 294920 | tf_op jit(solution)/shard_map/ppermute | solution.py:557
  86.4 13.5 %collective-permute-start.35 = (bf16[1,56,768]{2,1,0:T(8,128)(2,1)S(1)}, bf16[1,56,768]{2,1,0:T(8,128)(2,1)S(1)}, u32[]{:S(2)}, u32[]{:S(2)}) collective-permute-start(bf16[1,56,768]{2,1,0:T(8,128)(2,1)S(1)} %get-tuple-element.681), channel_id=1, source_target_pairs={{0,16},{1,17},{2,18},{3,19},{4,20},{5,21},{6,22},{7,23},{8,24},{9,... | collective-permute-start | bytes 258056 | tf_op jit(solution)/shard_map/ppermute | solution.py:577
  86.6 13.3 %collective-permute-start.34 = (bf16[1,48,768]{2,1,0:T(8,128)(2,1)S(1)}, bf16[1,48,768]{2,1,0:T(8,128)(2,1)S(1)}, u32[]{:S(2)}, u32[]{:S(2)}) collective-permute-start(bf16[1,48,768]{2,1,0:T(8,128)(2,1)S(1)} %get-tuple-element.680), channel_id=1, source_target_pairs={{0,16},{1,17},{2,18},{3,19},{4,20},{5,21},{6,22},{7,23},{8,24},{9,... | collective-permute-start | bytes 221192 | tf_op jit(solution)/shard_map/ppermute | solution.py:577
  (22 other events, 57.3 us)
